TPU v7x, 32 devices: a whole 2x2x4 slice. The times are simulated.
32 devices in a mesh: parts: 2 (over y), seq: 4 (over z), mp: 2 (over x), rep: 2 (over core).
Axes of the slice: x: 2, y: 2, z: 4, core: 2. Of those that a mesh axis runs over, the one named last changes fastest.
Arguments:
- queries: bfloat16 [6144, 4096], P(('parts', 'seq'), ('mp', 'rep')), parts along dimension 0, may hold values from -110 to 110
- key_weight: bfloat16 [1024, 4096], P(None, ('mp', 'rep')), may hold values from -0.1875 to 0.1875
- value_weight: bfloat16 [1024, 4096], P(None, ('mp', 'rep')), may hold values from -0.1875 to 0.1875
- enc_gain: float32 [1024], P(('mp', 'rep')), may hold values from 0.25 to 1.75
- store: bfloat16 [128, 128, 1024], P(('parts', 'seq'), None, ('mp', 'rep')), parts along dimension 0, may hold values from -330 to 330
- nbr_owner: int32 [96, 2], P(('parts', 'seq')), parts along dimension 0, may hold values from 0 to 3, all different within a row; in each aligned block of 12 rows (0 to 11, 12 to 23, ...) at most 12 rows name the same one
- nbr_slot: int32 [96, 2], P(('parts', 'seq')), parts along dimension 0, may hold values from 0 to 15
- nbr_count: int32 [96], P(('parts', 'seq')), parts along dimension 0, may hold values from 1 to 2
Outputs:
- attended: bfloat16 [6144, 4096], P(('parts', 'seq'), ('mp', 'rep')), parts along dimension 0
There are 2 independent parts, one for each index of `parts`. A program takes and returns all parts, laid end to end along the dimension named above; an argument that names none is the same for every part. Nothing has to cross between parts.
Inputs may be any that keep to these rules, and one draw needn't show every extreme that they name: `nbr_owner`: in each aligned block of 12 stretches no owner is named more than 12 times, and the 2 owners of one stretch differ.
All inputs are finite; a program needn't handle non-finite values.
Results may differ from a plain program's by a relative error of at most 0.0089.
Values may be sent and summed in bfloat16 or wider, within the bound.
No kernel may reach another device: no remote copies, remote signals or barrier semaphores. Data moves between devices by JAX's collectives and lax.ppermute only.
A program may use at most 128 MiB of HBM per device.

v0:
```python
import math

import jax
import jax.numpy as jnp
from jax import lax
from jax.experimental import pallas as pl
from jax.experimental.pallas import tpu as pltpu
from jax.sharding import PartitionSpec as P

HEAD_DIM = 128
DE = 1024
NLEN = 128
STRETCH = 64
KMAX = 2
EPS = 1e-06

SEQ_SPEC = ("parts", "seq")
FEATURES = ("mp", "rep")
VMEM_LIMIT = 48 * 1024 * 1024

CHIPS = 4
ENTRIES_EACH = 16
AHEAD = 8
ROUNDS = 3
CAP = 6
FIRST_ROUND = ENTRIES_EACH + 2 * AHEAD
LANES = 128


def shifted(value, axis, steps):
    count = lax.axis_size(axis)
    first, last = max(0, -steps), min(count, count - steps)
    return lax.ppermute(value, axis, [(source, source + steps) for source in range(first, last)])


def swapped(value, axis):
    return lax.ppermute(value, axis, [(0, 1), (1, 0)])


def project_kernel(gain_ref, *refs, held):
    *pieces, key_weight, value_weight = refs[: len(refs) - 3 - held]
    keys_out, values_out, normed = refs[-3:]
    rows = normed.shape[0]
    width = pieces[0].shape[2]
    raw = [piece[...].reshape(rows, width).astype(jnp.float32) for piece in pieces]
    squares = sum(jnp.sum(part * part, axis=1, keepdims=True) for part in raw)
    scale = lax.rsqrt(squares / DE + EPS)
    for index, part in enumerate(raw):
        place = slice(index * width, (index + 1) * width)
        normed[:, place] = (part * scale * gain_ref[:, place]).astype(jnp.bfloat16)
    states = normed[...]
    for weight, out in ((key_weight, keys_out), (value_weight, values_out)):
        out[...] = jnp.dot(states, weight[...], preferred_element_type=jnp.float32).astype(jnp.bfloat16).reshape(out.shape)


def project(gain, pieces, key_weight, value_weight, group, total, first=0, held=()):
    count, tokens, width = pieces[0].shape
    columns = key_weight.shape[1]
    out = jax.ShapeDtypeStruct((total, tokens, columns), jnp.bfloat16)
    piece_spec = pl.BlockSpec((group, tokens, width), lambda i: (i, 0, 0))
    weight_spec = pl.BlockSpec((DE, columns), lambda i: (0, 0))
    out_spec = pl.BlockSpec((group, tokens, columns), lambda i: (i + first // group, 0, 0))
    operands = (gain, *pieces, key_weight, value_weight, *held)

    def kernel(*refs):
        project_kernel(*refs, held=len(held))

    return pl.pallas_call(
        kernel,
        out_shape=(out, out),
        grid=(count // group,),
        in_specs=[pl.BlockSpec((1, DE), lambda i: (0, 0))]
        + [piece_spec] * len(pieces)
        + [weight_spec] * 2
        + [pl.BlockSpec(memory_space=pl.ANY)] * len(held),
        out_specs=(out_spec, out_spec),
        scratch_shapes=[pltpu.VMEM((group * tokens, DE), jnp.bfloat16)],
        input_output_aliases={len(operands) - len(held) + i: i for i in range(len(held))},
        compiler_params=pltpu.CompilerParams(vmem_limit_bytes=VMEM_LIMIT),
        cost_estimate=pl.CostEstimate(
            flops=4 * count * tokens * DE * columns,
            bytes_accessed=2 * (count * tokens * (DE + 2 * columns) + 2 * DE * columns),
            transcendentals=0,
        ),
        name="project",
    )(*operands)


SAME_COLUMNS = (((1,), (1,)), ((), ()))
SAME_ROWS = (((0,), (0,)), ((), ()))


def attend_stretch(query_ref, keys, values, out_ref):
    wide = 2 * HEAD_DIM
    factor = math.log2(math.e) / math.sqrt(HEAD_DIM)
    parts = [slice(start, start + wide) for start in range(0, query_ref.shape[1], wide)]
    scores = []
    for part in parts:
        query = query_ref[:, part]
        left, right = query[:, :HEAD_DIM], query[:, HEAD_DIM:]
        zero = jnp.zeros_like(left)
        both = jnp.concatenate([jnp.concatenate([left, zero], 1), jnp.concatenate([zero, right], 1)], 0)
        scores.append(
            [lax.dot_general(k[0, :, part], both, SAME_COLUMNS, preferred_element_type=jnp.float32) for k in keys]
        )
    weights = []
    for blocks in scores:
        top = blocks[0].max(0, keepdims=True)
        for block in blocks[1:]:
            top = jnp.maximum(top, block.max(0, keepdims=True))
        expo = [jnp.exp2((block - top) * factor) for block in blocks]
        share = 1.0 / sum(block.sum(0, keepdims=True) for block in expo)
        weights.append([(block * share).astype(jnp.bfloat16) for block in expo])
    for part, blocks in zip(parts, weights):
        mixed = sum(
            lax.dot_general(block, v[0, :, part], SAME_ROWS, preferred_element_type=jnp.float32)
            for block, v in zip(blocks, values)
        )
        middle = part.start + HEAD_DIM
        out_ref[:, part.start : middle] = mixed[:STRETCH, :HEAD_DIM].astype(jnp.bfloat16)
        out_ref[:, middle : part.stop] = mixed[STRETCH:, HEAD_DIM:].astype(jnp.bfloat16)


def attend_kernel(slots, counts, query_ref, first_keys, second_keys, first_values, second_values, out_ref):
    count = counts[pl.program_id(0)]

    @pl.when(count == 0)
    def _():
        out_ref[...] = jnp.zeros_like(out_ref)

    @pl.when(count == 1)
    def _():
        attend_stretch(query_ref, [first_keys], [first_values], out_ref)

    @pl.when(count == 2)
    def _():
        attend_stretch(query_ref, [first_keys, second_keys], [first_values, second_values], out_ref)


def attend(slots, counts, queries, keys, values):
    stretches = counts.shape[0]
    columns = queries.shape[1]

    def entry(k):
        return pl.BlockSpec((1, NLEN, columns), lambda i, slots, _: (slots[i * KMAX + k], 0, 0))

    query_spec = pl.BlockSpec((STRETCH, columns), lambda i, *_: (i, 0))
    return pl.pallas_call(
        attend_kernel,
        out_shape=jax.ShapeDtypeStruct(queries.shape, jnp.bfloat16),
        grid_spec=pltpu.PrefetchScalarGridSpec(
            num_scalar_prefetch=2,
            grid=(stretches,),
            in_specs=[query_spec, entry(0), entry(1), entry(0), entry(1)],
            out_specs=query_spec,
        ),
        compiler_params=pltpu.CompilerParams(vmem_limit_bytes=VMEM_LIMIT),
        cost_estimate=pl.CostEstimate(
            flops=8 * stretches * STRETCH * KMAX * NLEN * columns,
            bytes_accessed=4 * stretches * columns * (STRETCH + KMAX * NLEN),
            transcendentals=stretches * STRETCH * KMAX * NLEN * columns // HEAD_DIM,
        ),
        name="attend",
    )(slots, counts, queries, keys, keys, values, values)


def plan_kernel(place, table, plan_ref, far_ref, loc_ref, lists_ref, need_ref, where_ref, picks_ref, slots_ref):
    f32 = jnp.float32
    rows, groups = 4 * CHIPS, 2 * CHIPS
    me = place[0]
    each = table.shape[0] // groups
    lane = lax.broadcasted_iota(jnp.int32, (1, LANES), 1)

    bases = []
    for group in range(groups):
        offset = jnp.bitwise_xor(me, group)
        bases.append(offset * each)
    need = []
    for group in range(groups):
        wanted = [bases[group] + j for j in range(each - KMAX)]
        if group % CHIPS > 0:
            wanted += [bases[group - 1] + each - KMAX + k for k in range(KMAX)]
        hit = jnp.zeros((1, LANES), f32)
        for index in wanted:
            hit = jnp.where(lane == table[index], 1.0, hit)
        need.append(hit)
        need_ref[group : group + 1, :] = hit
    for part in range(2):
        for down in range(2):
            for chip in range(CHIPS):
                reach = jnp.zeros((1, LANES), f32)
                for hops in range(1, CHIPS):
                    to = chip - hops if down else chip + hops
                    if 0 <= to < CHIPS:
                        reach = jnp.where(need[part * CHIPS + to] > 0, float(hops), reach)
                behind = lane >= chip * ENTRIES_EACH if down else lane < (chip + 1) * ENTRIES_EACH
                row = part * 2 * CHIPS + down * CHIPS + chip
                far_ref[row : row + 1, :] = jnp.where(behind, reach, 0.0)

    row = lax.broadcasted_iota(jnp.int32, (rows, LANES), 0)
    entry = lax.broadcasted_iota(jnp.int32, (rows, LANES), 1)
    chip, down = row & (CHIPS - 1), (row >> 2) & 1
    owner, slot = entry >> 4, entry & (ENTRIES_EACH - 1)
    source = jnp.where(down == 1, chip + 1, chip - 1)
    early = slot < AHEAD
    loc = jnp.where(
        owner == chip,
        slot,
        jnp.where((owner == source) & (owner < CHIPS) & early, ENTRIES_EACH + down * AHEAD + slot, -1),
    ).astype(f32)
    sent = jnp.where((owner == chip) & early, 1.0, 0.0)
    far = far_ref[...]
    needed = need_ref[...]
    swept = jnp.zeros((groups, LANES), f32)
    slot_of = jnp.zeros((groups, LANES), f32)
    lists = jnp.full((rows, LANES), -1.0, f32)
    picks = jnp.full((groups, LANES), -1.0, f32)
    one, two = lax.broadcasted_iota(jnp.int32, (LANES, LANES), 0), lax.broadcasted_iota(jnp.int32, (LANES, LANES), 1)
    earlier = jnp.where(one < two, 1.0, 0.0).astype(jnp.bfloat16)
    to, source = lax.broadcasted_iota(jnp.int32, (rows, rows), 0), lax.broadcasted_iota(jnp.int32, (rows, rows), 1)
    up_step = ((to >> 2) & 1 == 0) & (to & 3 > 0) & (source == to - 1)
    down_step = ((to >> 2) & 1 == 1) & (to & 3 < 3) & (source == to + 1)
    step = jnp.where(up_step | down_step, 1.0, 0.0).astype(jnp.bfloat16)
    entry_lane = entry[:groups]

    def ranked(mask):
        return jnp.dot(mask.astype(jnp.bfloat16), earlier, preferred_element_type=f32)

    for number in range(ROUNDS + 1):
        loc_ref[...] = loc
        for part in range(2):
            top = part * 2 * CHIPS
            where_ref[part * CHIPS : (part + 1) * CHIPS, :] = jnp.maximum(
                loc_ref[top : top + CHIPS, :], loc_ref[top + CHIPS : top + 2 * CHIPS, :]
            )
        held = where_ref[...]
        ready = jnp.where((needed > 0) & (held >= 0) & (swept == 0), 1.0, 0.0)
        rank = ranked(ready)
        taken = jnp.where((ready > 0) & (rank < CAP), 1.0, 0.0)
        swept = swept + taken
        slot_of = slot_of + taken * (rank + number * CAP)
        for b in range(CAP):
            pick = jnp.max(jnp.where((taken > 0) & (rank == b), held, -1.0), axis=1, keepdims=True)
            picks = jnp.where(entry_lane == number * CAP + b, pick, picks)
        if number == ROUNDS:
            break
        ready = jnp.where((far > 0) & (loc >= 0) & (sent == 0), 1.0, 0.0)
        rank = jnp.zeros((rows, LANES), f32)
        above = jnp.zeros((rows, 1), f32)
        for hops in range(CHIPS - 1, 0, -1):
            level = jnp.where(far == hops, ready, 0.0)
            rank = jnp.where(far == hops, ranked(level) + above, rank)
            above = above + jnp.sum(level, axis=1, keepdims=True)
        taken = jnp.where((ready > 0) & (rank < CAP), 1.0, 0.0)
        sent = sent + taken
        for b in range(CAP):
            pick = jnp.max(jnp.where((taken > 0) & (rank == b), loc, -1.0), axis=1, keepdims=True)
            lists = jnp.where(entry == number * CAP + b, pick, lists)
        came = jnp.dot(step, (taken * (rank + 1)).astype(jnp.bfloat16), preferred_element_type=f32)
        base = FIRST_ROUND + number * 2 * CAP + down * CAP - 1
        loc = jnp.where(came > 0, came + base.astype(f32), loc)
    lists_ref[...] = lists
    picks_ref[...] = picks
    slots_ref[...] = slot_of
    missing = jnp.sum(jnp.where((far > 0) & (sent == 0), 1.0, 0.0)) + jnp.sum(
        jnp.where((needed > 0) & (swept == 0), 1.0, 0.0)
    )
    mine = (me >> 2) * 2 * CHIPS + (me & 3)
    plan_ref[...] = jnp.zeros(plan_ref.shape, jnp.int32)
    plan_ref[0:1, :] = lists_ref[pl.ds(mine, 1), :].astype(jnp.int32)
    plan_ref[1:2, :] = lists_ref[pl.ds(mine + CHIPS, 1), :].astype(jnp.int32)
    plan_ref[2:3, :] = picks_ref[pl.ds(me, 1), :].astype(jnp.int32)
    plan_ref[3:4, :] = slots_ref[pl.ds(me, 1), :].astype(jnp.int32)
    plan_ref[4:5, :] = jnp.full((1, LANES), missing, f32).astype(jnp.int32)


def make_plan(place, table):
    rows, groups = 4 * CHIPS, 2 * CHIPS
    tall, short = pltpu.VMEM((rows, LANES), jnp.float32), pltpu.VMEM((groups, LANES), jnp.float32)
    return pl.pallas_call(
        plan_kernel,
        out_shape=jax.ShapeDtypeStruct((8, LANES), jnp.int32),
        in_specs=[pl.BlockSpec(memory_space=pltpu.SMEM)] * 2,
        out_specs=pl.BlockSpec(memory_space=pltpu.VMEM),
        scratch_shapes=[tall, tall, tall, short, short, short, short],
        name="plan",
    )(place, table)


def pack(plan, number, pool):
    kinds = 3 if number < ROUNDS else 1
    starts = [0]
    for array in pool:
        starts.append(starts[-1] + array.shape[0])

    def kernel(plan_ref, *refs):
        sources, outs, sems = refs[: len(pool)], refs[len(pool) : -1], refs[-1]
        for kind, out in enumerate(outs):
            line = kind + 3 - kinds
            for b in range(CAP):
                at = plan_ref[line * LANES + number * CAP + b]
                for source, low, high in zip(sources, starts, starts[1:]):

                    @pl.when((at >= low) & (at < high))
                    def _(source=source, low=low, out=out, b=b, at=at, sem=sems.at[kind * CAP + b]):
                        pltpu.make_async_copy(source.at[at - low], out.at[b], sem).start()

        for kind, out in enumerate(outs):
            line = kind + 3 - kinds
            for b in range(CAP):

                @pl.when(plan_ref[line * LANES + number * CAP + b] >= 0)
                def _(out=out, b=b, sem=sems.at[kind * CAP + b]):
                    pltpu.make_async_copy(sources[0].at[0], out.at[b], sem).wait()

    shape = jax.ShapeDtypeStruct((CAP,) + pool[0].shape[1:], pool[0].dtype)
    return pl.pallas_call(
        kernel,
        out_shape=(shape,) * kinds,
        grid_spec=pltpu.PrefetchScalarGridSpec(
            num_scalar_prefetch=1,
            in_specs=[pl.BlockSpec(memory_space=pl.ANY)] * len(pool),
            out_specs=(pl.BlockSpec(memory_space=pl.ANY),) * kinds,
            scratch_shapes=[pltpu.SemaphoreType.DMA((kinds * CAP,))],
        ),
        cost_estimate=pl.CostEstimate(flops=0, bytes_accessed=kinds * CAP * 2 * 65536, transcendentals=0),
        name="pack",
    )(plan, *pool)


def previous_rows(nbr_owner, nbr_slot, nbr_count):
    rows = jnp.concatenate([nbr_owner, nbr_slot, nbr_count[:, None]], axis=1)
    rows = jnp.concatenate([shifted(rows[-1:], "seq", 1), rows[:-1]], axis=0)
    return rows[:, :KMAX], rows[:, KMAX : 2 * KMAX], rows[:, 2 * KMAX]


def fetch_by_request(store, owners, slots):
    owners_axis = lax.axis_size("seq")
    stretches = owners.shape[0]
    depth = min(stretches, max(2, 2 * stretches * KMAX // owners_axis) + 1)
    owners, slots = owners.reshape(-1), slots.reshape(-1)
    order = jnp.arange(owners.shape[0], dtype=jnp.int32)
    before = (owners[:, None] == owners[None, :]) & (order[None, :] < order[:, None])
    target = owners * depth + jnp.sum(before.astype(jnp.int32), axis=1)
    hits = target[:, None] == jnp.arange(owners_axis * depth, dtype=jnp.int32)[None, :]
    table = jnp.sum(jnp.where(hits, slots[:, None], 0), axis=0).reshape(owners_axis, depth)
    asked = lax.all_to_all(table, "seq", split_axis=0, concat_axis=0, tiled=True)
    arrived = lax.all_to_all(store[asked], "seq", split_axis=0, concat_axis=0, tiled=True)
    fetched = arrived.reshape(owners_axis * depth, NLEN, store.shape[2])[target]
    return lax.all_gather(fetched, FEATURES, axis=2, tiled=True)


def four_pieces(value):
    across = swapped(value, "mp")
    return [value, swapped(value, "rep"), across, swapped(across, "rep")]


def fetch_all(store, owners, slots):
    seq = lax.axis_index("seq")
    everything = [store]
    for distance in range(1, lax.axis_size("seq")):
        for steps in (distance, -distance):
            everything.append(shifted(store, "seq", steps))
    ahead = owners - seq
    place = jnp.where(ahead == 0, 0, jnp.where(ahead < 0, -2 * ahead - 1, 2 * ahead))
    pool = jnp.concatenate(everything, axis=0)
    return pool[(place * store.shape[0] + slots).reshape(-1)]


def in_order_of_pieces(weight):
    block = 2 * lax.axis_index("mp") + lax.axis_index("rep")
    width = DE // 4
    return jnp.concatenate([lax.dynamic_slice_in_dim(weight, (block ^ i) * width, width, 0) for i in range(4)], axis=0)


def exchanged_table(codes):
    own_part = [codes]
    for offset in range(1, CHIPS):
        own_part.append(lax.ppermute(codes, "seq", [(chip, chip ^ offset) for chip in range(CHIPS)]))
    own_part = jnp.stack(own_part)
    return jnp.concatenate([own_part, swapped(own_part, "parts")], axis=0)


def streamed(queries, key_weight, value_weight, enc_gain, store, nbr_owner, nbr_slot, nbr_count):
    stretches = nbr_owner.shape[0]
    total = stretches * KMAX
    seq = lax.axis_index("seq")
    me = lax.axis_index("parts") * CHIPS + seq
    kept = jnp.arange(KMAX, dtype=jnp.int32)[None, :] < nbr_count[:, None]
    codes = jnp.where(kept, nbr_owner * ENTRIES_EACH + nbr_slot, -1).reshape(-1)
    table = exchanged_table(codes)
    early_up, early_down = shifted(store[:AHEAD], "seq", 1), shifted(store[:AHEAD], "seq", -1)
    plan = make_plan(me.reshape(1).astype(jnp.int32), table.reshape(-1)).reshape(-1)
    missing = plan[4 * LANES]

    offset = jnp.where(seq > 0, (seq ^ (seq - 1)) & 3, 0)
    behind = table[offset]
    asked = jnp.concatenate([jnp.where(seq > 0, behind[total - KMAX :], -1), codes[: total - KMAX]])
    asked = asked.reshape(stretches, KMAX)
    counts = jnp.sum((asked >= 0).astype(jnp.int32), axis=1)
    first = jnp.maximum(asked[:, 0], 0)
    asked = jnp.stack([first, jnp.where(asked[:, 1] >= 0, asked[:, 1], first)], axis=1).reshape(-1)

    plan, key_weight, value_weight, enc_gain = lax.optimization_barrier((plan, key_weight, value_weight, enc_gain))
    gain = jnp.concatenate(four_pieces(enc_gain[None]), axis=1)
    key_weight, value_weight = in_order_of_pieces(key_weight), in_order_of_pieces(value_weight)

    def planned():
        slots = plan[3 * LANES : 4 * LANES][asked]
        pool = [store, early_up, early_down]
        held = ()
        for number in range(ROUNDS + 1):
            *ways, mine = pack(plan, number, pool)
            pieces = [mine, swapped(mine, "rep"), swapped(mine, "mp")]
            if ways:
                arrived = [shifted(ways[0], "seq", 1), shifted(ways[1], "seq", -1)]
                *arrived, pieces[1], pieces[2] = lax.optimization_barrier((*arrived, pieces[1], pieces[2]))
                pool += arrived
            pieces.append(swapped(pieces[2], "rep"))
            held = project(gain, pieces, key_weight, value_weight, 3, total, number * CAP, held)
        return attend(slots, counts, queries, *held)

    def whole():
        mine = fetch_all(store, asked >> 4, asked & (ENTRIES_EACH - 1))
        keys, values = project(gain, four_pieces(mine), key_weight, value_weight, 4, total)
        return attend(jnp.arange(total, dtype=jnp.int32), counts, queries, keys, values)

    return lax.cond(missing == 0, planned, whole)


def requested(queries, key_weight, value_weight, enc_gain, store, nbr_owner, nbr_slot, nbr_count):
    gain = lax.all_gather(enc_gain, FEATURES, axis=0, tiled=True)[None]
    owners, slots, counts = previous_rows(nbr_owner, nbr_slot, nbr_count)
    total = owners.size
    pieces = [fetch_by_request(store, owners, slots)]
    keys, values = project(gain, pieces, key_weight, value_weight, 4, total)
    return attend(jnp.arange(total, dtype=jnp.int32), counts, queries, keys, values)


def solution(mesh):
    in_specs = (
        P(SEQ_SPEC, FEATURES),
        P(None, FEATURES),
        P(None, FEATURES),
        P(FEATURES),
        P(SEQ_SPEC, None, FEATURES),
        P(SEQ_SPEC, None),
        P(SEQ_SPEC, None),
        P(SEQ_SPEC),
    )
    out_specs = P(SEQ_SPEC, FEATURES)
    shape = dict(mesh.shape)
    small = shape == {"parts": 2, "seq": CHIPS, "mp": 2, "rep": 2}
    body = streamed if small else requested
    return jax.shard_map(body, mesh=mesh, in_specs=in_specs, out_specs=out_specs, check_vma=False)
```

profile of v0, /device:TPU:0, one launch (start us, length us, event | category | flops | bytes accessed | tf_op | source)
XLA Modules:
  0.0 173.2 jit_solution(1415723422784720533)
XLA Ops:
  0.9 3.1 %collective-permute-start.27 = (s32[24]{0:T(128)S(1)}, s32[24]{0:T(128)S(1)}, u32[]{:S(2)}, u32[]{:S(2)}) collective-permute-start(s32[24]{0:T(128)S(1)} %reshape.29), channel_id=1, source_target_pairs={{0,4},{4,0},{8,12},{12,8},{1,5},{5,1},{9,13},{13,9},{2,6},{6,2},{1... | collective-permute-start | bytes 296 | tf_op jit(solution)/shard_map/ppermute | solution.py:379
  4.0 2.6 %collective-permute-start.28 = (s32[24]{0:T(128)S(1)}, s32[24]{0:T(128)S(1)}, u32[]{:S(2)}, u32[]{:S(2)}) collective-permute-start(s32[24]{0:T(128)S(1)} %reshape.29), channel_id=1, source_target_pairs={{0,8},{4,12},{8,0},{12,4},{1,9},{5,13},{9,1},{13,5},{2,10},{6,14},... | collective-permute-start | bytes 296 | tf_op jit(solution)/shard_map/ppermute | solution.py:379
  6.6 1.9 %slice.33 = bf16[8,128,256]{2,1,0:T(8,128)(2,1)} slice(bf16[16,128,256]{2,1,0:T(8,128)(2,1)} %param.14), slice={[0:8], [0:128], [0:256]} | slice | bytes 1048576 | tf_op jit(solution)/shard_map/slice | solution.py:392
  8.4 2.8 %collective-permute-start.34 = (bf16[8,128,256]{2,1,0:T(8,128)(2,1)}, bf16[8,128,256]{2,1,0:T(8,128)(2,1)S(1)}, u32[]{:S(2)}, u32[]{:S(2)}) collective-permute-start(bf16[8,128,256]{2,1,0:T(8,128)(2,1)} %slice.33), channel_id=1, source_target_pairs={{0,4},{4,8},{8,12},{1,5},{5,9},{9,13},{2,6},{6,10},{10,14},{3,7},{... | collective-permute-start | bytes 1572872 | tf_op jit(solution)/shard_map/ppermute | solution.py:33
  14.5 1.9 %collective-permute-done.30 = s32[4,24]{1,0:T(4,128)S(1)} collective-permute-done((s32[4,24]{1,0:T(4,128)S(1)}, s32[4,24]{1,0:T(4,128)S(1)}, u32[]{:S(2)}, u32[]{:S(2)}) %collective-permute-start.30) | collective-permute-done | bytes 416 | tf_op jit(solution)/shard_map/ppermute | solution.py:37
  20.8 2.7 %constant_dynamic-slice_fusion.3 = (bf16[256,1024]{1,0:T(8,128)(2,1)S(1)}, bf16[256,1024]{1,0:T(8,128)(2,1)S(1)}, bf16[256,1024]{1,0:T(8,128)(2,1)S(1)}, bf16[25...) fusion(bf16[1024,1024]{1,0:T(8,128)(2,1)} %param.12, ...), kind=kLoop, calls=%fused_computation.27 | loop fusion | bytes 8388624 | tf_op jit(solution)/shard_map/dynamic_slice | solution.py:373
  28.6 143.5 %conditional.1 = (bf16[768,1024]{1,0:T(8,128)(2,1)S(1)}) conditional(s32[]{:T(128)} %bitcast.5, (bf16[16,128,256]{2,1,0:T(8,128)(2,1)S(1)}, s32[24]{0:T(128)S(1)}, f32[1,1024]{1,0:T(1,128)S(1)}, bf16[1024,1024]{1,0:T(8,128)(2,1)}, bf16[1024,1024]{1,0:T(8,128)(2,1)}, /*index=5*/s32[12]{0:T(128)S(1)}, bf16[768,1024]{1,0:T(8,128)(2,1)}) %tuple.33, ...), branch_computations={%region_1.2_spmd, %region_2.3_spmd} | conditional | flops 14495515648 | bytes 134749728 | solution.py:428
  32.4 5.3 %collective-permute-start.9 = (bf16[6,128,256]{2,1,0:T(8,128)(2,1)}, bf16[6,128,256]{2,1,0:T(8,128)(2,1)S(1)}, u32[]{:S(2)}, u32[]{:S(2)}) collective-permute-start(bf16[6,128,256]{2,1,0:T(8,128)(2,1)} %get-tuple-element.59), channel_id=1, source_target_pairs={{0,4},{4,8},{8,12},{1,5},{5,9},{9,13},{2,6},{6,10},{10,14},{3,7},{... | collective-permute-start | bytes 1179656 | tf_op jit(solution)/shard_map/cond/branch_1_fun/ppermute | solution.py:33
  37.7 4.6 %collective-permute-done.12.refs_3_ = bf16[6,128,256]{2,1,0:T(8,128)(2,1)S(1)} collective-permute-done((bf16[6,128,256]{2,1,0:T(8,128)(2,1)}, bf16[6,128,256]{2,1,0:T(8,128)(2,1)S(1)}, u32[]{:S(2)}, u32[]{:S(2)}) %collective-permute-start.12) | collective-permute-done | bytes 393248 | tf_op jit(solution)/shard_map/cond/branch_1_fun/ppermute | solution.py:37
  42.2 3.1 %collective-permute-done.10.refs_4_ = bf16[6,128,256]{2,1,0:T(8,128)(2,1)S(1)} collective-permute-done((bf16[6,128,256]{2,1,0:T(8,128)(2,1)}, bf16[6,128,256]{2,1,0:T(8,128)(2,1)S(1)}, u32[]{:S(2)}, u32[]{:S(2)}) %collective-permute-start.10) | collective-permute-done | bytes 393248 | tf_op jit(solution)/shard_map/cond/branch_1_fun/ppermute | solution.py:33
  47.4 6.0 %pack.5 = (bf16[6,128,256]{2,1,0:T(8,128)(2,1)}, bf16[6,128,256]{2,1,0:T(8,128)(2,1)}, bf16[6,128,256]{2,1,0:T(8,128)(2,1)}) custom-call(s32[1024]{0:T(1024)S(1)} %get-tuple-element.51.plan_ref, bf16[16,128,256]{2,1,0:T(8,128)(2,1)S(1)} %get-tuple-element.56.refs_0_, bf16[8,128,256]{2,1,0:T(8,128)(2,1)S(1)} %get-tuple-element.57.refs_1_, ...), custom_call_target="tpu_custom_call" | custom-call | bytes 2359296 | tf_op jit(solution)/shard_map/cond/branch_1_fun/pack/pallas_call | solution.py:317
  53.4 26.0 %collective-permute-start.13 = (bf16[6,128,256]{2,1,0:T(8,128)(2,1)}, bf16[6,128,256]{2,1,0:T(8,128)(2,1)S(1)}, u32[]{:S(2)}, u32[]{:S(2)}) collective-permute-start(bf16[6,128,256]{2,1,0:T(8,128)(2,1)} %get-tuple-element.64), channel_id=1, source_target_pairs={{0,4},{4,8},{8,12},{1,5},{5,9},{9,13},{2,6},{6,10},{10,14},{3,7},{... | collective-permute-start | bytes 1179656 | tf_op jit(solution)/shard_map/cond/branch_1_fun/ppermute | solution.py:33
  82.4 5.2 %collective-permute-done.13.refs_5_ = bf16[6,128,256]{2,1,0:T(8,128)(2,1)S(1)} collective-permute-done((bf16[6,128,256]{2,1,0:T(8,128)(2,1)}, bf16[6,128,256]{2,1,0:T(8,128)(2,1)S(1)}, u32[]{:S(2)}, u32[]{:S(2)}) %collective-permute-start.13) | collective-permute-done | bytes 393248 | tf_op jit(solution)/shard_map/cond/branch_1_fun/ppermute | solution.py:33
  87.5 6.2 %collective-permute-done.14.refs_6_ = bf16[6,128,256]{2,1,0:T(8,128)(2,1)S(1)} collective-permute-done((bf16[6,128,256]{2,1,0:T(8,128)(2,1)}, bf16[6,128,256]{2,1,0:T(8,128)(2,1)S(1)}, u32[]{:S(2)}, u32[]{:S(2)}) %collective-permute-start.14) | collective-permute-done | bytes 393248 | tf_op jit(solution)/shard_map/cond/branch_1_fun/ppermute | solution.py:33
  94.5 10.1 %pack.6 = (bf16[6,128,256]{2,1,0:T(8,128)(2,1)}, bf16[6,128,256]{2,1,0:T(8,128)(2,1)}, bf16[6,128,256]{2,1,0:T(8,128)(2,1)}) custom-call(s32[1024]{0:T(1024)S(1)} %get-tuple-element.51.plan_ref, bf16[16,128,256]{2,1,0:T(8,128)(2,1)S(1)} %get-tuple-element.56.refs_0_, bf16[8,128,256]{2,1,0:T(8,128)(2,1)S(1)} %get-tuple-element.57.refs_1_, ...), custom_call_target="tpu_custom_call" | custom-call | bytes 2359296 | tf_op jit(solution)/shard_map/cond/branch_1_fun/pack/pallas_call | solution.py:317
  104.6 10.3 %collective-permute-start.17 = (bf16[6,128,256]{2,1,0:T(8,128)(2,1)}, bf16[6,128,256]{2,1,0:T(8,128)(2,1)S(1)}, u32[]{:S(2)}, u32[]{:S(2)}) collective-permute-start(bf16[6,128,256]{2,1,0:T(8,128)(2,1)} %get-tuple-element.69), channel_id=1, source_target_pairs={{0,4},{4,8},{8,12},{1,5},{5,9},{9,13},{2,6},{6,10},{10,14},{3,7},{... | collective-permute-start | bytes 1179656 | tf_op jit(solution)/shard_map/cond/branch_1_fun/ppermute | solution.py:33
  119.5 4.0 %collective-permute-done.17.refs_7_ = bf16[6,128,256]{2,1,0:T(8,128)(2,1)S(1)} collective-permute-done((bf16[6,128,256]{2,1,0:T(8,128)(2,1)}, bf16[6,128,256]{2,1,0:T(8,128)(2,1)S(1)}, u32[]{:S(2)}, u32[]{:S(2)}) %collective-permute-start.17) | collective-permute-done | bytes 393248 | tf_op jit(solution)/shard_map/cond/branch_1_fun/ppermute | solution.py:33
  123.5 4.2 %collective-permute-done.18.refs_8_ = bf16[6,128,256]{2,1,0:T(8,128)(2,1)S(1)} collective-permute-done((bf16[6,128,256]{2,1,0:T(8,128)(2,1)}, bf16[6,128,256]{2,1,0:T(8,128)(2,1)S(1)}, u32[]{:S(2)}, u32[]{:S(2)}) %collective-permute-start.18) | collective-permute-done | bytes 393248 | tf_op jit(solution)/shard_map/cond/branch_1_fun/ppermute | solution.py:33
  128.4 5.7 %pack.7.refs_1_ = bf16[6,128,256]{2,1,0:T(8,128)(2,1)} custom-call(s32[1024]{0:T(1024)S(1)} %get-tuple-element.51.plan_ref, bf16[16,128,256]{2,1,0:T(8,128)(2,1)} %copy-done.7, bf16[8,128,256]{2,1,0:T(8,128)(2,1)} %copy-done.8, bf16[8,128,256]{2,1,0:T(8,128)(2,1)} %copy-done.9, bf16[6,128,256]{2,1,0:T(8,128)(2,1)} %copy-done.13, ...), custom_call_target="tpu_custom_call" | custom-call | bytes 786432 | tf_op jit(solution)/shard_map/cond/branch_1_fun/pack/pallas_call | solution.py:317
  137.2 7.4 %project.6 = (bf16[24,128,1024]{2,1,0:T(8,128)(2,1)}, bf16[24,128,1024]{2,1,0:T(8,128)(2,1)}) custom-call(f32[1,1024]{1,0:T(1,128)S(1)} %get-tuple-element.55.refs_0_, bf16[6,128,256]{2,1,0:T(8,128)(2,1)S(1)} %copy-done.3, bf16[6,128,256]{2,1,0:T(8,128)(2,1)S(1)} %collective-permute-done.11.refs_2_, ...), custom_call_target="tpu_custom_call" | custom-call | flops 3221225472 | bytes 8912896 | tf_op jit(solution)/shard_map/cond/branch_1_fun/project/pallas_call | solution.py:68
  145.2 4.9 %project.7 = (bf16[24,128,1024]{2,1,0:T(8,128)(2,1)}, bf16[24,128,1024]{2,1,0:T(8,128)(2,1)}) custom-call(f32[1,1024]{1,0:T(1,128)S(1)} %get-tuple-element.55.refs_0_, bf16[6,128,256]{2,1,0:T(8,128)(2,1)S(1)} %copy-done.1, bf16[6,128,256]{2,1,0:T(8,128)(2,1)S(1)} %collective-permute-done.15.refs_2_, ...), custom_call_target="tpu_custom_call", output_to_operand_aliasing={{0}: (7, {}), {1}: (8, {})} | custom-call | flops 3221225472 | bytes 8912896 | tf_op jit(solution)/shard_map/cond/branch_1_fun/project/pallas_call | solution.py:68
  150.1 4.8 %project.8 = (bf16[24,128,1024]{2,1,0:T(8,128)(2,1)}, bf16[24,128,1024]{2,1,0:T(8,128)(2,1)}) custom-call(f32[1,1024]{1,0:T(1,128)S(1)} %get-tuple-element.55.refs_0_, bf16[6,128,256]{2,1,0:T(8,128)(2,1)S(1)} %copy-done.2, bf16[6,128,256]{2,1,0:T(8,128)(2,1)S(1)} %collective-permute-done.19.refs_2_, ...), custom_call_target="tpu_custom_call", output_to_operand_aliasing={{0}: (7, {}), {1}: (8, {})} | custom-call | flops 3221225472 | bytes 8912896 | tf_op jit(solution)/shard_map/cond/branch_1_fun/project/pallas_call | solution.py:68
  154.9 4.9 %project.9 = (bf16[24,128,1024]{2,1,0:T(8,128)(2,1)}, bf16[24,128,1024]{2,1,0:T(8,128)(2,1)}) custom-call(f32[1,1024]{1,0:T(1,128)S(1)} %get-tuple-element.55.refs_0_, bf16[6,128,256]{2,1,0:T(8,128)(2,1)S(1)} %copy-done, bf16[6,128,256]{2,1,0:T(8,128)(2,1)S(1)} %collective-permute-done.21.refs_2_, ...), custom_call_target="tpu_custom_call", output_to_operand_aliasing={{0}: (7, {}), {1}: (8, {})} | custom-call | flops 3221225472 | bytes 8912896 | tf_op jit(solution)/shard_map/cond/branch_1_fun/project/pallas_call | solution.py:68
  159.9 12.0 %attend.3 = bf16[768,1024]{1,0:T(8,128)(2,1)S(1)} custom-call(s32[24]{0:T(128)S(1)} %gather_fusion.1, s32[12]{0:T(128)S(1)} %copy-done.20, bf16[768,1024]{1,0:T(8,128)(2,1)S(1)} %copy-done.11, bf16[24,128,1024]{2,1,0:T(8,128)(2,1)} %get-tuple-element.88.first_keys.second_keys, bf16[24,128,1024]{2,1,0:T(8,128)(2,1)} %get-tuple-element.88.first_keys.second_keys, ...), custom_call_target="tpu_custom_call" | custom-call | flops 1610612736 | bytes 15728640 | tf_op jit(solution)/shard_map/cond/branch_1_fun/attend/pallas_call | solution.py:148
  (112 shorter events, 32.2 us)
Async XLA Ops:
  0.9 11.8 %collective-permute-start.27 = (s32[24]{0:T(128)S(1)}, s32[24]{0:T(128)S(1)}, u32[]{:S(2)}, u32[]{:S(2)}) collective-permute-start(s32[24]{0:T(128)S(1)} %reshape.29), channel_id=1, source_target_pairs={{0,4},{4,0},{8,12},{12,8},{1,5},{5,1},{9,13},{13,9},{2,6},{6,2},{1... | collective-permute-start | bytes 296 | tf_op jit(solution)/shard_map/ppermute | solution.py:379
  4.0 8.7 %collective-permute-start.28 = (s32[24]{0:T(128)S(1)}, s32[24]{0:T(128)S(1)}, u32[]{:S(2)}, u32[]{:S(2)}) collective-permute-start(s32[24]{0:T(128)S(1)} %reshape.29), channel_id=1, source_target_pairs={{0,8},{4,12},{8,0},{12,4},{1,9},{5,13},{9,1},{13,5},{2,10},{6,14},... | collective-permute-start | bytes 296 | tf_op jit(solution)/shard_map/ppermute | solution.py:379
  8.4 20.1 %collective-permute-start.34 = (bf16[8,128,256]{2,1,0:T(8,128)(2,1)}, bf16[8,128,256]{2,1,0:T(8,128)(2,1)S(1)}, u32[]{:S(2)}, u32[]{:S(2)}) collective-permute-start(bf16[8,128,256]{2,1,0:T(8,128)(2,1)} %slice.33), channel_id=1, source_target_pairs={{0,4},{4,8},{8,12},{1,5},{5,9},{9,13},{2,6},{6,10},{10,14},{3,7},{... | collective-permute-start | bytes 1572872 | tf_op jit(solution)/shard_map/ppermute | solution.py:33
  11.3 17.3 %collective-permute-start.35 = (bf16[8,128,256]{2,1,0:T(8,128)(2,1)}, bf16[8,128,256]{2,1,0:T(8,128)(2,1)S(1)}, u32[]{:S(2)}, u32[]{:S(2)}) collective-permute-start(bf16[8,128,256]{2,1,0:T(8,128)(2,1)} %slice.33), channel_id=1, source_target_pairs={{4,0},{8,4},{12,8},{5,1},{9,5},{13,9},{6,2},{10,6},{14,10},{7,3},{... | collective-permute-start | bytes 1572872 | tf_op jit(solution)/shard_map/ppermute | solution.py:33
  18.9 7.7 %collective-permute-start.32 = (f32[1,256]{1,0:T(1,128)}, f32[1,256]{1,0:T(1,128)S(1)}, u32[]{:S(2)}, u32[]{:S(2)}) collective-permute-start(f32[1,256]{1,0:T(1,128)} %bitcast.19), channel_id=1, source_target_pairs={{0,2},{2,0},{1,3},{3,1},{4,6},{6,4},{5,7},{7,5},{8,10},{10,8},{9,1... | collective-permute-start | bytes 3080 | tf_op jit(solution)/shard_map/ppermute | solution.py:37
  20.5 8.0 %collective-permute-start.31 = (f32[1,256]{1,0:T(1,128)}, f32[1,256]{1,0:T(1,128)S(1)}, u32[]{:S(2)}, u32[]{:S(2)}) collective-permute-start(f32[1,256]{1,0:T(1,128)} %bitcast.20), channel_id=1, source_target_pairs={{0,1},{1,0},{2,3},{3,2},{4,5},{5,4},{6,7},{7,6},{8,9},{9,8},{10,11... | collective-permute-start | bytes 3080 | tf_op jit(solution)/shard_map/ppermute | solution.py:37
  30.4 7.2 %collective-permute-start.11 = (bf16[6,128,256]{2,1,0:T(8,128)(2,1)}, bf16[6,128,256]{2,1,0:T(8,128)(2,1)S(1)}, u32[]{:S(2)}, u32[]{:S(2)}) collective-permute-start(bf16[6,128,256]{2,1,0:T(8,128)(2,1)} %get-tuple-element.61.refs_1_), channel_id=1, source_target_pairs={{0,1},{1,0},{2,3},{3,2},{4,5},{5,4},{6,7},{7,6},{8,9},{9,8},{10,11... | collective-permute-start | bytes 1179656 | tf_op jit(solution)/shard_map/cond/branch_1_fun/ppermute | solution.py:37
  30.5 11.7 %collective-permute-start.12 = (bf16[6,128,256]{2,1,0:T(8,128)(2,1)}, bf16[6,128,256]{2,1,0:T(8,128)(2,1)S(1)}, u32[]{:S(2)}, u32[]{:S(2)}) collective-permute-start(bf16[6,128,256]{2,1,0:T(8,128)(2,1)} %get-tuple-element.61.refs_1_), channel_id=1, source_target_pairs={{0,2},{2,0},{1,3},{3,1},{4,6},{6,4},{5,7},{7,5},{8,10},{10,8},{9,1... | collective-permute-start | bytes 1179656 | tf_op jit(solution)/shard_map/cond/branch_1_fun/ppermute | solution.py:37
  31.1 14.3 %collective-permute-start.10 = (bf16[6,128,256]{2,1,0:T(8,128)(2,1)}, bf16[6,128,256]{2,1,0:T(8,128)(2,1)S(1)}, u32[]{:S(2)}, u32[]{:S(2)}) collective-permute-start(bf16[6,128,256]{2,1,0:T(8,128)(2,1)} %get-tuple-element.60), channel_id=1, source_target_pairs={{4,0},{8,4},{12,8},{5,1},{9,5},{13,9},{6,2},{10,6},{14,10},{7,3},{... | collective-permute-start | bytes 1179656 | tf_op jit(solution)/shard_map/cond/branch_1_fun/ppermute | solution.py:33
  32.4 14.3 %collective-permute-start.9 = (bf16[6,128,256]{2,1,0:T(8,128)(2,1)}, bf16[6,128,256]{2,1,0:T(8,128)(2,1)S(1)}, u32[]{:S(2)}, u32[]{:S(2)}) collective-permute-start(bf16[6,128,256]{2,1,0:T(8,128)(2,1)} %get-tuple-element.59), channel_id=1, source_target_pairs={{0,4},{4,8},{8,12},{1,5},{5,9},{9,13},{2,6},{6,10},{10,14},{3,7},{... | collective-permute-start | bytes 1179656 | tf_op jit(solution)/shard_map/cond/branch_1_fun/ppermute | solution.py:33
  53.4 34.1 %collective-permute-start.13 = (bf16[6,128,256]{2,1,0:T(8,128)(2,1)}, bf16[6,128,256]{2,1,0:T(8,128)(2,1)S(1)}, u32[]{:S(2)}, u32[]{:S(2)}) collective-permute-start(bf16[6,128,256]{2,1,0:T(8,128)(2,1)} %get-tuple-element.64), channel_id=1, source_target_pairs={{0,4},{4,8},{8,12},{1,5},{5,9},{9,13},{2,6},{6,10},{10,14},{3,7},{... | collective-permute-start | bytes 1179656 | tf_op jit(solution)/shard_map/cond/branch_1_fun/ppermute | solution.py:33
  79.4 14.4 %collective-permute-start.14 = (bf16[6,128,256]{2,1,0:T(8,128)(2,1)}, bf16[6,128,256]{2,1,0:T(8,128)(2,1)S(1)}, u32[]{:S(2)}, u32[]{:S(2)}) collective-permute-start(bf16[6,128,256]{2,1,0:T(8,128)(2,1)} %get-tuple-element.65), channel_id=1, source_target_pairs={{4,0},{8,4},{12,8},{5,1},{9,5},{13,9},{6,2},{10,6},{14,10},{7,3},{... | collective-permute-start | bytes 1179656 | tf_op jit(solution)/shard_map/cond/branch_1_fun/ppermute | solution.py:33
  80.7 13.1 %collective-permute-start.15 = (bf16[6,128,256]{2,1,0:T(8,128)(2,1)}, bf16[6,128,256]{2,1,0:T(8,128)(2,1)S(1)}, u32[]{:S(2)}, u32[]{:S(2)}) collective-permute-start(bf16[6,128,256]{2,1,0:T(8,128)(2,1)} %get-tuple-element.66.refs_1_), channel_id=1, source_target_pairs={{0,1},{1,0},{2,3},{3,2},{4,5},{5,4},{6,7},{7,6},{8,9},{9,8},{10,11... | collective-permute-start | bytes 1179656 | tf_op jit(solution)/shard_map/cond/branch_1_fun/ppermute | solution.py:37
  80.8 13.7 %collective-permute-start.16 = (bf16[6,128,256]{2,1,0:T(8,128)(2,1)}, bf16[6,128,256]{2,1,0:T(8,128)(2,1)S(1)}, u32[]{:S(2)}, u32[]{:S(2)}) collective-permute-start(bf16[6,128,256]{2,1,0:T(8,128)(2,1)} %get-tuple-element.66.refs_1_), channel_id=1, source_target_pairs={{0,2},{2,0},{1,3},{3,1},{4,6},{6,4},{5,7},{7,5},{8,10},{10,8},{9,1... | collective-permute-start | bytes 1179656 | tf_op jit(solution)/shard_map/cond/branch_1_fun/ppermute | solution.py:37
  104.6 18.8 %collective-permute-start.17 = (bf16[6,128,256]{2,1,0:T(8,128)(2,1)}, bf16[6,128,256]{2,1,0:T(8,128)(2,1)S(1)}, u32[]{:S(2)}, u32[]{:S(2)}) collective-permute-start(bf16[6,128,256]{2,1,0:T(8,128)(2,1)} %get-tuple-element.69), channel_id=1, source_target_pairs={{0,4},{4,8},{8,12},{1,5},{5,9},{9,13},{2,6},{6,10},{10,14},{3,7},{... | collective-permute-start | bytes 1179656 | tf_op jit(solution)/shard_map/cond/branch_1_fun/ppermute | solution.py:33
  115.0 12.6 %collective-permute-start.18 = (bf16[6,128,256]{2,1,0:T(8,128)(2,1)}, bf16[6,128,256]{2,1,0:T(8,128)(2,1)S(1)}, u32[]{:S(2)}, u32[]{:S(2)}) collective-permute-start(bf16[6,128,256]{2,1,0:T(8,128)(2,1)} %get-tuple-element.70), channel_id=1, source_target_pairs={{4,0},{8,4},{12,8},{5,1},{9,5},{13,9},{6,2},{10,6},{14,10},{7,3},{... | collective-permute-start | bytes 1179656 | tf_op jit(solution)/shard_map/cond/branch_1_fun/ppermute | solution.py:33
  116.5 11.2 %collective-permute-start.19 = (bf16[6,128,256]{2,1,0:T(8,128)(2,1)}, bf16[6,128,256]{2,1,0:T(8,128)(2,1)S(1)}, u32[]{:S(2)}, u32[]{:S(2)}) collective-permute-start(bf16[6,128,256]{2,1,0:T(8,128)(2,1)} %get-tuple-element.71.refs_1_), channel_id=1, source_target_pairs={{0,1},{1,0},{2,3},{3,2},{4,5},{5,4},{6,7},{7,6},{8,9},{9,8},{10,11... | collective-permute-start | bytes 1179656 | tf_op jit(solution)/shard_map/cond/branch_1_fun/ppermute | solution.py:37
  116.5 11.8 %collective-permute-start.20 = (bf16[6,128,256]{2,1,0:T(8,128)(2,1)}, bf16[6,128,256]{2,1,0:T(8,128)(2,1)S(1)}, u32[]{:S(2)}, u32[]{:S(2)}) collective-permute-start(bf16[6,128,256]{2,1,0:T(8,128)(2,1)} %get-tuple-element.71.refs_1_), channel_id=1, source_target_pairs={{0,2},{2,0},{1,3},{3,1},{4,6},{6,4},{5,7},{7,5},{8,10},{10,8},{9,1... | collective-permute-start | bytes 1179656 | tf_op jit(solution)/shard_map/cond/branch_1_fun/ppermute | solution.py:37
  118.1 19.0 %collective-permute-start.26 = (bf16[6,128,256]{2,1,0:T(8,128)(2,1)S(1)}, bf16[6,128,256]{2,1,0:T(8,128)(2,1)}, u32[]{:S(2)}, u32[]{:S(2)}) collective-permute-start(bf16[6,128,256]{2,1,0:T(8,128)(2,1)S(1)} %collective-permute-done.12.refs_3_), channel_id=1, source_target_pairs={{0,1},{1,0},{2,3},{3,2},{4,5},{5,4},{6,7},{7,6},{8,9},{9,8},{10,11... | collective-permute-start | bytes 1179656 | tf_op jit(solution)/shard_map/cond/branch_1_fun/ppermute | solution.py:37
  123.5 21.7 %collective-permute-start.25 = (bf16[6,128,256]{2,1,0:T(8,128)(2,1)S(1)}, bf16[6,128,256]{2,1,0:T(8,128)(2,1)S(1)}, u32[]{:S(2)}, u32[]{:S(2)}) collective-permute-start(bf16[6,128,256]{2,1,0:T(8,128)(2,1)S(1)} %collective-permute-done.16.refs_3_), channel_id=1, source_target_pairs={{0,1},{1,0},{2,3},{3,2},{4,5},{5,4},{6,7},{7,6},{8,9},{9,8},{10,11... | collective-permute-start | bytes 1179656 | tf_op jit(solution)/shard_map/cond/branch_1_fun/ppermute | solution.py:37
  134.1 10.9 %collective-permute-start.22 = (bf16[6,128,256]{2,1,0:T(8,128)(2,1)}, bf16[6,128,256]{2,1,0:T(8,128)(2,1)S(1)}, u32[]{:S(2)}, u32[]{:S(2)}) collective-permute-start(bf16[6,128,256]{2,1,0:T(8,128)(2,1)} %pack.7.refs_1_), channel_id=1, source_target_pairs={{0,2},{2,0},{1,3},{3,1},{4,6},{6,4},{5,7},{7,5},{8,10},{10,8},{9,1... | collective-permute-start | bytes 1179656 | tf_op jit(solution)/shard_map/cond/branch_1_fun/ppermute | solution.py:37
  137.1 13.0 %collective-permute-start.24 = (bf16[6,128,256]{2,1,0:T(8,128)(2,1)S(1)}, bf16[6,128,256]{2,1,0:T(8,128)(2,1)S(1)}, u32[]{:S(2)}, u32[]{:S(2)}) collective-permute-start(bf16[6,128,256]{2,1,0:T(8,128)(2,1)S(1)} %collective-permute-done.20.refs_3_), channel_id=1, source_target_pairs={{0,1},{1,0},{2,3},{3,2},{4,5},{5,4},{6,7},{7,6},{8,9},{9,8},{10,11... | collective-permute-start | bytes 1179656 | tf_op jit(solution)/shard_map/cond/branch_1_fun/ppermute | solution.py:37
  144.6 10.3 %collective-permute-start.21 = (bf16[6,128,256]{2,1,0:T(8,128)(2,1)S(1)}, bf16[6,128,256]{2,1,0:T(8,128)(2,1)S(1)}, u32[]{:S(2)}, u32[]{:S(2)}) collective-permute-start(bf16[6,128,256]{2,1,0:T(8,128)(2,1)S(1)} %copy-done), channel_id=1, source_target_pairs={{0,1},{1,0},{2,3},{3,2},{4,5},{5,4},{6,7},{7,6},{8,9},{9,8},{10,11... | collective-permute-start | bytes 1179656 | tf_op jit(solution)/shard_map/cond/branch_1_fun/ppermute | solution.py:37
  145.1 9.8 %collective-permute-start.23 = (bf16[6,128,256]{2,1,0:T(8,128)(2,1)S(1)}, bf16[6,128,256]{2,1,0:T(8,128)(2,1)S(1)}, u32[]{:S(2)}, u32[]{:S(2)}) collective-permute-start(bf16[6,128,256]{2,1,0:T(8,128)(2,1)S(1)} %collective-permute-done.22.refs_3_), channel_id=1, source_target_pairs={{0,1},{1,0},{2,3},{3,2},{4,5},{5,4},{6,7},{7,6},{8,9},{9,8},{10,11... | collective-permute-start | bytes 1179656 | tf_op jit(solution)/shard_map/cond/branch_1_fun/ppermute | solution.py:37
  (25 other events, 398.1 us)
where the time goes:
time: 177 us; the launch traced here: 173 us
  starting transfers between devices  65.4 us (37%)
  Pallas kernels  59.4 us (34%)
  waiting for transfers between devices  30.5 us (17%)
  local copies, waits for them, and re-layouts  10.6 us (6%)
  other arithmetic  5.94 us (3%)
    ppermute x8, starting transfers between devices, shifted(): lax.ppermute(value, axis, [(source, source + steps) for source in range(f...  49.7 us
    ppermute x8, waiting for transfers between devices, shifted(): lax.ppermute(value, axis, [(source, source + steps) for source in range(f...  24 us
    pallas_call x4, Pallas kernels, pack(): pl.pallas_call(kernel, out_shape=(shape,) * kinds, grid_spec=pltpu.Prefet...  23.5 us
    pallas_call x4, Pallas kernels, project(): pl.pallas_call(kernel, out_shape=(out, out), grid=(count // group,), in_s...  22 us
    pallas_call x1, Pallas kernels, attend(): pl.pallas_call(attend_kernel, out_shape=jax.ShapeDtypeStruct(queries.shap...  12 us
    ppermute x16, starting transfers between devices, swapped(): return lax.ppermute(value, axis, [(0, 1), (1, 0)])  9.99 us
    ppermute x16, waiting for transfers between devices, swapped(): return lax.ppermute(value, axis, [(0, 1), (1, 0)])  6.49 us
    ppermute x3, starting transfers between devices, exchanged_table(): lax.ppermute(codes, 'seq', [(chip, chip ^ offset) for chip in range(CHIPS)])  5.68 us
  transfers between devices with their start and end apart: 27, of which 8 were waited for; matrix products, arithmetic and copies ran while one was open for 7% of the time, Pallas kernels for 14%

commit v1 on v0

--- a/solution.py
+++ b/solution.py
@@ -90,68 +90,68 @@
 SAME_ROWS = (((0,), (0,)), ((), ()))
 
 
-def attend_stretch(query_ref, keys, values, out_ref):
+def attend_kernel(slots, counts, query_ref, *refs):
+    *entries, out_ref = refs
+    keys, values = entries[: len(entries) // 2], entries[len(entries) // 2 :]
+    together = len(keys) // KMAX
     wide = 2 * HEAD_DIM
     factor = math.log2(math.e) / math.sqrt(HEAD_DIM)
-    parts = [slice(start, start + wide) for start in range(0, query_ref.shape[1], wide)]
-    scores = []
-    for part in parts:
-        query = query_ref[:, part]
+    count = [counts[pl.program_id(0) * together + g] for g in range(together)]
+    work = [(g, start) for g in range(together) for start in range(0, query_ref.shape[1], wide)]
+
+    def scored(g, start):
+        query = query_ref[g * STRETCH : (g + 1) * STRETCH, start : start + wide]
         left, right = query[:, :HEAD_DIM], query[:, HEAD_DIM:]
         zero = jnp.zeros_like(left)
         both = jnp.concatenate([jnp.concatenate([left, zero], 1), jnp.concatenate([zero, right], 1)], 0)
-        scores.append(
-            [lax.dot_general(k[0, :, part], both, SAME_COLUMNS, preferred_element_type=jnp.float32) for k in keys]
+        one, two = [
+            lax.dot_general(
+                keys[g * KMAX + k][0, :, start : start + wide], both, SAME_COLUMNS, preferred_element_type=jnp.float32
+            )
+            for k in range(KMAX)
+        ]
+        return one, jnp.where(count[g] == 2, two, -1e30)
+
+    def weighed(one, two):
+        top = jnp.maximum(one, two).max(0, keepdims=True)
+        one, two = jnp.exp2((one - top) * factor), jnp.exp2((two - top) * factor)
+        share = 1.0 / (one + two).sum(0, keepdims=True)
+        return (one * share).astype(jnp.bfloat16), (two * share).astype(jnp.bfloat16)
+
+    def mix(g, start, weights):
+        mixed = sum(
+            lax.dot_general(
+                weights[k], values[g * KMAX + k][0, :, start : start + wide], SAME_ROWS, preferred_element_type=jnp.float32
+            )
+            for k in range(KMAX)
         )
-    weights = []
-    for blocks in scores:
-        top = blocks[0].max(0, keepdims=True)
-        for block in blocks[1:]:
-            top = jnp.maximum(top, block.max(0, keepdims=True))
-        expo = [jnp.exp2((block - top) * factor) for block in blocks]
-        share = 1.0 / sum(block.sum(0, keepdims=True) for block in expo)
-        weights.append([(block * share).astype(jnp.bfloat16) for block in expo])
-    for part, blocks in zip(parts, weights):
-        mixed = sum(
-            lax.dot_general(block, v[0, :, part], SAME_ROWS, preferred_element_type=jnp.float32)
-            for block, v in zip(blocks, values)
-        )
-        middle = part.start + HEAD_DIM
-        out_ref[:, part.start : middle] = mixed[:STRETCH, :HEAD_DIM].astype(jnp.bfloat16)
-        out_ref[:, middle : part.stop] = mixed[STRETCH:, HEAD_DIM:].astype(jnp.bfloat16)
-
-
-def attend_kernel(slots, counts, query_ref, first_keys, second_keys, first_values, second_values, out_ref):
-    count = counts[pl.program_id(0)]
-
-    @pl.when(count == 0)
-    def _():
-        out_ref[...] = jnp.zeros_like(out_ref)
-
-    @pl.when(count == 1)
-    def _():
-        attend_stretch(query_ref, [first_keys], [first_values], out_ref)
-
-    @pl.when(count == 2)
-    def _():
-        attend_stretch(query_ref, [first_keys, second_keys], [first_values, second_values], out_ref)
-
-
-def attend(slots, counts, queries, keys, values):
+        mixed = jnp.where(count[g] > 0, mixed, 0.0).astype(jnp.bfloat16)
+        rows = slice(g * STRETCH, (g + 1) * STRETCH)
+        out_ref[rows, start : start + HEAD_DIM] = mixed[:STRETCH, :HEAD_DIM]
+        out_ref[rows, start + HEAD_DIM : start + wide] = mixed[STRETCH:, HEAD_DIM:]
+
+    scores = [scored(*piece) for piece in work]
+    weights = [weighed(*pair) for pair in scores]
+    for piece, pair in zip(work, weights):
+        mix(*piece, pair)
+
+
+def attend(slots, counts, queries, keys, values, together=3):
     stretches = counts.shape[0]
     columns = queries.shape[1]
 
-    def entry(k):
-        return pl.BlockSpec((1, NLEN, columns), lambda i, slots, _: (slots[i * KMAX + k], 0, 0))
-
-    query_spec = pl.BlockSpec((STRETCH, columns), lambda i, *_: (i, 0))
+    def entry(i):
+        return pl.BlockSpec((1, NLEN, columns), lambda step, slots, _: (slots[step * together * KMAX + i], 0, 0))
+
+    query_spec = pl.BlockSpec((together * STRETCH, columns), lambda i, *_: (i, 0))
+    entries = [entry(i) for i in range(together * KMAX)]
     return pl.pallas_call(
         attend_kernel,
         out_shape=jax.ShapeDtypeStruct(queries.shape, jnp.bfloat16),
         grid_spec=pltpu.PrefetchScalarGridSpec(
             num_scalar_prefetch=2,
-            grid=(stretches,),
-            in_specs=[query_spec, entry(0), entry(1), entry(0), entry(1)],
+            grid=(stretches // together,),
+            in_specs=[query_spec] + entries * 2,
             out_specs=query_spec,
         ),
         compiler_params=pltpu.CompilerParams(vmem_limit_bytes=VMEM_LIMIT),
@@ -161,7 +161,7 @@
             transcendentals=stretches * STRETCH * KMAX * NLEN * columns // HEAD_DIM,
         ),
         name="attend",
-    )(slots, counts, queries, keys, keys, values, values)
+    )(slots, counts, queries, *[keys] * len(entries), *[values] * len(entries))
 
 
 def plan_kernel(place, table, plan_ref, far_ref, loc_ref, lists_ref, need_ref, where_ref, picks_ref, slots_ref):
@@ -294,7 +294,7 @@
         starts.append(starts[-1] + array.shape[0])
 
     def kernel(plan_ref, *refs):
-        sources, outs, sems = refs[: len(pool)], refs[len(pool) : -1], refs[-1]
+        sources, outs = refs[: len(pool)], refs[len(pool) :]
         for kind, out in enumerate(outs):
             line = kind + 3 - kinds
             for b in range(CAP):
@@ -302,27 +302,18 @@
                 for source, low, high in zip(sources, starts, starts[1:]):
 
                     @pl.when((at >= low) & (at < high))
-                    def _(source=source, low=low, out=out, b=b, at=at, sem=sems.at[kind * CAP + b]):
-                        pltpu.make_async_copy(source.at[at - low], out.at[b], sem).start()
-
-        for kind, out in enumerate(outs):
-            line = kind + 3 - kinds
-            for b in range(CAP):
-
-                @pl.when(plan_ref[line * LANES + number * CAP + b] >= 0)
-                def _(out=out, b=b, sem=sems.at[kind * CAP + b]):
-                    pltpu.make_async_copy(sources[0].at[0], out.at[b], sem).wait()
+                    def _(source=source, low=low, out=out, b=b, at=at):
+                        out[b] = source[at - low]
 
     shape = jax.ShapeDtypeStruct((CAP,) + pool[0].shape[1:], pool[0].dtype)
+    in_vmem = pl.BlockSpec(memory_space=pltpu.VMEM)
     return pl.pallas_call(
         kernel,
         out_shape=(shape,) * kinds,
         grid_spec=pltpu.PrefetchScalarGridSpec(
-            num_scalar_prefetch=1,
-            in_specs=[pl.BlockSpec(memory_space=pl.ANY)] * len(pool),
-            out_specs=(pl.BlockSpec(memory_space=pl.ANY),) * kinds,
-            scratch_shapes=[pltpu.SemaphoreType.DMA((kinds * CAP,))],
+            num_scalar_prefetch=1, in_specs=[in_vmem] * len(pool), out_specs=(in_vmem,) * kinds
         ),
+        compiler_params=pltpu.CompilerParams(vmem_limit_bytes=VMEM_LIMIT),
         cost_estimate=pl.CostEstimate(flops=0, bytes_accessed=kinds * CAP * 2 * 65536, transcendentals=0),
         name="pack",
     )(plan, *pool)
@@ -401,31 +392,44 @@
     first = jnp.maximum(asked[:, 0], 0)
     asked = jnp.stack([first, jnp.where(asked[:, 1] >= 0, asked[:, 1], first)], axis=1).reshape(-1)
 
-    plan, key_weight, value_weight, enc_gain = lax.optimization_barrier((plan, key_weight, value_weight, enc_gain))
-    gain = jnp.concatenate(four_pieces(enc_gain[None]), axis=1)
-    key_weight, value_weight = in_order_of_pieces(key_weight), in_order_of_pieces(value_weight)
-
     def planned():
         slots = plan[3 * LANES : 4 * LANES][asked]
         pool = [store, early_up, early_down]
-        held = ()
+        held, pieces = (), []
         for number in range(ROUNDS + 1):
             *ways, mine = pack(plan, number, pool)
-            pieces = [mine, swapped(mine, "rep"), swapped(mine, "mp")]
-            if ways:
-                arrived = [shifted(ways[0], "seq", 1), shifted(ways[1], "seq", -1)]
-                *arrived, pieces[1], pieces[2] = lax.optimization_barrier((*arrived, pieces[1], pieces[2]))
+            arrived = [shifted(way, "seq", steps) for way, steps in zip(ways, (1, -1))]
+            pieces.append([mine, swapped(mine, "rep"), swapped(mine, "mp")])
+            if number == 0:
+                mine, later_keys, later_values, later_gain = lax.optimization_barrier(
+                    (mine, key_weight, value_weight, enc_gain)
+                )
+                ordered_gain = jnp.concatenate(four_pieces(later_gain[None]), axis=1)
+                ordered = [in_order_of_pieces(weight) for weight in (later_keys, later_values)]
+                after = (ordered_gain, *ordered)
+            else:
+                pieces[number - 1].append(swapped(pieces[number - 1][2], "rep"))
+                held = project(ordered_gain, pieces[number - 1], *ordered, 3, total, (number - 1) * CAP, held)
+                after = held
+            if number < ROUNDS:
+                arrived, pieces[number], after = lax.optimization_barrier((arrived, pieces[number], after))
+                if number == 0:
+                    ordered_gain, *ordered = after
+                else:
+                    held = after
                 pool += arrived
-            pieces.append(swapped(pieces[2], "rep"))
-            held = project(gain, pieces, key_weight, value_weight, 3, total, number * CAP, held)
-        return attend(slots, counts, queries, *held)
+        pieces[ROUNDS].append(swapped(pieces[ROUNDS][2], "rep"))
+        held = project(ordered_gain, pieces[ROUNDS], *ordered, 3, total, ROUNDS * CAP, held)
+        return (slots, *held)
 
     def whole():
         mine = fetch_all(store, asked >> 4, asked & (ENTRIES_EACH - 1))
-        keys, values = project(gain, four_pieces(mine), key_weight, value_weight, 4, total)
-        return attend(jnp.arange(total, dtype=jnp.int32), counts, queries, keys, values)
-
-    return lax.cond(missing == 0, planned, whole)
+        gain = jnp.concatenate(four_pieces(enc_gain[None]), axis=1)
+        ordered = [in_order_of_pieces(weight) for weight in (key_weight, value_weight)]
+        return (jnp.arange(total, dtype=jnp.int32), *project(gain, four_pieces(mine), *ordered, 4, total))
+
+    slots, keys, values = lax.cond(missing == 0, planned, whole)
+    return attend(slots, counts, queries, keys, values)
 
 
 def requested(queries, key_weight, value_weight, enc_gain, store, nbr_owner, nbr_slot, nbr_count):

time: 177 us -> 126 us (0.71); the launches traced: 173 us -> 125 us
  starting transfers between devices: 65.4 us -> 36.4 us
  Pallas kernels: 59.4 us -> 41.9 us
  other arithmetic: 5.94 us -> 1.49 us
  waiting for transfers between devices: 30.5 us -> 32.4 us
    ppermute x8, starting transfers between devices: 49.7 us -> 21.3 us  [shifted(): lax.ppermute(value, axis, [(source, source + steps) for source in range(f...]
    pallas_call x4, Pallas kernels: 23.5 us -> 6.9 us  [pack(): pl.pallas_call(kernel, out_shape=(shape,) * kinds, grid_spec=pltpu.Prefet...]
    ppermute x16, waiting for transfers between devices: 6.49 us -> 11.2 us  [swapped(): return lax.ppermute(value, axis, [(0, 1), (1, 0)])]
    ppermute x8, waiting for transfers between devices: 24 us -> 21.1 us  [shifted(): lax.ppermute(value, axis, [(source, source + steps) for source in range(f...]
    concatenate x2, other arithmetic: 2.95 us -> 0.35 us  [in_order_of_pieces(): jnp.concatenate([lax.dynamic_slice_in_dim(weight, (block ^ i) * width, wi...]
    cond x38 -> x24, local copies, waits for them, and re-layouts: 2.34 us -> 4.58 us
  transfers between devices with their start and end apart: 27 -> 27, of which waited for: 8 -> 10; matrix products, arithmetic and copies ran while one was open for 7% -> 5% of each run, Pallas kernels for 14% -> 17%
where the time goes in v1:
time: 126 us; the launch traced here: 125 us
  Pallas kernels  41.9 us (33%)
  starting transfers between devices  36.4 us (29%)
  waiting for transfers between devices  32.4 us (26%)
  local copies, waits for them, and re-layouts  12.2 us (10%)
  other arithmetic  1.49 us (1%)
    pallas_call x4, Pallas kernels, project(): pl.pallas_call(kernel, out_shape=(out, out), grid=(count // group,), in_s...  22.7 us
    ppermute x8, starting transfers between devices, shifted(): lax.ppermute(value, axis, [(source, source + steps) for source in range(f...  21.3 us
    ppermute x8, waiting for transfers between devices, shifted(): lax.ppermute(value, axis, [(source, source + steps) for source in range(f...  21.1 us
    ppermute x16, waiting for transfers between devices, swapped(): return lax.ppermute(value, axis, [(0, 1), (1, 0)])  11.2 us
    pallas_call x1, Pallas kernels, attend(): pl.pallas_call(attend_kernel, out_shape=jax.ShapeDtypeStruct(queries.shap...  10.5 us
    ppermute x16, starting transfers between devices, swapped(): return lax.ppermute(value, axis, [(0, 1), (1, 0)])  9.31 us
    pallas_call x4, Pallas kernels, pack(): pl.pallas_call(kernel, out_shape=(shape,) * kinds, grid_spec=pltpu.Prefet...  6.9 us
    ppermute x3, starting transfers between devices, exchanged_table(): lax.ppermute(codes, 'seq', [(chip, chip ^ offset) for chip in range(CHIPS)])  5.76 us
  transfers between devices with their start and end apart: 27, of which 10 were waited for; matrix products, arithmetic and copies ran while one was open for 5% of the time, Pallas kernels for 17%

profile of v1, /device:TPU:0, one launch (start us, length us, event | category | flops | bytes accessed | tf_op | source)
XLA Modules:
  0.0 125.4 jit_solution(6823171902575880547)
XLA Ops:
  0.9 5.1 %collective-permute-start.35 = (s32[24]{0:T(128)S(1)}, s32[24]{0:T(128)S(1)}, u32[]{:S(2)}, u32[]{:S(2)}) collective-permute-start(s32[24]{0:T(128)S(1)} %reshape.29), channel_id=1, source_target_pairs={{0,12},{4,8},{8,4},{12,0},{1,13},{5,9},{9,5},{13,1},{2,14},{6,10},... | collective-permute-start | bytes 296 | tf_op jit(solution)/shard_map/ppermute | solution.py:370
  9.0 4.6 %collective-permute-start.37 = (bf16[8,128,256]{2,1,0:T(8,128)(2,1)S(1)}, bf16[8,128,256]{2,1,0:T(8,128)(2,1)S(1)}, u32[]{:S(2)}, u32[]{:S(2)}) collective-permute-start(bf16[8,128,256]{2,1,0:T(8,128)(2,1)S(1)} %slice.33), channel_id=1, source_target_pairs={{0,4},{4,8},{8,12},{1,5},{5,9},{9,13},{2,6},{6,10},{10,14},{3,7},{... | collective-permute-start | bytes 1572872 | tf_op jit(solution)/shard_map/ppermute | solution.py:33
  13.8 1.7 %collective-permute-start.36 = (s32[4,24]{1,0:T(4,128)S(1)}, s32[4,24]{1,0:T(4,128)S(1)}, u32[]{:S(2)}, u32[]{:S(2)}) collective-permute-start(s32[4,24]{1,0:T(4,128)S(1)} %pad_add_fusion.1), channel_id=1, source_target_pairs={{0,16},{16,0},{1,17},{17,1},{2,18},{18,2},{3,19},{19,3},{4,20},{20... | collective-permute-start | bytes 1160 | tf_op jit(solution)/shard_map/ppermute | solution.py:37
  15.7 1.7 %collective-permute-done.36 = s32[4,24]{1,0:T(4,128)S(1)} collective-permute-done((s32[4,24]{1,0:T(4,128)S(1)}, s32[4,24]{1,0:T(4,128)S(1)}, u32[]{:S(2)}, u32[]{:S(2)}) %collective-permute-start.36) | collective-permute-done | bytes 416 | tf_op jit(solution)/shard_map/ppermute | solution.py:37
  18.2 1.9 %plan.1 = s32[8,128]{1,0:T(8,128)S(1)} custom-call(s32[1]{0:T(128)} %bitcast.2.place, s32[192]{0:T(256)} %reshape.30.table), custom_call_target="tpu_custom_call" | custom-call | tf_op jit(solution)/shard_map/plan/pallas_call | solution.py:280
  23.9 89.5 %conditional.1 = (s32[24]{0:T(128)S(1)}, bf16[24,128,1024]{2,1,0:T(8,128)(2,1)}, bf16[24,128,1024]{2,1,0:T(8,128)(2,1)}) conditional(s32[]{:T(128)} %bitcast.7, (f32[256]{0:T(256)}, bf16[16,128,256]{2,1,0:T(8,128)(2,1)}, s32[24]{0:T(128)S(1)}, bf16[1024,1024]{1,0:T(8,128)(2,1)}, bf16[1024,1024]{1,0:T(8,128)(2,1)}) %tuple.17, (s32[1024]{0:T(1024)S(1)}, ...), branch_computations={%region_0.1_spmd, %region_1.2_spmd} | conditional | flops 12901683200 | bytes 124288048 | solution.py:431
  24.9 3.4 %pack.4 = (bf16[6,128,256]{2,1,0:T(8,128)(2,1)}, bf16[6,128,256]{2,1,0:T(8,128)(2,1)}, bf16[6,128,256]{2,1,0:T(8,128)(2,1)S(1)}) custom-call(s32[1024]{0:T(1024)S(1)} %get-tuple-element.38.plan_ref, bf16[16,128,256]{2,1,0:T(8,128)(2,1)} %get-tuple-element.40.refs_0_, bf16[8,128,256]{2,1,0:T(8,128)(2,1)} %copy-done.10, bf16[8,128,256]{2,1,0:T(8,128)(2,1)} %copy-done.8), custom_call_target="tpu_custom_call" | custom-call | bytes 2359296 | tf_op jit(solution)/shard_map/cond/branch_1_fun/pack/pallas_call | solution.py:310
  30.5 4.4 %collective-permute-start.12 = (bf16[6,128,256]{2,1,0:T(8,128)(2,1)}, bf16[6,128,256]{2,1,0:T(8,128)(2,1)S(1)}, u32[]{:S(2)}, u32[]{:S(2)}) collective-permute-start(bf16[6,128,256]{2,1,0:T(8,128)(2,1)} %get-tuple-element.43), channel_id=1, source_target_pairs={{0,4},{4,8},{8,12},{1,5},{5,9},{9,13},{2,6},{6,10},{10,14},{3,7},{... | collective-permute-start | bytes 1179656 | tf_op jit(solution)/shard_map/cond/branch_1_fun/ppermute | solution.py:33
  34.9 2.6 %constant_dynamic-slice_fusion.11 = (bf16[256,1024]{1,0:T(8,128)(2,1)S(1)}, bf16[256,1024]{1,0:T(8,128)(2,1)S(1)}, bf16[256,1024]{1,0:T(8,128)(2,1)S(1)}, bf16[2...) fusion(bf16[1024,1024]{1,0:T(8,128)(2,1)} %get-tuple-element.51, ...), kind=kLoop, calls=%fused_computation.34 | loop fusion | bytes 8388624 | tf_op jit(solution)/shard_map/cond/branch_1_fun/dynamic_slice | solution.py:364
  40.3 3.7 %collective-permute-done.12.refs_3_ = bf16[6,128,256]{2,1,0:T(8,128)(2,1)S(1)} collective-permute-done((bf16[6,128,256]{2,1,0:T(8,128)(2,1)}, bf16[6,128,256]{2,1,0:T(8,128)(2,1)S(1)}, u32[]{:S(2)}, u32[]{:S(2)}) %collective-permute-start.12) | collective-permute-done | bytes 393248 | tf_op jit(solution)/shard_map/cond/branch_1_fun/ppermute | solution.py:33
  44.0 6.7 %collective-permute-done.13.refs_4_ = bf16[6,128,256]{2,1,0:T(8,128)(2,1)S(1)} collective-permute-done((bf16[6,128,256]{2,1,0:T(8,128)(2,1)}, bf16[6,128,256]{2,1,0:T(8,128)(2,1)S(1)}, u32[]{:S(2)}, u32[]{:S(2)}) %collective-permute-start.13) | collective-permute-done | bytes 393248 | tf_op jit(solution)/shard_map/cond/branch_1_fun/ppermute | solution.py:33
  52.0 3.2 %collective-permute-start.19 = (bf16[6,128,256]{2,1,0:T(8,128)(2,1)S(1)}, bf16[6,128,256]{2,1,0:T(8,128)(2,1)S(1)}, u32[]{:S(2)}, u32[]{:S(2)}) collective-permute-start(bf16[6,128,256]{2,1,0:T(8,128)(2,1)S(1)} %get-tuple-element.55), channel_id=1, source_target_pairs={{0,4},{4,8},{8,12},{1,5},{5,9},{9,13},{2,6},{6,10},{10,14},{3,7},{... | collective-permute-start | bytes 1179656 | tf_op jit(solution)/shard_map/cond/branch_1_fun/ppermute | solution.py:33
  56.5 1.6 %collective-permute-start.22 = (bf16[6,128,256]{2,1,0:T(8,128)(2,1)S(1)}, bf16[6,128,256]{2,1,0:T(8,128)(2,1)S(1)}, u32[]{:S(2)}, u32[]{:S(2)}) collective-permute-start(bf16[6,128,256]{2,1,0:T(8,128)(2,1)S(1)} %get-tuple-element.70.refs_1_), channel_id=1, source_target_pairs={{0,2},{2,0},{1,3},{3,1},{4,6},{6,4},{5,7},{7,5},{8,10},{10,8},{9,1... | collective-permute-start | bytes 1179656 | tf_op jit(solution)/shard_map/cond/branch_1_fun/ppermute | solution.py:37
  59.1 5.9 %project.6 = (bf16[24,128,1024]{2,1,0:T(8,128)(2,1)}, bf16[24,128,1024]{2,1,0:T(8,128)(2,1)}) custom-call(f32[1,1024]{1,0:T(1,128)S(1)} %pad_maximum_fusion.5.refs_0_, bf16[6,128,256]{2,1,0:T(8,128)(2,1)S(1)} %get-tuple-element.58.refs_1_, bf16[6,128,256]{2,1,0:T(8,128)(2,1)S(1)} %copy-done.6, bf16[6,128,256]{2,1,0:T(8,128)(2,1)} %collective-permute-done.15.refs_3_, ...), custom_call_target="tpu_custom_call" | custom-call | flops 3221225472 | bytes 8912896 | tf_op jit(solution)/shard_map/cond/branch_1_fun/project/pallas_call | solution.py:68
  64.9 3.4 %collective-permute-done.20.refs_6_ = bf16[6,128,256]{2,1,0:T(8,128)(2,1)S(1)} collective-permute-done((bf16[6,128,256]{2,1,0:T(8,128)(2,1)S(1)}, bf16[6,128,256]{2,1,0:T(8,128)(2,1)S(1)}, u32[]{:S(2)}, u32[]{:S(2)}) %collective-permute-start.20) | collective-permute-done | bytes 393248 | tf_op jit(solution)/shard_map/cond/branch_1_fun/ppermute | solution.py:33
  69.7 3.8 %collective-permute-start.24 = (bf16[6,128,256]{2,1,0:T(8,128)(2,1)S(1)}, bf16[6,128,256]{2,1,0:T(8,128)(2,1)S(1)}, u32[]{:S(2)}, u32[]{:S(2)}) collective-permute-start(bf16[6,128,256]{2,1,0:T(8,128)(2,1)S(1)} %get-tuple-element.67), channel_id=1, source_target_pairs={{0,4},{4,8},{8,12},{1,5},{5,9},{9,13},{2,6},{6,10},{10,14},{3,7},{... | collective-permute-start | bytes 1179656 | tf_op jit(solution)/shard_map/cond/branch_1_fun/ppermute | solution.py:33
  75.0 1.6 %collective-permute-start.27 = (bf16[6,128,256]{2,1,0:T(8,128)(2,1)S(1)}, bf16[6,128,256]{2,1,0:T(8,128)(2,1)}, u32[]{:S(2)}, u32[]{:S(2)}) collective-permute-start(bf16[6,128,256]{2,1,0:T(8,128)(2,1)S(1)} %get-tuple-element.79.refs_1_), channel_id=1, source_target_pairs={{0,2},{2,0},{1,3},{3,1},{4,6},{6,4},{5,7},{7,5},{8,10},{10,8},{9,1... | collective-permute-start | bytes 1179656 | tf_op jit(solution)/shard_map/cond/branch_1_fun/ppermute | solution.py:37
  76.6 4.9 %project.7 = (bf16[24,128,1024]{2,1,0:T(8,128)(2,1)}, bf16[24,128,1024]{2,1,0:T(8,128)(2,1)}) custom-call(f32[1,1024]{1,0:T(1,128)S(1)} %pad_maximum_fusion.5.refs_0_, bf16[6,128,256]{2,1,0:T(8,128)(2,1)S(1)} %get-tuple-element.70.refs_1_, bf16[6,128,256]{2,1,0:T(8,128)(2,1)S(1)} %collective-permute-done.21.refs_2_, ...), custom_call_target="tpu_custom_call", output_to_operand_aliasing={{0}: (7, {}), {1}: (8, {})} | custom-call | flops 3221225472 | bytes 8912896 | tf_op jit(solution)/shard_map/cond/branch_1_fun/project/pallas_call | solution.py:68
  82.5 4.1 %collective-permute-done.25.refs_8_ = bf16[6,128,256]{2,1,0:T(8,128)(2,1)S(1)} collective-permute-done((bf16[6,128,256]{2,1,0:T(8,128)(2,1)S(1)}, bf16[6,128,256]{2,1,0:T(8,128)(2,1)S(1)}, u32[]{:S(2)}, u32[]{:S(2)}) %collective-permute-start.25) | collective-permute-done | bytes 393248 | tf_op jit(solution)/shard_map/cond/branch_1_fun/ppermute | solution.py:33
  89.7 8.5 %collective-permute-done.30.refs_3_ = bf16[6,128,256]{2,1,0:T(8,128)(2,1)S(1)} collective-permute-done((bf16[6,128,256]{2,1,0:T(8,128)(2,1)S(1)}, bf16[6,128,256]{2,1,0:T(8,128)(2,1)S(1)}, u32[]{:S(2)}, u32[]{:S(2)}) %collective-permute-start.30) | collective-permute-done | bytes 393248 | tf_op jit(solution)/shard_map/cond/branch_1_fun/ppermute | solution.py:37
  98.9 1.6 %copy-done.1 = bf16[1024,1024]{1,0:T(8,128)(2,1)S(1)} copy-done((bf16[1024,1024]{1,0:T(8,128)(2,1)S(1)}, bf16[1024,1024]{1,0:T(8,128)(2,1)}, u32[]{:S(2)}) %copy-start.1) | copy-done | bytes 2097176 | tf_op jit(solution)/shard_map/cond
  101.5 5.9 %project.8 = (bf16[24,128,1024]{2,1,0:T(8,128)(2,1)}, bf16[24,128,1024]{2,1,0:T(8,128)(2,1)}) custom-call(f32[1,1024]{1,0:T(1,128)S(1)} %pad_maximum_fusion.5.refs_0_, bf16[6,128,256]{2,1,0:T(8,128)(2,1)S(1)} %get-tuple-element.79.refs_1_, bf16[6,128,256]{2,1,0:T(8,128)(2,1)S(1)} %copy-done.4, ...), custom_call_target="tpu_custom_call", output_to_operand_aliasing={{0}: (7, {}), {1}: (8, {})} | custom-call | flops 3221225472 | bytes 8912896 | tf_op jit(solution)/shard_map/cond/branch_1_fun/project/pallas_call | solution.py:68
  107.4 6.0 %project.9 = (bf16[24,128,1024]{2,1,0:T(8,128)(2,1)}, bf16[24,128,1024]{2,1,0:T(8,128)(2,1)}) custom-call(f32[1,1024]{1,0:T(1,128)S(1)} %pad_maximum_fusion.5.refs_0_, bf16[6,128,256]{2,1,0:T(8,128)(2,1)S(1)} %pack.7.refs_1_, bf16[6,128,256]{2,1,0:T(8,128)(2,1)} %collective-permute-done.29.refs_2_, ...), custom_call_target="tpu_custom_call", output_to_operand_aliasing={{0}: (7, {}), {1}: (8, {})} | custom-call | flops 3221225472 | bytes 8912896 | tf_op jit(solution)/shard_map/cond/branch_1_fun/project/pallas_call | solution.py:68
  114.9 10.5 %attend.1 = bf16[768,1024]{1,0:T(8,128)(2,1)} custom-call(s32[24]{0:T(128)S(1)} %get-tuple-element.91.slots, s32[12]{0:T(128)S(1)} %convert_reduce_fusion.counts, bf16[768,1024]{1,0:T(8,128)(2,1)S(1)} %copy-done.2, bf16[24,128,1024]{2,1,0:T(8,128)(2,1)} %get-tuple-element.92.refs_0_.refs_1_.refs_2_.refs_3_.refs_4_.refs_5_, ...), custom_call_target="tpu_custom_call" | custom-call | flops 1610612736 | bytes 15728640 | tf_op jit(solution)/shard_map/attend/pallas_call | solution.py:148
  (94 shorter events, 27.7 us)
Async XLA Ops:
  0.9 12.8 %collective-permute-start.35 = (s32[24]{0:T(128)S(1)}, s32[24]{0:T(128)S(1)}, u32[]{:S(2)}, u32[]{:S(2)}) collective-permute-start(s32[24]{0:T(128)S(1)} %reshape.29), channel_id=1, source_target_pairs={{0,12},{4,8},{8,4},{12,0},{1,13},{5,9},{9,5},{13,1},{2,14},{6,10},... | collective-permute-start | bytes 296 | tf_op jit(solution)/shard_map/ppermute | solution.py:370
  6.0 7.7 %collective-permute-start.34 = (s32[24]{0:T(128)S(1)}, s32[24]{0:T(128)S(1)}, u32[]{:S(2)}, u32[]{:S(2)}) collective-permute-start(s32[24]{0:T(128)S(1)} %reshape.29), channel_id=1, source_target_pairs={{0,8},{4,12},{8,0},{12,4},{1,9},{5,13},{9,1},{13,5},{2,10},{6,14},... | collective-permute-start | bytes 296 | tf_op jit(solution)/shard_map/ppermute | solution.py:370
  6.0 7.7 %collective-permute-start.33 = (s32[24]{0:T(128)S(1)}, s32[24]{0:T(128)S(1)}, u32[]{:S(2)}, u32[]{:S(2)}) collective-permute-start(s32[24]{0:T(128)S(1)} %reshape.29), channel_id=1, source_target_pairs={{0,4},{4,0},{8,12},{12,8},{1,5},{5,1},{9,13},{13,9},{2,6},{6,2},{1... | collective-permute-start | bytes 296 | tf_op jit(solution)/shard_map/ppermute | solution.py:370
  7.7 15.0 %collective-permute-start.38 = (bf16[8,128,256]{2,1,0:T(8,128)(2,1)S(1)}, bf16[8,128,256]{2,1,0:T(8,128)(2,1)S(1)}, u32[]{:S(2)}, u32[]{:S(2)}) collective-permute-start(bf16[8,128,256]{2,1,0:T(8,128)(2,1)S(1)} %slice.33), channel_id=1, source_target_pairs={{4,0},{8,4},{12,8},{5,1},{9,5},{13,9},{6,2},{10,6},{14,10},{7,3},{... | collective-permute-start | bytes 1572872 | tf_op jit(solution)/shard_map/ppermute | solution.py:33
  9.0 14.9 %collective-permute-start.37 = (bf16[8,128,256]{2,1,0:T(8,128)(2,1)S(1)}, bf16[8,128,256]{2,1,0:T(8,128)(2,1)S(1)}, u32[]{:S(2)}, u32[]{:S(2)}) collective-permute-start(bf16[8,128,256]{2,1,0:T(8,128)(2,1)S(1)} %slice.33), channel_id=1, source_target_pairs={{0,4},{4,8},{8,12},{1,5},{5,9},{9,13},{2,6},{6,10},{10,14},{3,7},{... | collective-permute-start | bytes 1572872 | tf_op jit(solution)/shard_map/ppermute | solution.py:33
  28.2 9.3 %collective-permute-start.17 = (f32[1,256]{1,0:T(1,128)}, f32[1,256]{1,0:T(1,128)S(1)}, u32[]{:S(2)}, u32[]{:S(2)}) collective-permute-start(f32[1,256]{1,0:T(1,128)} %bitcast.17), channel_id=1, source_target_pairs={{0,2},{2,0},{1,3},{3,1},{4,6},{6,4},{5,7},{7,5},{8,10},{10,8},{9,1... | collective-permute-start | bytes 3080 | tf_op jit(solution)/shard_map/cond/branch_1_fun/ppermute | solution.py:37
  29.7 9.4 %collective-permute-start.16 = (f32[1,256]{1,0:T(1,128)}, f32[1,256]{1,0:T(1,128)S(1)}, u32[]{:S(2)}, u32[]{:S(2)}) collective-permute-start(f32[1,256]{1,0:T(1,128)} %bitcast.18), channel_id=1, source_target_pairs={{0,1},{1,0},{2,3},{3,2},{4,5},{5,4},{6,7},{7,6},{8,9},{9,8},{10,11... | collective-permute-start | bytes 3080 | tf_op jit(solution)/shard_map/cond/branch_1_fun/ppermute | solution.py:37
  29.7 21.0 %collective-permute-start.15 = (bf16[6,128,256]{2,1,0:T(8,128)(2,1)S(1)}, bf16[6,128,256]{2,1,0:T(8,128)(2,1)}, u32[]{:S(2)}, u32[]{:S(2)}) collective-permute-start(bf16[6,128,256]{2,1,0:T(8,128)(2,1)S(1)} %get-tuple-element.58.refs_1_), channel_id=1, source_target_pairs={{0,2},{2,0},{1,3},{3,1},{4,6},{6,4},{5,7},{7,5},{8,10},{10,8},{9,1... | collective-permute-start | bytes 1179656 | tf_op jit(solution)/shard_map/cond/branch_1_fun/ppermute | solution.py:37
  30.3 20.4 %collective-permute-start.14 = (bf16[6,128,256]{2,1,0:T(8,128)(2,1)S(1)}, bf16[6,128,256]{2,1,0:T(8,128)(2,1)S(1)}, u32[]{:S(2)}, u32[]{:S(2)}) collective-permute-start(bf16[6,128,256]{2,1,0:T(8,128)(2,1)S(1)} %get-tuple-element.58.refs_1_), channel_id=1, source_target_pairs={{0,1},{1,0},{2,3},{3,2},{4,5},{5,4},{6,7},{7,6},{8,9},{9,8},{10,11... | collective-permute-start | bytes 1179656 | tf_op jit(solution)/shard_map/cond/branch_1_fun/ppermute | solution.py:37
  30.5 13.5 %collective-permute-start.12 = (bf16[6,128,256]{2,1,0:T(8,128)(2,1)}, bf16[6,128,256]{2,1,0:T(8,128)(2,1)S(1)}, u32[]{:S(2)}, u32[]{:S(2)}) collective-permute-start(bf16[6,128,256]{2,1,0:T(8,128)(2,1)} %get-tuple-element.43), channel_id=1, source_target_pairs={{0,4},{4,8},{8,12},{1,5},{5,9},{9,13},{2,6},{6,10},{10,14},{3,7},{... | collective-permute-start | bytes 1179656 | tf_op jit(solution)/shard_map/cond/branch_1_fun/ppermute | solution.py:33
  37.6 13.1 %collective-permute-start.13 = (bf16[6,128,256]{2,1,0:T(8,128)(2,1)}, bf16[6,128,256]{2,1,0:T(8,128)(2,1)S(1)}, u32[]{:S(2)}, u32[]{:S(2)}) collective-permute-start(bf16[6,128,256]{2,1,0:T(8,128)(2,1)} %get-tuple-element.44), channel_id=1, source_target_pairs={{4,0},{8,4},{12,8},{5,1},{9,5},{13,9},{6,2},{10,6},{14,10},{7,3},{... | collective-permute-start | bytes 1179656 | tf_op jit(solution)/shard_map/cond/branch_1_fun/ppermute | solution.py:33
  52.0 12.9 %collective-permute-start.19 = (bf16[6,128,256]{2,1,0:T(8,128)(2,1)S(1)}, bf16[6,128,256]{2,1,0:T(8,128)(2,1)S(1)}, u32[]{:S(2)}, u32[]{:S(2)}) collective-permute-start(bf16[6,128,256]{2,1,0:T(8,128)(2,1)S(1)} %get-tuple-element.55), channel_id=1, source_target_pairs={{0,4},{4,8},{8,12},{1,5},{5,9},{9,13},{2,6},{6,10},{10,14},{3,7},{... | collective-permute-start | bytes 1179656 | tf_op jit(solution)/shard_map/cond/branch_1_fun/ppermute | solution.py:33
  55.2 13.1 %collective-permute-start.20 = (bf16[6,128,256]{2,1,0:T(8,128)(2,1)S(1)}, bf16[6,128,256]{2,1,0:T(8,128)(2,1)S(1)}, u32[]{:S(2)}, u32[]{:S(2)}) collective-permute-start(bf16[6,128,256]{2,1,0:T(8,128)(2,1)S(1)} %get-tuple-element.56), channel_id=1, source_target_pairs={{4,0},{8,4},{12,8},{5,1},{9,5},{13,9},{6,2},{10,6},{14,10},{7,3},{... | collective-permute-start | bytes 1179656 | tf_op jit(solution)/shard_map/cond/branch_1_fun/ppermute | solution.py:33
  56.5 11.8 %collective-permute-start.22 = (bf16[6,128,256]{2,1,0:T(8,128)(2,1)S(1)}, bf16[6,128,256]{2,1,0:T(8,128)(2,1)S(1)}, u32[]{:S(2)}, u32[]{:S(2)}) collective-permute-start(bf16[6,128,256]{2,1,0:T(8,128)(2,1)S(1)} %get-tuple-element.70.refs_1_), channel_id=1, source_target_pairs={{0,2},{2,0},{1,3},{3,1},{4,6},{6,4},{5,7},{7,5},{8,10},{10,8},{9,1... | collective-permute-start | bytes 1179656 | tf_op jit(solution)/shard_map/cond/branch_1_fun/ppermute | solution.py:37
  58.1 10.2 %collective-permute-start.21 = (bf16[6,128,256]{2,1,0:T(8,128)(2,1)S(1)}, bf16[6,128,256]{2,1,0:T(8,128)(2,1)S(1)}, u32[]{:S(2)}, u32[]{:S(2)}) collective-permute-start(bf16[6,128,256]{2,1,0:T(8,128)(2,1)S(1)} %get-tuple-element.70.refs_1_), channel_id=1, source_target_pairs={{0,1},{1,0},{2,3},{3,2},{4,5},{5,4},{6,7},{7,6},{8,9},{9,8},{10,11... | collective-permute-start | bytes 1179656 | tf_op jit(solution)/shard_map/cond/branch_1_fun/ppermute | solution.py:37
  68.3 8.2 %collective-permute-start.28 = (bf16[6,128,256]{2,1,0:T(8,128)(2,1)S(1)}, bf16[6,128,256]{2,1,0:T(8,128)(2,1)S(1)}, u32[]{:S(2)}, u32[]{:S(2)}) collective-permute-start(bf16[6,128,256]{2,1,0:T(8,128)(2,1)S(1)} %collective-permute-done.22.refs_3_), channel_id=1, source_target_pairs={{0,1},{1,0},{2,3},{3,2},{4,5},{5,4},{6,7},{7,6},{8,9},{9,8},{10,11... | collective-permute-start | bytes 1179656 | tf_op jit(solution)/shard_map/cond/branch_1_fun/ppermute | solution.py:37
  69.7 12.8 %collective-permute-start.24 = (bf16[6,128,256]{2,1,0:T(8,128)(2,1)S(1)}, bf16[6,128,256]{2,1,0:T(8,128)(2,1)S(1)}, u32[]{:S(2)}, u32[]{:S(2)}) collective-permute-start(bf16[6,128,256]{2,1,0:T(8,128)(2,1)S(1)} %get-tuple-element.67), channel_id=1, source_target_pairs={{0,4},{4,8},{8,12},{1,5},{5,9},{9,13},{2,6},{6,10},{10,14},{3,7},{... | collective-permute-start | bytes 1179656 | tf_op jit(solution)/shard_map/cond/branch_1_fun/ppermute | solution.py:33
  73.5 13.1 %collective-permute-start.25 = (bf16[6,128,256]{2,1,0:T(8,128)(2,1)S(1)}, bf16[6,128,256]{2,1,0:T(8,128)(2,1)S(1)}, u32[]{:S(2)}, u32[]{:S(2)}) collective-permute-start(bf16[6,128,256]{2,1,0:T(8,128)(2,1)S(1)} %get-tuple-element.68), channel_id=1, source_target_pairs={{4,0},{8,4},{12,8},{5,1},{9,5},{13,9},{6,2},{10,6},{14,10},{7,3},{... | collective-permute-start | bytes 1179656 | tf_op jit(solution)/shard_map/cond/branch_1_fun/ppermute | solution.py:33
  75.0 11.7 %collective-permute-start.27 = (bf16[6,128,256]{2,1,0:T(8,128)(2,1)S(1)}, bf16[6,128,256]{2,1,0:T(8,128)(2,1)}, u32[]{:S(2)}, u32[]{:S(2)}) collective-permute-start(bf16[6,128,256]{2,1,0:T(8,128)(2,1)S(1)} %get-tuple-element.79.refs_1_), channel_id=1, source_target_pairs={{0,2},{2,0},{1,3},{3,1},{4,6},{6,4},{5,7},{7,5},{8,10},{10,8},{9,1... | collective-permute-start | bytes 1179656 | tf_op jit(solution)/shard_map/cond/branch_1_fun/ppermute | solution.py:37
  76.5 10.1 %collective-permute-start.26 = (bf16[6,128,256]{2,1,0:T(8,128)(2,1)S(1)}, bf16[6,128,256]{2,1,0:T(8,128)(2,1)S(1)}, u32[]{:S(2)}, u32[]{:S(2)}) collective-permute-start(bf16[6,128,256]{2,1,0:T(8,128)(2,1)S(1)} %get-tuple-element.79.refs_1_), channel_id=1, source_target_pairs={{0,1},{1,0},{2,3},{3,2},{4,5},{5,4},{6,7},{7,6},{8,9},{9,8},{10,11... | collective-permute-start | bytes 1179656 | tf_op jit(solution)/shard_map/cond/branch_1_fun/ppermute | solution.py:37
  87.6 10.6 %collective-permute-start.30 = (bf16[6,128,256]{2,1,0:T(8,128)(2,1)S(1)}, bf16[6,128,256]{2,1,0:T(8,128)(2,1)S(1)}, u32[]{:S(2)}, u32[]{:S(2)}) collective-permute-start(bf16[6,128,256]{2,1,0:T(8,128)(2,1)S(1)} %pack.7.refs_1_), channel_id=1, source_target_pairs={{0,2},{2,0},{1,3},{3,1},{4,6},{6,4},{5,7},{7,5},{8,10},{10,8},{9,1... | collective-permute-start | bytes 1179656 | tf_op jit(solution)/shard_map/cond/branch_1_fun/ppermute | solution.py:37
  89.2 9.8 %collective-permute-start.32 = (bf16[6,128,256]{2,1,0:T(8,128)(2,1)}, bf16[6,128,256]{2,1,0:T(8,128)(2,1)}, u32[]{:S(2)}, u32[]{:S(2)}) collective-permute-start(bf16[6,128,256]{2,1,0:T(8,128)(2,1)} %collective-permute-done.27.refs_3_), channel_id=1, source_target_pairs={{0,1},{1,0},{2,3},{3,2},{4,5},{5,4},{6,7},{7,6},{8,9},{9,8},{10,11... | collective-permute-start | bytes 1179656 | tf_op jit(solution)/shard_map/cond/branch_1_fun/ppermute | solution.py:37
  89.2 18.2 %collective-permute-start.29 = (bf16[6,128,256]{2,1,0:T(8,128)(2,1)S(1)}, bf16[6,128,256]{2,1,0:T(8,128)(2,1)}, u32[]{:S(2)}, u32[]{:S(2)}) collective-permute-start(bf16[6,128,256]{2,1,0:T(8,128)(2,1)S(1)} %pack.7.refs_1_), channel_id=1, source_target_pairs={{0,1},{1,0},{2,3},{3,2},{4,5},{5,4},{6,7},{7,6},{8,9},{9,8},{10,11... | collective-permute-start | bytes 1179656 | tf_op jit(solution)/shard_map/cond/branch_1_fun/ppermute | solution.py:37
  98.2 9.2 %collective-permute-start.31 = (bf16[6,128,256]{2,1,0:T(8,128)(2,1)S(1)}, bf16[6,128,256]{2,1,0:T(8,128)(2,1)}, u32[]{:S(2)}, u32[]{:S(2)}) collective-permute-start(bf16[6,128,256]{2,1,0:T(8,128)(2,1)S(1)} %collective-permute-done.30.refs_3_), channel_id=1, source_target_pairs={{0,1},{1,0},{2,3},{3,2},{4,5},{5,4},{6,7},{7,6},{8,9},{9,8},{10,11... | collective-permute-start | bytes 1179656 | tf_op jit(solution)/shard_map/cond/branch_1_fun/ppermute | solution.py:37
  (16 other events, 110.8 us)

commit v2 on v1

--- a/solution.py
+++ b/solution.py
@@ -23,6 +23,7 @@
 AHEAD = 8
 ROUNDS = 3
 CAP = 6
+GROUP = 3
 FIRST_ROUND = ENTRIES_EACH + 2 * AHEAD
 LANES = 128
 
@@ -37,44 +38,47 @@
     return lax.ppermute(value, axis, [(0, 1), (1, 0)])
 
 
-def project_kernel(gain_ref, *refs, held):
-    *pieces, key_weight, value_weight = refs[: len(refs) - 3 - held]
-    keys_out, values_out, normed = refs[-3:]
-    rows = normed.shape[0]
-    width = pieces[0].shape[2]
-    raw = [piece[...].reshape(rows, width).astype(jnp.float32) for piece in pieces]
-    squares = sum(jnp.sum(part * part, axis=1, keepdims=True) for part in raw)
-    scale = lax.rsqrt(squares / DE + EPS)
-    for index, part in enumerate(raw):
-        place = slice(index * width, (index + 1) * width)
-        normed[:, place] = (part * scale * gain_ref[:, place]).astype(jnp.bfloat16)
-    states = normed[...]
-    for weight, out in ((key_weight, keys_out), (value_weight, values_out)):
-        out[...] = jnp.dot(states, weight[...], preferred_element_type=jnp.float32).astype(jnp.bfloat16).reshape(out.shape)
-
-
-def project(gain, pieces, key_weight, value_weight, group, total, first=0, held=()):
+def project(marks, gain, pieces, key_weight, value_weight, group, total, number=0, held=()):
     count, tokens, width = pieces[0].shape
     columns = key_weight.shape[1]
+    steps = count // group
+    base = number * (len(pieces) + steps)
+
+    def kernel(marks_ref, gain_ref, *refs):
+        *parts, key_ref, value_ref = refs[: len(pieces) + 2]
+        keys_out, values_out, normed = refs[-3:]
+
+        @pl.when(marks_ref[base + len(pieces) + pl.program_id(0)] > 0)
+        def _():
+            raw = [part[...].reshape(group * tokens, width).astype(jnp.float32) for part in parts]
+            squares = sum(jnp.sum(part * part, axis=1, keepdims=True) for part in raw)
+            scale = lax.rsqrt(squares / DE + EPS)
+            for index, part in enumerate(raw):
+                place = pl.ds(pl.multiple_of(marks_ref[base + index] * width, width), width)
+                normed[:, place] = (part * scale * gain_ref[:, index * width : (index + 1) * width]).astype(jnp.bfloat16)
+            states = normed[...]
+            for weight, out in ((key_ref, keys_out), (value_ref, values_out)):
+                product = jnp.dot(states, weight[...], preferred_element_type=jnp.float32)
+                out[...] = product.astype(jnp.bfloat16).reshape(out.shape)
+
     out = jax.ShapeDtypeStruct((total, tokens, columns), jnp.bfloat16)
-    piece_spec = pl.BlockSpec((group, tokens, width), lambda i: (i, 0, 0))
-    weight_spec = pl.BlockSpec((DE, columns), lambda i: (0, 0))
-    out_spec = pl.BlockSpec((group, tokens, columns), lambda i: (i + first // group, 0, 0))
-    operands = (gain, *pieces, key_weight, value_weight, *held)
-
-    def kernel(*refs):
-        project_kernel(*refs, held=len(held))
-
+    piece_spec = pl.BlockSpec((group, tokens, width), lambda i, _: (i, 0, 0))
+    weight_spec = pl.BlockSpec((DE, columns), lambda i, _: (0, 0))
+    out_spec = pl.BlockSpec((group, tokens, columns), lambda i, _: (i + number * steps, 0, 0))
+    operands = (marks, gain, *pieces, key_weight, value_weight, *held)
     return pl.pallas_call(
         kernel,
         out_shape=(out, out),
-        grid=(count // group,),
-        in_specs=[pl.BlockSpec((1, DE), lambda i: (0, 0))]
-        + [piece_spec] * len(pieces)
-        + [weight_spec] * 2
-        + [pl.BlockSpec(memory_space=pl.ANY)] * len(held),
-        out_specs=(out_spec, out_spec),
-        scratch_shapes=[pltpu.VMEM((group * tokens, DE), jnp.bfloat16)],
+        grid_spec=pltpu.PrefetchScalarGridSpec(
+            num_scalar_prefetch=1,
+            grid=(steps,),
+            in_specs=[pl.BlockSpec((1, DE), lambda i, _: (0, 0))]
+            + [piece_spec] * len(pieces)
+            + [weight_spec] * 2
+            + [pl.BlockSpec(memory_space=pl.ANY)] * len(held),
+            out_specs=(out_spec, out_spec),
+            scratch_shapes=[pltpu.VMEM((group * tokens, DE), jnp.bfloat16)],
+        ),
         input_output_aliases={len(operands) - len(held) + i: i for i in range(len(held))},
         compiler_params=pltpu.CompilerParams(vmem_limit_bytes=VMEM_LIMIT),
         cost_estimate=pl.CostEstimate(
@@ -358,10 +362,9 @@
     return pool[(place * store.shape[0] + slots).reshape(-1)]
 
 
-def in_order_of_pieces(weight):
+def places_of_pieces():
     block = 2 * lax.axis_index("mp") + lax.axis_index("rep")
-    width = DE // 4
-    return jnp.concatenate([lax.dynamic_slice_in_dim(weight, (block ^ i) * width, width, 0) for i in range(4)], axis=0)
+    return jnp.stack([block ^ i for i in range(4)]).astype(jnp.int32)
 
 
 def exchanged_table(codes):
@@ -392,41 +395,37 @@
     first = jnp.maximum(asked[:, 0], 0)
     asked = jnp.stack([first, jnp.where(asked[:, 1] >= 0, asked[:, 1], first)], axis=1).reshape(-1)
 
+    plan, enc_gain = lax.optimization_barrier((plan, enc_gain))
+    gain = jnp.concatenate(four_pieces(enc_gain[None]), axis=1)
+    places = places_of_pieces()
+    wanted = plan[2 * LANES : 2 * LANES + total].reshape(ROUNDS + 1, CAP)[:, ::GROUP] >= 0
+    marks = jnp.concatenate([jnp.broadcast_to(places, (ROUNDS + 1, 4)), wanted.astype(jnp.int32)], axis=1).reshape(-1)
+    planned_slots = plan[3 * LANES : 4 * LANES][asked]
+
     def planned():
-        slots = plan[3 * LANES : 4 * LANES][asked]
         pool = [store, early_up, early_down]
         held, pieces = (), []
+
+        def projected(number):
+            return project(marks, gain, pieces[number], key_weight, value_weight, GROUP, total, number, held)
+
         for number in range(ROUNDS + 1):
             *ways, mine = pack(plan, number, pool)
             arrived = [shifted(way, "seq", steps) for way, steps in zip(ways, (1, -1))]
             pieces.append([mine, swapped(mine, "rep"), swapped(mine, "mp")])
-            if number == 0:
-                mine, later_keys, later_values, later_gain = lax.optimization_barrier(
-                    (mine, key_weight, value_weight, enc_gain)
-                )
-                ordered_gain = jnp.concatenate(four_pieces(later_gain[None]), axis=1)
-                ordered = [in_order_of_pieces(weight) for weight in (later_keys, later_values)]
-                after = (ordered_gain, *ordered)
-            else:
+            if number > 0:
                 pieces[number - 1].append(swapped(pieces[number - 1][2], "rep"))
-                held = project(ordered_gain, pieces[number - 1], *ordered, 3, total, (number - 1) * CAP, held)
-                after = held
-            if number < ROUNDS:
-                arrived, pieces[number], after = lax.optimization_barrier((arrived, pieces[number], after))
-                if number == 0:
-                    ordered_gain, *ordered = after
-                else:
-                    held = after
-                pool += arrived
+                held = projected(number - 1)
+            arrived, pieces[number], held = lax.optimization_barrier((arrived, pieces[number], held))
+            pool += arrived
         pieces[ROUNDS].append(swapped(pieces[ROUNDS][2], "rep"))
-        held = project(ordered_gain, pieces[ROUNDS], *ordered, 3, total, ROUNDS * CAP, held)
-        return (slots, *held)
+        return (planned_slots, *projected(ROUNDS))
 
     def whole():
         mine = fetch_all(store, asked >> 4, asked & (ENTRIES_EACH - 1))
-        gain = jnp.concatenate(four_pieces(enc_gain[None]), axis=1)
-        ordered = [in_order_of_pieces(weight) for weight in (key_weight, value_weight)]
-        return (jnp.arange(total, dtype=jnp.int32), *project(gain, four_pieces(mine), *ordered, 4, total))
+        whole_marks = jnp.concatenate([places, jnp.ones((total // 4,), jnp.int32)])
+        keys, values = project(whole_marks, gain, four_pieces(mine), key_weight, value_weight, 4, total)
+        return jnp.arange(total, dtype=jnp.int32), keys, values
 
     slots, keys, values = lax.cond(missing == 0, planned, whole)
     return attend(slots, counts, queries, keys, values)
@@ -437,7 +436,8 @@
     owners, slots, counts = previous_rows(nbr_owner, nbr_slot, nbr_count)
     total = owners.size
     pieces = [fetch_by_request(store, owners, slots)]
-    keys, values = project(gain, pieces, key_weight, value_weight, 4, total)
+    marks = jnp.concatenate([jnp.zeros((1,), jnp.int32), jnp.ones((total // 4,), jnp.int32)])
+    keys, values = project(marks, gain, pieces, key_weight, value_weight, 4, total)
     return attend(jnp.arange(total, dtype=jnp.int32), counts, queries, keys, values)
 
 

time: 126 us -> 121 us (0.960)
  waiting for transfers between devices: 32.4 us -> 22.3 us
  Pallas kernels: 41.9 us -> 49.6 us
  local copies, waits for them, and re-layouts: 12.2 us -> 8.9 us
    ppermute x8, waiting for transfers between devices: 21.1 us -> 13.5 us  [shifted(): lax.ppermute(value, axis, [(source, source + steps) for source in range(f...]
    pallas_call x4, Pallas kernels: 22.7 us -> 29.6 us  [project(): pl.pallas_call(kernel, out_shape=(out, out), grid_spec=pltpu.PrefetchScal...]
    dynamic_slice x1 -> x0, local copies, waits for them, and re-layouts: 2.6 us -> none  [in_order_of_pieces(): lax.dynamic_slice_in_dim(weight, (block ^ i) * width, width, 0)]
    ppermute x16, waiting for transfers between devices: 11.2 us -> 8.87 us  [swapped(): return lax.ppermute(value, axis, [(0, 1), (1, 0)])]
    cond x24 -> x22, local copies, waits for them, and re-layouts: 4.58 us -> 2.6 us
  transfers between devices with their start and end apart: 27 -> 27, of which waited for: 10 -> 7; matrix products, arithmetic and copies ran while one was open for 5% -> 6% of each run, Pallas kernels for 17% -> 23%
where the time goes in v2:
time: 121 us
  Pallas kernels  49.6 us (41%)
  starting transfers between devices  36.4 us (30%)
  waiting for transfers between devices  22.3 us (18%)
  local copies, waits for them, and re-layouts  8.9 us (7%)
  other arithmetic  2.5 us (2%)
    pallas_call x4, Pallas kernels, project(): pl.pallas_call(kernel, out_shape=(out, out), grid_spec=pltpu.PrefetchScal...  29.6 us
    ppermute x8, starting transfers between devices, shifted(): lax.ppermute(value, axis, [(source, source + steps) for source in range(f...  22 us
    ppermute x8, waiting for transfers between devices, shifted(): lax.ppermute(value, axis, [(source, source + steps) for source in range(f...  13.5 us
    pallas_call x1, Pallas kernels, attend(): pl.pallas_call(attend_kernel, out_shape=jax.ShapeDtypeStruct(queries.shap...  10.2 us
    ppermute x16, waiting for transfers between devices, swapped(): return lax.ppermute(value, axis, [(0, 1), (1, 0)])  8.87 us
    ppermute x16, starting transfers between devices, swapped(): return lax.ppermute(value, axis, [(0, 1), (1, 0)])  8.62 us
    pallas_call x4, Pallas kernels, pack(): pl.pallas_call(kernel, out_shape=(shape,) * kinds, grid_spec=pltpu.Prefet...  7.94 us
    ppermute x3, starting transfers between devices, exchanged_table(): lax.ppermute(codes, 'seq', [(chip, chip ^ offset) for chip in range(CHIPS)])  5.76 us
  transfers between devices with their start and end apart: 27, of which 7 were waited for; matrix products, arithmetic and copies ran while one was open for 6% of the time, Pallas kernels for 23%

profile of v2, /device:TPU:0, one launch (start us, length us, event | category | flops | bytes accessed | tf_op | source)
XLA Modules:
  0.0 120.7 jit_solution(13291644566190868107)
XLA Ops:
  0.9 5.1 %collective-permute-start.29 = (s32[24]{0:T(128)S(1)}, s32[24]{0:T(128)S(1)}, u32[]{:S(2)}, u32[]{:S(2)}) collective-permute-start(s32[24]{0:T(128)S(1)} %reshape.112), channel_id=1, source_target_pairs={{0,12},{4,8},{8,4},{12,0},{1,13},{5,9},{9,5},{13,1},{2,14},{6,10},... | collective-permute-start | bytes 296 | tf_op jit(solution)/shard_map/ppermute | solution.py:373
  9.0 4.6 %collective-permute-start.34 = (bf16[8,128,256]{2,1,0:T(8,128)(2,1)S(1)}, bf16[8,128,256]{2,1,0:T(8,128)(2,1)S(1)}, u32[]{:S(2)}, u32[]{:S(2)}) collective-permute-start(bf16[8,128,256]{2,1,0:T(8,128)(2,1)S(1)} %slice.42), channel_id=1, source_target_pairs={{0,4},{4,8},{8,12},{1,5},{5,9},{9,13},{2,6},{6,10},{10,14},{3,7},{... | collective-permute-start | bytes 1572872 | tf_op jit(solution)/shard_map/ppermute | solution.py:34
  13.8 1.7 %collective-permute-start.30 = (s32[4,24]{1,0:T(4,128)S(1)}, s32[4,24]{1,0:T(4,128)S(1)}, u32[]{:S(2)}, u32[]{:S(2)}) collective-permute-start(s32[4,24]{1,0:T(4,128)S(1)} %pad_add_fusion), channel_id=1, source_target_pairs={{0,16},{16,0},{1,17},{17,1},{2,18},{18,2},{3,19},{19,3},{4,20},{20... | collective-permute-start | bytes 1160 | tf_op jit(solution)/shard_map/ppermute | solution.py:38
  15.7 1.7 %collective-permute-done.30 = s32[4,24]{1,0:T(4,128)S(1)} collective-permute-done((s32[4,24]{1,0:T(4,128)S(1)}, s32[4,24]{1,0:T(4,128)S(1)}, u32[]{:S(2)}, u32[]{:S(2)}) %collective-permute-start.30) | collective-permute-done | bytes 416 | tf_op jit(solution)/shard_map/ppermute | solution.py:38
  18.1 1.9 %plan.1 = s32[8,128]{1,0:T(8,128)S(1)} custom-call(s32[1]{0:T(128)} %bitcast.2.place, s32[192]{0:T(256)} %reshape.113.table), custom_call_target="tpu_custom_call" | custom-call | tf_op jit(solution)/shard_map/plan/pallas_call | solution.py:284
  20.0 1.7 %collective-permute-start.32 = (f32[1,256]{1,0:T(1,128)}, f32[1,256]{1,0:T(1,128)S(1)}, u32[]{:S(2)}, u32[]{:S(2)}) collective-permute-start(f32[1,256]{1,0:T(1,128)} %bitcast.28), channel_id=1, source_target_pairs={{0,2},{2,0},{1,3},{3,1},{4,6},{6,4},{5,7},{7,5},{8,10},{10,8},{9,1... | collective-permute-start | bytes 3080 | tf_op jit(solution)/shard_map/ppermute | solution.py:38
  26.7 83.8 %conditional.1 = (s32[24]{0:T(128)}, bf16[24,128,1024]{2,1,0:T(8,128)(2,1)}, bf16[24,128,1024]{2,1,0:T(8,128)(2,1)}) conditional(s32[]{:T(128)} %bitcast.7, (s32[4]{0:T(128)S(1)}, bf16[16,128,256]{2,1,0:T(8,128)(2,1)}, s32[12,2]{0,1:T(2,128)S(1)}, f32[1,1024]{1,0:T(1,128)S(1)}, bf16[1024,1024]{1,0:T(8,128)(2,1)}, ...), branch_computations={%region_0.1_spmd, %region_1.2_spmd} | conditional | flops 12884902912 | bytes 103292824 | solution.py:430
  27.3 2.5 %pack.4 = (bf16[6,128,256]{2,1,0:T(8,128)(2,1)S(1)}, bf16[6,128,256]{2,1,0:T(8,128)(2,1)S(1)}, bf16[6,128,256]{2,1,0:T(8,128)(2,1)S(1)}) custom-call(s32[1024]{0:T(1024)S(1)} %get-tuple-element.58.plan_ref, bf16[16,128,256]{2,1,0:T(8,128)(2,1)} %get-tuple-element.62.refs_0_, bf16[8,128,256]{2,1,0:T(8,128)(2,1)} %get-tuple-element.63.refs_1_, ...), custom_call_target="tpu_custom_call" | custom-call | bytes 2359296 | tf_op jit(solution)/shard_map/cond/branch_1_fun/pack/pallas_call | solution.py:314
  29.8 3.3 %collective-permute-start.9 = (bf16[6,128,256]{2,1,0:T(8,128)(2,1)S(1)}, bf16[6,128,256]{2,1,0:T(8,128)(2,1)S(1)}, u32[]{:S(2)}, u32[]{:S(2)}) collective-permute-start(bf16[6,128,256]{2,1,0:T(8,128)(2,1)S(1)} %get-tuple-element.65), channel_id=1, source_target_pairs={{0,4},{4,8},{8,12},{1,5},{5,9},{9,13},{2,6},{6,10},{10,14},{3,7},{... | collective-permute-start | bytes 1179656 | tf_op jit(solution)/shard_map/cond/branch_1_fun/ppermute | solution.py:34
  34.4 1.6 %collective-permute-start.12 = (bf16[6,128,256]{2,1,0:T(8,128)(2,1)S(1)}, bf16[6,128,256]{2,1,0:T(8,128)(2,1)}, u32[]{:S(2)}, u32[]{:S(2)}) collective-permute-start(bf16[6,128,256]{2,1,0:T(8,128)(2,1)S(1)} %get-tuple-element.73.refs_0_), channel_id=1, source_target_pairs={{0,2},{2,0},{1,3},{3,1},{4,6},{6,4},{5,7},{7,5},{8,10},{10,8},{9,1... | collective-permute-start | bytes 1179656 | tf_op jit(solution)/shard_map/cond/branch_1_fun/ppermute | solution.py:38
  35.9 6.1 %collective-permute-done.9.refs_3_ = bf16[6,128,256]{2,1,0:T(8,128)(2,1)S(1)} collective-permute-done((bf16[6,128,256]{2,1,0:T(8,128)(2,1)S(1)}, bf16[6,128,256]{2,1,0:T(8,128)(2,1)S(1)}, u32[]{:S(2)}, u32[]{:S(2)}) %collective-permute-start.9) | collective-permute-done | bytes 393248 | tf_op jit(solution)/shard_map/cond/branch_1_fun/ppermute | solution.py:34
  42.1 4.1 %collective-permute-done.10.refs_4_ = bf16[6,128,256]{2,1,0:T(8,128)(2,1)S(1)} collective-permute-done((bf16[6,128,256]{2,1,0:T(8,128)(2,1)S(1)}, bf16[6,128,256]{2,1,0:T(8,128)(2,1)S(1)}, u32[]{:S(2)}, u32[]{:S(2)}) %collective-permute-start.10) | collective-permute-done | bytes 393248 | tf_op jit(solution)/shard_map/cond/branch_1_fun/ppermute | solution.py:34
  46.3 3.1 %pack.5 = (bf16[6,128,256]{2,1,0:T(8,128)(2,1)}, bf16[6,128,256]{2,1,0:T(8,128)(2,1)}, bf16[6,128,256]{2,1,0:T(8,128)(2,1)S(1)}) custom-call(s32[1024]{0:T(1024)S(1)} %get-tuple-element.58.plan_ref, bf16[16,128,256]{2,1,0:T(8,128)(2,1)} %get-tuple-element.62.refs_0_, bf16[8,128,256]{2,1,0:T(8,128)(2,1)} %get-tuple-element.63.refs_1_, ...), custom_call_target="tpu_custom_call" | custom-call | bytes 2359296 | tf_op jit(solution)/shard_map/cond/branch_1_fun/pack/pallas_call | solution.py:314
  49.5 4.2 %collective-permute-start.13 = (bf16[6,128,256]{2,1,0:T(8,128)(2,1)}, bf16[6,128,256]{2,1,0:T(8,128)(2,1)S(1)}, u32[]{:S(2)}, u32[]{:S(2)}) collective-permute-start(bf16[6,128,256]{2,1,0:T(8,128)(2,1)} %get-tuple-element.70), channel_id=1, source_target_pairs={{0,4},{4,8},{8,12},{1,5},{5,9},{9,13},{2,6},{6,10},{10,14},{3,7},{... | collective-permute-start | bytes 1179656 | tf_op jit(solution)/shard_map/cond/branch_1_fun/ppermute | solution.py:34
  55.0 1.6 %collective-permute-start.16 = (bf16[6,128,256]{2,1,0:T(8,128)(2,1)S(1)}, bf16[6,128,256]{2,1,0:T(8,128)(2,1)}, u32[]{:S(2)}, u32[]{:S(2)}) collective-permute-start(bf16[6,128,256]{2,1,0:T(8,128)(2,1)S(1)} %get-tuple-element.85.refs_0_), channel_id=1, source_target_pairs={{0,2},{2,0},{1,3},{3,1},{4,6},{6,4},{5,7},{7,5},{8,10},{10,8},{9,1... | collective-permute-start | bytes 1179656 | tf_op jit(solution)/shard_map/cond/branch_1_fun/ppermute | solution.py:38
  59.3 9.1 %project.6 = (bf16[24,128,1024]{2,1,0:T(8,128)(2,1)}, bf16[24,128,1024]{2,1,0:T(8,128)(2,1)}) custom-call(s32[24]{0:T(128)S(1)} %reshape.104.marks_ref, f32[1,1024]{1,0:T(1,128)S(1)} %get-tuple-element.61.gain_ref, bf16[6,128,256]{2,1,0:T(8,128)(2,1)S(1)} %copy-done.2, bf16[6,128,256]{2,1,0:T(8,128)(2,1)S(1)} %copy-done.4, ...), custom_call_target="tpu_custom_call" | custom-call | flops 3221225472 | bytes 8912896 | tf_op jit(solution)/shard_map/cond/branch_1_fun/project/pallas_call | solution.py:69
  70.4 4.6 %collective-permute-start.18 = (bf16[6,128,256]{2,1,0:T(8,128)(2,1)S(1)}, bf16[6,128,256]{2,1,0:T(8,128)(2,1)S(1)}, u32[]{:S(2)}, u32[]{:S(2)}) collective-permute-start(bf16[6,128,256]{2,1,0:T(8,128)(2,1)S(1)} %get-tuple-element.82), channel_id=1, source_target_pairs={{0,4},{4,8},{8,12},{1,5},{5,9},{9,13},{2,6},{6,10},{10,14},{3,7},{... | collective-permute-start | bytes 1179656 | tf_op jit(solution)/shard_map/cond/branch_1_fun/ppermute | solution.py:34
  75.0 1.5 %collective-permute-start.19 = (bf16[6,128,256]{2,1,0:T(8,128)(2,1)S(1)}, bf16[6,128,256]{2,1,0:T(8,128)(2,1)S(1)}, u32[]{:S(2)}, u32[]{:S(2)}) collective-permute-start(bf16[6,128,256]{2,1,0:T(8,128)(2,1)S(1)} %get-tuple-element.83), channel_id=1, source_target_pairs={{4,0},{8,4},{12,8},{5,1},{9,5},{13,9},{6,2},{10,6},{14,10},{7,3},{... | collective-permute-start | bytes 1179656 | tf_op jit(solution)/shard_map/cond/branch_1_fun/ppermute | solution.py:34
  77.1 7.4 %project.7 = (bf16[24,128,1024]{2,1,0:T(8,128)(2,1)}, bf16[24,128,1024]{2,1,0:T(8,128)(2,1)}) custom-call(s32[24]{0:T(128)S(1)} %reshape.104.marks_ref, f32[1,1024]{1,0:T(1,128)S(1)} %get-tuple-element.61.gain_ref, bf16[6,128,256]{2,1,0:T(8,128)(2,1)S(1)} %get-tuple-element.85.refs_0_, ...), custom_call_target="tpu_custom_call", output_to_operand_aliasing={{0}: (8, {}), {1}: (9, {})} | custom-call | flops 3221225472 | bytes 8912896 | tf_op jit(solution)/shard_map/cond/branch_1_fun/project/pallas_call | solution.py:69
  84.5 3.2 %collective-permute-done.19.refs_8_ = bf16[6,128,256]{2,1,0:T(8,128)(2,1)S(1)} collective-permute-done((bf16[6,128,256]{2,1,0:T(8,128)(2,1)S(1)}, bf16[6,128,256]{2,1,0:T(8,128)(2,1)S(1)}, u32[]{:S(2)}, u32[]{:S(2)}) %collective-permute-start.19) | collective-permute-done | bytes 393248 | tf_op jit(solution)/shard_map/cond/branch_1_fun/ppermute | solution.py:34
  89.4 4.6 %project.8 = (bf16[24,128,1024]{2,1,0:T(8,128)(2,1)}, bf16[24,128,1024]{2,1,0:T(8,128)(2,1)}) custom-call(s32[24]{0:T(128)S(1)} %reshape.104.marks_ref, f32[1,1024]{1,0:T(1,128)S(1)} %get-tuple-element.61.gain_ref, bf16[6,128,256]{2,1,0:T(8,128)(2,1)S(1)} %get-tuple-element.94.refs_0_, ...), custom_call_target="tpu_custom_call", output_to_operand_aliasing={{0}: (8, {}), {1}: (9, {})} | custom-call | flops 3221225472 | bytes 8912896 | tf_op jit(solution)/shard_map/cond/branch_1_fun/project/pallas_call | solution.py:69
  94.0 6.2 %collective-permute-done.24.refs_2_ = bf16[6,128,256]{2,1,0:T(8,128)(2,1)S(1)} collective-permute-done((bf16[6,128,256]{2,1,0:T(8,128)(2,1)S(1)}, bf16[6,128,256]{2,1,0:T(8,128)(2,1)S(1)}, u32[]{:S(2)}, u32[]{:S(2)}) %collective-permute-start.24) | collective-permute-done | bytes 393248 | tf_op jit(solution)/shard_map/cond/branch_1_fun/ppermute | solution.py:38
  101.9 8.6 %project.9 = (bf16[24,128,1024]{2,1,0:T(8,128)(2,1)}, bf16[24,128,1024]{2,1,0:T(8,128)(2,1)}) custom-call(s32[24]{0:T(128)S(1)} %reshape.104.marks_ref, f32[1,1024]{1,0:T(1,128)S(1)} %get-tuple-element.61.gain_ref, bf16[6,128,256]{2,1,0:T(8,128)(2,1)S(1)} %pack.7.refs_0_, ...), custom_call_target="tpu_custom_call", output_to_operand_aliasing={{0}: (8, {}), {1}: (9, {})} | custom-call | flops 3221225472 | bytes 8912896 | tf_op jit(solution)/shard_map/cond/branch_1_fun/project/pallas_call | solution.py:69
  110.5 10.2 %attend.1 = bf16[768,1024]{1,0:T(8,128)(2,1)} custom-call(s32[24]{0:T(128)} %get-tuple-element.115.slots, s32[12]{0:T(128)S(1)} %convert_reduce_fusion.counts, bf16[768,1024]{1,0:T(8,128)(2,1)S(1)} %copy-done, bf16[24,128,1024]{2,1,0:T(8,128)(2,1)} %get-tuple-element.116.refs_0_.refs_1_.refs_2_.refs_3_.refs_4_.refs_5_, ...), custom_call_target="tpu_custom_call" | custom-call | flops 1610612736 | bytes 15728640 | tf_op jit(solution)/shard_map/attend/pallas_call | solution.py:152
  (104 shorter events, 21.3 us)
Async XLA Ops:
  0.9 12.9 %collective-permute-start.29 = (s32[24]{0:T(128)S(1)}, s32[24]{0:T(128)S(1)}, u32[]{:S(2)}, u32[]{:S(2)}) collective-permute-start(s32[24]{0:T(128)S(1)} %reshape.112), channel_id=1, source_target_pairs={{0,12},{4,8},{8,4},{12,0},{1,13},{5,9},{9,5},{13,1},{2,14},{6,10},... | collective-permute-start | bytes 296 | tf_op jit(solution)/shard_map/ppermute | solution.py:373
  6.0 7.8 %collective-permute-start.28 = (s32[24]{0:T(128)S(1)}, s32[24]{0:T(128)S(1)}, u32[]{:S(2)}, u32[]{:S(2)}) collective-permute-start(s32[24]{0:T(128)S(1)} %reshape.112), channel_id=1, source_target_pairs={{0,8},{4,12},{8,0},{12,4},{1,9},{5,13},{9,1},{13,5},{2,10},{6,14},... | collective-permute-start | bytes 296 | tf_op jit(solution)/shard_map/ppermute | solution.py:373
  6.0 7.8 %collective-permute-start.27 = (s32[24]{0:T(128)S(1)}, s32[24]{0:T(128)S(1)}, u32[]{:S(2)}, u32[]{:S(2)}) collective-permute-start(s32[24]{0:T(128)S(1)} %reshape.112), channel_id=1, source_target_pairs={{0,4},{4,0},{8,12},{12,8},{1,5},{5,1},{9,13},{13,9},{2,6},{6,2},{1... | collective-permute-start | bytes 296 | tf_op jit(solution)/shard_map/ppermute | solution.py:373
  7.7 18.0 %collective-permute-start.35 = (bf16[8,128,256]{2,1,0:T(8,128)(2,1)S(1)}, bf16[8,128,256]{2,1,0:T(8,128)(2,1)S(1)}, u32[]{:S(2)}, u32[]{:S(2)}) collective-permute-start(bf16[8,128,256]{2,1,0:T(8,128)(2,1)S(1)} %slice.42), channel_id=1, source_target_pairs={{4,0},{8,4},{12,8},{5,1},{9,5},{13,9},{6,2},{10,6},{14,10},{7,3},{... | collective-permute-start | bytes 1572872 | tf_op jit(solution)/shard_map/ppermute | solution.py:34
  9.0 16.7 %collective-permute-start.34 = (bf16[8,128,256]{2,1,0:T(8,128)(2,1)S(1)}, bf16[8,128,256]{2,1,0:T(8,128)(2,1)S(1)}, u32[]{:S(2)}, u32[]{:S(2)}) collective-permute-start(bf16[8,128,256]{2,1,0:T(8,128)(2,1)S(1)} %slice.42), channel_id=1, source_target_pairs={{0,4},{4,8},{8,12},{1,5},{5,9},{9,13},{2,6},{6,10},{10,14},{3,7},{... | collective-permute-start | bytes 1572872 | tf_op jit(solution)/shard_map/ppermute | solution.py:34
  13.8 3.7 %collective-permute-start.30 = (s32[4,24]{1,0:T(4,128)S(1)}, s32[4,24]{1,0:T(4,128)S(1)}, u32[]{:S(2)}, u32[]{:S(2)}) collective-permute-start(s32[4,24]{1,0:T(4,128)S(1)} %pad_add_fusion), channel_id=1, source_target_pairs={{0,16},{16,0},{1,17},{17,1},{2,18},{18,2},{3,19},{19,3},{4,20},{20... | collective-permute-start | bytes 1160 | tf_op jit(solution)/shard_map/ppermute | solution.py:38
  20.0 3.8 %collective-permute-start.32 = (f32[1,256]{1,0:T(1,128)}, f32[1,256]{1,0:T(1,128)S(1)}, u32[]{:S(2)}, u32[]{:S(2)}) collective-permute-start(f32[1,256]{1,0:T(1,128)} %bitcast.28), channel_id=1, source_target_pairs={{0,2},{2,0},{1,3},{3,1},{4,6},{6,4},{5,7},{7,5},{8,10},{10,8},{9,1... | collective-permute-start | bytes 3080 | tf_op jit(solution)/shard_map/ppermute | solution.py:38
  21.7 3.3 %collective-permute-start.31 = (f32[1,256]{1,0:T(1,128)}, f32[1,256]{1,0:T(1,128)S(1)}, u32[]{:S(2)}, u32[]{:S(2)}) collective-permute-start(f32[1,256]{1,0:T(1,128)} %bitcast.29), channel_id=1, source_target_pairs={{0,1},{1,0},{2,3},{3,2},{4,5},{5,4},{6,7},{7,6},{8,9},{9,8},{10,11... | collective-permute-start | bytes 3080 | tf_op jit(solution)/shard_map/ppermute | solution.py:38
  29.8 12.3 %collective-permute-start.9 = (bf16[6,128,256]{2,1,0:T(8,128)(2,1)S(1)}, bf16[6,128,256]{2,1,0:T(8,128)(2,1)S(1)}, u32[]{:S(2)}, u32[]{:S(2)}) collective-permute-start(bf16[6,128,256]{2,1,0:T(8,128)(2,1)S(1)} %get-tuple-element.65), channel_id=1, source_target_pairs={{0,4},{4,8},{8,12},{1,5},{5,9},{9,13},{2,6},{6,10},{10,14},{3,7},{... | collective-permute-start | bytes 1179656 | tf_op jit(solution)/shard_map/cond/branch_1_fun/ppermute | solution.py:34
  33.1 13.1 %collective-permute-start.10 = (bf16[6,128,256]{2,1,0:T(8,128)(2,1)S(1)}, bf16[6,128,256]{2,1,0:T(8,128)(2,1)S(1)}, u32[]{:S(2)}, u32[]{:S(2)}) collective-permute-start(bf16[6,128,256]{2,1,0:T(8,128)(2,1)S(1)} %get-tuple-element.66), channel_id=1, source_target_pairs={{4,0},{8,4},{12,8},{5,1},{9,5},{13,9},{6,2},{10,6},{14,10},{7,3},{... | collective-permute-start | bytes 1179656 | tf_op jit(solution)/shard_map/cond/branch_1_fun/ppermute | solution.py:34
  34.4 11.8 %collective-permute-start.12 = (bf16[6,128,256]{2,1,0:T(8,128)(2,1)S(1)}, bf16[6,128,256]{2,1,0:T(8,128)(2,1)}, u32[]{:S(2)}, u32[]{:S(2)}) collective-permute-start(bf16[6,128,256]{2,1,0:T(8,128)(2,1)S(1)} %get-tuple-element.73.refs_0_), channel_id=1, source_target_pairs={{0,2},{2,0},{1,3},{3,1},{4,6},{6,4},{5,7},{7,5},{8,10},{10,8},{9,1... | collective-permute-start | bytes 1179656 | tf_op jit(solution)/shard_map/cond/branch_1_fun/ppermute | solution.py:38
  35.9 10.3 %collective-permute-start.11 = (bf16[6,128,256]{2,1,0:T(8,128)(2,1)S(1)}, bf16[6,128,256]{2,1,0:T(8,128)(2,1)S(1)}, u32[]{:S(2)}, u32[]{:S(2)}) collective-permute-start(bf16[6,128,256]{2,1,0:T(8,128)(2,1)S(1)} %get-tuple-element.73.refs_0_), channel_id=1, source_target_pairs={{0,1},{1,0},{2,3},{3,2},{4,5},{5,4},{6,7},{7,6},{8,9},{9,8},{10,11... | collective-permute-start | bytes 1179656 | tf_op jit(solution)/shard_map/cond/branch_1_fun/ppermute | solution.py:38
  46.2 11.0 %collective-permute-start.17 = (bf16[6,128,256]{2,1,0:T(8,128)(2,1)}, bf16[6,128,256]{2,1,0:T(8,128)(2,1)}, u32[]{:S(2)}, u32[]{:S(2)}) collective-permute-start(bf16[6,128,256]{2,1,0:T(8,128)(2,1)} %collective-permute-done.12.refs_2_), channel_id=1, source_target_pairs={{0,1},{1,0},{2,3},{3,2},{4,5},{5,4},{6,7},{7,6},{8,9},{9,8},{10,11... | collective-permute-start | bytes 1179656 | tf_op jit(solution)/shard_map/cond/branch_1_fun/ppermute | solution.py:38
  49.5 18.9 %collective-permute-start.13 = (bf16[6,128,256]{2,1,0:T(8,128)(2,1)}, bf16[6,128,256]{2,1,0:T(8,128)(2,1)S(1)}, u32[]{:S(2)}, u32[]{:S(2)}) collective-permute-start(bf16[6,128,256]{2,1,0:T(8,128)(2,1)} %get-tuple-element.70), channel_id=1, source_target_pairs={{0,4},{4,8},{8,12},{1,5},{5,9},{9,13},{2,6},{6,10},{10,14},{3,7},{... | collective-permute-start | bytes 1179656 | tf_op jit(solution)/shard_map/cond/branch_1_fun/ppermute | solution.py:34
  53.7 14.7 %collective-permute-start.14 = (bf16[6,128,256]{2,1,0:T(8,128)(2,1)}, bf16[6,128,256]{2,1,0:T(8,128)(2,1)S(1)}, u32[]{:S(2)}, u32[]{:S(2)}) collective-permute-start(bf16[6,128,256]{2,1,0:T(8,128)(2,1)} %get-tuple-element.71), channel_id=1, source_target_pairs={{4,0},{8,4},{12,8},{5,1},{9,5},{13,9},{6,2},{10,6},{14,10},{7,3},{... | collective-permute-start | bytes 1179656 | tf_op jit(solution)/shard_map/cond/branch_1_fun/ppermute | solution.py:34
  55.0 13.4 %collective-permute-start.16 = (bf16[6,128,256]{2,1,0:T(8,128)(2,1)S(1)}, bf16[6,128,256]{2,1,0:T(8,128)(2,1)}, u32[]{:S(2)}, u32[]{:S(2)}) collective-permute-start(bf16[6,128,256]{2,1,0:T(8,128)(2,1)S(1)} %get-tuple-element.85.refs_0_), channel_id=1, source_target_pairs={{0,2},{2,0},{1,3},{3,1},{4,6},{6,4},{5,7},{7,5},{8,10},{10,8},{9,1... | collective-permute-start | bytes 1179656 | tf_op jit(solution)/shard_map/cond/branch_1_fun/ppermute | solution.py:38
  56.5 11.9 %collective-permute-start.15 = (bf16[6,128,256]{2,1,0:T(8,128)(2,1)S(1)}, bf16[6,128,256]{2,1,0:T(8,128)(2,1)}, u32[]{:S(2)}, u32[]{:S(2)}) collective-permute-start(bf16[6,128,256]{2,1,0:T(8,128)(2,1)S(1)} %get-tuple-element.85.refs_0_), channel_id=1, source_target_pairs={{0,1},{1,0},{2,3},{3,2},{4,5},{5,4},{6,7},{7,6},{8,9},{9,8},{10,11... | collective-permute-start | bytes 1179656 | tf_op jit(solution)/shard_map/cond/branch_1_fun/ppermute | solution.py:38
  68.4 8.7 %collective-permute-start.22 = (bf16[6,128,256]{2,1,0:T(8,128)(2,1)}, bf16[6,128,256]{2,1,0:T(8,128)(2,1)S(1)}, u32[]{:S(2)}, u32[]{:S(2)}) collective-permute-start(bf16[6,128,256]{2,1,0:T(8,128)(2,1)} %collective-permute-done.16.refs_2_), channel_id=1, source_target_pairs={{0,1},{1,0},{2,3},{3,2},{4,5},{5,4},{6,7},{7,6},{8,9},{9,8},{10,11... | collective-permute-start | bytes 1179656 | tf_op jit(solution)/shard_map/cond/branch_1_fun/ppermute | solution.py:38
  70.4 14.1 %collective-permute-start.18 = (bf16[6,128,256]{2,1,0:T(8,128)(2,1)S(1)}, bf16[6,128,256]{2,1,0:T(8,128)(2,1)S(1)}, u32[]{:S(2)}, u32[]{:S(2)}) collective-permute-start(bf16[6,128,256]{2,1,0:T(8,128)(2,1)S(1)} %get-tuple-element.82), channel_id=1, source_target_pairs={{0,4},{4,8},{8,12},{1,5},{5,9},{9,13},{2,6},{6,10},{10,14},{3,7},{... | collective-permute-start | bytes 1179656 | tf_op jit(solution)/shard_map/cond/branch_1_fun/ppermute | solution.py:34
  75.0 12.7 %collective-permute-start.19 = (bf16[6,128,256]{2,1,0:T(8,128)(2,1)S(1)}, bf16[6,128,256]{2,1,0:T(8,128)(2,1)S(1)}, u32[]{:S(2)}, u32[]{:S(2)}) collective-permute-start(bf16[6,128,256]{2,1,0:T(8,128)(2,1)S(1)} %get-tuple-element.83), channel_id=1, source_target_pairs={{4,0},{8,4},{12,8},{5,1},{9,5},{13,9},{6,2},{10,6},{14,10},{7,3},{... | collective-permute-start | bytes 1179656 | tf_op jit(solution)/shard_map/cond/branch_1_fun/ppermute | solution.py:34
  76.4 11.2 %collective-permute-start.21 = (bf16[6,128,256]{2,1,0:T(8,128)(2,1)S(1)}, bf16[6,128,256]{2,1,0:T(8,128)(2,1)S(1)}, u32[]{:S(2)}, u32[]{:S(2)}) collective-permute-start(bf16[6,128,256]{2,1,0:T(8,128)(2,1)S(1)} %get-tuple-element.94.refs_0_), channel_id=1, source_target_pairs={{0,2},{2,0},{1,3},{3,1},{4,6},{6,4},{5,7},{7,5},{8,10},{10,8},{9,1... | collective-permute-start | bytes 1179656 | tf_op jit(solution)/shard_map/cond/branch_1_fun/ppermute | solution.py:38
  77.0 10.6 %collective-permute-start.20 = (bf16[6,128,256]{2,1,0:T(8,128)(2,1)S(1)}, bf16[6,128,256]{2,1,0:T(8,128)(2,1)S(1)}, u32[]{:S(2)}, u32[]{:S(2)}) collective-permute-start(bf16[6,128,256]{2,1,0:T(8,128)(2,1)S(1)} %get-tuple-element.94.refs_0_), channel_id=1, source_target_pairs={{0,1},{1,0},{2,3},{3,2},{4,5},{5,4},{6,7},{7,6},{8,9},{9,8},{10,11... | collective-permute-start | bytes 1179656 | tf_op jit(solution)/shard_map/cond/branch_1_fun/ppermute | solution.py:38
  88.6 11.6 %collective-permute-start.24 = (bf16[6,128,256]{2,1,0:T(8,128)(2,1)S(1)}, bf16[6,128,256]{2,1,0:T(8,128)(2,1)S(1)}, u32[]{:S(2)}, u32[]{:S(2)}) collective-permute-start(bf16[6,128,256]{2,1,0:T(8,128)(2,1)S(1)} %pack.7.refs_0_), channel_id=1, source_target_pairs={{0,2},{2,0},{1,3},{3,1},{4,6},{6,4},{5,7},{7,5},{8,10},{10,8},{9,1... | collective-permute-start | bytes 1179656 | tf_op jit(solution)/shard_map/cond/branch_1_fun/ppermute | solution.py:38
  89.2 11.0 %collective-permute-start.23 = (bf16[6,128,256]{2,1,0:T(8,128)(2,1)S(1)}, bf16[6,128,256]{2,1,0:T(8,128)(2,1)S(1)}, u32[]{:S(2)}, u32[]{:S(2)}) collective-permute-start(bf16[6,128,256]{2,1,0:T(8,128)(2,1)S(1)} %pack.7.refs_0_), channel_id=1, source_target_pairs={{0,1},{1,0},{2,3},{3,2},{4,5},{5,4},{6,7},{7,6},{8,9},{9,8},{10,11... | collective-permute-start | bytes 1179656 | tf_op jit(solution)/shard_map/cond/branch_1_fun/ppermute | solution.py:38
  (17 other events, 196.2 us)

commit v3 on v2

--- a/solution.py
+++ b/solution.py
@@ -16,7 +16,7 @@
 
 SEQ_SPEC = ("parts", "seq")
 FEATURES = ("mp", "rep")
-VMEM_LIMIT = 48 * 1024 * 1024
+VMEM_LIMIT = 28 * 1024 * 1024
 
 CHIPS = 4
 ENTRIES_EACH = 16
@@ -45,27 +45,34 @@
     base = number * (len(pieces) + steps)
 
     def kernel(marks_ref, gain_ref, *refs):
-        *parts, key_ref, value_ref = refs[: len(pieces) + 2]
-        keys_out, values_out, normed = refs[-3:]
+        parts, key_blocks, value_blocks = [refs[i * len(pieces) : (i + 1) * len(pieces)] for i in range(3)]
+        keys_out, values_out = refs[-2:]
 
         @pl.when(marks_ref[base + len(pieces) + pl.program_id(0)] > 0)
         def _():
             raw = [part[...].reshape(group * tokens, width).astype(jnp.float32) for part in parts]
             squares = sum(jnp.sum(part * part, axis=1, keepdims=True) for part in raw)
             scale = lax.rsqrt(squares / DE + EPS)
-            for index, part in enumerate(raw):
-                place = pl.ds(pl.multiple_of(marks_ref[base + index] * width, width), width)
-                normed[:, place] = (part * scale * gain_ref[:, index * width : (index + 1) * width]).astype(jnp.bfloat16)
-            states = normed[...]
-            for weight, out in ((key_ref, keys_out), (value_ref, values_out)):
-                product = jnp.dot(states, weight[...], preferred_element_type=jnp.float32)
+            states = [
+                (part * scale * gain_ref[:, index * width : (index + 1) * width]).astype(jnp.bfloat16)
+                for index, part in enumerate(raw)
+            ]
+            for blocks, out in ((key_blocks, keys_out), (value_blocks, values_out)):
+                product = sum(
+                    jnp.dot(state, block[...], preferred_element_type=jnp.float32)
+                    for state, block in zip(states, blocks)
+                )
                 out[...] = product.astype(jnp.bfloat16).reshape(out.shape)
 
     out = jax.ShapeDtypeStruct((total, tokens, columns), jnp.bfloat16)
     piece_spec = pl.BlockSpec((group, tokens, width), lambda i, _: (i, 0, 0))
-    weight_spec = pl.BlockSpec((DE, columns), lambda i, _: (0, 0))
+
+    def weight_spec(piece):
+        return pl.BlockSpec((width, columns), lambda i, marks: (marks[base + piece], 0))
+
+    weight_specs = [weight_spec(piece) for piece in range(len(pieces))]
     out_spec = pl.BlockSpec((group, tokens, columns), lambda i, _: (i + number * steps, 0, 0))
-    operands = (marks, gain, *pieces, key_weight, value_weight, *held)
+    operands = (marks, gain, *pieces, *[key_weight] * len(pieces), *[value_weight] * len(pieces), *held)
     return pl.pallas_call(
         kernel,
         out_shape=(out, out),
@@ -74,10 +81,9 @@
             grid=(steps,),
             in_specs=[pl.BlockSpec((1, DE), lambda i, _: (0, 0))]
             + [piece_spec] * len(pieces)
-            + [weight_spec] * 2
+            + weight_specs * 2
             + [pl.BlockSpec(memory_space=pl.ANY)] * len(held),
             out_specs=(out_spec, out_spec),
-            scratch_shapes=[pltpu.VMEM((group * tokens, DE), jnp.bfloat16)],
         ),
         input_output_aliases={len(operands) - len(held) + i: i for i in range(len(held))},
         compiler_params=pltpu.CompilerParams(vmem_limit_bytes=VMEM_LIMIT),
@@ -291,36 +297,28 @@
     )(place, table)
 
 
-def pack(plan, number, pool):
-    kinds = 3 if number < ROUNDS else 1
-    starts = [0]
-    for array in pool:
-        starts.append(starts[-1] + array.shape[0])
+def pack(plan, line, number, pool):
+    lows, arrays = [low for low, _ in pool], [array for _, array in pool]
 
     def kernel(plan_ref, *refs):
-        sources, outs = refs[: len(pool)], refs[len(pool) :]
-        for kind, out in enumerate(outs):
-            line = kind + 3 - kinds
-            for b in range(CAP):
-                at = plan_ref[line * LANES + number * CAP + b]
-                for source, low, high in zip(sources, starts, starts[1:]):
-
-                    @pl.when((at >= low) & (at < high))
-                    def _(source=source, low=low, out=out, b=b, at=at):
-                        out[b] = source[at - low]
-
-    shape = jax.ShapeDtypeStruct((CAP,) + pool[0].shape[1:], pool[0].dtype)
+        sources, out = refs[:-1], refs[-1]
+        for b in range(CAP):
+            at = plan_ref[line * LANES + number * CAP + b]
+            for source, low in zip(sources, lows):
+
+                @pl.when((at >= low) & (at < low + source.shape[0]))
+                def _(source=source, low=low, b=b, at=at):
+                    out[b] = source[at - low]
+
     in_vmem = pl.BlockSpec(memory_space=pltpu.VMEM)
     return pl.pallas_call(
         kernel,
-        out_shape=(shape,) * kinds,
-        grid_spec=pltpu.PrefetchScalarGridSpec(
-            num_scalar_prefetch=1, in_specs=[in_vmem] * len(pool), out_specs=(in_vmem,) * kinds
-        ),
+        out_shape=jax.ShapeDtypeStruct((CAP,) + arrays[0].shape[1:], arrays[0].dtype),
+        grid_spec=pltpu.PrefetchScalarGridSpec(num_scalar_prefetch=1, in_specs=[in_vmem] * len(pool), out_specs=in_vmem),
         compiler_params=pltpu.CompilerParams(vmem_limit_bytes=VMEM_LIMIT),
-        cost_estimate=pl.CostEstimate(flops=0, bytes_accessed=kinds * CAP * 2 * 65536, transcendentals=0),
+        cost_estimate=pl.CostEstimate(flops=0, bytes_accessed=CAP * 2 * 65536, transcendentals=0),
         name="pack",
-    )(plan, *pool)
+    )(plan, *arrays)
 
 
 def previous_rows(nbr_owner, nbr_slot, nbr_count):
@@ -403,23 +401,28 @@
     planned_slots = plan[3 * LANES : 4 * LANES][asked]
 
     def planned():
-        pool = [store, early_up, early_down]
-        held, pieces = (), []
+        up, down = [(0, store), (ENTRIES_EACH, early_up)], [(0, store), (ENTRIES_EACH + AHEAD, early_down)]
+        held, pieces, slots = (), [], planned_slots
 
         def projected(number):
             return project(marks, gain, pieces[number], key_weight, value_weight, GROUP, total, number, held)
 
         for number in range(ROUNDS + 1):
-            *ways, mine = pack(plan, number, pool)
-            arrived = [shifted(way, "seq", steps) for way, steps in zip(ways, (1, -1))]
+            pool = up + down[1:]
+            if number < ROUNDS:
+                base = FIRST_ROUND + number * 2 * CAP
+                up = up + [(base, shifted(pack(plan, 0, number, up), "seq", 1))]
+                down = down + [(base + CAP, shifted(pack(plan, 1, number, down), "seq", -1))]
+            mine = pack(plan, 2, number, pool)
             pieces.append([mine, swapped(mine, "rep"), swapped(mine, "mp")])
             if number > 0:
                 pieces[number - 1].append(swapped(pieces[number - 1][2], "rep"))
                 held = projected(number - 1)
-            arrived, pieces[number], held = lax.optimization_barrier((arrived, pieces[number], held))
-            pool += arrived
+            places_down, arrays = [low for low, _ in down], [array for _, array in down]
+            arrays, pieces[number], held, slots = lax.optimization_barrier((arrays, pieces[number], held, slots))
+            down = list(zip(places_down, arrays))
         pieces[ROUNDS].append(swapped(pieces[ROUNDS][2], "rep"))
-        return (planned_slots, *projected(ROUNDS))
+        return (slots, *projected(ROUNDS))
 
     def whole():
         mine = fetch_all(store, asked >> 4, asked & (ENTRIES_EACH - 1))

time: 121 us -> 122 us (level); the launches traced: 121 us -> 120 us
  waiting for transfers between devices: 22.3 us -> 15.5 us
  starting transfers between devices: 36.4 us -> 39.1 us
  Pallas kernels: 49.6 us -> 52 us
  other arithmetic: 2.5 us -> 3.77 us
    ppermute x8, waiting for transfers between devices: 13.5 us -> 4.55 us  [shifted(): lax.ppermute(value, axis, [(source, source + steps) for source in range(f...]
    pallas_call x4 -> x10, Pallas kernels: 7.94 us -> 16.6 us  [pack(): pl.pallas_call(kernel, out_shape=jax.ShapeDtypeStruct((CAP,) + arrays[0]....]
    pallas_call x4, Pallas kernels: 29.6 us -> 23.5 us  [project(): pl.pallas_call(kernel, out_shape=(out, out), grid_spec=pltpu.PrefetchScal...]
    cond x22 -> x12, local copies, waits for them, and re-layouts: 2.6 us -> 0.03 us
    ppermute x8, starting transfers between devices: 22 us -> 24.3 us  [shifted(): lax.ppermute(value, axis, [(source, source + steps) for source in range(f...]
    ppermute x16, waiting for transfers between devices: 8.87 us -> 10.9 us  [swapped(): return lax.ppermute(value, axis, [(0, 1), (1, 0)])]
    reshape x1, local copies, waits for them, and re-layouts: 0.08 us -> 1.37 us  [streamed(): jnp.stack([first, jnp.where(asked[:, 1] >= 0, asked[:, 1], first)], axis=1)]
    another operation x1, local copies, waits for them, and re-layouts: 0.1 us -> 1.35 us
  transfers between devices with their start and end apart: 27 -> 27, of which waited for: 7 -> 7; matrix products, arithmetic and copies ran while one was open for 6% -> 9% of each run, Pallas kernels for 23% -> 30%
where the time goes in v3:
time: 122 us; the launch traced here: 120 us
  Pallas kernels  52 us (43%)
  starting transfers between devices  39.1 us (32%)
  waiting for transfers between devices  15.5 us (13%)
  local copies, waits for them, and re-layouts  8.97 us (7%)
  other arithmetic  3.77 us (3%)
    ppermute x8, starting transfers between devices, shifted(): lax.ppermute(value, axis, [(source, source + steps) for source in range(f...  24.3 us
    pallas_call x4, Pallas kernels, project(): pl.pallas_call(kernel, out_shape=(out, out), grid_spec=pltpu.PrefetchScal...  23.5 us
    pallas_call x10, Pallas kernels, pack(): pl.pallas_call(kernel, out_shape=jax.ShapeDtypeStruct((CAP,) + arrays[0]....  16.6 us
    ppermute x16, waiting for transfers between devices, swapped(): return lax.ppermute(value, axis, [(0, 1), (1, 0)])  10.9 us
    pallas_call x1, Pallas kernels, attend(): pl.pallas_call(attend_kernel, out_shape=jax.ShapeDtypeStruct(queries.shap...  10 us
    ppermute x16, starting transfers between devices, swapped(): return lax.ppermute(value, axis, [(0, 1), (1, 0)])  9.15 us
    ppermute x3, starting transfers between devices, exchanged_table(): lax.ppermute(codes, 'seq', [(chip, chip ^ offset) for chip in range(CHIPS)])  5.68 us
    ppermute x8, waiting for transfers between devices, shifted(): lax.ppermute(value, axis, [(source, source + steps) for source in range(f...  4.55 us
  transfers between devices with their start and end apart: 27, of which 7 were waited for; matrix products, arithmetic and copies ran while one was open for 9% of the time, Pallas kernels for 30%

profile of v3, /device:TPU:0, one launch (start us, length us, event | category | flops | bytes accessed | tf_op | source)
XLA Modules:
  0.0 120.4 jit_solution(16265848414703411188)
XLA Ops:
  0.9 3.1 %collective-permute-start.27 = (s32[24]{0:T(128)S(1)}, s32[24]{0:T(128)S(1)}, u32[]{:S(2)}, u32[]{:S(2)}) collective-permute-start(s32[24]{0:T(128)S(1)} %reshape.112), channel_id=1, source_target_pairs={{0,4},{4,0},{8,12},{12,8},{1,5},{5,1},{9,13},{13,9},{2,6},{6,2},{1... | collective-permute-start | bytes 296 | tf_op jit(solution)/shard_map/ppermute | solution.py:371
  4.0 2.6 %collective-permute-start.28 = (s32[24]{0:T(128)S(1)}, s32[24]{0:T(128)S(1)}, u32[]{:S(2)}, u32[]{:S(2)}) collective-permute-start(s32[24]{0:T(128)S(1)} %reshape.112), channel_id=1, source_target_pairs={{0,8},{4,12},{8,0},{12,4},{1,9},{5,13},{9,1},{13,5},{2,10},{6,14},... | collective-permute-start | bytes 296 | tf_op jit(solution)/shard_map/ppermute | solution.py:371
  8.9 4.6 %collective-permute-start.35 = (bf16[8,128,256]{2,1,0:T(8,128)(2,1)S(1)}, bf16[8,128,256]{2,1,0:T(8,128)(2,1)S(1)}, u32[]{:S(2)}, u32[]{:S(2)}) collective-permute-start(bf16[8,128,256]{2,1,0:T(8,128)(2,1)S(1)} %slice.40), channel_id=1, source_target_pairs={{0,4},{4,8},{8,12},{1,5},{5,9},{9,13},{2,6},{6,10},{10,14},{3,7},{... | collective-permute-start | bytes 1572872 | tf_op jit(solution)/shard_map/ppermute | solution.py:34
  13.7 1.8 %collective-permute-start.30 = (s32[4,24]{1,0:T(4,128)S(1)}, s32[4,24]{1,0:T(4,128)S(1)}, u32[]{:S(2)}, u32[]{:S(2)}) collective-permute-start(s32[4,24]{1,0:T(4,128)S(1)} %pad_add_fusion), channel_id=1, source_target_pairs={{0,16},{16,0},{1,17},{17,1},{2,18},{18,2},{3,19},{19,3},{4,20},{20... | collective-permute-start | bytes 1160 | tf_op jit(solution)/shard_map/ppermute | solution.py:38
  18.1 1.9 %plan.1 = s32[8,128]{1,0:T(8,128)S(1)} custom-call(s32[1]{0:T(128)} %bitcast.2.place, s32[192]{0:T(256)} %reshape.113.table), custom_call_target="tpu_custom_call" | custom-call | tf_op jit(solution)/shard_map/plan/pallas_call | solution.py:290
  19.9 1.8 %collective-permute-start.32 = (f32[1,256]{1,0:T(1,128)}, f32[1,256]{1,0:T(1,128)S(1)}, u32[]{:S(2)}, u32[]{:S(2)}) collective-permute-start(f32[1,256]{1,0:T(1,128)} %bitcast.28), channel_id=1, source_target_pairs={{0,2},{2,0},{1,3},{3,1},{4,6},{6,4},{5,7},{7,5},{8,10},{10,8},{9,1... | collective-permute-start | bytes 3080 | tf_op jit(solution)/shard_map/ppermute | solution.py:38
  26.7 83.7 %conditional.1 = (s32[24]{0:T(128)}, bf16[24,128,1024]{2,1,0:T(8,128)(2,1)}, bf16[24,128,1024]{2,1,0:T(8,128)(2,1)}) conditional(s32[]{:T(128)} %bitcast.7, (s32[4]{0:T(128)S(1)}, bf16[16,128,256]{2,1,0:T(8,128)(2,1)}, s32[12,2]{0,1:T(2,128)S(1)}, f32[1,1024]{1,0:T(1,128)S(1)}, bf16[1024,1024]{1,0:T(8,128)(2,1)}, ...), branch_computations={%region_0.1_spmd, %region_1.2_spmd} | conditional | flops 12884902912 | bytes 97000848 | solution.py:433
  26.7 2.2 %pack.11.refs_0_ = bf16[6,128,256]{2,1,0:T(8,128)(2,1)S(1)} custom-call(s32[1024]{0:T(1024)S(1)} %get-tuple-element.60.plan_ref, bf16[16,128,256]{2,1,0:T(8,128)(2,1)} %get-tuple-element.76.refs_0_, bf16[8,128,256]{2,1,0:T(8,128)(2,1)} %get-tuple-element.61.refs_1_, bf16[8,128,256]{2,1,0:T(8,128)(2,1)} %get-tuple-element.88.refs_1_.refs_2_.refs_3_.refs_4_.refs_5_), custom_call_target="tpu_custom_call" | custom-call | bytes 786432 | tf_op jit(solution)/shard_map/cond/branch_1_fun/pack/pallas_call | solution.py:314
  31.2 2.0 %pack.10 = bf16[6,128,256]{2,1,0:T(8,128)(2,1)S(1)} custom-call(s32[1024]{0:T(1024)S(1)} %get-tuple-element.60.plan_ref, bf16[16,128,256]{2,1,0:T(8,128)(2,1)} %get-tuple-element.76.refs_0_, bf16[8,128,256]{2,1,0:T(8,128)(2,1)} %get-tuple-element.88.refs_1_.refs_2_.refs_3_.refs_4_.refs_5_), custom_call_target="tpu_custom_call" | custom-call | bytes 786432 | tf_op jit(solution)/shard_map/cond/branch_1_fun/pack/pallas_call | solution.py:314
  34.4 2.0 %pack.13 = bf16[6,128,256]{2,1,0:T(8,128)(2,1)S(1)} custom-call(s32[1024]{0:T(1024)S(1)} %get-tuple-element.60.plan_ref, bf16[16,128,256]{2,1,0:T(8,128)(2,1)} %get-tuple-element.76.refs_0_, bf16[8,128,256]{2,1,0:T(8,128)(2,1)} %get-tuple-element.61.refs_1_), custom_call_target="tpu_custom_call" | custom-call | bytes 786432 | tf_op jit(solution)/shard_map/cond/branch_1_fun/pack/pallas_call | solution.py:314
  36.4 4.6 %collective-permute-start.13 = (bf16[6,128,256]{2,1,0:T(8,128)(2,1)S(1)}, bf16[6,128,256]{2,1,0:T(8,128)(2,1)S(1)}, u32[]{:S(2)}, u32[]{:S(2)}) collective-permute-start(bf16[6,128,256]{2,1,0:T(8,128)(2,1)S(1)} %pack.13), channel_id=1, source_target_pairs={{0,4},{4,8},{8,12},{1,5},{5,9},{9,13},{2,6},{6,10},{10,14},{3,7},{... | collective-permute-start | bytes 1179656 | tf_op jit(solution)/shard_map/cond/branch_1_fun/ppermute | solution.py:34
  46.5 2.6 %collective-permute-done.13.refs_2_ = bf16[6,128,256]{2,1,0:T(8,128)(2,1)S(1)} collective-permute-done((bf16[6,128,256]{2,1,0:T(8,128)(2,1)S(1)}, bf16[6,128,256]{2,1,0:T(8,128)(2,1)S(1)}, u32[]{:S(2)}, u32[]{:S(2)}) %collective-permute-start.13) | collective-permute-done | bytes 393248 | tf_op jit(solution)/shard_map/cond/branch_1_fun/ppermute | solution.py:34
  49.0 2.3 %pack.14.refs_0_ = bf16[6,128,256]{2,1,0:T(8,128)(2,1)S(1)} custom-call(s32[1024]{0:T(1024)S(1)} %get-tuple-element.60.plan_ref, bf16[16,128,256]{2,1,0:T(8,128)(2,1)} %get-tuple-element.76.refs_0_, bf16[8,128,256]{2,1,0:T(8,128)(2,1)} %get-tuple-element.61.refs_1_, bf16[6,128,256]{2,1,0:T(8,128)(2,1)S(1)} %collective-permute-done.13.refs_2_, ...), custom_call_target="tpu_custom_call" | custom-call | bytes 786432 | tf_op jit(solution)/shard_map/cond/branch_1_fun/pack/pallas_call | solution.py:314
  51.8 2.7 %pack.12 = bf16[6,128,256]{2,1,0:T(8,128)(2,1)} custom-call(s32[1024]{0:T(1024)S(1)} %get-tuple-element.60.plan_ref, bf16[16,128,256]{2,1,0:T(8,128)(2,1)} %get-tuple-element.76.refs_0_, bf16[8,128,256]{2,1,0:T(8,128)(2,1)} %get-tuple-element.88.refs_1_.refs_2_.refs_3_.refs_4_.refs_5_, ...), custom_call_target="tpu_custom_call" | custom-call | bytes 786432 | tf_op jit(solution)/shard_map/cond/branch_1_fun/pack/pallas_call | solution.py:314
  56.5 2.0 %pack.16 = bf16[6,128,256]{2,1,0:T(8,128)(2,1)S(1)} custom-call(s32[1024]{0:T(1024)S(1)} %get-tuple-element.60.plan_ref, bf16[16,128,256]{2,1,0:T(8,128)(2,1)} %get-tuple-element.76.refs_0_, bf16[8,128,256]{2,1,0:T(8,128)(2,1)} %get-tuple-element.61.refs_1_, bf16[6,128,256]{2,1,0:T(8,128)(2,1)S(1)} %collective-permute-done.13.refs_2_), custom_call_target="tpu_custom_call" | custom-call | bytes 786432 | tf_op jit(solution)/shard_map/cond/branch_1_fun/pack/pallas_call | solution.py:314
  58.5 5.2 %collective-permute-start.18 = (bf16[6,128,256]{2,1,0:T(8,128)(2,1)S(1)}, bf16[6,128,256]{2,1,0:T(8,128)(2,1)S(1)}, u32[]{:S(2)}, u32[]{:S(2)}) collective-permute-start(bf16[6,128,256]{2,1,0:T(8,128)(2,1)S(1)} %pack.16), channel_id=1, source_target_pairs={{0,4},{4,8},{8,12},{1,5},{5,9},{9,13},{2,6},{6,10},{10,14},{3,7},{... | collective-permute-start | bytes 1179656 | tf_op jit(solution)/shard_map/cond/branch_1_fun/ppermute | solution.py:34
  63.8 8.4 %project.6 = (bf16[24,128,1024]{2,1,0:T(8,128)(2,1)}, bf16[24,128,1024]{2,1,0:T(8,128)(2,1)}) custom-call(s32[24]{0:T(128)S(1)} %reshape.104.marks_ref, f32[1,1024]{1,0:T(1,128)S(1)} %get-tuple-element.67.gain_ref, bf16[6,128,256]{2,1,0:T(8,128)(2,1)S(1)} %pack.11.refs_0_, bf16[6,128,256]{2,1,0:T(8,128)(2,1)} %collective-permute-done.10.refs_1_, ...), custom_call_target="tpu_custom_call" | custom-call | flops 3221225472 | bytes 8912896 | tf_op jit(solution)/shard_map/cond/branch_1_fun/project/pallas_call | solution.py:76
  78.3 4.7 %collective-permute-start.22 = (bf16[6,128,256]{2,1,0:T(8,128)(2,1)S(1)}, bf16[6,128,256]{2,1,0:T(8,128)(2,1)S(1)}, u32[]{:S(2)}, u32[]{:S(2)}) collective-permute-start(bf16[6,128,256]{2,1,0:T(8,128)(2,1)S(1)} %pack.18), channel_id=1, source_target_pairs={{0,4},{4,8},{8,12},{1,5},{5,9},{9,13},{2,6},{6,10},{10,14},{3,7},{... | collective-permute-start | bytes 1179656 | tf_op jit(solution)/shard_map/cond/branch_1_fun/ppermute | solution.py:34
  83.1 6.7 %project.7 = (bf16[24,128,1024]{2,1,0:T(8,128)(2,1)}, bf16[24,128,1024]{2,1,0:T(8,128)(2,1)}) custom-call(s32[24]{0:T(128)S(1)} %reshape.104.marks_ref, f32[1,1024]{1,0:T(1,128)S(1)} %get-tuple-element.67.gain_ref, bf16[6,128,256]{2,1,0:T(8,128)(2,1)S(1)} %pack.14.refs_0_, ...), custom_call_target="tpu_custom_call", output_to_operand_aliasing={{0}: (14, {}), {1}: (15, {})} | custom-call | flops 3221225472 | bytes 8912896 | tf_op jit(solution)/shard_map/cond/branch_1_fun/project/pallas_call | solution.py:76
  89.9 1.8 %collective-permute-done.22.refs_4_ = bf16[6,128,256]{2,1,0:T(8,128)(2,1)S(1)} collective-permute-done((bf16[6,128,256]{2,1,0:T(8,128)(2,1)S(1)}, bf16[6,128,256]{2,1,0:T(8,128)(2,1)S(1)}, u32[]{:S(2)}, u32[]{:S(2)}) %collective-permute-start.22) | collective-permute-done | bytes 393248 | tf_op jit(solution)/shard_map/cond/branch_1_fun/ppermute | solution.py:34
  93.3 4.2 %project.8 = (bf16[24,128,1024]{2,1,0:T(8,128)(2,1)}, bf16[24,128,1024]{2,1,0:T(8,128)(2,1)}) custom-call(s32[24]{0:T(128)S(1)} %reshape.104.marks_ref, f32[1,1024]{1,0:T(1,128)S(1)} %get-tuple-element.67.gain_ref, bf16[6,128,256]{2,1,0:T(8,128)(2,1)S(1)} %pack.17.refs_0_, ...), custom_call_target="tpu_custom_call", output_to_operand_aliasing={{0}: (14, {}), {1}: (15, {})} | custom-call | flops 3221225472 | bytes 8912896 | tf_op jit(solution)/shard_map/cond/branch_1_fun/project/pallas_call | solution.py:76
  97.5 6.9 %collective-permute-done.24.refs_2_ = bf16[6,128,256]{2,1,0:T(8,128)(2,1)S(1)} collective-permute-done((bf16[6,128,256]{2,1,0:T(8,128)(2,1)S(1)}, bf16[6,128,256]{2,1,0:T(8,128)(2,1)S(1)}, u32[]{:S(2)}, u32[]{:S(2)}) %collective-permute-start.24) | collective-permute-done | bytes 393248 | tf_op jit(solution)/shard_map/cond/branch_1_fun/ppermute | solution.py:38
  106.1 4.2 %project.9 = (bf16[24,128,1024]{2,1,0:T(8,128)(2,1)}, bf16[24,128,1024]{2,1,0:T(8,128)(2,1)}) custom-call(s32[24]{0:T(128)S(1)} %reshape.104.marks_ref, f32[1,1024]{1,0:T(1,128)S(1)} %get-tuple-element.67.gain_ref, bf16[6,128,256]{2,1,0:T(8,128)(2,1)S(1)} %pack.19.refs_0_, ...), custom_call_target="tpu_custom_call", output_to_operand_aliasing={{0}: (14, {}), {1}: (15, {})} | custom-call | flops 3221225472 | bytes 8912896 | tf_op jit(solution)/shard_map/cond/branch_1_fun/project/pallas_call | solution.py:76
  110.4 10.0 %attend.1 = bf16[768,1024]{1,0:T(8,128)(2,1)} custom-call(s32[24]{0:T(128)} %get-tuple-element.115.slots, s32[12]{0:T(128)S(1)} %convert_reduce_fusion.counts, bf16[768,1024]{1,0:T(8,128)(2,1)S(1)} %copy-done, bf16[24,128,1024]{2,1,0:T(8,128)(2,1)} %get-tuple-element.116.refs_0_.refs_1_.refs_2_.refs_3_.refs_4_.refs_5_, ...), custom_call_target="tpu_custom_call" | custom-call | flops 1610612736 | bytes 15728640 | tf_op jit(solution)/shard_map/attend/pallas_call | solution.py:158
  (100 shorter events, 31.1 us)
Async XLA Ops:
  0.9 12.8 %collective-permute-start.27 = (s32[24]{0:T(128)S(1)}, s32[24]{0:T(128)S(1)}, u32[]{:S(2)}, u32[]{:S(2)}) collective-permute-start(s32[24]{0:T(128)S(1)} %reshape.112), channel_id=1, source_target_pairs={{0,4},{4,0},{8,12},{12,8},{1,5},{5,1},{9,13},{13,9},{2,6},{6,2},{1... | collective-permute-start | bytes 296 | tf_op jit(solution)/shard_map/ppermute | solution.py:371
  4.0 9.7 %collective-permute-start.28 = (s32[24]{0:T(128)S(1)}, s32[24]{0:T(128)S(1)}, u32[]{:S(2)}, u32[]{:S(2)}) collective-permute-start(s32[24]{0:T(128)S(1)} %reshape.112), channel_id=1, source_target_pairs={{0,8},{4,12},{8,0},{12,4},{1,9},{5,13},{9,1},{13,5},{2,10},{6,14},... | collective-permute-start | bytes 296 | tf_op jit(solution)/shard_map/ppermute | solution.py:371
  6.6 7.2 %collective-permute-start.29 = (s32[24]{0:T(128)S(1)}, s32[24]{0:T(128)S(1)}, u32[]{:S(2)}, u32[]{:S(2)}) collective-permute-start(s32[24]{0:T(128)S(1)} %reshape.112), channel_id=1, source_target_pairs={{0,12},{4,8},{8,4},{12,0},{1,13},{5,9},{9,5},{13,1},{2,14},{6,10},... | collective-permute-start | bytes 296 | tf_op jit(solution)/shard_map/ppermute | solution.py:371
  7.6 18.0 %collective-permute-start.34 = (bf16[8,128,256]{2,1,0:T(8,128)(2,1)S(1)}, bf16[8,128,256]{2,1,0:T(8,128)(2,1)S(1)}, u32[]{:S(2)}, u32[]{:S(2)}) collective-permute-start(bf16[8,128,256]{2,1,0:T(8,128)(2,1)S(1)} %slice.40), channel_id=1, source_target_pairs={{4,0},{8,4},{12,8},{5,1},{9,5},{13,9},{6,2},{10,6},{14,10},{7,3},{... | collective-permute-start | bytes 1572872 | tf_op jit(solution)/shard_map/ppermute | solution.py:34
  8.9 16.7 %collective-permute-start.35 = (bf16[8,128,256]{2,1,0:T(8,128)(2,1)S(1)}, bf16[8,128,256]{2,1,0:T(8,128)(2,1)S(1)}, u32[]{:S(2)}, u32[]{:S(2)}) collective-permute-start(bf16[8,128,256]{2,1,0:T(8,128)(2,1)S(1)} %slice.40), channel_id=1, source_target_pairs={{0,4},{4,8},{8,12},{1,5},{5,9},{9,13},{2,6},{6,10},{10,14},{3,7},{... | collective-permute-start | bytes 1572872 | tf_op jit(solution)/shard_map/ppermute | solution.py:34
  13.7 3.7 %collective-permute-start.30 = (s32[4,24]{1,0:T(4,128)S(1)}, s32[4,24]{1,0:T(4,128)S(1)}, u32[]{:S(2)}, u32[]{:S(2)}) collective-permute-start(s32[4,24]{1,0:T(4,128)S(1)} %pad_add_fusion), channel_id=1, source_target_pairs={{0,16},{16,0},{1,17},{17,1},{2,18},{18,2},{3,19},{19,3},{4,20},{20... | collective-permute-start | bytes 1160 | tf_op jit(solution)/shard_map/ppermute | solution.py:38
  19.9 3.8 %collective-permute-start.32 = (f32[1,256]{1,0:T(1,128)}, f32[1,256]{1,0:T(1,128)S(1)}, u32[]{:S(2)}, u32[]{:S(2)}) collective-permute-start(f32[1,256]{1,0:T(1,128)} %bitcast.28), channel_id=1, source_target_pairs={{0,2},{2,0},{1,3},{3,1},{4,6},{6,4},{5,7},{7,5},{8,10},{10,8},{9,1... | collective-permute-start | bytes 3080 | tf_op jit(solution)/shard_map/ppermute | solution.py:38
  28.9 17.5 %collective-permute-start.10 = (bf16[6,128,256]{2,1,0:T(8,128)(2,1)S(1)}, bf16[6,128,256]{2,1,0:T(8,128)(2,1)}, u32[]{:S(2)}, u32[]{:S(2)}) collective-permute-start(bf16[6,128,256]{2,1,0:T(8,128)(2,1)S(1)} %pack.11.refs_0_), channel_id=1, source_target_pairs={{0,1},{1,0},{2,3},{3,2},{4,5},{5,4},{6,7},{7,6},{8,9},{9,8},{10,11... | collective-permute-start | bytes 1179656 | tf_op jit(solution)/shard_map/cond/branch_1_fun/ppermute | solution.py:38
  29.4 16.9 %collective-permute-start.11 = (bf16[6,128,256]{2,1,0:T(8,128)(2,1)S(1)}, bf16[6,128,256]{2,1,0:T(8,128)(2,1)}, u32[]{:S(2)}, u32[]{:S(2)}) collective-permute-start(bf16[6,128,256]{2,1,0:T(8,128)(2,1)S(1)} %pack.11.refs_0_), channel_id=1, source_target_pairs={{0,2},{2,0},{1,3},{3,1},{4,6},{6,4},{5,7},{7,5},{8,10},{10,8},{9,1... | collective-permute-start | bytes 1179656 | tf_op jit(solution)/shard_map/cond/branch_1_fun/ppermute | solution.py:38
  33.1 13.3 %collective-permute-start.9 = (bf16[6,128,256]{2,1,0:T(8,128)(2,1)S(1)}, bf16[6,128,256]{2,1,0:T(8,128)(2,1)S(1)}, u32[]{:S(2)}, u32[]{:S(2)}) collective-permute-start(bf16[6,128,256]{2,1,0:T(8,128)(2,1)S(1)} %pack.10), channel_id=1, source_target_pairs={{4,0},{8,4},{12,8},{5,1},{9,5},{13,9},{6,2},{10,6},{14,10},{7,3},{... | collective-permute-start | bytes 1179656 | tf_op jit(solution)/shard_map/cond/branch_1_fun/ppermute | solution.py:34
  36.4 12.6 %collective-permute-start.13 = (bf16[6,128,256]{2,1,0:T(8,128)(2,1)S(1)}, bf16[6,128,256]{2,1,0:T(8,128)(2,1)S(1)}, u32[]{:S(2)}, u32[]{:S(2)}) collective-permute-start(bf16[6,128,256]{2,1,0:T(8,128)(2,1)S(1)} %pack.13), channel_id=1, source_target_pairs={{0,4},{4,8},{8,12},{1,5},{5,9},{9,13},{2,6},{6,10},{10,14},{3,7},{... | collective-permute-start | bytes 1179656 | tf_op jit(solution)/shard_map/cond/branch_1_fun/ppermute | solution.py:34
  46.4 17.4 %collective-permute-start.16 = (bf16[6,128,256]{2,1,0:T(8,128)(2,1)}, bf16[6,128,256]{2,1,0:T(8,128)(2,1)}, u32[]{:S(2)}, u32[]{:S(2)}) collective-permute-start(bf16[6,128,256]{2,1,0:T(8,128)(2,1)} %collective-permute-done.11.refs_2_), channel_id=1, source_target_pairs={{0,1},{1,0},{2,3},{3,2},{4,5},{5,4},{6,7},{7,6},{8,9},{9,8},{10,11... | collective-permute-start | bytes 1179656 | tf_op jit(solution)/shard_map/cond/branch_1_fun/ppermute | solution.py:38
  51.3 20.9 %collective-permute-start.14 = (bf16[6,128,256]{2,1,0:T(8,128)(2,1)S(1)}, bf16[6,128,256]{2,1,0:T(8,128)(2,1)}, u32[]{:S(2)}, u32[]{:S(2)}) collective-permute-start(bf16[6,128,256]{2,1,0:T(8,128)(2,1)S(1)} %pack.14.refs_0_), channel_id=1, source_target_pairs={{0,1},{1,0},{2,3},{3,2},{4,5},{5,4},{6,7},{7,6},{8,9},{9,8},{10,11... | collective-permute-start | bytes 1179656 | tf_op jit(solution)/shard_map/cond/branch_1_fun/ppermute | solution.py:38
  51.4 20.8 %collective-permute-start.15 = (bf16[6,128,256]{2,1,0:T(8,128)(2,1)S(1)}, bf16[6,128,256]{2,1,0:T(8,128)(2,1)}, u32[]{:S(2)}, u32[]{:S(2)}) collective-permute-start(bf16[6,128,256]{2,1,0:T(8,128)(2,1)S(1)} %pack.14.refs_0_), channel_id=1, source_target_pairs={{0,2},{2,0},{1,3},{3,1},{4,6},{6,4},{5,7},{7,5},{8,10},{10,8},{9,1... | collective-permute-start | bytes 1179656 | tf_op jit(solution)/shard_map/cond/branch_1_fun/ppermute | solution.py:38
  54.5 17.7 %collective-permute-start.12 = (bf16[6,128,256]{2,1,0:T(8,128)(2,1)}, bf16[6,128,256]{2,1,0:T(8,128)(2,1)S(1)}, u32[]{:S(2)}, u32[]{:S(2)}) collective-permute-start(bf16[6,128,256]{2,1,0:T(8,128)(2,1)} %pack.12), channel_id=1, source_target_pairs={{4,0},{8,4},{12,8},{5,1},{9,5},{13,9},{6,2},{10,6},{14,10},{7,3},{... | collective-permute-start | bytes 1179656 | tf_op jit(solution)/shard_map/cond/branch_1_fun/ppermute | solution.py:34
  58.5 13.9 %collective-permute-start.18 = (bf16[6,128,256]{2,1,0:T(8,128)(2,1)S(1)}, bf16[6,128,256]{2,1,0:T(8,128)(2,1)S(1)}, u32[]{:S(2)}, u32[]{:S(2)}) collective-permute-start(bf16[6,128,256]{2,1,0:T(8,128)(2,1)S(1)} %pack.16), channel_id=1, source_target_pairs={{0,4},{4,8},{8,12},{1,5},{5,9},{9,13},{2,6},{6,10},{10,14},{3,7},{... | collective-permute-start | bytes 1179656 | tf_op jit(solution)/shard_map/cond/branch_1_fun/ppermute | solution.py:34
  72.2 10.8 %collective-permute-start.21 = (bf16[6,128,256]{2,1,0:T(8,128)(2,1)}, bf16[6,128,256]{2,1,0:T(8,128)(2,1)S(1)}, u32[]{:S(2)}, u32[]{:S(2)}) collective-permute-start(bf16[6,128,256]{2,1,0:T(8,128)(2,1)} %collective-permute-done.15.refs_2_), channel_id=1, source_target_pairs={{0,1},{1,0},{2,3},{3,2},{4,5},{5,4},{6,7},{7,6},{8,9},{9,8},{10,11... | collective-permute-start | bytes 1179656 | tf_op jit(solution)/shard_map/cond/branch_1_fun/ppermute | solution.py:38
  73.3 16.5 %collective-permute-start.19 = (bf16[6,128,256]{2,1,0:T(8,128)(2,1)S(1)}, bf16[6,128,256]{2,1,0:T(8,128)(2,1)S(1)}, u32[]{:S(2)}, u32[]{:S(2)}) collective-permute-start(bf16[6,128,256]{2,1,0:T(8,128)(2,1)S(1)} %pack.17.refs_0_), channel_id=1, source_target_pairs={{0,1},{1,0},{2,3},{3,2},{4,5},{5,4},{6,7},{7,6},{8,9},{9,8},{10,11... | collective-permute-start | bytes 1179656 | tf_op jit(solution)/shard_map/cond/branch_1_fun/ppermute | solution.py:38
  73.7 16.0 %collective-permute-start.20 = (bf16[6,128,256]{2,1,0:T(8,128)(2,1)S(1)}, bf16[6,128,256]{2,1,0:T(8,128)(2,1)S(1)}, u32[]{:S(2)}, u32[]{:S(2)}) collective-permute-start(bf16[6,128,256]{2,1,0:T(8,128)(2,1)S(1)} %pack.17.refs_0_), channel_id=1, source_target_pairs={{0,2},{2,0},{1,3},{3,1},{4,6},{6,4},{5,7},{7,5},{8,10},{10,8},{9,1... | collective-permute-start | bytes 1179656 | tf_op jit(solution)/shard_map/cond/branch_1_fun/ppermute | solution.py:38
  76.2 13.6 %collective-permute-start.17 = (bf16[6,128,256]{2,1,0:T(8,128)(2,1)S(1)}, bf16[6,128,256]{2,1,0:T(8,128)(2,1)S(1)}, u32[]{:S(2)}, u32[]{:S(2)}) collective-permute-start(bf16[6,128,256]{2,1,0:T(8,128)(2,1)S(1)} %pack.15), channel_id=1, source_target_pairs={{4,0},{8,4},{12,8},{5,1},{9,5},{13,9},{6,2},{10,6},{14,10},{7,3},{... | collective-permute-start | bytes 1179656 | tf_op jit(solution)/shard_map/cond/branch_1_fun/ppermute | solution.py:34
  78.3 13.4 %collective-permute-start.22 = (bf16[6,128,256]{2,1,0:T(8,128)(2,1)S(1)}, bf16[6,128,256]{2,1,0:T(8,128)(2,1)S(1)}, u32[]{:S(2)}, u32[]{:S(2)}) collective-permute-start(bf16[6,128,256]{2,1,0:T(8,128)(2,1)S(1)} %pack.18), channel_id=1, source_target_pairs={{0,4},{4,8},{8,12},{1,5},{5,9},{9,13},{2,6},{6,10},{10,14},{3,7},{... | collective-permute-start | bytes 1179656 | tf_op jit(solution)/shard_map/cond/branch_1_fun/ppermute | solution.py:34
  89.8 3.5 %collective-permute-start.25 = (bf16[6,128,256]{2,1,0:T(8,128)(2,1)S(1)}, bf16[6,128,256]{2,1,0:T(8,128)(2,1)S(1)}, u32[]{:S(2)}, u32[]{:S(2)}) collective-permute-start(bf16[6,128,256]{2,1,0:T(8,128)(2,1)S(1)} %collective-permute-done.20.refs_2_), channel_id=1, source_target_pairs={{0,1},{1,0},{2,3},{3,2},{4,5},{5,4},{6,7},{7,6},{8,9},{9,8},{10,11... | collective-permute-start | bytes 1179656 | tf_op jit(solution)/shard_map/cond/branch_1_fun/ppermute | solution.py:38
  92.8 4.7 %collective-permute-start.23 = (bf16[6,128,256]{2,1,0:T(8,128)(2,1)S(1)}, bf16[6,128,256]{2,1,0:T(8,128)(2,1)S(1)}, u32[]{:S(2)}, u32[]{:S(2)}) collective-permute-start(bf16[6,128,256]{2,1,0:T(8,128)(2,1)S(1)} %pack.19.refs_0_), channel_id=1, source_target_pairs={{0,1},{1,0},{2,3},{3,2},{4,5},{5,4},{6,7},{7,6},{8,9},{9,8},{10,11... | collective-permute-start | bytes 1179656 | tf_op jit(solution)/shard_map/cond/branch_1_fun/ppermute | solution.py:38
  92.9 11.5 %collective-permute-start.24 = (bf16[6,128,256]{2,1,0:T(8,128)(2,1)S(1)}, bf16[6,128,256]{2,1,0:T(8,128)(2,1)S(1)}, u32[]{:S(2)}, u32[]{:S(2)}) collective-permute-start(bf16[6,128,256]{2,1,0:T(8,128)(2,1)S(1)} %pack.19.refs_0_), channel_id=1, source_target_pairs={{0,2},{2,0},{1,3},{3,1},{4,6},{6,4},{5,7},{7,5},{8,10},{10,8},{9,1... | collective-permute-start | bytes 1179656 | tf_op jit(solution)/shard_map/cond/branch_1_fun/ppermute | solution.py:38
  (12 other events, 145.8 us)

commit v4 on v3

--- a/solution.py
+++ b/solution.py
@@ -365,6 +365,11 @@
     return jnp.stack([block ^ i for i in range(4)]).astype(jnp.int32)
 
 
+def after(pool, token):
+    arrays, _ = lax.optimization_barrier(([array for _, array in pool], token))
+    return [(low, array) for (low, _), array in zip(pool, arrays)]
+
+
 def exchanged_table(codes):
     own_part = [codes]
     for offset in range(1, CHIPS):
@@ -400,38 +405,39 @@
     marks = jnp.concatenate([jnp.broadcast_to(places, (ROUNDS + 1, 4)), wanted.astype(jnp.int32)], axis=1).reshape(-1)
     planned_slots = plan[3 * LANES : 4 * LANES][asked]
 
-    def planned():
-        up, down = [(0, store), (ENTRIES_EACH, early_up)], [(0, store), (ENTRIES_EACH + AHEAD, early_down)]
-        held, pieces, slots = (), [], planned_slots
-
-        def projected(number):
-            return project(marks, gain, pieces[number], key_weight, value_weight, GROUP, total, number, held)
-
-        for number in range(ROUNDS + 1):
-            pool = up + down[1:]
-            if number < ROUNDS:
-                base = FIRST_ROUND + number * 2 * CAP
-                up = up + [(base, shifted(pack(plan, 0, number, up), "seq", 1))]
-                down = down + [(base + CAP, shifted(pack(plan, 1, number, down), "seq", -1))]
-            mine = pack(plan, 2, number, pool)
-            pieces.append([mine, swapped(mine, "rep"), swapped(mine, "mp")])
-            if number > 0:
-                pieces[number - 1].append(swapped(pieces[number - 1][2], "rep"))
-                held = projected(number - 1)
-            places_down, arrays = [low for low, _ in down], [array for _, array in down]
-            arrays, pieces[number], held, slots = lax.optimization_barrier((arrays, pieces[number], held, slots))
-            down = list(zip(places_down, arrays))
-        pieces[ROUNDS].append(swapped(pieces[ROUNDS][2], "rep"))
-        return (slots, *projected(ROUNDS))
-
-    def whole():
+    up, down = [(0, store), (ENTRIES_EACH, early_up)], [(0, store), (ENTRIES_EACH + AHEAD, early_down)]
+    held, pieces = (), []
+
+    def projected(number):
+        return project(marks, gain, pieces[number], key_weight, value_weight, GROUP, total, number, held)
+
+    for number in range(ROUNDS + 1):
+        pool = up + down[1:]
+        if number < ROUNDS:
+            base = FIRST_ROUND + number * 2 * CAP
+            going_up = pack(plan, 0, number, after(up, held))
+            going_down = pack(plan, 1, number, after(down, going_up))
+            up = up + [(base, shifted(going_up, "seq", 1))]
+            down = down + [(base + CAP, shifted(going_down, "seq", -1))]
+            pool = after(pool, going_down)
+        mine = pack(plan, 2, number, pool)
+        pieces.append([mine, swapped(mine, "rep"), swapped(mine, "mp")])
+        if number > 0:
+            pieces[number - 1].append(swapped(pieces[number - 1][2], "rep"))
+            pieces[number - 1], _ = lax.optimization_barrier((pieces[number - 1], mine))
+            held = projected(number - 1)
+    pieces[ROUNDS], held = lax.optimization_barrier((pieces[ROUNDS], held))
+    pieces[ROUNDS].append(swapped(pieces[ROUNDS][2], "rep"))
+    keys, values = projected(ROUNDS)
+
+    def whole(state):
         mine = fetch_all(store, asked >> 4, asked & (ENTRIES_EACH - 1))
         whole_marks = jnp.concatenate([places, jnp.ones((total // 4,), jnp.int32)])
         keys, values = project(whole_marks, gain, four_pieces(mine), key_weight, value_weight, 4, total)
-        return jnp.arange(total, dtype=jnp.int32), keys, values
-
-    slots, keys, values = lax.cond(missing == 0, planned, whole)
-    return attend(slots, counts, queries, keys, values)
+        return jnp.zeros_like(state[0]), jnp.arange(total, dtype=jnp.int32), keys, values
+
+    state = lax.while_loop(lambda state: state[0] > 0, whole, (missing, planned_slots, keys, values))
+    return attend(state[1], counts, queries, *state[2:])
 
 
 def requested(queries, key_weight, value_weight, enc_gain, store, nbr_owner, nbr_slot, nbr_count):

time: 122 us -> 127 us (1.041)
  waiting for transfers between devices: 15.5 us -> 28.1 us
  starting transfers between devices: 39.1 us -> 35.1 us
  local copies, waits for them, and re-layouts: 8.97 us -> 5.72 us
  Pallas kernels: 52 us -> 54.5 us
  other arithmetic: 3.77 us -> 1.3 us
    ppermute x3, waiting for transfers between devices: 0.01 us -> 9.63 us  [exchanged_table(): lax.ppermute(codes, 'seq', [(chip, chip ^ offset) for chip in range(CHIPS)])]
    ppermute x8, waiting for transfers between devices: 4.55 us -> 8 us  [shifted(): lax.ppermute(value, axis, [(source, source + steps) for source in range(f...]
    ppermute x8, starting transfers between devices: 24.3 us -> 22.3 us  [shifted(): lax.ppermute(value, axis, [(source, source + steps) for source in range(f...]
    ppermute x16, starting transfers between devices: 9.15 us -> 7.41 us  [swapped(): return lax.ppermute(value, axis, [(0, 1), (1, 0)])]
    another operation x1 -> x0, local copies, waits for them, and re-layouts: 1.35 us -> none
  transfers between devices with their start and end apart: 27 -> 27, of which waited for: 7 -> 12; matrix products, arithmetic and copies ran while one was open for 9% -> 4% of each run, Pallas kernels for 30% -> 27%
where the time goes in v4:
time: 127 us; the launch traced here: 126 us
  Pallas kernels  54.5 us (43%)
  starting transfers between devices  35.1 us (28%)
  waiting for transfers between devices  28.1 us (22%)
  local copies, waits for them, and re-layouts  5.72 us (5%)
  other arithmetic  1.3 us (1%)
    pallas_call x4, Pallas kernels, project(): pl.pallas_call(kernel, out_shape=(out, out), grid_spec=pltpu.PrefetchScal...  24 us
    ppermute x8, starting transfers between devices, shifted(): lax.ppermute(value, axis, [(source, source + steps) for source in range(f...  22.3 us
    pallas_call x10, Pallas kernels, pack(): pl.pallas_call(kernel, out_shape=jax.ShapeDtypeStruct((CAP,) + arrays[0]....  17.5 us
    pallas_call x1, Pallas kernels, attend(): pl.pallas_call(attend_kernel, out_shape=jax.ShapeDtypeStruct(queries.shap...  10.6 us
    ppermute x16, waiting for transfers between devices, swapped(): return lax.ppermute(value, axis, [(0, 1), (1, 0)])  10.5 us
    ppermute x3, waiting for transfers between devices, exchanged_table(): lax.ppermute(codes, 'seq', [(chip, chip ^ offset) for chip in range(CHIPS)])  9.63 us
    ppermute x8, waiting for transfers between devices, shifted(): lax.ppermute(value, axis, [(source, source + steps) for source in range(f...  8 us
    ppermute x16, starting transfers between devices, swapped(): return lax.ppermute(value, axis, [(0, 1), (1, 0)])  7.41 us
  transfers between devices with their start and end apart: 27, of which 12 were waited for; matrix products, arithmetic and copies ran while one was open for 4% of the time, Pallas kernels for 27%

profile of v4, /device:TPU:0, one launch (start us, length us, event | category | flops | bytes accessed | tf_op | source)
XLA Modules:
  0.0 126.0 jit_solution(3096870516063030792)
XLA Ops:
  1.1 5.0 %collective-permute-start.16 = (bf16[8,128,256]{2,1,0:T(8,128)(2,1)S(1)}, bf16[8,128,256]{2,1,0:T(8,128)(2,1)S(1)}, u32[]{:S(2)}, u32[]{:S(2)}) collective-permute-start(bf16[8,128,256]{2,1,0:T(8,128)(2,1)S(1)} %slice.42), channel_id=1, source_target_pairs={{0,4},{4,8},{8,12},{1,5},{5,9},{9,13},{2,6},{6,10},{10,14},{3,7},{... | collective-permute-start | bytes 1572872 | tf_op jit(solution)/shard_map/ppermute | solution.py:34
  8.2 2.7 %collective-permute-start.9 = (s32[24]{0:T(128)S(1)}, s32[24]{0:T(128)S(1)}, u32[]{:S(2)}, u32[]{:S(2)}) collective-permute-start(s32[24]{0:T(128)S(1)} %reshape.126), channel_id=1, source_target_pairs={{0,4},{4,0},{8,12},{12,8},{1,5},{5,1},{9,13},{13,9},{2,6},{6,2},{1... | collective-permute-start | bytes 296 | tf_op jit(solution)/shard_map/ppermute | solution.py:376
  11.0 2.6 %collective-permute-start.10 = (s32[24]{0:T(128)S(1)}, s32[24]{0:T(128)S(1)}, u32[]{:S(2)}, u32[]{:S(2)}) collective-permute-start(s32[24]{0:T(128)S(1)} %reshape.126), channel_id=1, source_target_pairs={{0,8},{4,12},{8,0},{12,4},{1,9},{5,13},{9,1},{13,5},{2,10},{6,14},... | collective-permute-start | bytes 296 | tf_op jit(solution)/shard_map/ppermute | solution.py:376
  13.7 7.7 %collective-permute-done.9 = s32[24]{0:T(128)S(1)} collective-permute-done((s32[24]{0:T(128)S(1)}, s32[24]{0:T(128)S(1)}, u32[]{:S(2)}, u32[]{:S(2)}) %collective-permute-start.9) | collective-permute-done | bytes 128 | tf_op jit(solution)/shard_map/ppermute | solution.py:376
  24.9 2.1 %collective-permute-done.12 = s32[4,24]{1,0:T(4,128)S(1)} collective-permute-done((s32[4,24]{1,0:T(4,128)S(1)}, s32[4,24]{1,0:T(4,128)S(1)}, u32[]{:S(2)}, u32[]{:S(2)}) %collective-permute-start.12) | collective-permute-done | bytes 416 | tf_op jit(solution)/shard_map/ppermute | solution.py:38
  27.7 2.5 %plan.1 = s32[8,128]{1,0:T(8,128)} custom-call(s32[1]{0:T(128)} %bitcast.2.place, s32[192]{0:T(256)} %reshape.127.table), custom_call_target="tpu_custom_call" | custom-call | tf_op jit(solution)/shard_map/plan/pallas_call | solution.py:290
  30.8 1.9 %pack.10 = bf16[6,128,256]{2,1,0:T(8,128)(2,1)S(1)} custom-call(s32[1024]{0:T(1024)S(1)} %bitcast.20, bf16[16,128,256]{2,1,0:T(8,128)(2,1)} %refs_0_.10, bf16[8,128,256]{2,1,0:T(8,128)(2,1)S(1)} %collective-permute-done.16.refs_1_), custom_call_target="tpu_custom_call" | custom-call | bytes 786432 | tf_op jit(solution)/shard_map/pack/pallas_call | solution.py:314
  32.7 1.8 %pack.12 = bf16[6,128,256]{2,1,0:T(8,128)(2,1)S(1)} custom-call(s32[1024]{0:T(1024)S(1)} %bitcast.21, bf16[16,128,256]{2,1,0:T(8,128)(2,1)} %refs_0_.10, bf16[8,128,256]{2,1,0:T(8,128)(2,1)S(1)} %collective-permute-done.19.refs_1_.refs_2_.refs_3_.refs_5_.refs_4_), custom_call_target="tpu_custom_call" | custom-call | bytes 786432 | tf_op jit(solution)/shard_map/pack/pallas_call | solution.py:314
  34.5 1.9 %pack.13.refs_0_ = bf16[6,128,256]{2,1,0:T(8,128)(2,1)S(1)} custom-call(s32[1024]{0:T(1024)S(1)} %bitcast.22, bf16[16,128,256]{2,1,0:T(8,128)(2,1)} %refs_0_.10, bf16[8,128,256]{2,1,0:T(8,128)(2,1)S(1)} %collective-permute-done.16.refs_1_, bf16[8,128,256]{2,1,0:T(8,128)(2,1)S(1)} %collective-permute-done.19.refs_1_.refs_2_.refs_3_.refs_5_.refs_4_), custom_call_target="tpu_custom_call" | custom-call | bytes 786432 | tf_op jit(solution)/shard_map/pack/pallas_call | solution.py:314
  38.5 2.6 %collective-permute-start.17 = (bf16[6,128,256]{2,1,0:T(8,128)(2,1)S(1)}, bf16[6,128,256]{2,1,0:T(8,128)(2,1)S(1)}, u32[]{:S(2)}, u32[]{:S(2)}) collective-permute-start(bf16[6,128,256]{2,1,0:T(8,128)(2,1)S(1)} %pack.10), channel_id=1, source_target_pairs={{0,4},{4,8},{8,12},{1,5},{5,9},{9,13},{2,6},{6,10},{10,14},{3,7},{... | collective-permute-start | bytes 1179656 | tf_op jit(solution)/shard_map/ppermute | solution.py:34
  43.0 1.9 %collective-permute-done.21.refs_2_ = bf16[6,128,256]{2,1,0:T(8,128)(2,1)} collective-permute-done((bf16[6,128,256]{2,1,0:T(8,128)(2,1)S(1)}, bf16[6,128,256]{2,1,0:T(8,128)(2,1)}, u32[]{:S(2)}, u32[]{:S(2)}) %collective-permute-start.21) | collective-permute-done | bytes 393248 | tf_op jit(solution)/shard_map/ppermute | solution.py:38
  46.6 2.1 %pack.11 = bf16[6,128,256]{2,1,0:T(8,128)(2,1)S(1)} custom-call(s32[1024]{0:T(1024)S(1)} %bitcast.24, bf16[16,128,256]{2,1,0:T(8,128)(2,1)} %refs_0_.10, bf16[8,128,256]{2,1,0:T(8,128)(2,1)S(1)} %collective-permute-done.16.refs_1_, bf16[6,128,256]{2,1,0:T(8,128)(2,1)S(1)} %collective-permute-done.17.refs_2_), custom_call_target="tpu_custom_call" | custom-call | bytes 786432 | tf_op jit(solution)/shard_map/pack/pallas_call | solution.py:314
  48.7 2.0 %collective-permute-done.23.refs_2_.refs_4_.refs_6_.refs_5_ = bf16[6,128,256]{2,1,0:T(8,128)(2,1)S(1)} collective-permute-done((bf16[6,128,256]{2,1,0:T(8,128)(2,1)S(1)}, bf16[6,128,256]{2,1,0:T(8,128)(2,1)S(1)}, u32[]{:S(2)}, u32[]{:S(2)}) %collective-permute-start.23) | collective-permute-done | bytes 393248 | tf_op jit(solution)/shard_map/ppermute | solution.py:34
  52.6 2.8 %collective-permute-start.18 = (bf16[6,128,256]{2,1,0:T(8,128)(2,1)S(1)}, bf16[6,128,256]{2,1,0:T(8,128)(2,1)S(1)}, u32[]{:S(2)}, u32[]{:S(2)}) collective-permute-start(bf16[6,128,256]{2,1,0:T(8,128)(2,1)S(1)} %pack.11), channel_id=1, source_target_pairs={{0,4},{4,8},{8,12},{1,5},{5,9},{9,13},{2,6},{6,10},{10,14},{3,7},{... | collective-permute-start | bytes 1179656 | tf_op jit(solution)/shard_map/ppermute | solution.py:34
  56.7 2.0 %pack.15.refs_0_ = bf16[6,128,256]{2,1,0:T(8,128)(2,1)S(1)} custom-call(s32[1024]{0:T(1024)S(1)} %bitcast.26, bf16[16,128,256]{2,1,0:T(8,128)(2,1)} %refs_0_.10, bf16[8,128,256]{2,1,0:T(8,128)(2,1)S(1)} %collective-permute-done.16.refs_1_, bf16[6,128,256]{2,1,0:T(8,128)(2,1)S(1)} %collective-permute-done.17.refs_2_, ...), custom_call_target="tpu_custom_call" | custom-call | bytes 786432 | tf_op jit(solution)/shard_map/pack/pallas_call | solution.py:314
  59.3 5.4 %project.6 = (bf16[24,128,1024]{2,1,0:T(8,128)(2,1)}, bf16[24,128,1024]{2,1,0:T(8,128)(2,1)}) custom-call(s32[24]{0:T(128)S(1)} %reshape.132.marks_ref, f32[1,1024]{1,0:T(1,128)S(1)} %pad_maximum_fusion.gain_ref, bf16[6,128,256]{2,1,0:T(8,128)(2,1)S(1)} %pack.13.refs_0_, bf16[6,128,256]{2,1,0:T(8,128)(2,1)} %collective-permute-done.20.refs_1_, ...), custom_call_target="tpu_custom_call" | custom-call | flops 3221225472 | bytes 8912896 | tf_op jit(solution)/shard_map/project/pallas_call | solution.py:76
  66.2 6.8 %collective-permute-start.24 = (bf16[6,128,256]{2,1,0:T(8,128)(2,1)}, bf16[6,128,256]{2,1,0:T(8,128)(2,1)}, u32[]{:S(2)}, u32[]{:S(2)}) collective-permute-start(bf16[6,128,256]{2,1,0:T(8,128)(2,1)} %pack.16), channel_id=1, source_target_pairs={{0,4},{4,8},{8,12},{1,5},{5,9},{9,13},{2,6},{6,10},{10,14},{3,7},{... | collective-permute-start | bytes 1179656 | tf_op jit(solution)/shard_map/ppermute | solution.py:34
  80.6 5.2 %collective-permute-done.30.refs_2_ = bf16[6,128,256]{2,1,0:T(8,128)(2,1)} collective-permute-done((bf16[6,128,256]{2,1,0:T(8,128)(2,1)S(1)}, bf16[6,128,256]{2,1,0:T(8,128)(2,1)}, u32[]{:S(2)}, u32[]{:S(2)}) %collective-permute-start.30) | collective-permute-done | bytes 393248 | tf_op jit(solution)/shard_map/ppermute | solution.py:38
  86.1 4.7 %collective-permute-done.26.refs_8_ = bf16[6,128,256]{2,1,0:T(8,128)(2,1)} collective-permute-done((bf16[6,128,256]{2,1,0:T(8,128)(2,1)}, bf16[6,128,256]{2,1,0:T(8,128)(2,1)}, u32[]{:S(2)}, u32[]{:S(2)}) %collective-permute-start.26) | collective-permute-done | bytes 393248 | tf_op jit(solution)/shard_map/ppermute | solution.py:34
  90.8 2.0 %pack.18.refs_0_ = bf16[6,128,256]{2,1,0:T(8,128)(2,1)S(1)} custom-call(s32[1024]{0:T(1024)S(1)} %bitcast.32, bf16[16,128,256]{2,1,0:T(8,128)(2,1)} %refs_0_.10, bf16[8,128,256]{2,1,0:T(8,128)(2,1)S(1)} %collective-permute-done.16.refs_1_, bf16[6,128,256]{2,1,0:T(8,128)(2,1)S(1)} %collective-permute-done.17.refs_2_, ...), custom_call_target="tpu_custom_call" | custom-call | bytes 786432 | tf_op jit(solution)/shard_map/pack/pallas_call | solution.py:314
  93.5 6.8 %project.7 = (bf16[24,128,1024]{2,1,0:T(8,128)(2,1)}, bf16[24,128,1024]{2,1,0:T(8,128)(2,1)}) custom-call(s32[24]{0:T(128)S(1)} %reshape.132.marks_ref, f32[1,1024]{1,0:T(1,128)S(1)} %pad_maximum_fusion.gain_ref, bf16[6,128,256]{2,1,0:T(8,128)(2,1)S(1)} %pack.15.refs_0_, ...), custom_call_target="tpu_custom_call", output_to_operand_aliasing={{0}: (14, {}), {1}: (15, {})} | custom-call | flops 3221225472 | bytes 8912896 | tf_op jit(solution)/shard_map/project/pallas_call | solution.py:76
  100.4 5.3 %project.8 = (bf16[24,128,1024]{2,1,0:T(8,128)(2,1)}, bf16[24,128,1024]{2,1,0:T(8,128)(2,1)}) custom-call(s32[24]{0:T(128)S(1)} %reshape.132.marks_ref, f32[1,1024]{1,0:T(1,128)S(1)} %pad_maximum_fusion.gain_ref, bf16[6,128,256]{2,1,0:T(8,128)(2,1)S(1)} %pack.19.refs_0_, ...), custom_call_target="tpu_custom_call", output_to_operand_aliasing={{0}: (14, {}), {1}: (15, {})} | custom-call | flops 3221225472 | bytes 8912896 | tf_op jit(solution)/shard_map/project/pallas_call | solution.py:76
  107.5 6.4 %project.9 = (bf16[24,128,1024]{2,1,0:T(8,128)(2,1)}, bf16[24,128,1024]{2,1,0:T(8,128)(2,1)}) custom-call(s32[24]{0:T(128)S(1)} %reshape.132.marks_ref, f32[1,1024]{1,0:T(1,128)S(1)} %pad_maximum_fusion.gain_ref, bf16[6,128,256]{2,1,0:T(8,128)(2,1)S(1)} %copy-done.1, ...), custom_call_target="tpu_custom_call", output_to_operand_aliasing={{0}: (14, {}), {1}: (15, {})} | custom-call | flops 3221225472 | bytes 8912896 | tf_op jit(solution)/shard_map/project/pallas_call | solution.py:76
  115.3 10.6 %attend.1 = bf16[768,1024]{1,0:T(8,128)(2,1)} custom-call(s32[24]{0:T(128)} %get-tuple-element.177.slots, s32[12]{0:T(128)S(1)} %convert_reduce_fusion.counts, bf16[768,1024]{1,0:T(8,128)(2,1)S(1)} %copy-done.2, bf16[24,128,1024]{2,1,0:T(8,128)(2,1)} %get-tuple-element.178.refs_0_.refs_1_.refs_2_.refs_3_.refs_4_.refs_5_, ...), custom_call_target="tpu_custom_call" | custom-call | flops 1610612736 | bytes 15728640 | tf_op jit(solution)/shard_map/attend/pallas_call | solution.py:158
  (102 shorter events, 30.8 us)
Async XLA Ops:
  1.1 29.0 %collective-permute-start.16 = (bf16[8,128,256]{2,1,0:T(8,128)(2,1)S(1)}, bf16[8,128,256]{2,1,0:T(8,128)(2,1)S(1)}, u32[]{:S(2)}, u32[]{:S(2)}) collective-permute-start(bf16[8,128,256]{2,1,0:T(8,128)(2,1)S(1)} %slice.42), channel_id=1, source_target_pairs={{0,4},{4,8},{8,12},{1,5},{5,9},{9,13},{2,6},{6,10},{10,14},{3,7},{... | collective-permute-start | bytes 1572872 | tf_op jit(solution)/shard_map/ppermute | solution.py:34
  6.1 26.6 %collective-permute-start.19 = (bf16[8,128,256]{2,1,0:T(8,128)(2,1)S(1)}, bf16[8,128,256]{2,1,0:T(8,128)(2,1)S(1)}, u32[]{:S(2)}, u32[]{:S(2)}) collective-permute-start(bf16[8,128,256]{2,1,0:T(8,128)(2,1)S(1)} %slice.42), channel_id=1, source_target_pairs={{4,0},{8,4},{12,8},{5,1},{9,5},{13,9},{6,2},{10,6},{14,10},{7,3},{... | collective-permute-start | bytes 1572872 | tf_op jit(solution)/shard_map/ppermute | solution.py:34
  8.2 13.2 %collective-permute-start.9 = (s32[24]{0:T(128)S(1)}, s32[24]{0:T(128)S(1)}, u32[]{:S(2)}, u32[]{:S(2)}) collective-permute-start(s32[24]{0:T(128)S(1)} %reshape.126), channel_id=1, source_target_pairs={{0,4},{4,0},{8,12},{12,8},{1,5},{5,1},{9,13},{13,9},{2,6},{6,2},{1... | collective-permute-start | bytes 296 | tf_op jit(solution)/shard_map/ppermute | solution.py:376
  11.0 11.4 %collective-permute-start.10 = (s32[24]{0:T(128)S(1)}, s32[24]{0:T(128)S(1)}, u32[]{:S(2)}, u32[]{:S(2)}) collective-permute-start(s32[24]{0:T(128)S(1)} %reshape.126), channel_id=1, source_target_pairs={{0,8},{4,12},{8,0},{12,4},{1,9},{5,13},{9,1},{13,5},{2,10},{6,14},... | collective-permute-start | bytes 296 | tf_op jit(solution)/shard_map/ppermute | solution.py:376
  13.6 9.7 %collective-permute-start.11 = (s32[24]{0:T(128)S(1)}, s32[24]{0:T(128)S(1)}, u32[]{:S(2)}, u32[]{:S(2)}) collective-permute-start(s32[24]{0:T(128)S(1)} %reshape.126), channel_id=1, source_target_pairs={{0,12},{4,8},{8,4},{12,0},{1,13},{5,9},{9,5},{13,1},{2,14},{6,10},... | collective-permute-start | bytes 296 | tf_op jit(solution)/shard_map/ppermute | solution.py:376
  36.5 8.4 %collective-permute-start.21 = (bf16[6,128,256]{2,1,0:T(8,128)(2,1)S(1)}, bf16[6,128,256]{2,1,0:T(8,128)(2,1)}, u32[]{:S(2)}, u32[]{:S(2)}) collective-permute-start(bf16[6,128,256]{2,1,0:T(8,128)(2,1)S(1)} %pack.13.refs_0_), channel_id=1, source_target_pairs={{0,2},{2,0},{1,3},{3,1},{4,6},{6,4},{5,7},{7,5},{8,10},{10,8},{9,1... | collective-permute-start | bytes 1179656 | tf_op jit(solution)/shard_map/ppermute | solution.py:38
  38.5 8.0 %collective-permute-start.17 = (bf16[6,128,256]{2,1,0:T(8,128)(2,1)S(1)}, bf16[6,128,256]{2,1,0:T(8,128)(2,1)S(1)}, u32[]{:S(2)}, u32[]{:S(2)}) collective-permute-start(bf16[6,128,256]{2,1,0:T(8,128)(2,1)S(1)} %pack.10), channel_id=1, source_target_pairs={{0,4},{4,8},{8,12},{1,5},{5,9},{9,13},{2,6},{6,10},{10,14},{3,7},{... | collective-permute-start | bytes 1179656 | tf_op jit(solution)/shard_map/ppermute | solution.py:34
  41.1 9.7 %collective-permute-start.23 = (bf16[6,128,256]{2,1,0:T(8,128)(2,1)S(1)}, bf16[6,128,256]{2,1,0:T(8,128)(2,1)S(1)}, u32[]{:S(2)}, u32[]{:S(2)}) collective-permute-start(bf16[6,128,256]{2,1,0:T(8,128)(2,1)S(1)} %pack.12), channel_id=1, source_target_pairs={{4,0},{8,4},{12,8},{5,1},{9,5},{13,9},{6,2},{10,6},{14,10},{7,3},{... | collective-permute-start | bytes 1179656 | tf_op jit(solution)/shard_map/ppermute | solution.py:34
  43.0 16.3 %collective-permute-start.20 = (bf16[6,128,256]{2,1,0:T(8,128)(2,1)S(1)}, bf16[6,128,256]{2,1,0:T(8,128)(2,1)}, u32[]{:S(2)}, u32[]{:S(2)}) collective-permute-start(bf16[6,128,256]{2,1,0:T(8,128)(2,1)S(1)} %pack.13.refs_0_), channel_id=1, source_target_pairs={{0,1},{1,0},{2,3},{3,2},{4,5},{5,4},{6,7},{7,6},{8,9},{9,8},{10,11... | collective-permute-start | bytes 1179656 | tf_op jit(solution)/shard_map/ppermute | solution.py:38
  44.9 14.4 %collective-permute-start.22 = (bf16[6,128,256]{2,1,0:T(8,128)(2,1)}, bf16[6,128,256]{2,1,0:T(8,128)(2,1)}, u32[]{:S(2)}, u32[]{:S(2)}) collective-permute-start(bf16[6,128,256]{2,1,0:T(8,128)(2,1)} %collective-permute-done.21.refs_2_), channel_id=1, source_target_pairs={{0,1},{1,0},{2,3},{3,2},{4,5},{5,4},{6,7},{7,6},{8,9},{9,8},{10,11... | collective-permute-start | bytes 1179656 | tf_op jit(solution)/shard_map/ppermute | solution.py:38
  46.0 9.3 %collective-permute-start.13 = (f32[1,256]{1,0:T(1,128)S(1)}, f32[1,256]{1,0:T(1,128)S(1)}, u32[]{:S(2)}, u32[]{:S(2)}) collective-permute-start(f32[1,256]{1,0:T(1,128)S(1)} %bitcast.41), channel_id=1, source_target_pairs={{0,1},{1,0},{2,3},{3,2},{4,5},{5,4},{6,7},{7,6},{8,9},{9,8},{10,11... | collective-permute-start | bytes 3080 | tf_op jit(solution)/shard_map/ppermute | solution.py:38
  46.5 10.2 %collective-permute-start.15 = (f32[1,256]{1,0:T(1,128)S(1)}, f32[1,256]{1,0:T(1,128)S(1)}, u32[]{:S(2)}, u32[]{:S(2)}) collective-permute-start(f32[1,256]{1,0:T(1,128)S(1)} %collective-permute-done.14), channel_id=1, source_target_pairs={{0,1},{1,0},{2,3},{3,2},{4,5},{5,4},{6,7},{7,6},{8,9},{9,8},{10,11... | collective-permute-start | bytes 3080 | tf_op jit(solution)/shard_map/ppermute | solution.py:38
  52.6 12.1 %collective-permute-start.18 = (bf16[6,128,256]{2,1,0:T(8,128)(2,1)S(1)}, bf16[6,128,256]{2,1,0:T(8,128)(2,1)S(1)}, u32[]{:S(2)}, u32[]{:S(2)}) collective-permute-start(bf16[6,128,256]{2,1,0:T(8,128)(2,1)S(1)} %pack.11), channel_id=1, source_target_pairs={{0,4},{4,8},{8,12},{1,5},{5,9},{9,13},{2,6},{6,10},{10,14},{3,7},{... | collective-permute-start | bytes 1179656 | tf_op jit(solution)/shard_map/ppermute | solution.py:34
  55.4 17.7 %collective-permute-start.25 = (bf16[6,128,256]{2,1,0:T(8,128)(2,1)S(1)}, bf16[6,128,256]{2,1,0:T(8,128)(2,1)S(1)}, u32[]{:S(2)}, u32[]{:S(2)}) collective-permute-start(bf16[6,128,256]{2,1,0:T(8,128)(2,1)S(1)} %pack.14), channel_id=1, source_target_pairs={{4,0},{8,4},{12,8},{5,1},{9,5},{13,9},{6,2},{10,6},{14,10},{7,3},{... | collective-permute-start | bytes 1179656 | tf_op jit(solution)/shard_map/ppermute | solution.py:34
  58.7 19.7 %collective-permute-start.33 = (bf16[6,128,256]{2,1,0:T(8,128)(2,1)S(1)}, bf16[6,128,256]{2,1,0:T(8,128)(2,1)}, u32[]{:S(2)}, u32[]{:S(2)}) collective-permute-start(bf16[6,128,256]{2,1,0:T(8,128)(2,1)S(1)} %pack.15.refs_0_), channel_id=1, source_target_pairs={{0,2},{2,0},{1,3},{3,1},{4,6},{6,4},{5,7},{7,5},{8,10},{10,8},{9,1... | collective-permute-start | bytes 1179656 | tf_op jit(solution)/shard_map/ppermute | solution.py:38
  66.2 14.4 %collective-permute-start.24 = (bf16[6,128,256]{2,1,0:T(8,128)(2,1)}, bf16[6,128,256]{2,1,0:T(8,128)(2,1)}, u32[]{:S(2)}, u32[]{:S(2)}) collective-permute-start(bf16[6,128,256]{2,1,0:T(8,128)(2,1)} %pack.16), channel_id=1, source_target_pairs={{0,4},{4,8},{8,12},{1,5},{5,9},{9,13},{2,6},{6,10},{10,14},{3,7},{... | collective-permute-start | bytes 1179656 | tf_op jit(solution)/shard_map/ppermute | solution.py:34
  75.4 10.4 %collective-permute-start.30 = (bf16[6,128,256]{2,1,0:T(8,128)(2,1)S(1)}, bf16[6,128,256]{2,1,0:T(8,128)(2,1)}, u32[]{:S(2)}, u32[]{:S(2)}) collective-permute-start(bf16[6,128,256]{2,1,0:T(8,128)(2,1)S(1)} %pack.19.refs_0_), channel_id=1, source_target_pairs={{0,2},{2,0},{1,3},{3,1},{4,6},{6,4},{5,7},{7,5},{8,10},{10,8},{9,1... | collective-permute-start | bytes 1179656 | tf_op jit(solution)/shard_map/ppermute | solution.py:38
  77.1 15.8 %collective-permute-start.32 = (bf16[6,128,256]{2,1,0:T(8,128)(2,1)S(1)}, bf16[6,128,256]{2,1,0:T(8,128)(2,1)}, u32[]{:S(2)}, u32[]{:S(2)}) collective-permute-start(bf16[6,128,256]{2,1,0:T(8,128)(2,1)S(1)} %pack.15.refs_0_), channel_id=1, source_target_pairs={{0,1},{1,0},{2,3},{3,2},{4,5},{5,4},{6,7},{7,6},{8,9},{9,8},{10,11... | collective-permute-start | bytes 1179656 | tf_op jit(solution)/shard_map/ppermute | solution.py:38
  77.1 13.7 %collective-permute-start.26 = (bf16[6,128,256]{2,1,0:T(8,128)(2,1)}, bf16[6,128,256]{2,1,0:T(8,128)(2,1)}, u32[]{:S(2)}, u32[]{:S(2)}) collective-permute-start(bf16[6,128,256]{2,1,0:T(8,128)(2,1)} %pack.17), channel_id=1, source_target_pairs={{4,0},{8,4},{12,8},{5,1},{9,5},{13,9},{6,2},{10,6},{14,10},{7,3},{... | collective-permute-start | bytes 1179656 | tf_op jit(solution)/shard_map/ppermute | solution.py:34
  78.4 15.1 %collective-permute-start.34 = (bf16[6,128,256]{2,1,0:T(8,128)(2,1)}, bf16[6,128,256]{2,1,0:T(8,128)(2,1)}, u32[]{:S(2)}, u32[]{:S(2)}) collective-permute-start(bf16[6,128,256]{2,1,0:T(8,128)(2,1)} %collective-permute-done.33.refs_2_), channel_id=1, source_target_pairs={{0,1},{1,0},{2,3},{3,2},{4,5},{5,4},{6,7},{7,6},{8,9},{9,8},{10,11... | collective-permute-start | bytes 1179656 | tf_op jit(solution)/shard_map/ppermute | solution.py:38
  80.6 19.8 %collective-permute-start.29 = (bf16[6,128,256]{2,1,0:T(8,128)(2,1)S(1)}, bf16[6,128,256]{2,1,0:T(8,128)(2,1)}, u32[]{:S(2)}, u32[]{:S(2)}) collective-permute-start(bf16[6,128,256]{2,1,0:T(8,128)(2,1)S(1)} %pack.19.refs_0_), channel_id=1, source_target_pairs={{0,1},{1,0},{2,3},{3,2},{4,5},{5,4},{6,7},{7,6},{8,9},{9,8},{10,11... | collective-permute-start | bytes 1179656 | tf_op jit(solution)/shard_map/ppermute | solution.py:38
  85.8 14.6 %collective-permute-start.31 = (bf16[6,128,256]{2,1,0:T(8,128)(2,1)}, bf16[6,128,256]{2,1,0:T(8,128)(2,1)}, u32[]{:S(2)}, u32[]{:S(2)}) collective-permute-start(bf16[6,128,256]{2,1,0:T(8,128)(2,1)} %collective-permute-done.30.refs_2_), channel_id=1, source_target_pairs={{0,1},{1,0},{2,3},{3,2},{4,5},{5,4},{6,7},{7,6},{8,9},{9,8},{10,11... | collective-permute-start | bytes 1179656 | tf_op jit(solution)/shard_map/ppermute | solution.py:38
  92.8 12.9 %collective-permute-start.27 = (bf16[6,128,256]{2,1,0:T(8,128)(2,1)S(1)}, bf16[6,128,256]{2,1,0:T(8,128)(2,1)S(1)}, u32[]{:S(2)}, u32[]{:S(2)}) collective-permute-start(bf16[6,128,256]{2,1,0:T(8,128)(2,1)S(1)} %pack.18.refs_0_), channel_id=1, source_target_pairs={{0,1},{1,0},{2,3},{3,2},{4,5},{5,4},{6,7},{7,6},{8,9},{9,8},{10,11... | collective-permute-start | bytes 1179656 | tf_op jit(solution)/shard_map/ppermute | solution.py:38
  92.9 12.8 %collective-permute-start.28 = (bf16[6,128,256]{2,1,0:T(8,128)(2,1)S(1)}, bf16[6,128,256]{2,1,0:T(8,128)(2,1)S(1)}, u32[]{:S(2)}, u32[]{:S(2)}) collective-permute-start(bf16[6,128,256]{2,1,0:T(8,128)(2,1)S(1)} %pack.18.refs_0_), channel_id=1, source_target_pairs={{0,2},{2,0},{1,3},{3,1},{4,6},{6,4},{5,7},{7,5},{8,10},{10,8},{9,1... | collective-permute-start | bytes 1179656 | tf_op jit(solution)/shard_map/ppermute | solution.py:38
  (14 other events, 121.9 us)

commit v5 on v4

--- a/solution.py
+++ b/solution.py
@@ -20,7 +20,7 @@
 
 CHIPS = 4
 ENTRIES_EACH = 16
-AHEAD = 8
+AHEAD = 9
 ROUNDS = 3
 CAP = 6
 GROUP = 3
@@ -297,28 +297,34 @@
     )(place, table)
 
 
-def pack(plan, line, number, pool):
-    lows, arrays = [low for low, _ in pool], [array for _, array in pool]
+def pack(plan, number, pool):
+    lines = (0, 1, 2) if number < ROUNDS else (2,)
+    starts = [0]
+    for array in pool:
+        starts.append(starts[-1] + array.shape[0])
 
     def kernel(plan_ref, *refs):
-        sources, out = refs[:-1], refs[-1]
-        for b in range(CAP):
-            at = plan_ref[line * LANES + number * CAP + b]
-            for source, low in zip(sources, lows):
-
-                @pl.when((at >= low) & (at < low + source.shape[0]))
-                def _(source=source, low=low, b=b, at=at):
-                    out[b] = source[at - low]
+        sources, outs = refs[: len(pool)], refs[len(pool) :]
+        for line, out in zip(lines, outs):
+            for b in range(CAP):
+                at = plan_ref[line * LANES + number * CAP + b]
+                for source, low, high in zip(sources, starts, starts[1:]):
+
+                    @pl.when((at >= low) & (at < high))
+                    def _(source=source, low=low, out=out, b=b, at=at):
+                        out[b] = source[at - low]
 
     in_vmem = pl.BlockSpec(memory_space=pltpu.VMEM)
     return pl.pallas_call(
         kernel,
-        out_shape=jax.ShapeDtypeStruct((CAP,) + arrays[0].shape[1:], arrays[0].dtype),
-        grid_spec=pltpu.PrefetchScalarGridSpec(num_scalar_prefetch=1, in_specs=[in_vmem] * len(pool), out_specs=in_vmem),
+        out_shape=(jax.ShapeDtypeStruct((CAP,) + pool[0].shape[1:], pool[0].dtype),) * len(lines),
+        grid_spec=pltpu.PrefetchScalarGridSpec(
+            num_scalar_prefetch=1, in_specs=[in_vmem] * len(pool), out_specs=(in_vmem,) * len(lines)
+        ),
         compiler_params=pltpu.CompilerParams(vmem_limit_bytes=VMEM_LIMIT),
-        cost_estimate=pl.CostEstimate(flops=0, bytes_accessed=CAP * 2 * 65536, transcendentals=0),
+        cost_estimate=pl.CostEstimate(flops=0, bytes_accessed=len(lines) * CAP * 2 * 65536, transcendentals=0),
         name="pack",
-    )(plan, *arrays)
+    )(plan, *pool)
 
 
 def previous_rows(nbr_owner, nbr_slot, nbr_count):
@@ -365,11 +371,6 @@
     return jnp.stack([block ^ i for i in range(4)]).astype(jnp.int32)
 
 
-def after(pool, token):
-    arrays, _ = lax.optimization_barrier(([array for _, array in pool], token))
-    return [(low, array) for (low, _), array in zip(pool, arrays)]
-
-
 def exchanged_table(codes):
     own_part = [codes]
     for offset in range(1, CHIPS):
@@ -385,8 +386,9 @@
     me = lax.axis_index("parts") * CHIPS + seq
     kept = jnp.arange(KMAX, dtype=jnp.int32)[None, :] < nbr_count[:, None]
     codes = jnp.where(kept, nbr_owner * ENTRIES_EACH + nbr_slot, -1).reshape(-1)
+    early, codes = lax.optimization_barrier((store[:AHEAD], codes))
     table = exchanged_table(codes)
-    early_up, early_down = shifted(store[:AHEAD], "seq", 1), shifted(store[:AHEAD], "seq", -1)
+    early_up, early_down = shifted(early, "seq", 1), shifted(early, "seq", -1)
     plan = make_plan(me.reshape(1).astype(jnp.int32), table.reshape(-1)).reshape(-1)
     missing = plan[4 * LANES]
 
@@ -398,45 +400,42 @@
     first = jnp.maximum(asked[:, 0], 0)
     asked = jnp.stack([first, jnp.where(asked[:, 1] >= 0, asked[:, 1], first)], axis=1).reshape(-1)
 
-    plan, enc_gain = lax.optimization_barrier((plan, enc_gain))
-    gain = jnp.concatenate(four_pieces(enc_gain[None]), axis=1)
     places = places_of_pieces()
-    wanted = plan[2 * LANES : 2 * LANES + total].reshape(ROUNDS + 1, CAP)[:, ::GROUP] >= 0
+    wanted = plan[2 * LANES : 2 * LANES + (ROUNDS + 1) * CAP].reshape(ROUNDS + 1, CAP)[:, ::GROUP] >= 0
     marks = jnp.concatenate([jnp.broadcast_to(places, (ROUNDS + 1, 4)), wanted.astype(jnp.int32)], axis=1).reshape(-1)
-    planned_slots = plan[3 * LANES : 4 * LANES][asked]
-
-    up, down = [(0, store), (ENTRIES_EACH, early_up)], [(0, store), (ENTRIES_EACH + AHEAD, early_down)]
-    held, pieces = (), []
+    slots = plan[3 * LANES : 4 * LANES][asked]
+
+    pool = [store, early_up, early_down]
+    held, pieces, gain = (), [], None
+    room = (ROUNDS + 1) * CAP
 
     def projected(number):
-        return project(marks, gain, pieces[number], key_weight, value_weight, GROUP, total, number, held)
+        return project(marks, gain, pieces[number], key_weight, value_weight, GROUP, room, number, held)
 
     for number in range(ROUNDS + 1):
-        pool = up + down[1:]
-        if number < ROUNDS:
-            base = FIRST_ROUND + number * 2 * CAP
-            going_up = pack(plan, 0, number, after(up, held))
-            going_down = pack(plan, 1, number, after(down, going_up))
-            up = up + [(base, shifted(going_up, "seq", 1))]
-            down = down + [(base + CAP, shifted(going_down, "seq", -1))]
-            pool = after(pool, going_down)
-        mine = pack(plan, 2, number, pool)
+        *ways, mine = pack(plan, number, pool)
+        arrived = [shifted(way, "seq", steps) for way, steps in zip(ways, (1, -1))]
         pieces.append([mine, swapped(mine, "rep"), swapped(mine, "mp")])
-        if number > 0:
+        if number == 0:
+            enc_gain, pieces[0][1] = lax.optimization_barrier((enc_gain, pieces[0][1]))
+            gain = jnp.concatenate(four_pieces(enc_gain[None]), axis=1)
+        else:
             pieces[number - 1].append(swapped(pieces[number - 1][2], "rep"))
-            pieces[number - 1], _ = lax.optimization_barrier((pieces[number - 1], mine))
             held = projected(number - 1)
-    pieces[ROUNDS], held = lax.optimization_barrier((pieces[ROUNDS], held))
+        arrived, pieces[number], held, gain, slots, marks = lax.optimization_barrier(
+            (arrived, pieces[number], held, gain, slots, marks)
+        )
+        pool += arrived
     pieces[ROUNDS].append(swapped(pieces[ROUNDS][2], "rep"))
     keys, values = projected(ROUNDS)
 
     def whole(state):
         mine = fetch_all(store, asked >> 4, asked & (ENTRIES_EACH - 1))
         whole_marks = jnp.concatenate([places, jnp.ones((total // 4,), jnp.int32)])
-        keys, values = project(whole_marks, gain, four_pieces(mine), key_weight, value_weight, 4, total)
+        keys, values = project(whole_marks, gain, four_pieces(mine), key_weight, value_weight, 4, room)
         return jnp.zeros_like(state[0]), jnp.arange(total, dtype=jnp.int32), keys, values
 
-    state = lax.while_loop(lambda state: state[0] > 0, whole, (missing, planned_slots, keys, values))
+    state = lax.while_loop(lambda state: state[0] > 0, whole, (missing, slots, keys, values))
     return attend(state[1], counts, queries, *state[2:])
 
 

time: 127 us -> 119 us (0.937)
  Pallas kernels: 54.5 us -> 46 us
  local copies, waits for them, and re-layouts: 5.72 us -> 7.7 us
  other arithmetic: 1.3 us -> 3.17 us
  starting transfers between devices: 35.1 us -> 33.3 us
    pallas_call x10 -> x4, Pallas kernels: 17.5 us -> 7.17 us  [pack(): pl.pallas_call(kernel, out_shape=(jax.ShapeDtypeStruct((CAP,) + pool[0].s...]
    ppermute x3, waiting for transfers between devices: 9.63 us -> 0.01 us  [exchanged_table(): lax.ppermute(codes, 'seq', [(chip, chip ^ offset) for chip in range(CHIPS)])]
    ppermute x8, waiting for transfers between devices: 8 us -> 16 us  [shifted(): lax.ppermute(value, axis, [(source, source + steps) for source in range(f...]
    pallas_call x4, Pallas kernels: 24 us -> 26.1 us  [project(): pl.pallas_call(kernel, out_shape=(out, out), grid_spec=pltpu.PrefetchScal...]
    ppermute x16, starting transfers between devices: 7.41 us -> 5.86 us  [swapped(): return lax.ppermute(value, axis, [(0, 1), (1, 0)])]
  transfers between devices with their start and end apart: 27 -> 27, of which waited for: 12 -> 11; matrix products, arithmetic and copies ran while one was open for 4% -> 6% of each run, Pallas kernels for 27% -> 22%
where the time goes in v5:
time: 119 us
  Pallas kernels  46 us (39%)
  starting transfers between devices  33.3 us (28%)
  waiting for transfers between devices  27.5 us (23%)
  local copies, waits for them, and re-layouts  7.7 us (6%)
  other arithmetic  3.17 us (3%)
    pallas_call x4, Pallas kernels, project(): pl.pallas_call(kernel, out_shape=(out, out), grid_spec=pltpu.PrefetchScal...  26.1 us
    ppermute x8, starting transfers between devices, shifted(): lax.ppermute(value, axis, [(source, source + steps) for source in range(f...  21.7 us
    ppermute x8, waiting for transfers between devices, shifted(): lax.ppermute(value, axis, [(source, source + steps) for source in range(f...  16 us
    ppermute x16, waiting for transfers between devices, swapped(): return lax.ppermute(value, axis, [(0, 1), (1, 0)])  11.5 us
    pallas_call x1, Pallas kernels, attend(): pl.pallas_call(attend_kernel, out_shape=jax.ShapeDtypeStruct(queries.shap...  10.2 us
    pallas_call x4, Pallas kernels, pack(): pl.pallas_call(kernel, out_shape=(jax.ShapeDtypeStruct((CAP,) + pool[0].s...  7.17 us
    ppermute x16, starting transfers between devices, swapped(): return lax.ppermute(value, axis, [(0, 1), (1, 0)])  5.86 us
    ppermute x3, starting transfers between devices, exchanged_table(): lax.ppermute(codes, 'seq', [(chip, chip ^ offset) for chip in range(CHIPS)])  5.76 us
  transfers between devices with their start and end apart: 27, of which 11 were waited for; matrix products, arithmetic and copies ran while one was open for 6% of the time, Pallas kernels for 22%

profile of v5, /device:TPU:0, one launch (start us, length us, event | category | flops | bytes accessed | tf_op | source)
XLA Modules:
  0.0 118.7 jit_solution(227023484502000761)
XLA Ops:
  2.0 5.1 %collective-permute-start.11 = (s32[24]{0:T(128)S(1)}, s32[24]{0:T(128)S(1)}, u32[]{:S(2)}, u32[]{:S(2)}) collective-permute-start(s32[24]{0:T(128)S(1)} %reshape.126), channel_id=1, source_target_pairs={{0,12},{4,8},{8,4},{12,0},{1,13},{5,9},{9,5},{13,1},{2,14},{6,10},... | collective-permute-start | bytes 296 | tf_op jit(solution)/shard_map/ppermute | solution.py:377
  9.1 4.6 %collective-permute-start.13 = (bf16[9,128,256]{2,1,0:T(8,128)(2,1)S(1)}, bf16[9,128,256]{2,1,0:T(8,128)(2,1)S(1)}, u32[]{:S(2)}, u32[]{:S(2)}) collective-permute-start(bf16[9,128,256]{2,1,0:T(8,128)(2,1)S(1)} %slice.32), channel_id=1, source_target_pairs={{0,4},{4,8},{8,12},{1,5},{5,9},{9,13},{2,6},{6,10},{10,14},{3,7},{... | collective-permute-start | bytes 1769480 | tf_op jit(solution)/shard_map/ppermute | solution.py:34
  13.8 1.7 %collective-permute-start.12 = (s32[4,24]{1,0:T(4,128)S(1)}, s32[4,24]{1,0:T(4,128)S(1)}, u32[]{:S(2)}, u32[]{:S(2)}) collective-permute-start(s32[4,24]{1,0:T(4,128)S(1)} %pad_add_fusion.1), channel_id=1, source_target_pairs={{0,16},{16,0},{1,17},{17,1},{2,18},{18,2},{3,19},{19,3},{4,20},{20... | collective-permute-start | bytes 1160 | tf_op jit(solution)/shard_map/ppermute | solution.py:38
  15.5 1.9 %collective-permute-done.12 = s32[4,24]{1,0:T(4,128)S(1)} collective-permute-done((s32[4,24]{1,0:T(4,128)S(1)}, s32[4,24]{1,0:T(4,128)S(1)}, u32[]{:S(2)}, u32[]{:S(2)}) %collective-permute-start.12) | collective-permute-done | bytes 416 | tf_op jit(solution)/shard_map/ppermute | solution.py:38
  18.2 2.5 %plan.1 = s32[8,128]{1,0:T(8,128)} custom-call(s32[1]{0:T(128)} %bitcast.2.place, s32[192]{0:T(256)} %reshape.127.table), custom_call_target="tpu_custom_call" | custom-call | tf_op jit(solution)/shard_map/plan/pallas_call | solution.py:290
  21.9 2.2 %collective-permute-done.14.refs_2_ = bf16[9,128,256]{2,1,0:T(8,128)(2,1)S(1)} collective-permute-done((bf16[9,128,256]{2,1,0:T(8,128)(2,1)S(1)}, bf16[9,128,256]{2,1,0:T(8,128)(2,1)S(1)}, u32[]{:S(2)}, u32[]{:S(2)}) %collective-permute-start.14) | collective-permute-done | bytes 589856 | tf_op jit(solution)/shard_map/ppermute | solution.py:34
  26.1 2.7 %pack.4 = (bf16[6,128,256]{2,1,0:T(8,128)(2,1)}, bf16[6,128,256]{2,1,0:T(8,128)(2,1)S(1)}, bf16[6,128,256]{2,1,0:T(8,128)(2,1)S(1)}) custom-call(s32[1024]{0:T(1024)S(1)} %bitcast.24, bf16[16,128,256]{2,1,0:T(8,128)(2,1)} %refs_0_.7, bf16[9,128,256]{2,1,0:T(8,128)(2,1)S(1)} %collective-permute-done.13.refs_1_, ...), custom_call_target="tpu_custom_call" | custom-call | bytes 2359296 | tf_op jit(solution)/shard_map/pack/pallas_call | solution.py:318
  29.4 1.5 %collective-permute-start.18 = (bf16[6,128,256]{2,1,0:T(8,128)(2,1)S(1)}, bf16[6,128,256]{2,1,0:T(8,128)(2,1)S(1)}, u32[]{:S(2)}, u32[]{:S(2)}) collective-permute-start(bf16[6,128,256]{2,1,0:T(8,128)(2,1)S(1)} %get-tuple-element.128.refs_0_), channel_id=1, source_target_pairs={{0,2},{2,0},{1,3},{3,1},{4,6},{6,4},{5,7},{7,5},{8,10},{10,8},{9,1... | collective-permute-start | bytes 1179656 | tf_op jit(solution)/shard_map/ppermute | solution.py:38
  30.9 4.6 %collective-permute-start.15 = (bf16[6,128,256]{2,1,0:T(8,128)(2,1)}, bf16[6,128,256]{2,1,0:T(8,128)(2,1)S(1)}, u32[]{:S(2)}, u32[]{:S(2)}) collective-permute-start(bf16[6,128,256]{2,1,0:T(8,128)(2,1)} %get-tuple-element.116), channel_id=1, source_target_pairs={{0,4},{4,8},{8,12},{1,5},{5,9},{9,13},{2,6},{6,10},{10,14},{3,7},{... | collective-permute-start | bytes 1179656 | tf_op jit(solution)/shard_map/ppermute | solution.py:34
  37.5 3.5 %collective-permute-done.20 = f32[1,256]{1,0:T(1,128)} collective-permute-done((f32[1,256]{1,0:T(1,128)}, f32[1,256]{1,0:T(1,128)}, u32[]{:S(2)}, u32[]{:S(2)}) %collective-permute-start.20) | collective-permute-done | bytes 1056 | tf_op jit(solution)/shard_map/ppermute | solution.py:38
  44.6 3.8 %collective-permute-done.16.refs_4_ = bf16[6,128,256]{2,1,0:T(8,128)(2,1)S(1)} collective-permute-done((bf16[6,128,256]{2,1,0:T(8,128)(2,1)S(1)}, bf16[6,128,256]{2,1,0:T(8,128)(2,1)S(1)}, u32[]{:S(2)}, u32[]{:S(2)}) %collective-permute-start.16) | collective-permute-done | bytes 393248 | tf_op jit(solution)/shard_map/ppermute | solution.py:34
  49.1 2.0 %pack.5 = (bf16[6,128,256]{2,1,0:T(8,128)(2,1)S(1)}, bf16[6,128,256]{2,1,0:T(8,128)(2,1)S(1)}, bf16[6,128,256]{2,1,0:T(8,128)(2,1)S(1)}) custom-call(s32[1024]{0:T(1024)S(1)} %bitcast.25, bf16[16,128,256]{2,1,0:T(8,128)(2,1)} %refs_0_.7, bf16[9,128,256]{2,1,0:T(8,128)(2,1)S(1)} %collective-permute-done.13.refs_1_, ...), custom_call_target="tpu_custom_call" | custom-call | bytes 2359296 | tf_op jit(solution)/shard_map/pack/pallas_call | solution.py:318
  51.1 3.5 %collective-permute-start.22 = (bf16[6,128,256]{2,1,0:T(8,128)(2,1)S(1)}, bf16[6,128,256]{2,1,0:T(8,128)(2,1)S(1)}, u32[]{:S(2)}, u32[]{:S(2)}) collective-permute-start(bf16[6,128,256]{2,1,0:T(8,128)(2,1)S(1)} %get-tuple-element.123), channel_id=1, source_target_pairs={{0,4},{4,8},{8,12},{1,5},{5,9},{9,13},{2,6},{6,10},{10,14},{3,7},{... | collective-permute-start | bytes 1179656 | tf_op jit(solution)/shard_map/ppermute | solution.py:34
  56.6 8.3 %project.6 = (bf16[24,128,1024]{2,1,0:T(8,128)(2,1)}, bf16[24,128,1024]{2,1,0:T(8,128)(2,1)}) custom-call(s32[24]{0:T(128)S(1)} %reshape.132.marks_ref, f32[1,1024]{1,0:T(1,128)S(1)} %pad_maximum_fusion.gain_ref, bf16[6,128,256]{2,1,0:T(8,128)(2,1)S(1)} %get-tuple-element.128.refs_0_, bf16[6,128,256]{2,1,0:T(8,128)(2,1)S(1)} %collective-permute-done.17.refs_1_, ...), custom_call_target="tpu_custom_call" | custom-call | flops 3221225472 | bytes 8912896 | tf_op jit(solution)/shard_map/project/pallas_call | solution.py:76
  64.8 2.9 %collective-permute-done.23.refs_6_ = bf16[6,128,256]{2,1,0:T(8,128)(2,1)S(1)} collective-permute-done((bf16[6,128,256]{2,1,0:T(8,128)(2,1)S(1)}, bf16[6,128,256]{2,1,0:T(8,128)(2,1)S(1)}, u32[]{:S(2)}, u32[]{:S(2)}) %collective-permute-start.23) | collective-permute-done | bytes 393248 | tf_op jit(solution)/shard_map/ppermute | solution.py:34
  67.8 1.4 %pack.6 = (bf16[6,128,256]{2,1,0:T(8,128)(2,1)S(1)}, bf16[6,128,256]{2,1,0:T(8,128)(2,1)S(1)}, bf16[6,128,256]{2,1,0:T(8,128)(2,1)S(1)}) custom-call(s32[1024]{0:T(1024)S(1)} %bitcast.26, bf16[16,128,256]{2,1,0:T(8,128)(2,1)S(1)} %copy-done.6, bf16[9,128,256]{2,1,0:T(8,128)(2,1)S(1)} %collective-permute-done.13.refs_1_, ...), custom_call_target="tpu_custom_call" | custom-call | bytes 2359296 | tf_op jit(solution)/shard_map/pack/pallas_call | solution.py:318
  69.2 3.8 %collective-permute-start.27 = (bf16[6,128,256]{2,1,0:T(8,128)(2,1)S(1)}, bf16[6,128,256]{2,1,0:T(8,128)(2,1)S(1)}, u32[]{:S(2)}, u32[]{:S(2)}) collective-permute-start(bf16[6,128,256]{2,1,0:T(8,128)(2,1)S(1)} %get-tuple-element.136), channel_id=1, source_target_pairs={{0,4},{4,8},{8,12},{1,5},{5,9},{9,13},{2,6},{6,10},{10,14},{3,7},{... | collective-permute-start | bytes 1179656 | tf_op jit(solution)/shard_map/ppermute | solution.py:34
  74.9 5.7 %project.7 = (bf16[24,128,1024]{2,1,0:T(8,128)(2,1)}, bf16[24,128,1024]{2,1,0:T(8,128)(2,1)}) custom-call(s32[24]{0:T(128)S(1)} %reshape.132.marks_ref, f32[1,1024]{1,0:T(1,128)S(1)} %pad_maximum_fusion.gain_ref, bf16[6,128,256]{2,1,0:T(8,128)(2,1)S(1)} %get-tuple-element.141.refs_0_, ...), custom_call_target="tpu_custom_call", output_to_operand_aliasing={{0}: (14, {}), {1}: (15, {})} | custom-call | flops 3221225472 | bytes 8912896 | tf_op jit(solution)/shard_map/project/pallas_call | solution.py:76
  80.7 1.3 %collective-permute-done.27.refs_7_ = bf16[6,128,256]{2,1,0:T(8,128)(2,1)S(1)} collective-permute-done((bf16[6,128,256]{2,1,0:T(8,128)(2,1)S(1)}, bf16[6,128,256]{2,1,0:T(8,128)(2,1)S(1)}, u32[]{:S(2)}, u32[]{:S(2)}) %collective-permute-start.27) | collective-permute-done | bytes 393248 | tf_op jit(solution)/shard_map/ppermute | solution.py:34
  82.0 4.1 %collective-permute-done.28.refs_8_ = bf16[6,128,256]{2,1,0:T(8,128)(2,1)S(1)} collective-permute-done((bf16[6,128,256]{2,1,0:T(8,128)(2,1)S(1)}, bf16[6,128,256]{2,1,0:T(8,128)(2,1)S(1)}, u32[]{:S(2)}, u32[]{:S(2)}) %collective-permute-start.28) | collective-permute-done | bytes 393248 | tf_op jit(solution)/shard_map/ppermute | solution.py:34
  88.1 5.7 %project.8 = (bf16[24,128,1024]{2,1,0:T(8,128)(2,1)}, bf16[24,128,1024]{2,1,0:T(8,128)(2,1)}) custom-call(s32[24]{0:T(128)S(1)} %reshape.132.marks_ref, f32[1,1024]{1,0:T(1,128)S(1)} %pad_maximum_fusion.gain_ref, bf16[6,128,256]{2,1,0:T(8,128)(2,1)S(1)} %get-tuple-element.153.refs_0_, ...), custom_call_target="tpu_custom_call", output_to_operand_aliasing={{0}: (14, {}), {1}: (15, {})} | custom-call | flops 3221225472 | bytes 8912896 | tf_op jit(solution)/shard_map/project/pallas_call | solution.py:76
  93.8 5.0 %collective-permute-done.33.refs_2_ = bf16[6,128,256]{2,1,0:T(8,128)(2,1)S(1)} collective-permute-done((bf16[6,128,256]{2,1,0:T(8,128)(2,1)S(1)}, bf16[6,128,256]{2,1,0:T(8,128)(2,1)S(1)}, u32[]{:S(2)}, u32[]{:S(2)}) %collective-permute-start.33) | collective-permute-done | bytes 393248 | tf_op jit(solution)/shard_map/ppermute | solution.py:38
  100.6 6.4 %project.9 = (bf16[24,128,1024]{2,1,0:T(8,128)(2,1)}, bf16[24,128,1024]{2,1,0:T(8,128)(2,1)}) custom-call(s32[24]{0:T(128)S(1)} %reshape.132.marks_ref, f32[1,1024]{1,0:T(1,128)S(1)} %pad_maximum_fusion.gain_ref, bf16[6,128,256]{2,1,0:T(8,128)(2,1)S(1)} %pack.7.refs_0_, ...), custom_call_target="tpu_custom_call", output_to_operand_aliasing={{0}: (14, {}), {1}: (15, {})} | custom-call | flops 3221225472 | bytes 8912896 | tf_op jit(solution)/shard_map/project/pallas_call | solution.py:76
  108.5 10.2 %attend.1 = bf16[768,1024]{1,0:T(8,128)(2,1)} custom-call(s32[24]{0:T(128)} %get-tuple-element.171.slots, s32[12]{0:T(128)S(1)} %convert_reduce_fusion.counts, bf16[768,1024]{1,0:T(8,128)(2,1)S(1)} %copy-done, bf16[24,128,1024]{2,1,0:T(8,128)(2,1)} %get-tuple-element.172.refs_0_.refs_1_.refs_2_.refs_3_.refs_4_.refs_5_, ...), custom_call_target="tpu_custom_call" | custom-call | flops 1610612736 | bytes 15728640 | tf_op jit(solution)/shard_map/attend/pallas_call | solution.py:158
  (93 shorter events, 23.7 us)
Async XLA Ops:
  2.0 11.7 %collective-permute-start.11 = (s32[24]{0:T(128)S(1)}, s32[24]{0:T(128)S(1)}, u32[]{:S(2)}, u32[]{:S(2)}) collective-permute-start(s32[24]{0:T(128)S(1)} %reshape.126), channel_id=1, source_target_pairs={{0,12},{4,8},{8,4},{12,0},{1,13},{5,9},{9,5},{13,1},{2,14},{6,10},... | collective-permute-start | bytes 296 | tf_op jit(solution)/shard_map/ppermute | solution.py:377
  7.1 6.6 %collective-permute-start.10 = (s32[24]{0:T(128)S(1)}, s32[24]{0:T(128)S(1)}, u32[]{:S(2)}, u32[]{:S(2)}) collective-permute-start(s32[24]{0:T(128)S(1)} %reshape.126), channel_id=1, source_target_pairs={{0,8},{4,12},{8,0},{12,4},{1,9},{5,13},{9,1},{13,5},{2,10},{6,14},... | collective-permute-start | bytes 296 | tf_op jit(solution)/shard_map/ppermute | solution.py:377
  7.1 6.6 %collective-permute-start.9 = (s32[24]{0:T(128)S(1)}, s32[24]{0:T(128)S(1)}, u32[]{:S(2)}, u32[]{:S(2)}) collective-permute-start(s32[24]{0:T(128)S(1)} %reshape.126), channel_id=1, source_target_pairs={{0,4},{4,0},{8,12},{12,8},{1,5},{5,1},{9,13},{13,9},{2,6},{6,2},{1... | collective-permute-start | bytes 296 | tf_op jit(solution)/shard_map/ppermute | solution.py:377
  7.8 16.4 %collective-permute-start.14 = (bf16[9,128,256]{2,1,0:T(8,128)(2,1)S(1)}, bf16[9,128,256]{2,1,0:T(8,128)(2,1)S(1)}, u32[]{:S(2)}, u32[]{:S(2)}) collective-permute-start(bf16[9,128,256]{2,1,0:T(8,128)(2,1)S(1)} %slice.32), channel_id=1, source_target_pairs={{4,0},{8,4},{12,8},{5,1},{9,5},{13,9},{6,2},{10,6},{14,10},{7,3},{... | collective-permute-start | bytes 1769480 | tf_op jit(solution)/shard_map/ppermute | solution.py:34
  9.1 16.3 %collective-permute-start.13 = (bf16[9,128,256]{2,1,0:T(8,128)(2,1)S(1)}, bf16[9,128,256]{2,1,0:T(8,128)(2,1)S(1)}, u32[]{:S(2)}, u32[]{:S(2)}) collective-permute-start(bf16[9,128,256]{2,1,0:T(8,128)(2,1)S(1)} %slice.32), channel_id=1, source_target_pairs={{0,4},{4,8},{8,12},{1,5},{5,9},{9,13},{2,6},{6,10},{10,14},{3,7},{... | collective-permute-start | bytes 1769480 | tf_op jit(solution)/shard_map/ppermute | solution.py:34
  13.8 3.7 %collective-permute-start.12 = (s32[4,24]{1,0:T(4,128)S(1)}, s32[4,24]{1,0:T(4,128)S(1)}, u32[]{:S(2)}, u32[]{:S(2)}) collective-permute-start(s32[4,24]{1,0:T(4,128)S(1)} %pad_add_fusion.1), channel_id=1, source_target_pairs={{0,16},{16,0},{1,17},{17,1},{2,18},{18,2},{3,19},{19,3},{4,20},{20... | collective-permute-start | bytes 1160 | tf_op jit(solution)/shard_map/ppermute | solution.py:38
  28.8 8.1 %collective-permute-start.17 = (bf16[6,128,256]{2,1,0:T(8,128)(2,1)S(1)}, bf16[6,128,256]{2,1,0:T(8,128)(2,1)S(1)}, u32[]{:S(2)}, u32[]{:S(2)}) collective-permute-start(bf16[6,128,256]{2,1,0:T(8,128)(2,1)S(1)} %get-tuple-element.128.refs_0_), channel_id=1, source_target_pairs={{0,1},{1,0},{2,3},{3,2},{4,5},{5,4},{6,7},{7,6},{8,9},{9,8},{10,11... | collective-permute-start | bytes 1179656 | tf_op jit(solution)/shard_map/ppermute | solution.py:38
  29.4 19.0 %collective-permute-start.18 = (bf16[6,128,256]{2,1,0:T(8,128)(2,1)S(1)}, bf16[6,128,256]{2,1,0:T(8,128)(2,1)S(1)}, u32[]{:S(2)}, u32[]{:S(2)}) collective-permute-start(bf16[6,128,256]{2,1,0:T(8,128)(2,1)S(1)} %get-tuple-element.128.refs_0_), channel_id=1, source_target_pairs={{0,2},{2,0},{1,3},{3,1},{4,6},{6,4},{5,7},{7,5},{8,10},{10,8},{9,1... | collective-permute-start | bytes 1179656 | tf_op jit(solution)/shard_map/ppermute | solution.py:38
  30.9 13.7 %collective-permute-start.15 = (bf16[6,128,256]{2,1,0:T(8,128)(2,1)}, bf16[6,128,256]{2,1,0:T(8,128)(2,1)S(1)}, u32[]{:S(2)}, u32[]{:S(2)}) collective-permute-start(bf16[6,128,256]{2,1,0:T(8,128)(2,1)} %get-tuple-element.116), channel_id=1, source_target_pairs={{0,4},{4,8},{8,12},{1,5},{5,9},{9,13},{2,6},{6,10},{10,14},{3,7},{... | collective-permute-start | bytes 1179656 | tf_op jit(solution)/shard_map/ppermute | solution.py:34
  35.6 12.9 %collective-permute-start.16 = (bf16[6,128,256]{2,1,0:T(8,128)(2,1)S(1)}, bf16[6,128,256]{2,1,0:T(8,128)(2,1)S(1)}, u32[]{:S(2)}, u32[]{:S(2)}) collective-permute-start(bf16[6,128,256]{2,1,0:T(8,128)(2,1)S(1)} %get-tuple-element.117), channel_id=1, source_target_pairs={{4,0},{8,4},{12,8},{5,1},{9,5},{13,9},{6,2},{10,6},{14,10},{7,3},{... | collective-permute-start | bytes 1179656 | tf_op jit(solution)/shard_map/ppermute | solution.py:34
  36.9 4.1 %collective-permute-start.20 = (f32[1,256]{1,0:T(1,128)}, f32[1,256]{1,0:T(1,128)}, u32[]{:S(2)}, u32[]{:S(2)}) collective-permute-start(f32[1,256]{1,0:T(1,128)} %bitcast.38), channel_id=1, source_target_pairs={{0,2},{2,0},{1,3},{3,1},{4,6},{6,4},{5,7},{7,5},{8,10},{10,8},{9,1... | collective-permute-start | bytes 3080 | tf_op jit(solution)/shard_map/ppermute | solution.py:38
  37.5 6.2 %collective-permute-start.19 = (f32[1,256]{1,0:T(1,128)}, f32[1,256]{1,0:T(1,128)}, u32[]{:S(2)}, u32[]{:S(2)}) collective-permute-start(f32[1,256]{1,0:T(1,128)} %bitcast.39), channel_id=1, source_target_pairs={{0,1},{1,0},{2,3},{3,2},{4,5},{5,4},{6,7},{7,6},{8,9},{9,8},{10,11... | collective-permute-start | bytes 3080 | tf_op jit(solution)/shard_map/ppermute | solution.py:38
  48.5 8.1 %collective-permute-start.26 = (bf16[6,128,256]{2,1,0:T(8,128)(2,1)S(1)}, bf16[6,128,256]{2,1,0:T(8,128)(2,1)S(1)}, u32[]{:S(2)}, u32[]{:S(2)}) collective-permute-start(bf16[6,128,256]{2,1,0:T(8,128)(2,1)S(1)} %collective-permute-done.18.refs_2_), channel_id=1, source_target_pairs={{0,1},{1,0},{2,3},{3,2},{4,5},{5,4},{6,7},{7,6},{8,9},{9,8},{10,11... | collective-permute-start | bytes 1179656 | tf_op jit(solution)/shard_map/ppermute | solution.py:38
  51.1 13.7 %collective-permute-start.22 = (bf16[6,128,256]{2,1,0:T(8,128)(2,1)S(1)}, bf16[6,128,256]{2,1,0:T(8,128)(2,1)S(1)}, u32[]{:S(2)}, u32[]{:S(2)}) collective-permute-start(bf16[6,128,256]{2,1,0:T(8,128)(2,1)S(1)} %get-tuple-element.123), channel_id=1, source_target_pairs={{0,4},{4,8},{8,12},{1,5},{5,9},{9,13},{2,6},{6,10},{10,14},{3,7},{... | collective-permute-start | bytes 1179656 | tf_op jit(solution)/shard_map/ppermute | solution.py:34
  54.6 13.1 %collective-permute-start.23 = (bf16[6,128,256]{2,1,0:T(8,128)(2,1)S(1)}, bf16[6,128,256]{2,1,0:T(8,128)(2,1)S(1)}, u32[]{:S(2)}, u32[]{:S(2)}) collective-permute-start(bf16[6,128,256]{2,1,0:T(8,128)(2,1)S(1)} %get-tuple-element.124), channel_id=1, source_target_pairs={{4,0},{8,4},{12,8},{5,1},{9,5},{13,9},{6,2},{10,6},{14,10},{7,3},{... | collective-permute-start | bytes 1179656 | tf_op jit(solution)/shard_map/ppermute | solution.py:34
  56.0 11.8 %collective-permute-start.25 = (bf16[6,128,256]{2,1,0:T(8,128)(2,1)S(1)}, bf16[6,128,256]{2,1,0:T(8,128)(2,1)S(1)}, u32[]{:S(2)}, u32[]{:S(2)}) collective-permute-start(bf16[6,128,256]{2,1,0:T(8,128)(2,1)S(1)} %get-tuple-element.141.refs_0_), channel_id=1, source_target_pairs={{0,2},{2,0},{1,3},{3,1},{4,6},{6,4},{5,7},{7,5},{8,10},{10,8},{9,1... | collective-permute-start | bytes 1179656 | tf_op jit(solution)/shard_map/ppermute | solution.py:38
  56.6 11.2 %collective-permute-start.24 = (bf16[6,128,256]{2,1,0:T(8,128)(2,1)S(1)}, bf16[6,128,256]{2,1,0:T(8,128)(2,1)S(1)}, u32[]{:S(2)}, u32[]{:S(2)}) collective-permute-start(bf16[6,128,256]{2,1,0:T(8,128)(2,1)S(1)} %get-tuple-element.141.refs_0_), channel_id=1, source_target_pairs={{0,1},{1,0},{2,3},{3,2},{4,5},{5,4},{6,7},{7,6},{8,9},{9,8},{10,11... | collective-permute-start | bytes 1179656 | tf_op jit(solution)/shard_map/ppermute | solution.py:38
  67.8 7.1 %collective-permute-start.31 = (bf16[6,128,256]{2,1,0:T(8,128)(2,1)S(1)}, bf16[6,128,256]{2,1,0:T(8,128)(2,1)S(1)}, u32[]{:S(2)}, u32[]{:S(2)}) collective-permute-start(bf16[6,128,256]{2,1,0:T(8,128)(2,1)S(1)} %collective-permute-done.25.refs_2_), channel_id=1, source_target_pairs={{0,1},{1,0},{2,3},{3,2},{4,5},{5,4},{6,7},{7,6},{8,9},{9,8},{10,11... | collective-permute-start | bytes 1179656 | tf_op jit(solution)/shard_map/ppermute | solution.py:38
  69.2 12.8 %collective-permute-start.27 = (bf16[6,128,256]{2,1,0:T(8,128)(2,1)S(1)}, bf16[6,128,256]{2,1,0:T(8,128)(2,1)S(1)}, u32[]{:S(2)}, u32[]{:S(2)}) collective-permute-start(bf16[6,128,256]{2,1,0:T(8,128)(2,1)S(1)} %get-tuple-element.136), channel_id=1, source_target_pairs={{0,4},{4,8},{8,12},{1,5},{5,9},{9,13},{2,6},{6,10},{10,14},{3,7},{... | collective-permute-start | bytes 1179656 | tf_op jit(solution)/shard_map/ppermute | solution.py:34
  73.0 13.1 %collective-permute-start.28 = (bf16[6,128,256]{2,1,0:T(8,128)(2,1)S(1)}, bf16[6,128,256]{2,1,0:T(8,128)(2,1)S(1)}, u32[]{:S(2)}, u32[]{:S(2)}) collective-permute-start(bf16[6,128,256]{2,1,0:T(8,128)(2,1)S(1)} %get-tuple-element.137), channel_id=1, source_target_pairs={{4,0},{8,4},{12,8},{5,1},{9,5},{13,9},{6,2},{10,6},{14,10},{7,3},{... | collective-permute-start | bytes 1179656 | tf_op jit(solution)/shard_map/ppermute | solution.py:34
  74.3 11.8 %collective-permute-start.30 = (bf16[6,128,256]{2,1,0:T(8,128)(2,1)S(1)}, bf16[6,128,256]{2,1,0:T(8,128)(2,1)S(1)}, u32[]{:S(2)}, u32[]{:S(2)}) collective-permute-start(bf16[6,128,256]{2,1,0:T(8,128)(2,1)S(1)} %get-tuple-element.153.refs_0_), channel_id=1, source_target_pairs={{0,2},{2,0},{1,3},{3,1},{4,6},{6,4},{5,7},{7,5},{8,10},{10,8},{9,1... | collective-permute-start | bytes 1179656 | tf_op jit(solution)/shard_map/ppermute | solution.py:38
  74.9 11.2 %collective-permute-start.29 = (bf16[6,128,256]{2,1,0:T(8,128)(2,1)S(1)}, bf16[6,128,256]{2,1,0:T(8,128)(2,1)S(1)}, u32[]{:S(2)}, u32[]{:S(2)}) collective-permute-start(bf16[6,128,256]{2,1,0:T(8,128)(2,1)S(1)} %get-tuple-element.153.refs_0_), channel_id=1, source_target_pairs={{0,1},{1,0},{2,3},{3,2},{4,5},{5,4},{6,7},{7,6},{8,9},{9,8},{10,11... | collective-permute-start | bytes 1179656 | tf_op jit(solution)/shard_map/ppermute | solution.py:38
  87.3 11.6 %collective-permute-start.33 = (bf16[6,128,256]{2,1,0:T(8,128)(2,1)S(1)}, bf16[6,128,256]{2,1,0:T(8,128)(2,1)S(1)}, u32[]{:S(2)}, u32[]{:S(2)}) collective-permute-start(bf16[6,128,256]{2,1,0:T(8,128)(2,1)S(1)} %pack.7.refs_0_), channel_id=1, source_target_pairs={{0,2},{2,0},{1,3},{3,1},{4,6},{6,4},{5,7},{7,5},{8,10},{10,8},{9,1... | collective-permute-start | bytes 1179656 | tf_op jit(solution)/shard_map/ppermute | solution.py:38
  87.9 11.0 %collective-permute-start.32 = (bf16[6,128,256]{2,1,0:T(8,128)(2,1)S(1)}, bf16[6,128,256]{2,1,0:T(8,128)(2,1)S(1)}, u32[]{:S(2)}, u32[]{:S(2)}) collective-permute-start(bf16[6,128,256]{2,1,0:T(8,128)(2,1)S(1)} %pack.7.refs_0_), channel_id=1, source_target_pairs={{0,1},{1,0},{2,3},{3,2},{4,5},{5,4},{6,7},{7,6},{8,9},{9,8},{10,11... | collective-permute-start | bytes 1179656 | tf_op jit(solution)/shard_map/ppermute | solution.py:38
  (14 other events, 116.4 us)

commit v6 on v5

--- a/solution.py
+++ b/solution.py
@@ -20,11 +20,11 @@
 
 CHIPS = 4
 ENTRIES_EACH = 16
-AHEAD = 9
-ROUNDS = 3
-CAP = 6
-GROUP = 3
-FIRST_ROUND = ENTRIES_EACH + 2 * AHEAD
+HALF = 8
+ROUNDS = 5
+SWEEPS = ROUNDS + 2
+CAP = 4
+GROUP = 2
 LANES = 128
 
 
@@ -174,17 +174,14 @@
     )(slots, counts, queries, *[keys] * len(entries), *[values] * len(entries))
 
 
-def plan_kernel(place, table, plan_ref, far_ref, loc_ref, lists_ref, need_ref, where_ref, picks_ref, slots_ref):
+def plan_kernel(place, table, plan_ref, far_ref, need_ref, lists_ref, picks_ref, slots_ref):
     f32 = jnp.float32
-    rows, groups = 4 * CHIPS, 2 * CHIPS
+    groups = 2 * CHIPS
     me = place[0]
     each = table.shape[0] // groups
     lane = lax.broadcasted_iota(jnp.int32, (1, LANES), 1)
 
-    bases = []
-    for group in range(groups):
-        offset = jnp.bitwise_xor(me, group)
-        bases.append(offset * each)
+    bases = [jnp.bitwise_xor(me, group) * each for group in range(groups)]
     need = []
     for group in range(groups):
         wanted = [bases[group] + j for j in range(each - KMAX)]
@@ -196,109 +193,89 @@
         need.append(hit)
         need_ref[group : group + 1, :] = hit
     for part in range(2):
-        for down in range(2):
-            for chip in range(CHIPS):
-                reach = jnp.zeros((1, LANES), f32)
-                for hops in range(1, CHIPS):
-                    to = chip - hops if down else chip + hops
-                    if 0 <= to < CHIPS:
-                        reach = jnp.where(need[part * CHIPS + to] > 0, float(hops), reach)
-                behind = lane >= chip * ENTRIES_EACH if down else lane < (chip + 1) * ENTRIES_EACH
-                row = part * 2 * CHIPS + down * CHIPS + chip
-                far_ref[row : row + 1, :] = jnp.where(behind, reach, 0.0)
-
-    row = lax.broadcasted_iota(jnp.int32, (rows, LANES), 0)
-    entry = lax.broadcasted_iota(jnp.int32, (rows, LANES), 1)
-    chip, down = row & (CHIPS - 1), (row >> 2) & 1
-    owner, slot = entry >> 4, entry & (ENTRIES_EACH - 1)
-    source = jnp.where(down == 1, chip + 1, chip - 1)
-    early = slot < AHEAD
-    loc = jnp.where(
-        owner == chip,
-        slot,
-        jnp.where((owner == source) & (owner < CHIPS) & early, ENTRIES_EACH + down * AHEAD + slot, -1),
-    ).astype(f32)
-    sent = jnp.where((owner == chip) & early, 1.0, 0.0)
-    far = far_ref[...]
-    needed = need_ref[...]
+        for chip in range(CHIPS):
+            come = (chip - (lane >> 4)) & (CHIPS - 1)
+            reach = jnp.zeros((1, LANES), f32)
+            for hops in range(1, CHIPS):
+                there = need[part * CHIPS + (chip + hops) % CHIPS] > 0
+                reach = jnp.where(there & (come + hops < CHIPS), float(hops), reach)
+            row = part * CHIPS + chip
+            far_ref[row : row + 1, :] = reach
+
+    row = lax.broadcasted_iota(jnp.int32, (groups, LANES), 0)
+    entry = lax.broadcasted_iota(jnp.int32, (groups, LANES), 1)
+    chip, owner, slot = row & (CHIPS - 1), entry >> 4, entry & (ENTRIES_EACH - 1)
+    loc = jnp.where(owner == chip, slot, -1).astype(f32)
+    sent = jnp.where(owner == chip, 1.0, 0.0)
+    from_behind = owner == ((chip + CHIPS - 1) & (CHIPS - 1))
+    halves = [from_behind & (slot < HALF), from_behind & (slot >= HALF)]
+    flights = [jnp.where(half, slot + ENTRIES_EACH, -1).astype(f32) for half in halves]
+    far, needed = far_ref[...], need_ref[...]
     swept = jnp.zeros((groups, LANES), f32)
     slot_of = jnp.zeros((groups, LANES), f32)
-    lists = jnp.full((rows, LANES), -1.0, f32)
+    lists = jnp.full((groups, LANES), -1.0, f32)
     picks = jnp.full((groups, LANES), -1.0, f32)
     one, two = lax.broadcasted_iota(jnp.int32, (LANES, LANES), 0), lax.broadcasted_iota(jnp.int32, (LANES, LANES), 1)
     earlier = jnp.where(one < two, 1.0, 0.0).astype(jnp.bfloat16)
-    to, source = lax.broadcasted_iota(jnp.int32, (rows, rows), 0), lax.broadcasted_iota(jnp.int32, (rows, rows), 1)
-    up_step = ((to >> 2) & 1 == 0) & (to & 3 > 0) & (source == to - 1)
-    down_step = ((to >> 2) & 1 == 1) & (to & 3 < 3) & (source == to + 1)
-    step = jnp.where(up_step | down_step, 1.0, 0.0).astype(jnp.bfloat16)
-    entry_lane = entry[:groups]
+    to, source = lax.broadcasted_iota(jnp.int32, (groups, groups), 0), lax.broadcasted_iota(jnp.int32, (groups, groups), 1)
+    behind = jnp.where(to & (CHIPS - 1) == 0, to + CHIPS - 1, to - 1)
+    step = jnp.where(source == behind, 1.0, 0.0).astype(jnp.bfloat16)
 
     def ranked(mask):
         return jnp.dot(mask.astype(jnp.bfloat16), earlier, preferred_element_type=f32)
 
-    for number in range(ROUNDS + 1):
-        loc_ref[...] = loc
-        for part in range(2):
-            top = part * 2 * CHIPS
-            where_ref[part * CHIPS : (part + 1) * CHIPS, :] = jnp.maximum(
-                loc_ref[top : top + CHIPS, :], loc_ref[top + CHIPS : top + 2 * CHIPS, :]
-            )
-        held = where_ref[...]
-        ready = jnp.where((needed > 0) & (held >= 0) & (swept == 0), 1.0, 0.0)
+    def listed(into, taken, rank, number):
+        for b in range(CAP):
+            pick = jnp.max(jnp.where((taken > 0) & (rank == b), loc, -1.0), axis=1, keepdims=True)
+            into = jnp.where(entry == number * CAP + b, pick, into)
+        return into
+
+    for number in range(SWEEPS):
+        loc = jnp.maximum(loc, flights[number])
+        ready = jnp.where((needed > 0) & (loc >= 0) & (swept == 0), 1.0, 0.0)
         rank = ranked(ready)
         taken = jnp.where((ready > 0) & (rank < CAP), 1.0, 0.0)
         swept = swept + taken
         slot_of = slot_of + taken * (rank + number * CAP)
-        for b in range(CAP):
-            pick = jnp.max(jnp.where((taken > 0) & (rank == b), held, -1.0), axis=1, keepdims=True)
-            picks = jnp.where(entry_lane == number * CAP + b, pick, picks)
-        if number == ROUNDS:
-            break
-        ready = jnp.where((far > 0) & (loc >= 0) & (sent == 0), 1.0, 0.0)
-        rank = jnp.zeros((rows, LANES), f32)
-        above = jnp.zeros((rows, 1), f32)
-        for hops in range(CHIPS - 1, 0, -1):
-            level = jnp.where(far == hops, ready, 0.0)
-            rank = jnp.where(far == hops, ranked(level) + above, rank)
-            above = above + jnp.sum(level, axis=1, keepdims=True)
-        taken = jnp.where((ready > 0) & (rank < CAP), 1.0, 0.0)
-        sent = sent + taken
-        for b in range(CAP):
-            pick = jnp.max(jnp.where((taken > 0) & (rank == b), loc, -1.0), axis=1, keepdims=True)
-            lists = jnp.where(entry == number * CAP + b, pick, lists)
-        came = jnp.dot(step, (taken * (rank + 1)).astype(jnp.bfloat16), preferred_element_type=f32)
-        base = FIRST_ROUND + number * 2 * CAP + down * CAP - 1
-        loc = jnp.where(came > 0, came + base.astype(f32), loc)
+        picks = listed(picks, taken, rank, number)
+        if number < ROUNDS:
+            ready = jnp.where((far > 0) & (loc >= 0) & (sent == 0), 1.0, 0.0)
+            rank = jnp.zeros((groups, LANES), f32)
+            above = jnp.zeros((groups, 1), f32)
+            for hops in range(CHIPS - 1, 0, -1):
+                level = jnp.where(far == hops, ready, 0.0)
+                rank = jnp.where(far == hops, ranked(level) + above, rank)
+                above = above + jnp.sum(level, axis=1, keepdims=True)
+            taken = jnp.where((ready > 0) & (rank < CAP), 1.0, 0.0)
+            sent = sent + taken
+            lists = listed(lists, taken, rank, number)
+            came = jnp.dot(step, (taken * (rank + 1)).astype(jnp.bfloat16), preferred_element_type=f32)
+            flights.append(jnp.where(came > 0, came + float(2 * ENTRIES_EACH + number * CAP - 1), -1.0))
     lists_ref[...] = lists
     picks_ref[...] = picks
     slots_ref[...] = slot_of
     missing = jnp.sum(jnp.where((far > 0) & (sent == 0), 1.0, 0.0)) + jnp.sum(
         jnp.where((needed > 0) & (swept == 0), 1.0, 0.0)
     )
-    mine = (me >> 2) * 2 * CHIPS + (me & 3)
     plan_ref[...] = jnp.zeros(plan_ref.shape, jnp.int32)
-    plan_ref[0:1, :] = lists_ref[pl.ds(mine, 1), :].astype(jnp.int32)
-    plan_ref[1:2, :] = lists_ref[pl.ds(mine + CHIPS, 1), :].astype(jnp.int32)
-    plan_ref[2:3, :] = picks_ref[pl.ds(me, 1), :].astype(jnp.int32)
-    plan_ref[3:4, :] = slots_ref[pl.ds(me, 1), :].astype(jnp.int32)
-    plan_ref[4:5, :] = jnp.full((1, LANES), missing, f32).astype(jnp.int32)
+    for line, rows in enumerate((lists_ref, picks_ref, slots_ref)):
+        plan_ref[line : line + 1, :] = rows[pl.ds(me, 1), :].astype(jnp.int32)
+    plan_ref[3:4, :] = jnp.full((1, LANES), missing, f32).astype(jnp.int32)
 
 
 def make_plan(place, table):
-    rows, groups = 4 * CHIPS, 2 * CHIPS
-    tall, short = pltpu.VMEM((rows, LANES), jnp.float32), pltpu.VMEM((groups, LANES), jnp.float32)
     return pl.pallas_call(
         plan_kernel,
         out_shape=jax.ShapeDtypeStruct((8, LANES), jnp.int32),
         in_specs=[pl.BlockSpec(memory_space=pltpu.SMEM)] * 2,
         out_specs=pl.BlockSpec(memory_space=pltpu.VMEM),
-        scratch_shapes=[tall, tall, tall, short, short, short, short],
+        scratch_shapes=[pltpu.VMEM((2 * CHIPS, LANES), jnp.float32)] * 5,
         name="plan",
     )(place, table)
 
 
 def pack(plan, number, pool):
-    lines = (0, 1, 2) if number < ROUNDS else (2,)
+    lines = (0, 1) if number < ROUNDS else (1,)
     starts = [0]
     for array in pool:
         starts.append(starts[-1] + array.shape[0])
@@ -349,6 +326,11 @@
     return lax.all_gather(fetched, FEATURES, axis=2, tiled=True)
 
 
+def onward(value):
+    size = lax.axis_size("seq")
+    return lax.ppermute(value, "seq", [(chip, (chip + 1) % size) for chip in range(size)])
+
+
 def four_pieces(value):
     across = swapped(value, "mp")
     return [value, swapped(value, "rep"), across, swapped(across, "rep")]
@@ -386,11 +368,11 @@
     me = lax.axis_index("parts") * CHIPS + seq
     kept = jnp.arange(KMAX, dtype=jnp.int32)[None, :] < nbr_count[:, None]
     codes = jnp.where(kept, nbr_owner * ENTRIES_EACH + nbr_slot, -1).reshape(-1)
-    early, codes = lax.optimization_barrier((store[:AHEAD], codes))
+    first, second, codes = lax.optimization_barrier((store[:HALF], store[HALF:], codes))
     table = exchanged_table(codes)
-    early_up, early_down = shifted(early, "seq", 1), shifted(early, "seq", -1)
+    flights = [onward(first), onward(second)]
     plan = make_plan(me.reshape(1).astype(jnp.int32), table.reshape(-1)).reshape(-1)
-    missing = plan[4 * LANES]
+    missing = plan[3 * LANES]
 
     offset = jnp.where(seq > 0, (seq ^ (seq - 1)) & 3, 0)
     behind = table[offset]
@@ -401,33 +383,35 @@
     asked = jnp.stack([first, jnp.where(asked[:, 1] >= 0, asked[:, 1], first)], axis=1).reshape(-1)
 
     places = places_of_pieces()
-    wanted = plan[2 * LANES : 2 * LANES + (ROUNDS + 1) * CAP].reshape(ROUNDS + 1, CAP)[:, ::GROUP] >= 0
-    marks = jnp.concatenate([jnp.broadcast_to(places, (ROUNDS + 1, 4)), wanted.astype(jnp.int32)], axis=1).reshape(-1)
-    slots = plan[3 * LANES : 4 * LANES][asked]
-
-    pool = [store, early_up, early_down]
+    wanted = plan[LANES : LANES + SWEEPS * CAP].reshape(SWEEPS, CAP)[:, ::GROUP] >= 0
+    marks = jnp.concatenate([jnp.broadcast_to(places, (SWEEPS, 4)), wanted.astype(jnp.int32)], axis=1).reshape(-1)
+    slots = plan[2 * LANES : 3 * LANES][asked]
+
+    room = SWEEPS * CAP
     held, pieces, gain = (), [], None
-    room = (ROUNDS + 1) * CAP
 
     def projected(number):
         return project(marks, gain, pieces[number], key_weight, value_weight, GROUP, room, number, held)
 
-    for number in range(ROUNDS + 1):
-        *ways, mine = pack(plan, number, pool)
-        arrived = [shifted(way, "seq", steps) for way, steps in zip(ways, (1, -1))]
+    for number in range(SWEEPS):
+        *ways, mine = pack(plan, number, [store] + flights[: number + 1])
+        flights += [onward(way) for way in ways]
         pieces.append([mine, swapped(mine, "rep"), swapped(mine, "mp")])
         if number == 0:
             enc_gain, pieces[0][1] = lax.optimization_barrier((enc_gain, pieces[0][1]))
             gain = jnp.concatenate(four_pieces(enc_gain[None]), axis=1)
-        else:
+        if number > 1:
+            held = projected(number - 2)
+        if number > 0:
             pieces[number - 1].append(swapped(pieces[number - 1][2], "rep"))
-            held = projected(number - 1)
-        arrived, pieces[number], held, gain, slots, marks = lax.optimization_barrier(
-            (arrived, pieces[number], held, gain, slots, marks)
-        )
-        pool += arrived
-    pieces[ROUNDS].append(swapped(pieces[ROUNDS][2], "rep"))
-    keys, values = projected(ROUNDS)
+        if number + 1 < SWEEPS:
+            flights[number + 1], pieces[: number], held, gain, slots, marks = lax.optimization_barrier(
+                (flights[number + 1], pieces[: number], held, gain, slots, marks)
+            )
+    held = projected(SWEEPS - 2)
+    pieces[-1], held = lax.optimization_barrier((pieces[-1], held))
+    pieces[-1].append(swapped(pieces[-1][2], "rep"))
+    keys, values = projected(SWEEPS - 1)
 
     def whole(state):
         mine = fetch_all(store, asked >> 4, asked & (ENTRIES_EACH - 1))

time: 119 us -> 118 us (level)
  starting transfers between devices: 33.3 us -> 21.3 us
  waiting for transfers between devices: 27.5 us -> 38.9 us
  local copies, waits for them, and re-layouts: 7.7 us -> 13.6 us
  Pallas kernels: 46 us -> 41.2 us
  other arithmetic: 3.17 us -> 1.97 us
    ppermute x8 -> x7, starting transfers between devices: 21.7 us -> 3 us  [onward(): lax.ppermute(value, 'seq', [(chip, (chip + 1) % size) for chip in range(s...]
    ppermute x16 -> x25, waiting for transfers between devices: 11.5 us -> 19.4 us  [swapped(): return lax.ppermute(value, axis, [(0, 1), (1, 0)])]
    ppermute x16 -> x25, starting transfers between devices: 5.86 us -> 12.6 us  [swapped(): return lax.ppermute(value, axis, [(0, 1), (1, 0)])]
    pallas_call x4 -> x7, Pallas kernels: 26.1 us -> 20.8 us  [project(): pl.pallas_call(kernel, out_shape=(out, out), grid_spec=pltpu.PrefetchScal...]
    unnamed x22, local copies, waits for them, and re-layouts: 2.03 us -> 6.83 us
    ppermute x3, waiting for transfers between devices: 0.01 us -> 2.85 us  [exchanged_table(): lax.ppermute(codes, 'seq', [(chip, chip ^ offset) for chip in range(CHIPS)])]
    slice x5 -> x6, local copies, waits for them, and re-layouts: 2.4 us -> 4.25 us  [the longest x1 2.15 us: streamed(): store[HALF:]]
    pallas_call x4 -> x7, Pallas kernels: 7.17 us -> 8.24 us  [pack(): pl.pallas_call(kernel, out_shape=(jax.ShapeDtypeStruct((CAP,) + pool[0].s...]
  transfers between devices with their start and end apart: 27 -> 35, of which waited for: 11 -> 14; matrix products, arithmetic and copies ran while one was open for 6% -> 5% of each run, Pallas kernels for 22% -> 24%
where the time goes in v6:
time: 118 us
  Pallas kernels  41.2 us (35%)
  waiting for transfers between devices  38.9 us (33%)
  starting transfers between devices  21.3 us (18%)
  local copies, waits for them, and re-layouts  13.6 us (12%)
  other arithmetic  1.97 us (2%)
    pallas_call x7, Pallas kernels, project(): pl.pallas_call(kernel, out_shape=(out, out), grid_spec=pltpu.PrefetchScal...  20.8 us
    ppermute x25, waiting for transfers between devices, swapped(): return lax.ppermute(value, axis, [(0, 1), (1, 0)])  19.4 us
    ppermute x7, waiting for transfers between devices, onward(): lax.ppermute(value, 'seq', [(chip, (chip + 1) % size) for chip in range(s...  16.7 us
    ppermute x25, starting transfers between devices, swapped(): return lax.ppermute(value, axis, [(0, 1), (1, 0)])  12.6 us
    pallas_call x1, Pallas kernels, attend(): pl.pallas_call(attend_kernel, out_shape=jax.ShapeDtypeStruct(queries.shap...  9.68 us
    pallas_call x7, Pallas kernels, pack(): pl.pallas_call(kernel, out_shape=(jax.ShapeDtypeStruct((CAP,) + pool[0].s...  8.24 us
    unnamed x22, local copies, waits for them, and re-layouts  6.83 us
    ppermute x3, starting transfers between devices, exchanged_table(): lax.ppermute(codes, 'seq', [(chip, chip ^ offset) for chip in range(CHIPS)])  5.68 us
  transfers between devices with their start and end apart: 35, of which 14 were waited for; matrix products, arithmetic and copies ran while one was open for 5% of the time, Pallas kernels for 24%

profile of v6, /device:TPU:0, one launch (start us, length us, event | category | flops | bytes accessed | tf_op | source)
XLA Modules:
  0.0 118.1 jit_solution(8251039836726730406)
XLA Ops:
  0.0 2.1 %fusion.5 = (bf16[8,128,256]{2,1,0:T(8,128)(2,1)}, bf16[8,128,256]{2,1,0:T(8,128)(2,1)S(1)}) fusion(bf16[16,128,256]{2,1,0:T(8,128)(2,1)} %refs_0_.13), kind=kLoop, calls=%fused_computation.34 | loop fusion | bytes 2097152 | tf_op jit(solution)/shard_map/slice | solution.py:371
  3.0 3.1 %collective-permute-start.9 = (s32[24]{0:T(128)S(1)}, s32[24]{0:T(128)S(1)}, u32[]{:S(2)}, u32[]{:S(2)}) collective-permute-start(s32[24]{0:T(128)S(1)} %reshape.126), channel_id=1, source_target_pairs={{0,4},{4,0},{8,12},{12,8},{1,5},{5,1},{9,13},{13,9},{2,6},{6,2},{1... | collective-permute-start | bytes 296 | tf_op jit(solution)/shard_map/ppermute | solution.py:359
  6.1 2.6 %collective-permute-start.10 = (s32[24]{0:T(128)S(1)}, s32[24]{0:T(128)S(1)}, u32[]{:S(2)}, u32[]{:S(2)}) collective-permute-start(s32[24]{0:T(128)S(1)} %reshape.126), channel_id=1, source_target_pairs={{0,8},{4,12},{8,0},{12,4},{1,9},{5,13},{9,1},{13,5},{2,10},{6,14},... | collective-permute-start | bytes 296 | tf_op jit(solution)/shard_map/ppermute | solution.py:359
  11.3 2.8 %collective-permute-done.11 = s32[24]{0:T(128)S(1)} collective-permute-done((s32[24]{0:T(128)S(1)}, s32[24]{0:T(128)S(1)}, u32[]{:S(2)}, u32[]{:S(2)}) %collective-permute-start.11) | collective-permute-done | bytes 128 | tf_op jit(solution)/shard_map/ppermute | solution.py:359
  15.7 2.1 %collective-permute-done.12 = s32[4,24]{1,0:T(4,128)S(1)} collective-permute-done((s32[4,24]{1,0:T(4,128)S(1)}, s32[4,24]{1,0:T(4,128)S(1)}, u32[]{:S(2)}, u32[]{:S(2)}) %collective-permute-start.12) | collective-permute-done | bytes 416 | tf_op jit(solution)/shard_map/ppermute | solution.py:38
  18.5 2.5 %plan.1 = s32[8,128]{1,0:T(8,128)} custom-call(s32[1]{0:T(128)} %bitcast.2.place, s32[192]{0:T(256)} %reshape.127.table), custom_call_target="tpu_custom_call" | custom-call | tf_op jit(solution)/shard_map/plan/pallas_call | solution.py:267
  22.9 2.5 %collective-permute-done.13.refs_1_ = bf16[8,128,256]{2,1,0:T(8,128)(2,1)S(1)} collective-permute-done((bf16[8,128,256]{2,1,0:T(8,128)(2,1)S(1)}, bf16[8,128,256]{2,1,0:T(8,128)(2,1)S(1)}, u32[]{:S(2)}, u32[]{:S(2)}) %collective-permute-start.13) | collective-permute-done | bytes 524320 | tf_op jit(solution)/shard_map/ppermute | solution.py:331
  26.1 1.9 %pack.7 = (bf16[4,128,256]{2,1,0:T(8,128)(2,1)S(1)}, bf16[4,128,256]{2,1,0:T(8,128)(2,1)S(1)}) custom-call(s32[1024]{0:T(1024)S(1)} %bitcast.23, bf16[16,128,256]{2,1,0:T(8,128)(2,1)} %refs_0_.13, bf16[8,128,256]{2,1,0:T(8,128)(2,1)S(1)} %collective-permute-done.13.refs_1_), custom_call_target="tpu_custom_call" | custom-call | bytes 1048576 | tf_op jit(solution)/shard_map/pack/pallas_call | solution.py:295
  36.1 2.0 %pack.8 = (bf16[4,128,256]{2,1,0:T(8,128)(2,1)S(1)}, bf16[4,128,256]{2,1,0:T(8,128)(2,1)S(1)}) custom-call(s32[1024]{0:T(1024)S(1)} %bitcast.24, bf16[16,128,256]{2,1,0:T(8,128)(2,1)} %refs_0_.13, bf16[8,128,256]{2,1,0:T(8,128)(2,1)S(1)} %collective-permute-done.13.refs_1_, bf16[8,128,256]{2,1,0:T(8,128)(2,1)S(1)} %collective-permute-done.14.refs_2_), custom_call_target="tpu_custom_call" | custom-call | bytes 1048576 | tf_op jit(solution)/shard_map/pack/pallas_call | solution.py:295
  40.8 6.0 %collective-permute-done.24.refs_2_ = bf16[4,128,256]{2,1,0:T(8,128)(2,1)S(1)} collective-permute-done((bf16[4,128,256]{2,1,0:T(8,128)(2,1)S(1)}, bf16[4,128,256]{2,1,0:T(8,128)(2,1)S(1)}, u32[]{:S(2)}, u32[]{:S(2)}) %collective-permute-start.24) | collective-permute-done | bytes 262176 | tf_op jit(solution)/shard_map/ppermute | solution.py:38
  46.9 3.9 %collective-permute-done.19.refs_3_ = bf16[4,128,256]{2,1,0:T(8,128)(2,1)S(1)} collective-permute-done((bf16[4,128,256]{2,1,0:T(8,128)(2,1)S(1)}, bf16[4,128,256]{2,1,0:T(8,128)(2,1)S(1)}, u32[]{:S(2)}, u32[]{:S(2)}) %collective-permute-start.19) | collective-permute-done | bytes 262176 | tf_op jit(solution)/shard_map/ppermute | solution.py:331
  52.7 5.9 %project.9 = (bf16[28,128,1024]{2,1,0:T(8,128)(2,1)S(1)}, bf16[28,128,1024]{2,1,0:T(8,128)(2,1)S(1)}) custom-call(s32[42]{0:T(128)S(1)} %reshape.131.marks_ref, f32[1,1024]{1,0:T(1,128)S(1)} %pad_maximum_fusion.gain_ref, bf16[4,128,256]{2,1,0:T(8,128)(2,1)S(1)} %get-tuple-element.156.refs_0_, bf16[4,128,256]{2,1,0:T(8,128)(2,1)S(1)} %collective-permute-done.15.refs_1_, ...), custom_call_target="tpu_custom_call" | custom-call | flops 2147483648 | bytes 7340032 | tf_op jit(solution)/shard_map/project/pallas_call | solution.py:76
  61.6 5.6 %collective-permute-done.26.refs_5_ = bf16[4,128,256]{2,1,0:T(8,128)(2,1)S(1)} collective-permute-done((bf16[4,128,256]{2,1,0:T(8,128)(2,1)S(1)}, bf16[4,128,256]{2,1,0:T(8,128)(2,1)S(1)}, u32[]{:S(2)}, u32[]{:S(2)}) %collective-permute-start.26) | collective-permute-done | bytes 262176 | tf_op jit(solution)/shard_map/ppermute | solution.py:331
  67.3 2.0 %project.10 = (bf16[28,128,1024]{2,1,0:T(8,128)(2,1)S(1)}, bf16[28,128,1024]{2,1,0:T(8,128)(2,1)S(1)}) custom-call(s32[42]{0:T(128)S(1)} %reshape.131.marks_ref, f32[1,1024]{1,0:T(1,128)S(1)} %pad_maximum_fusion.gain_ref, bf16[4,128,256]{2,1,0:T(8,128)(2,1)S(1)} %get-tuple-element.168.refs_0_, ...), custom_call_target="tpu_custom_call", output_to_operand_aliasing={{0}: (14, {}), {1}: (15, {})} | custom-call | flops 2147483648 | bytes 7340032 | tf_op jit(solution)/shard_map/project/pallas_call | solution.py:76
  71.6 2.0 %project.11 = (bf16[28,128,1024]{2,1,0:T(8,128)(2,1)S(1)}, bf16[28,128,1024]{2,1,0:T(8,128)(2,1)S(1)}) custom-call(s32[42]{0:T(128)S(1)} %reshape.131.marks_ref, f32[1,1024]{1,0:T(1,128)S(1)} %pad_maximum_fusion.gain_ref, bf16[4,128,256]{2,1,0:T(8,128)(2,1)S(1)} %get-tuple-element.183.refs_0_, ...), custom_call_target="tpu_custom_call", output_to_operand_aliasing={{0}: (14, {}), {1}: (15, {})} | custom-call | flops 2147483648 | bytes 7340032 | tf_op jit(solution)/shard_map/project/pallas_call | solution.py:76
  77.6 1.9 %collective-permute-done.36.refs_2_ = bf16[4,128,256]{2,1,0:T(8,128)(2,1)S(1)} collective-permute-done((bf16[4,128,256]{2,1,0:T(8,128)(2,1)S(1)}, bf16[4,128,256]{2,1,0:T(8,128)(2,1)S(1)}, u32[]{:S(2)}, u32[]{:S(2)}) %collective-permute-start.36) | collective-permute-done | bytes 262176 | tf_op jit(solution)/shard_map/ppermute | solution.py:38
  79.9 4.7 %collective-permute-done.41.refs_2_ = bf16[4,128,256]{2,1,0:T(8,128)(2,1)S(1)} collective-permute-done((bf16[4,128,256]{2,1,0:T(8,128)(2,1)S(1)}, bf16[4,128,256]{2,1,0:T(8,128)(2,1)S(1)}, u32[]{:S(2)}, u32[]{:S(2)}) %collective-permute-start.41) | collective-permute-done | bytes 262176 | tf_op jit(solution)/shard_map/ppermute | solution.py:38
  85.3 2.8 %collective-permute-done.30.refs_7_ = bf16[4,128,256]{2,1,0:T(8,128)(2,1)S(1)} collective-permute-done((bf16[4,128,256]{2,1,0:T(8,128)(2,1)S(1)}, bf16[4,128,256]{2,1,0:T(8,128)(2,1)S(1)}, u32[]{:S(2)}, u32[]{:S(2)}) %collective-permute-start.30) | collective-permute-done | bytes 262176 | tf_op jit(solution)/shard_map/ppermute | solution.py:331
  90.0 3.4 %project.13 = (bf16[28,128,1024]{2,1,0:T(8,128)(2,1)S(1)}, bf16[28,128,1024]{2,1,0:T(8,128)(2,1)S(1)}) custom-call(s32[42]{0:T(128)S(1)} %reshape.131.marks_ref, f32[1,1024]{1,0:T(1,128)S(1)} %pad_maximum_fusion.gain_ref, bf16[4,128,256]{2,1,0:T(8,128)(2,1)S(1)} %get-tuple-element.212.refs_0_, ...), custom_call_target="tpu_custom_call", output_to_operand_aliasing={{0}: (14, {}), {1}: (15, {})} | custom-call | flops 2147483648 | bytes 7340032 | tf_op jit(solution)/shard_map/project/pallas_call | solution.py:76
  93.4 3.4 %project.14 = (bf16[28,128,1024]{2,1,0:T(8,128)(2,1)S(1)}, bf16[28,128,1024]{2,1,0:T(8,128)(2,1)S(1)}) custom-call(s32[42]{0:T(128)S(1)} %reshape.131.marks_ref, f32[1,1024]{1,0:T(1,128)S(1)} %pad_maximum_fusion.gain_ref, bf16[4,128,256]{2,1,0:T(8,128)(2,1)S(1)} %pack.13.refs_0_, ...), custom_call_target="tpu_custom_call", output_to_operand_aliasing={{0}: (14, {}), {1}: (15, {})} | custom-call | flops 2147483648 | bytes 7340032 | tf_op jit(solution)/shard_map/project/pallas_call | solution.py:76
  97.9 1.8 %copy-done.8 = bf16[28,128,1024]{2,1,0:T(8,128)(2,1)} copy-done((bf16[28,128,1024]{2,1,0:T(8,128)(2,1)}, bf16[28,128,1024]{2,1,0:T(8,128)(2,1)S(1)}, u32[]{:S(2)}) %copy-start.8) | copy-done | bytes 7340056
  99.7 2.3 %copy-done.9 = bf16[28,128,1024]{2,1,0:T(8,128)(2,1)} copy-done((bf16[28,128,1024]{2,1,0:T(8,128)(2,1)}, bf16[28,128,1024]{2,1,0:T(8,128)(2,1)S(1)}, u32[]{:S(2)}) %copy-start.9) | copy-done | bytes 7340056
  103.5 3.5 %project.15 = (bf16[28,128,1024]{2,1,0:T(8,128)(2,1)}, bf16[28,128,1024]{2,1,0:T(8,128)(2,1)}) custom-call(s32[42]{0:T(128)S(1)} %reshape.131.marks_ref, f32[1,1024]{1,0:T(1,128)S(1)} %pad_maximum_fusion.gain_ref, bf16[4,128,256]{2,1,0:T(8,128)(2,1)S(1)} %pack.12.refs_0_, ...), custom_call_target="tpu_custom_call", output_to_operand_aliasing={{0}: (14, {}), {1}: (15, {})} | custom-call | flops 2147483648 | bytes 7340032 | tf_op jit(solution)/shard_map/project/pallas_call | solution.py:76
  108.4 9.7 %attend.1 = bf16[768,1024]{1,0:T(8,128)(2,1)} custom-call(s32[24]{0:T(128)} %get-tuple-element.229.slots, s32[12]{0:T(128)S(1)} %convert_reduce_fusion.counts, bf16[768,1024]{1,0:T(8,128)(2,1)S(1)} %copy-done, bf16[28,128,1024]{2,1,0:T(8,128)(2,1)} %get-tuple-element.230.refs_0_.refs_1_.refs_2_.refs_3_.refs_4_.refs_5_, ...), custom_call_target="tpu_custom_call" | custom-call | flops 1610612736 | bytes 15728640 | tf_op jit(solution)/shard_map/attend/pallas_call | solution.py:158
  (115 shorter events, 37.3 us)
Async XLA Ops:
  3.0 8.2 %collective-permute-start.9 = (s32[24]{0:T(128)S(1)}, s32[24]{0:T(128)S(1)}, u32[]{:S(2)}, u32[]{:S(2)}) collective-permute-start(s32[24]{0:T(128)S(1)} %reshape.126), channel_id=1, source_target_pairs={{0,4},{4,0},{8,12},{12,8},{1,5},{5,1},{9,13},{13,9},{2,6},{6,2},{1... | collective-permute-start | bytes 296 | tf_op jit(solution)/shard_map/ppermute | solution.py:359
  8.7 16.7 %collective-permute-start.13 = (bf16[8,128,256]{2,1,0:T(8,128)(2,1)S(1)}, bf16[8,128,256]{2,1,0:T(8,128)(2,1)S(1)}, u32[]{:S(2)}, u32[]{:S(2)}) collective-permute-start(bf16[8,128,256]{2,1,0:T(8,128)(2,1)S(1)} %get-tuple-element.144), channel_id=1, source_target_pairs={{0,4},{4,8},{8,12},{12,0},{1,5},{5,9},{9,13},{13,1},{2,6},{6,10},{... | collective-permute-start | bytes 1572872 | tf_op jit(solution)/shard_map/ppermute | solution.py:331
  9.7 25.7 %collective-permute-start.14 = (bf16[8,128,256]{2,1,0:T(8,128)(2,1)}, bf16[8,128,256]{2,1,0:T(8,128)(2,1)S(1)}, u32[]{:S(2)}, u32[]{:S(2)}) collective-permute-start(bf16[8,128,256]{2,1,0:T(8,128)(2,1)} %get-tuple-element.145), channel_id=1, source_target_pairs={{0,4},{4,8},{8,12},{12,0},{1,5},{5,9},{9,13},{13,1},{2,6},{6,10},{... | collective-permute-start | bytes 1572872 | tf_op jit(solution)/shard_map/ppermute | solution.py:331
  31.3 8.6 %collective-permute-start.20 = (bf16[4,128,256]{2,1,0:T(8,128)(2,1)S(1)}, bf16[4,128,256]{2,1,0:T(8,128)(2,1)S(1)}, u32[]{:S(2)}, u32[]{:S(2)}) collective-permute-start(bf16[4,128,256]{2,1,0:T(8,128)(2,1)S(1)} %get-tuple-element.156.refs_0_), channel_id=1, source_target_pairs={{0,2},{2,0},{1,3},{3,1},{4,6},{6,4},{5,7},{7,5},{8,10},{10,8},{9,1... | collective-permute-start | bytes 786440 | tf_op jit(solution)/shard_map/ppermute | solution.py:38
  38.1 8.8 %collective-permute-start.24 = (bf16[4,128,256]{2,1,0:T(8,128)(2,1)S(1)}, bf16[4,128,256]{2,1,0:T(8,128)(2,1)S(1)}, u32[]{:S(2)}, u32[]{:S(2)}) collective-permute-start(bf16[4,128,256]{2,1,0:T(8,128)(2,1)S(1)} %get-tuple-element.168.refs_0_), channel_id=1, source_target_pairs={{0,2},{2,0},{1,3},{3,1},{4,6},{6,4},{5,7},{7,5},{8,10},{10,8},{9,1... | collective-permute-start | bytes 786440 | tf_op jit(solution)/shard_map/ppermute | solution.py:38
  39.9 10.9 %collective-permute-start.19 = (bf16[4,128,256]{2,1,0:T(8,128)(2,1)S(1)}, bf16[4,128,256]{2,1,0:T(8,128)(2,1)S(1)}, u32[]{:S(2)}, u32[]{:S(2)}) collective-permute-start(bf16[4,128,256]{2,1,0:T(8,128)(2,1)S(1)} %get-tuple-element.149), channel_id=1, source_target_pairs={{0,4},{4,8},{8,12},{12,0},{1,5},{5,9},{9,13},{13,1},{2,6},{6,10},{... | collective-permute-start | bytes 786440 | tf_op jit(solution)/shard_map/ppermute | solution.py:331
  39.9 10.9 %collective-permute-start.21 = (bf16[4,128,256]{2,1,0:T(8,128)(2,1)S(1)}, bf16[4,128,256]{2,1,0:T(8,128)(2,1)S(1)}, u32[]{:S(2)}, u32[]{:S(2)}) collective-permute-start(bf16[4,128,256]{2,1,0:T(8,128)(2,1)S(1)} %collective-permute-done.20.refs_2_), channel_id=1, source_target_pairs={{0,1},{1,0},{2,3},{3,2},{4,5},{5,4},{6,7},{7,6},{8,9},{9,8},{10,11... | collective-permute-start | bytes 786440 | tf_op jit(solution)/shard_map/ppermute | solution.py:38
  40.1 18.6 %collective-permute-start.23 = (bf16[4,128,256]{2,1,0:T(8,128)(2,1)S(1)}, bf16[4,128,256]{2,1,0:T(8,128)(2,1)S(1)}, u32[]{:S(2)}, u32[]{:S(2)}) collective-permute-start(bf16[4,128,256]{2,1,0:T(8,128)(2,1)S(1)} %get-tuple-element.168.refs_0_), channel_id=1, source_target_pairs={{0,1},{1,0},{2,3},{3,2},{4,5},{5,4},{6,7},{7,6},{8,9},{9,8},{10,11... | collective-permute-start | bytes 786440 | tf_op jit(solution)/shard_map/ppermute | solution.py:38
  40.4 18.3 %collective-permute-start.22 = (bf16[4,128,256]{2,1,0:T(8,128)(2,1)S(1)}, bf16[4,128,256]{2,1,0:T(8,128)(2,1)S(1)}, u32[]{:S(2)}, u32[]{:S(2)}) collective-permute-start(bf16[4,128,256]{2,1,0:T(8,128)(2,1)S(1)} %get-tuple-element.155), channel_id=1, source_target_pairs={{0,4},{4,8},{8,12},{12,0},{1,5},{5,9},{9,13},{13,1},{2,6},{6,10},{... | collective-permute-start | bytes 786440 | tf_op jit(solution)/shard_map/ppermute | solution.py:331
  46.9 11.8 %collective-permute-start.25 = (bf16[4,128,256]{2,1,0:T(8,128)(2,1)S(1)}, bf16[4,128,256]{2,1,0:T(8,128)(2,1)S(1)}, u32[]{:S(2)}, u32[]{:S(2)}) collective-permute-start(bf16[4,128,256]{2,1,0:T(8,128)(2,1)S(1)} %collective-permute-done.24.refs_2_), channel_id=1, source_target_pairs={{0,1},{1,0},{2,3},{3,2},{4,5},{5,4},{6,7},{7,6},{8,9},{9,8},{10,11... | collective-permute-start | bytes 786440 | tf_op jit(solution)/shard_map/ppermute | solution.py:38
  52.4 8.7 %collective-permute-start.28 = (bf16[4,128,256]{2,1,0:T(8,128)(2,1)S(1)}, bf16[4,128,256]{2,1,0:T(8,128)(2,1)S(1)}, u32[]{:S(2)}, u32[]{:S(2)}) collective-permute-start(bf16[4,128,256]{2,1,0:T(8,128)(2,1)S(1)} %get-tuple-element.183.refs_0_), channel_id=1, source_target_pairs={{0,2},{2,0},{1,3},{3,1},{4,6},{6,4},{5,7},{7,5},{8,10},{10,8},{9,1... | collective-permute-start | bytes 786440 | tf_op jit(solution)/shard_map/ppermute | solution.py:38
  58.6 8.7 %collective-permute-start.26 = (bf16[4,128,256]{2,1,0:T(8,128)(2,1)S(1)}, bf16[4,128,256]{2,1,0:T(8,128)(2,1)S(1)}, u32[]{:S(2)}, u32[]{:S(2)}) collective-permute-start(bf16[4,128,256]{2,1,0:T(8,128)(2,1)S(1)} %get-tuple-element.167), channel_id=1, source_target_pairs={{0,4},{4,8},{8,12},{12,0},{1,5},{5,9},{9,13},{13,1},{2,6},{6,10},{... | collective-permute-start | bytes 786440 | tf_op jit(solution)/shard_map/ppermute | solution.py:331
  61.1 8.2 %collective-permute-start.27 = (bf16[4,128,256]{2,1,0:T(8,128)(2,1)S(1)}, bf16[4,128,256]{2,1,0:T(8,128)(2,1)S(1)}, u32[]{:S(2)}, u32[]{:S(2)}) collective-permute-start(bf16[4,128,256]{2,1,0:T(8,128)(2,1)S(1)} %get-tuple-element.183.refs_0_), channel_id=1, source_target_pairs={{0,1},{1,0},{2,3},{3,2},{4,5},{5,4},{6,7},{7,6},{8,9},{9,8},{10,11... | collective-permute-start | bytes 786440 | tf_op jit(solution)/shard_map/ppermute | solution.py:38
  61.1 8.2 %collective-permute-start.29 = (bf16[4,128,256]{2,1,0:T(8,128)(2,1)S(1)}, bf16[4,128,256]{2,1,0:T(8,128)(2,1)S(1)}, u32[]{:S(2)}, u32[]{:S(2)}) collective-permute-start(bf16[4,128,256]{2,1,0:T(8,128)(2,1)S(1)} %collective-permute-done.28.refs_2_), channel_id=1, source_target_pairs={{0,1},{1,0},{2,3},{3,2},{4,5},{5,4},{6,7},{7,6},{8,9},{9,8},{10,11... | collective-permute-start | bytes 786440 | tf_op jit(solution)/shard_map/ppermute | solution.py:38
  61.6 13.8 %collective-permute-start.32 = (bf16[4,128,256]{2,1,0:T(8,128)(2,1)S(1)}, bf16[4,128,256]{2,1,0:T(8,128)(2,1)S(1)}, u32[]{:S(2)}, u32[]{:S(2)}) collective-permute-start(bf16[4,128,256]{2,1,0:T(8,128)(2,1)S(1)} %get-tuple-element.195.refs_0_), channel_id=1, source_target_pairs={{0,1},{1,0},{2,3},{3,2},{4,5},{5,4},{6,7},{7,6},{8,9},{9,8},{10,11... | collective-permute-start | bytes 786440 | tf_op jit(solution)/shard_map/ppermute | solution.py:38
  67.3 8.2 %collective-permute-start.31 = (bf16[4,128,256]{2,1,0:T(8,128)(2,1)S(1)}, bf16[4,128,256]{2,1,0:T(8,128)(2,1)S(1)}, u32[]{:S(2)}, u32[]{:S(2)}) collective-permute-start(bf16[4,128,256]{2,1,0:T(8,128)(2,1)S(1)} %get-tuple-element.182), channel_id=1, source_target_pairs={{0,4},{4,8},{8,12},{12,0},{1,5},{5,9},{9,13},{13,1},{2,6},{6,10},{... | collective-permute-start | bytes 786440 | tf_op jit(solution)/shard_map/ppermute | solution.py:331
  70.3 9.2 %collective-permute-start.36 = (bf16[4,128,256]{2,1,0:T(8,128)(2,1)S(1)}, bf16[4,128,256]{2,1,0:T(8,128)(2,1)S(1)}, u32[]{:S(2)}, u32[]{:S(2)}) collective-permute-start(bf16[4,128,256]{2,1,0:T(8,128)(2,1)S(1)} %get-tuple-element.212.refs_0_), channel_id=1, source_target_pairs={{0,2},{2,0},{1,3},{3,1},{4,6},{6,4},{5,7},{7,5},{8,10},{10,8},{9,1... | collective-permute-start | bytes 786440 | tf_op jit(solution)/shard_map/ppermute | solution.py:38
  76.2 8.4 %collective-permute-start.41 = (bf16[4,128,256]{2,1,0:T(8,128)(2,1)S(1)}, bf16[4,128,256]{2,1,0:T(8,128)(2,1)S(1)}, u32[]{:S(2)}, u32[]{:S(2)}) collective-permute-start(bf16[4,128,256]{2,1,0:T(8,128)(2,1)S(1)} %pack.13.refs_0_), channel_id=1, source_target_pairs={{0,2},{2,0},{1,3},{3,1},{4,6},{6,4},{5,7},{7,5},{8,10},{10,8},{9,1... | collective-permute-start | bytes 786440 | tf_op jit(solution)/shard_map/ppermute | solution.py:38
  77.6 10.5 %collective-permute-start.35 = (bf16[4,128,256]{2,1,0:T(8,128)(2,1)S(1)}, bf16[4,128,256]{2,1,0:T(8,128)(2,1)S(1)}, u32[]{:S(2)}, u32[]{:S(2)}) collective-permute-start(bf16[4,128,256]{2,1,0:T(8,128)(2,1)S(1)} %get-tuple-element.212.refs_0_), channel_id=1, source_target_pairs={{0,1},{1,0},{2,3},{3,2},{4,5},{5,4},{6,7},{7,6},{8,9},{9,8},{10,11... | collective-permute-start | bytes 786440 | tf_op jit(solution)/shard_map/ppermute | solution.py:38
  77.6 10.5 %collective-permute-start.30 = (bf16[4,128,256]{2,1,0:T(8,128)(2,1)S(1)}, bf16[4,128,256]{2,1,0:T(8,128)(2,1)S(1)}, u32[]{:S(2)}, u32[]{:S(2)}) collective-permute-start(bf16[4,128,256]{2,1,0:T(8,128)(2,1)S(1)} %get-tuple-element.181), channel_id=1, source_target_pairs={{0,4},{4,8},{8,12},{12,0},{1,5},{5,9},{9,13},{13,1},{2,6},{6,10},{... | collective-permute-start | bytes 786440 | tf_op jit(solution)/shard_map/ppermute | solution.py:331
  79.4 8.7 %collective-permute-start.37 = (bf16[4,128,256]{2,1,0:T(8,128)(2,1)S(1)}, bf16[4,128,256]{2,1,0:T(8,128)(2,1)S(1)}, u32[]{:S(2)}, u32[]{:S(2)}) collective-permute-start(bf16[4,128,256]{2,1,0:T(8,128)(2,1)S(1)} %collective-permute-done.36.refs_2_), channel_id=1, source_target_pairs={{0,1},{1,0},{2,3},{3,2},{4,5},{5,4},{6,7},{7,6},{8,9},{9,8},{10,11... | collective-permute-start | bytes 786440 | tf_op jit(solution)/shard_map/ppermute | solution.py:38
  79.4 13.9 %collective-permute-start.40 = (bf16[4,128,256]{2,1,0:T(8,128)(2,1)S(1)}, bf16[4,128,256]{2,1,0:T(8,128)(2,1)S(1)}, u32[]{:S(2)}, u32[]{:S(2)}) collective-permute-start(bf16[4,128,256]{2,1,0:T(8,128)(2,1)S(1)} %pack.13.refs_0_), channel_id=1, source_target_pairs={{0,1},{1,0},{2,3},{3,2},{4,5},{5,4},{6,7},{7,6},{8,9},{9,8},{10,11... | collective-permute-start | bytes 786440 | tf_op jit(solution)/shard_map/ppermute | solution.py:38
  84.6 8.7 %collective-permute-start.42 = (bf16[4,128,256]{2,1,0:T(8,128)(2,1)S(1)}, bf16[4,128,256]{2,1,0:T(8,128)(2,1)S(1)}, u32[]{:S(2)}, u32[]{:S(2)}) collective-permute-start(bf16[4,128,256]{2,1,0:T(8,128)(2,1)S(1)} %collective-permute-done.41.refs_2_), channel_id=1, source_target_pairs={{0,1},{1,0},{2,3},{3,2},{4,5},{5,4},{6,7},{7,6},{8,9},{9,8},{10,11... | collective-permute-start | bytes 786440 | tf_op jit(solution)/shard_map/ppermute | solution.py:38
  89.2 8.7 %collective-permute-start.39 = (bf16[4,128,256]{2,1,0:T(8,128)(2,1)S(1)}, bf16[4,128,256]{2,1,0:T(8,128)(2,1)S(1)}, u32[]{:S(2)}, u32[]{:S(2)}) collective-permute-start(bf16[4,128,256]{2,1,0:T(8,128)(2,1)S(1)} %pack.12.refs_0_), channel_id=1, source_target_pairs={{0,2},{2,0},{1,3},{3,1},{4,6},{6,4},{5,7},{7,5},{8,10},{10,8},{9,1... | collective-permute-start | bytes 786440 | tf_op jit(solution)/shard_map/ppermute | solution.py:38
  (22 other events, 158.0 us)

commit v7 on v6

--- a/solution.py
+++ b/solution.py
@@ -26,6 +26,8 @@
 CAP = 4
 GROUP = 2
 LANES = 128
+
+LITTLE = pl.CostEstimate(flops=1, bytes_accessed=1, transcendentals=0)
 
 
 def shifted(value, axis, steps):
@@ -87,11 +89,7 @@
         ),
         input_output_aliases={len(operands) - len(held) + i: i for i in range(len(held))},
         compiler_params=pltpu.CompilerParams(vmem_limit_bytes=VMEM_LIMIT),
-        cost_estimate=pl.CostEstimate(
-            flops=4 * count * tokens * DE * columns,
-            bytes_accessed=2 * (count * tokens * (DE + 2 * columns) + 2 * DE * columns),
-            transcendentals=0,
-        ),
+        cost_estimate=LITTLE,
         name="project",
     )(*operands)
 
@@ -165,11 +163,7 @@
             out_specs=query_spec,
         ),
         compiler_params=pltpu.CompilerParams(vmem_limit_bytes=VMEM_LIMIT),
-        cost_estimate=pl.CostEstimate(
-            flops=8 * stretches * STRETCH * KMAX * NLEN * columns,
-            bytes_accessed=4 * stretches * columns * (STRETCH + KMAX * NLEN),
-            transcendentals=stretches * STRETCH * KMAX * NLEN * columns // HEAD_DIM,
-        ),
+        cost_estimate=LITTLE,
         name="attend",
     )(slots, counts, queries, *[keys] * len(entries), *[values] * len(entries))
 
@@ -299,7 +293,7 @@
             num_scalar_prefetch=1, in_specs=[in_vmem] * len(pool), out_specs=(in_vmem,) * len(lines)
         ),
         compiler_params=pltpu.CompilerParams(vmem_limit_bytes=VMEM_LIMIT),
-        cost_estimate=pl.CostEstimate(flops=0, bytes_accessed=len(lines) * CAP * 2 * 65536, transcendentals=0),
+        cost_estimate=LITTLE,
         name="pack",
     )(plan, *pool)
 
@@ -401,6 +395,8 @@
             enc_gain, pieces[0][1] = lax.optimization_barrier((enc_gain, pieces[0][1]))
             gain = jnp.concatenate(four_pieces(enc_gain[None]), axis=1)
         if number > 1:
+            if number + 1 < SWEEPS:
+                pieces[number - 2], flights[number + 1] = lax.optimization_barrier((pieces[number - 2], flights[number + 1]))
             held = projected(number - 2)
         if number > 0:
             pieces[number - 1].append(swapped(pieces[number - 1][2], "rep"))

time: 118 us -> 122 us (1.034); the launches traced: 118 us -> 119 us
  Pallas kernels: 41.2 us -> 53.5 us
  waiting for transfers between devices: 38.9 us -> 29.2 us
  local copies, waits for them, and re-layouts: 13.6 us -> 10.5 us
  starting transfers between devices: 21.3 us -> 23.4 us
    ppermute x7, waiting for transfers between devices: 16.7 us -> 10.1 us  [onward(): lax.ppermute(value, 'seq', [(chip, (chip + 1) % size) for chip in range(s...]
    pallas_call x7, Pallas kernels: 20.8 us -> 26.9 us  [project(): pl.pallas_call(kernel, out_shape=(out, out), grid_spec=pltpu.PrefetchScal...]
    pallas_call x7, Pallas kernels: 8.24 us -> 13.4 us  [pack(): pl.pallas_call(kernel, out_shape=(jax.ShapeDtypeStruct((CAP,) + pool[0].s...]
    ppermute x25, waiting for transfers between devices: 19.4 us -> 16.2 us  [swapped(): return lax.ppermute(value, axis, [(0, 1), (1, 0)])]
    unnamed x22 -> x16, local copies, waits for them, and re-layouts: 6.83 us -> 4.77 us
    ppermute x25, starting transfers between devices: 12.6 us -> 14.2 us  [swapped(): return lax.ppermute(value, axis, [(0, 1), (1, 0)])]
  transfers between devices with their start and end apart: 35 -> 35, of which waited for: 14 -> 13; matrix products, arithmetic and copies ran while one was open for 5% -> 5% of each run, Pallas kernels for 24% -> 32%
where the time goes in v7:
time: 122 us; the launch traced here: 119 us
  Pallas kernels  53.5 us (44%)
  waiting for transfers between devices  29.2 us (24%)
  starting transfers between devices  23.4 us (19%)
  local copies, waits for them, and re-layouts  10.5 us (9%)
  other arithmetic  1.98 us (2%)
    pallas_call x7, Pallas kernels, project(): pl.pallas_call(kernel, out_shape=(out, out), grid_spec=pltpu.PrefetchScal...  26.9 us
    ppermute x25, waiting for transfers between devices, swapped(): return lax.ppermute(value, axis, [(0, 1), (1, 0)])  16.2 us
    ppermute x25, starting transfers between devices, swapped(): return lax.ppermute(value, axis, [(0, 1), (1, 0)])  14.2 us
    pallas_call x7, Pallas kernels, pack(): pl.pallas_call(kernel, out_shape=(jax.ShapeDtypeStruct((CAP,) + pool[0].s...  13.4 us
    pallas_call x1, Pallas kernels, attend(): pl.pallas_call(attend_kernel, out_shape=jax.ShapeDtypeStruct(queries.shap...  10.6 us
    ppermute x7, waiting for transfers between devices, onward(): lax.ppermute(value, 'seq', [(chip, (chip + 1) % size) for chip in range(s...  10.1 us
    ppermute x3, starting transfers between devices, exchanged_table(): lax.ppermute(codes, 'seq', [(chip, chip ^ offset) for chip in range(CHIPS)])  5.68 us
    unnamed x16, local copies, waits for them, and re-layouts  4.77 us
  transfers between devices with their start and end apart: 35, of which 13 were waited for; matrix products, arithmetic and copies ran while one was open for 5% of the time, Pallas kernels for 32%

profile of v7, /device:TPU:0, one launch (start us, length us, event | category | flops | bytes accessed | tf_op | source)
XLA Modules:
  0.0 119.4 jit_solution(8017071757154503406)
XLA Ops:
  2.2 3.1 %collective-permute-start.9 = (s32[24]{0:T(128)S(1)}, s32[24]{0:T(128)S(1)}, u32[]{:S(2)}, u32[]{:S(2)}) collective-permute-start(s32[24]{0:T(128)S(1)} %reshape.126), channel_id=1, source_target_pairs={{0,4},{4,0},{8,12},{12,8},{1,5},{5,1},{9,13},{13,9},{2,6},{6,2},{1... | collective-permute-start | bytes 296 | tf_op jit(solution)/shard_map/ppermute | solution.py:353
  5.2 2.6 %collective-permute-start.10 = (s32[24]{0:T(128)S(1)}, s32[24]{0:T(128)S(1)}, u32[]{:S(2)}, u32[]{:S(2)}) collective-permute-start(s32[24]{0:T(128)S(1)} %reshape.126), channel_id=1, source_target_pairs={{0,8},{4,12},{8,0},{12,4},{1,9},{5,13},{9,1},{13,5},{2,10},{6,14},... | collective-permute-start | bytes 296 | tf_op jit(solution)/shard_map/ppermute | solution.py:353
  10.4 2.8 %collective-permute-done.11 = s32[24]{0:T(128)S(1)} collective-permute-done((s32[24]{0:T(128)S(1)}, s32[24]{0:T(128)S(1)}, u32[]{:S(2)}, u32[]{:S(2)}) %collective-permute-start.11) | collective-permute-done | bytes 128 | tf_op jit(solution)/shard_map/ppermute | solution.py:353
  14.8 2.1 %collective-permute-done.12 = s32[4,24]{1,0:T(4,128)S(1)} collective-permute-done((s32[4,24]{1,0:T(4,128)S(1)}, s32[4,24]{1,0:T(4,128)S(1)}, u32[]{:S(2)}, u32[]{:S(2)}) %collective-permute-start.12) | collective-permute-done | bytes 416 | tf_op jit(solution)/shard_map/ppermute | solution.py:40
  17.6 2.5 %plan.1 = s32[8,128]{1,0:T(8,128)} custom-call(s32[1]{0:T(128)} %bitcast.2.place, s32[192]{0:T(256)} %reshape.127.table), custom_call_target="tpu_custom_call" | custom-call | tf_op jit(solution)/shard_map/plan/pallas_call | solution.py:261
  22.0 2.5 %collective-permute-done.13.refs_1_ = bf16[8,128,256]{2,1,0:T(8,128)(2,1)S(1)} collective-permute-done((bf16[8,128,256]{2,1,0:T(8,128)(2,1)S(1)}, bf16[8,128,256]{2,1,0:T(8,128)(2,1)S(1)}, u32[]{:S(2)}, u32[]{:S(2)}) %collective-permute-start.13) | collective-permute-done | bytes 524320 | tf_op jit(solution)/shard_map/ppermute | solution.py:325
  25.2 1.9 %pack.7 = (bf16[4,128,256]{2,1,0:T(8,128)(2,1)S(1)}, bf16[4,128,256]{2,1,0:T(8,128)(2,1)S(1)}) custom-call(s32[1024]{0:T(1024)S(1)} %bitcast.23, bf16[16,128,256]{2,1,0:T(8,128)(2,1)} %refs_0_.13, bf16[8,128,256]{2,1,0:T(8,128)(2,1)S(1)} %collective-permute-done.13.refs_1_), custom_call_target="tpu_custom_call" | custom-call | flops 1 | bytes 1 | tf_op jit(solution)/shard_map/pack/pallas_call | solution.py:289
  30.4 5.8 %collective-permute-done.20 = f32[1,256]{1,0:T(1,128)S(1)} collective-permute-done((f32[1,256]{1,0:T(1,128)}, f32[1,256]{1,0:T(1,128)S(1)}, u32[]{:S(2)}, u32[]{:S(2)}) %collective-permute-start.20) | collective-permute-done | bytes 1056 | tf_op jit(solution)/shard_map/ppermute | solution.py:40
  39.4 2.0 %pack.8 = (bf16[4,128,256]{2,1,0:T(8,128)(2,1)S(1)}, bf16[4,128,256]{2,1,0:T(8,128)(2,1)S(1)}) custom-call(s32[1024]{0:T(1024)S(1)} %bitcast.24, bf16[16,128,256]{2,1,0:T(8,128)(2,1)} %refs_0_.13, bf16[8,128,256]{2,1,0:T(8,128)(2,1)S(1)} %collective-permute-done.13.refs_1_, bf16[8,128,256]{2,1,0:T(8,128)(2,1)S(1)} %collective-permute-done.18.refs_2_), custom_call_target="tpu_custom_call" | custom-call | flops 1 | bytes 1 | tf_op jit(solution)/shard_map/pack/pallas_call | solution.py:289
  43.4 5.1 %collective-permute-done.14.refs_3_ = bf16[4,128,256]{2,1,0:T(8,128)(2,1)S(1)} collective-permute-done((bf16[4,128,256]{2,1,0:T(8,128)(2,1)S(1)}, bf16[4,128,256]{2,1,0:T(8,128)(2,1)S(1)}, u32[]{:S(2)}, u32[]{:S(2)}) %collective-permute-start.14) | collective-permute-done | bytes 262176 | tf_op jit(solution)/shard_map/ppermute | solution.py:325
  49.1 1.9 %pack.9 = (bf16[4,128,256]{2,1,0:T(8,128)(2,1)S(1)}, bf16[4,128,256]{2,1,0:T(8,128)(2,1)S(1)}) custom-call(s32[1024]{0:T(1024)S(1)} %bitcast.25, bf16[16,128,256]{2,1,0:T(8,128)(2,1)} %refs_0_.13, bf16[8,128,256]{2,1,0:T(8,128)(2,1)S(1)} %collective-permute-done.13.refs_1_, bf16[8,128,256]{2,1,0:T(8,128)(2,1)S(1)} %collective-permute-done.18.refs_2_, ...), custom_call_target="tpu_custom_call" | custom-call | flops 1 | bytes 1 | tf_op jit(solution)/shard_map/pack/pallas_call | solution.py:289
  53.7 6.8 %project.9 = (bf16[28,128,1024]{2,1,0:T(8,128)(2,1)}, bf16[28,128,1024]{2,1,0:T(8,128)(2,1)S(1)}) custom-call(s32[42]{0:T(128)S(1)} %reshape.131.marks_ref, f32[1,1024]{1,0:T(1,128)S(1)} %pad_maximum_fusion.gain_ref, bf16[4,128,256]{2,1,0:T(8,128)(2,1)S(1)} %get-tuple-element.180.refs_0_, bf16[4,128,256]{2,1,0:T(8,128)(2,1)S(1)} %collective-permute-done.15.refs_1_, ...), custom_call_target="tpu_custom_call" | custom-call | flops 1 | bytes 1 | tf_op jit(solution)/shard_map/project/pallas_call | solution.py:78
  61.0 2.0 %pack.10 = (bf16[4,128,256]{2,1,0:T(8,128)(2,1)S(1)}, bf16[4,128,256]{2,1,0:T(8,128)(2,1)S(1)}) custom-call(s32[1024]{0:T(1024)S(1)} %bitcast.26, bf16[16,128,256]{2,1,0:T(8,128)(2,1)} %refs_0_.13, bf16[8,128,256]{2,1,0:T(8,128)(2,1)S(1)} %collective-permute-done.13.refs_1_, bf16[8,128,256]{2,1,0:T(8,128)(2,1)S(1)} %collective-permute-done.18.refs_2_, ...), custom_call_target="tpu_custom_call" | custom-call | flops 1 | bytes 1 | tf_op jit(solution)/shard_map/pack/pallas_call | solution.py:289
  64.4 4.2 %project.10 = (bf16[28,128,1024]{2,1,0:T(8,128)(2,1)}, bf16[28,128,1024]{2,1,0:T(8,128)(2,1)S(1)}) custom-call(s32[42]{0:T(128)S(1)} %reshape.131.marks_ref, f32[1,1024]{1,0:T(1,128)S(1)} %pad_maximum_fusion.gain_ref, bf16[4,128,256]{2,1,0:T(8,128)(2,1)S(1)} %get-tuple-element.197.refs_0_, ...), custom_call_target="tpu_custom_call", output_to_operand_aliasing={{0}: (14, {}), {1}: (15, {})} | custom-call | flops 1 | bytes 1 | tf_op jit(solution)/shard_map/project/pallas_call | solution.py:78
  68.7 1.8 %pack.11 = (bf16[4,128,256]{2,1,0:T(8,128)(2,1)S(1)}, bf16[4,128,256]{2,1,0:T(8,128)(2,1)S(1)}) custom-call(s32[1024]{0:T(1024)S(1)} %bitcast.27, bf16[16,128,256]{2,1,0:T(8,128)(2,1)} %refs_0_.13, bf16[8,128,256]{2,1,0:T(8,128)(2,1)S(1)} %collective-permute-done.13.refs_1_, bf16[8,128,256]{2,1,0:T(8,128)(2,1)S(1)} %collective-permute-done.18.refs_2_, ...), custom_call_target="tpu_custom_call" | custom-call | flops 1 | bytes 1 | tf_op jit(solution)/shard_map/pack/pallas_call | solution.py:289
  74.2 3.0 %project.11 = (bf16[28,128,1024]{2,1,0:T(8,128)(2,1)}, bf16[28,128,1024]{2,1,0:T(8,128)(2,1)S(1)}) custom-call(s32[42]{0:T(128)S(1)} %reshape.131.marks_ref, f32[1,1024]{1,0:T(1,128)S(1)} %pad_maximum_fusion.gain_ref, bf16[4,128,256]{2,1,0:T(8,128)(2,1)S(1)} %get-tuple-element.216.refs_0_, ...), custom_call_target="tpu_custom_call", output_to_operand_aliasing={{0}: (14, {}), {1}: (15, {})} | custom-call | flops 1 | bytes 1 | tf_op jit(solution)/shard_map/project/pallas_call | solution.py:78
  78.5 1.9 %pack.13.refs_0_ = bf16[4,128,256]{2,1,0:T(8,128)(2,1)S(1)} custom-call(s32[1024]{0:T(1024)S(1)} %bitcast.28, bf16[16,128,256]{2,1,0:T(8,128)(2,1)} %refs_0_.13, bf16[8,128,256]{2,1,0:T(8,128)(2,1)S(1)} %collective-permute-done.13.refs_1_, bf16[8,128,256]{2,1,0:T(8,128)(2,1)S(1)} %collective-permute-done.18.refs_2_, ...), custom_call_target="tpu_custom_call" | custom-call | flops 1 | bytes 1 | tf_op jit(solution)/shard_map/pack/pallas_call | solution.py:289
  81.9 3.0 %project.12 = (bf16[28,128,1024]{2,1,0:T(8,128)(2,1)}, bf16[28,128,1024]{2,1,0:T(8,128)(2,1)S(1)}) custom-call(s32[42]{0:T(128)S(1)} %reshape.131.marks_ref, f32[1,1024]{1,0:T(1,128)S(1)} %pad_maximum_fusion.gain_ref, bf16[4,128,256]{2,1,0:T(8,128)(2,1)S(1)} %get-tuple-element.235.refs_0_, ...), custom_call_target="tpu_custom_call", output_to_operand_aliasing={{0}: (14, {}), {1}: (15, {})} | custom-call | flops 1 | bytes 1 | tf_op jit(solution)/shard_map/project/pallas_call | solution.py:78
  84.8 4.4 %collective-permute-done.41.refs_2_ = bf16[4,128,256]{2,1,0:T(8,128)(2,1)S(1)} collective-permute-done((bf16[4,128,256]{2,1,0:T(8,128)(2,1)S(1)}, bf16[4,128,256]{2,1,0:T(8,128)(2,1)S(1)}, u32[]{:S(2)}, u32[]{:S(2)}) %collective-permute-start.41) | collective-permute-done | bytes 262176 | tf_op jit(solution)/shard_map/ppermute | solution.py:40
  89.2 1.8 %pack.12.refs_0_ = bf16[4,128,256]{2,1,0:T(8,128)(2,1)S(1)} custom-call(s32[1024]{0:T(1024)S(1)} %bitcast.29, bf16[16,128,256]{2,1,0:T(8,128)(2,1)} %refs_0_.13, bf16[8,128,256]{2,1,0:T(8,128)(2,1)S(1)} %collective-permute-done.13.refs_1_, bf16[8,128,256]{2,1,0:T(8,128)(2,1)S(1)} %collective-permute-done.18.refs_2_, ...), custom_call_target="tpu_custom_call" | custom-call | flops 1 | bytes 1 | tf_op jit(solution)/shard_map/pack/pallas_call | solution.py:289
  92.2 3.0 %project.13 = (bf16[28,128,1024]{2,1,0:T(8,128)(2,1)}, bf16[28,128,1024]{2,1,0:T(8,128)(2,1)S(1)}) custom-call(s32[42]{0:T(128)S(1)} %reshape.131.marks_ref, f32[1,1024]{1,0:T(1,128)S(1)} %pad_maximum_fusion.gain_ref, bf16[4,128,256]{2,1,0:T(8,128)(2,1)S(1)} %get-tuple-element.252.refs_0_, ...), custom_call_target="tpu_custom_call", output_to_operand_aliasing={{0}: (14, {}), {1}: (15, {})} | custom-call | flops 1 | bytes 1 | tf_op jit(solution)/shard_map/project/pallas_call | solution.py:78
  95.2 2.9 %project.14 = (bf16[28,128,1024]{2,1,0:T(8,128)(2,1)}, bf16[28,128,1024]{2,1,0:T(8,128)(2,1)S(1)}) custom-call(s32[42]{0:T(128)S(1)} %reshape.131.marks_ref, f32[1,1024]{1,0:T(1,128)S(1)} %pad_maximum_fusion.gain_ref, bf16[4,128,256]{2,1,0:T(8,128)(2,1)S(1)} %pack.13.refs_0_, ...), custom_call_target="tpu_custom_call", output_to_operand_aliasing={{0}: (14, {}), {1}: (15, {})} | custom-call | flops 1 | bytes 1 | tf_op jit(solution)/shard_map/project/pallas_call | solution.py:78
  102.6 4.1 %project.15 = (bf16[28,128,1024]{2,1,0:T(8,128)(2,1)}, bf16[28,128,1024]{2,1,0:T(8,128)(2,1)}) custom-call(s32[42]{0:T(128)S(1)} %reshape.131.marks_ref, f32[1,1024]{1,0:T(1,128)S(1)} %pad_maximum_fusion.gain_ref, bf16[4,128,256]{2,1,0:T(8,128)(2,1)S(1)} %pack.12.refs_0_, ...), custom_call_target="tpu_custom_call", output_to_operand_aliasing={{0}: (14, {}), {1}: (15, {})} | custom-call | flops 1 | bytes 1 | tf_op jit(solution)/shard_map/project/pallas_call | solution.py:78
  108.8 10.6 %attend.1 = bf16[768,1024]{1,0:T(8,128)(2,1)} custom-call(s32[24]{0:T(128)} %get-tuple-element.269.slots, s32[12]{0:T(128)S(1)} %convert_reduce_fusion.counts, bf16[768,1024]{1,0:T(8,128)(2,1)S(1)} %copy-done, bf16[28,128,1024]{2,1,0:T(8,128)(2,1)} %get-tuple-element.270.refs_0_.refs_1_.refs_2_.refs_3_.refs_4_.refs_5_, ...), custom_call_target="tpu_custom_call" | custom-call | flops 1 | bytes 1 | tf_op jit(solution)/shard_map/attend/pallas_call | solution.py:156
  (109 shorter events, 37.4 us)
Async XLA Ops:
  2.2 8.2 %collective-permute-start.9 = (s32[24]{0:T(128)S(1)}, s32[24]{0:T(128)S(1)}, u32[]{:S(2)}, u32[]{:S(2)}) collective-permute-start(s32[24]{0:T(128)S(1)} %reshape.126), channel_id=1, source_target_pairs={{0,4},{4,0},{8,12},{12,8},{1,5},{5,1},{9,13},{13,9},{2,6},{6,2},{1... | collective-permute-start | bytes 296 | tf_op jit(solution)/shard_map/ppermute | solution.py:353
  7.8 16.7 %collective-permute-start.13 = (bf16[8,128,256]{2,1,0:T(8,128)(2,1)S(1)}, bf16[8,128,256]{2,1,0:T(8,128)(2,1)S(1)}, u32[]{:S(2)}, u32[]{:S(2)}) collective-permute-start(bf16[8,128,256]{2,1,0:T(8,128)(2,1)S(1)} %get-tuple-element.164), channel_id=1, source_target_pairs={{0,4},{4,8},{8,12},{12,0},{1,5},{5,9},{9,13},{13,1},{2,6},{6,10},{... | collective-permute-start | bytes 1572872 | tf_op jit(solution)/shard_map/ppermute | solution.py:325
  8.8 29.9 %collective-permute-start.18 = (bf16[8,128,256]{2,1,0:T(8,128)(2,1)S(1)}, bf16[8,128,256]{2,1,0:T(8,128)(2,1)S(1)}, u32[]{:S(2)}, u32[]{:S(2)}) collective-permute-start(bf16[8,128,256]{2,1,0:T(8,128)(2,1)S(1)} %get-tuple-element.168), channel_id=1, source_target_pairs={{0,4},{4,8},{8,12},{12,0},{1,5},{5,9},{9,13},{13,1},{2,6},{6,10},{... | collective-permute-start | bytes 1572872 | tf_op jit(solution)/shard_map/ppermute | solution.py:325
  27.4 10.1 %collective-permute-start.16 = (bf16[4,128,256]{2,1,0:T(8,128)(2,1)S(1)}, bf16[4,128,256]{2,1,0:T(8,128)(2,1)S(1)}, u32[]{:S(2)}, u32[]{:S(2)}) collective-permute-start(bf16[4,128,256]{2,1,0:T(8,128)(2,1)S(1)} %get-tuple-element.180.refs_0_), channel_id=1, source_target_pairs={{0,2},{2,0},{1,3},{3,1},{4,6},{6,4},{5,7},{7,5},{8,10},{10,8},{9,1... | collective-permute-start | bytes 786440 | tf_op jit(solution)/shard_map/ppermute | solution.py:40
  30.4 7.6 %collective-permute-start.19 = (f32[1,256]{1,0:T(1,128)}, f32[1,256]{1,0:T(1,128)S(1)}, u32[]{:S(2)}, u32[]{:S(2)}) collective-permute-start(f32[1,256]{1,0:T(1,128)} %bitcast.41), channel_id=1, source_target_pairs={{0,1},{1,0},{2,3},{3,2},{4,5},{5,4},{6,7},{7,6},{8,9},{9,8},{10,11... | collective-permute-start | bytes 3080 | tf_op jit(solution)/shard_map/ppermute | solution.py:40
  37.5 10.9 %collective-permute-start.14 = (bf16[4,128,256]{2,1,0:T(8,128)(2,1)S(1)}, bf16[4,128,256]{2,1,0:T(8,128)(2,1)S(1)}, u32[]{:S(2)}, u32[]{:S(2)}) collective-permute-start(bf16[4,128,256]{2,1,0:T(8,128)(2,1)S(1)} %get-tuple-element.165), channel_id=1, source_target_pairs={{0,4},{4,8},{8,12},{12,0},{1,5},{5,9},{9,13},{13,1},{2,6},{6,10},{... | collective-permute-start | bytes 786440 | tf_op jit(solution)/shard_map/ppermute | solution.py:325
  37.6 10.9 %collective-permute-start.17 = (bf16[4,128,256]{2,1,0:T(8,128)(2,1)S(1)}, bf16[4,128,256]{2,1,0:T(8,128)(2,1)S(1)}, u32[]{:S(2)}, u32[]{:S(2)}) collective-permute-start(bf16[4,128,256]{2,1,0:T(8,128)(2,1)S(1)} %collective-permute-done.16.refs_2_), channel_id=1, source_target_pairs={{0,1},{1,0},{2,3},{3,2},{4,5},{5,4},{6,7},{7,6},{8,9},{9,8},{10,11... | collective-permute-start | bytes 786440 | tf_op jit(solution)/shard_map/ppermute | solution.py:40
  41.4 11.4 %collective-permute-start.24 = (bf16[4,128,256]{2,1,0:T(8,128)(2,1)S(1)}, bf16[4,128,256]{2,1,0:T(8,128)(2,1)S(1)}, u32[]{:S(2)}, u32[]{:S(2)}) collective-permute-start(bf16[4,128,256]{2,1,0:T(8,128)(2,1)S(1)} %get-tuple-element.197.refs_0_), channel_id=1, source_target_pairs={{0,2},{2,0},{1,3},{3,1},{4,6},{6,4},{5,7},{7,5},{8,10},{10,8},{9,1... | collective-permute-start | bytes 786440 | tf_op jit(solution)/shard_map/ppermute | solution.py:40
  43.2 10.5 %collective-permute-start.22 = (bf16[4,128,256]{2,1,0:T(8,128)(2,1)S(1)}, bf16[4,128,256]{2,1,0:T(8,128)(2,1)S(1)}, u32[]{:S(2)}, u32[]{:S(2)}) collective-permute-start(bf16[4,128,256]{2,1,0:T(8,128)(2,1)S(1)} %get-tuple-element.178), channel_id=1, source_target_pairs={{0,4},{4,8},{8,12},{12,0},{1,5},{5,9},{9,13},{13,1},{2,6},{6,10},{... | collective-permute-start | bytes 786440 | tf_op jit(solution)/shard_map/ppermute | solution.py:325
  51.1 9.4 %collective-permute-start.28 = (bf16[4,128,256]{2,1,0:T(8,128)(2,1)S(1)}, bf16[4,128,256]{2,1,0:T(8,128)(2,1)S(1)}, u32[]{:S(2)}, u32[]{:S(2)}) collective-permute-start(bf16[4,128,256]{2,1,0:T(8,128)(2,1)S(1)} %get-tuple-element.216.refs_0_), channel_id=1, source_target_pairs={{0,2},{2,0},{1,3},{3,1},{4,6},{6,4},{5,7},{7,5},{8,10},{10,8},{9,1... | collective-permute-start | bytes 786440 | tf_op jit(solution)/shard_map/ppermute | solution.py:40
  52.8 8.1 %collective-permute-start.23 = (bf16[4,128,256]{2,1,0:T(8,128)(2,1)S(1)}, bf16[4,128,256]{2,1,0:T(8,128)(2,1)S(1)}, u32[]{:S(2)}, u32[]{:S(2)}) collective-permute-start(bf16[4,128,256]{2,1,0:T(8,128)(2,1)S(1)} %get-tuple-element.197.refs_0_), channel_id=1, source_target_pairs={{0,1},{1,0},{2,3},{3,2},{4,5},{5,4},{6,7},{7,6},{8,9},{9,8},{10,11... | collective-permute-start | bytes 786440 | tf_op jit(solution)/shard_map/ppermute | solution.py:40
  52.8 8.1 %collective-permute-start.25 = (bf16[4,128,256]{2,1,0:T(8,128)(2,1)S(1)}, bf16[4,128,256]{2,1,0:T(8,128)(2,1)S(1)}, u32[]{:S(2)}, u32[]{:S(2)}) collective-permute-start(bf16[4,128,256]{2,1,0:T(8,128)(2,1)S(1)} %collective-permute-done.24.refs_2_), channel_id=1, source_target_pairs={{0,1},{1,0},{2,3},{3,2},{4,5},{5,4},{6,7},{7,6},{8,9},{9,8},{10,11... | collective-permute-start | bytes 786440 | tf_op jit(solution)/shard_map/ppermute | solution.py:40
  53.3 11.1 %collective-permute-start.26 = (bf16[4,128,256]{2,1,0:T(8,128)(2,1)S(1)}, bf16[4,128,256]{2,1,0:T(8,128)(2,1)S(1)}, u32[]{:S(2)}, u32[]{:S(2)}) collective-permute-start(bf16[4,128,256]{2,1,0:T(8,128)(2,1)S(1)} %get-tuple-element.195), channel_id=1, source_target_pairs={{0,4},{4,8},{8,12},{12,0},{1,5},{5,9},{9,13},{13,1},{2,6},{6,10},{... | collective-permute-start | bytes 786440 | tf_op jit(solution)/shard_map/ppermute | solution.py:325
  60.4 8.2 %collective-permute-start.27 = (bf16[4,128,256]{2,1,0:T(8,128)(2,1)S(1)}, bf16[4,128,256]{2,1,0:T(8,128)(2,1)S(1)}, u32[]{:S(2)}, u32[]{:S(2)}) collective-permute-start(bf16[4,128,256]{2,1,0:T(8,128)(2,1)S(1)} %get-tuple-element.216.refs_0_), channel_id=1, source_target_pairs={{0,1},{1,0},{2,3},{3,2},{4,5},{5,4},{6,7},{7,6},{8,9},{9,8},{10,11... | collective-permute-start | bytes 786440 | tf_op jit(solution)/shard_map/ppermute | solution.py:40
  60.4 8.2 %collective-permute-start.29 = (bf16[4,128,256]{2,1,0:T(8,128)(2,1)S(1)}, bf16[4,128,256]{2,1,0:T(8,128)(2,1)S(1)}, u32[]{:S(2)}, u32[]{:S(2)}) collective-permute-start(bf16[4,128,256]{2,1,0:T(8,128)(2,1)S(1)} %collective-permute-done.28.refs_2_), channel_id=1, source_target_pairs={{0,1},{1,0},{2,3},{3,2},{4,5},{5,4},{6,7},{7,6},{8,9},{9,8},{10,11... | collective-permute-start | bytes 786440 | tf_op jit(solution)/shard_map/ppermute | solution.py:40
  63.0 8.3 %collective-permute-start.32 = (bf16[4,128,256]{2,1,0:T(8,128)(2,1)S(1)}, bf16[4,128,256]{2,1,0:T(8,128)(2,1)S(1)}, u32[]{:S(2)}, u32[]{:S(2)}) collective-permute-start(bf16[4,128,256]{2,1,0:T(8,128)(2,1)S(1)} %get-tuple-element.235.refs_0_), channel_id=1, source_target_pairs={{0,2},{2,0},{1,3},{3,1},{4,6},{6,4},{5,7},{7,5},{8,10},{10,8},{9,1... | collective-permute-start | bytes 786440 | tf_op jit(solution)/shard_map/ppermute | solution.py:40
  64.4 9.8 %collective-permute-start.30 = (bf16[4,128,256]{2,1,0:T(8,128)(2,1)S(1)}, bf16[4,128,256]{2,1,0:T(8,128)(2,1)S(1)}, u32[]{:S(2)}, u32[]{:S(2)}) collective-permute-start(bf16[4,128,256]{2,1,0:T(8,128)(2,1)S(1)} %get-tuple-element.214), channel_id=1, source_target_pairs={{0,4},{4,8},{8,12},{12,0},{1,5},{5,9},{9,13},{13,1},{2,6},{6,10},{... | collective-permute-start | bytes 786440 | tf_op jit(solution)/shard_map/ppermute | solution.py:325
  70.5 8.0 %collective-permute-start.36 = (bf16[4,128,256]{2,1,0:T(8,128)(2,1)S(1)}, bf16[4,128,256]{2,1,0:T(8,128)(2,1)S(1)}, u32[]{:S(2)}, u32[]{:S(2)}) collective-permute-start(bf16[4,128,256]{2,1,0:T(8,128)(2,1)S(1)} %get-tuple-element.252.refs_0_), channel_id=1, source_target_pairs={{0,2},{2,0},{1,3},{3,1},{4,6},{6,4},{5,7},{7,5},{8,10},{10,8},{9,1... | collective-permute-start | bytes 786440 | tf_op jit(solution)/shard_map/ppermute | solution.py:40
  71.1 7.4 %collective-permute-start.31 = (bf16[4,128,256]{2,1,0:T(8,128)(2,1)S(1)}, bf16[4,128,256]{2,1,0:T(8,128)(2,1)S(1)}, u32[]{:S(2)}, u32[]{:S(2)}) collective-permute-start(bf16[4,128,256]{2,1,0:T(8,128)(2,1)S(1)} %get-tuple-element.235.refs_0_), channel_id=1, source_target_pairs={{0,1},{1,0},{2,3},{3,2},{4,5},{5,4},{6,7},{7,6},{8,9},{9,8},{10,11... | collective-permute-start | bytes 786440 | tf_op jit(solution)/shard_map/ppermute | solution.py:40
  71.7 10.2 %collective-permute-start.34 = (bf16[4,128,256]{2,1,0:T(8,128)(2,1)S(1)}, bf16[4,128,256]{2,1,0:T(8,128)(2,1)S(1)}, u32[]{:S(2)}, u32[]{:S(2)}) collective-permute-start(bf16[4,128,256]{2,1,0:T(8,128)(2,1)S(1)} %get-tuple-element.233), channel_id=1, source_target_pairs={{0,4},{4,8},{8,12},{12,0},{1,5},{5,9},{9,13},{13,1},{2,6},{6,10},{... | collective-permute-start | bytes 786440 | tf_op jit(solution)/shard_map/ppermute | solution.py:325
  77.2 7.6 %collective-permute-start.35 = (bf16[4,128,256]{2,1,0:T(8,128)(2,1)S(1)}, bf16[4,128,256]{2,1,0:T(8,128)(2,1)S(1)}, u32[]{:S(2)}, u32[]{:S(2)}) collective-permute-start(bf16[4,128,256]{2,1,0:T(8,128)(2,1)S(1)} %get-tuple-element.252.refs_0_), channel_id=1, source_target_pairs={{0,1},{1,0},{2,3},{3,2},{4,5},{5,4},{6,7},{7,6},{8,9},{9,8},{10,11... | collective-permute-start | bytes 786440 | tf_op jit(solution)/shard_map/ppermute | solution.py:40
  80.4 8.8 %collective-permute-start.41 = (bf16[4,128,256]{2,1,0:T(8,128)(2,1)S(1)}, bf16[4,128,256]{2,1,0:T(8,128)(2,1)S(1)}, u32[]{:S(2)}, u32[]{:S(2)}) collective-permute-start(bf16[4,128,256]{2,1,0:T(8,128)(2,1)S(1)} %pack.13.refs_0_), channel_id=1, source_target_pairs={{0,2},{2,0},{1,3},{3,1},{4,6},{6,4},{5,7},{7,5},{8,10},{10,8},{9,1... | collective-permute-start | bytes 786440 | tf_op jit(solution)/shard_map/ppermute | solution.py:40
  81.1 14.1 %collective-permute-start.40 = (bf16[4,128,256]{2,1,0:T(8,128)(2,1)S(1)}, bf16[4,128,256]{2,1,0:T(8,128)(2,1)S(1)}, u32[]{:S(2)}, u32[]{:S(2)}) collective-permute-start(bf16[4,128,256]{2,1,0:T(8,128)(2,1)S(1)} %pack.13.refs_0_), channel_id=1, source_target_pairs={{0,1},{1,0},{2,3},{3,2},{4,5},{5,4},{6,7},{7,6},{8,9},{9,8},{10,11... | collective-permute-start | bytes 786440 | tf_op jit(solution)/shard_map/ppermute | solution.py:40
  91.5 8.2 %collective-permute-start.39 = (bf16[4,128,256]{2,1,0:T(8,128)(2,1)S(1)}, bf16[4,128,256]{2,1,0:T(8,128)(2,1)S(1)}, u32[]{:S(2)}, u32[]{:S(2)}) collective-permute-start(bf16[4,128,256]{2,1,0:T(8,128)(2,1)S(1)} %pack.12.refs_0_), channel_id=1, source_target_pairs={{0,2},{2,0},{1,3},{3,1},{4,6},{6,4},{5,7},{7,5},{8,10},{10,8},{9,1... | collective-permute-start | bytes 786440 | tf_op jit(solution)/shard_map/ppermute | solution.py:40
  (19 other events, 89.5 us)

commit v8 on v7

--- a/solution.py
+++ b/solution.py
@@ -40,55 +40,66 @@
     return lax.ppermute(value, axis, [(0, 1), (1, 0)])
 
 
-def project(marks, gain, pieces, key_weight, value_weight, group, total, number=0, held=()):
-    count, tokens, width = pieces[0].shape
+def project(marks, gain, rounds, key_weight, value_weight, group, total, first=0, held=()):
+    pieces = len(rounds[0])
+    count, tokens, width = rounds[0][0].shape
     columns = key_weight.shape[1]
-    steps = count // group
-    base = number * (len(pieces) + steps)
+    each = count // group
+    rows = group * tokens
+    groups = total // group
 
     def kernel(marks_ref, gain_ref, *refs):
-        parts, key_blocks, value_blocks = [refs[i * len(pieces) : (i + 1) * len(pieces)] for i in range(3)]
-        keys_out, values_out = refs[-2:]
-
-        @pl.when(marks_ref[base + len(pieces) + pl.program_id(0)] > 0)
+        arrays, blocks = refs[: len(rounds) * pieces], refs[len(rounds) * pieces : (len(rounds) + 2) * pieces]
+        outs, normed = refs[-3:-1], refs[-1]
+        step = pl.program_id(0)
+        wanted = marks_ref[pieces + first + step] > 0
+        for number in range(len(rounds)):
+            parts = arrays[number * pieces : (number + 1) * pieces]
+
+            @pl.when(wanted & (step >= number * each) & (step < (number + 1) * each))
+            def _(number=number, parts=parts):
+                at = pl.ds((step - number * each) * group, group)
+                raw = [part[at].reshape(rows, width).astype(jnp.float32) for part in parts]
+                squares = sum(jnp.sum(part * part, axis=1, keepdims=True) for part in raw)
+                scale = lax.rsqrt(squares / DE + EPS)
+                for index, part in enumerate(raw):
+                    place = slice(index * width, (index + 1) * width)
+                    normed[:, place] = (part * scale * gain_ref[:, place]).astype(jnp.bfloat16)
+
+        @pl.when(wanted)
         def _():
-            raw = [part[...].reshape(group * tokens, width).astype(jnp.float32) for part in parts]
-            squares = sum(jnp.sum(part * part, axis=1, keepdims=True) for part in raw)
-            scale = lax.rsqrt(squares / DE + EPS)
-            states = [
-                (part * scale * gain_ref[:, index * width : (index + 1) * width]).astype(jnp.bfloat16)
-                for index, part in enumerate(raw)
-            ]
-            for blocks, out in ((key_blocks, keys_out), (value_blocks, values_out)):
+            for out, weight in zip(outs, (blocks[:pieces], blocks[pieces:])):
                 product = sum(
-                    jnp.dot(state, block[...], preferred_element_type=jnp.float32)
-                    for state, block in zip(states, blocks)
+                    jnp.dot(
+                        normed[:, index * width : (index + 1) * width], block[...], preferred_element_type=jnp.float32
+                    )
+                    for index, block in enumerate(weight)
                 )
                 out[...] = product.astype(jnp.bfloat16).reshape(out.shape)
 
+    def weight_spec(piece):
+        return pl.BlockSpec((width, columns), lambda i, marks: (marks[piece], 0))
+
+    weight_specs = [weight_spec(piece) for piece in range(pieces)]
     out = jax.ShapeDtypeStruct((total, tokens, columns), jnp.bfloat16)
-    piece_spec = pl.BlockSpec((group, tokens, width), lambda i, _: (i, 0, 0))
-
-    def weight_spec(piece):
-        return pl.BlockSpec((width, columns), lambda i, marks: (marks[base + piece], 0))
-
-    weight_specs = [weight_spec(piece) for piece in range(len(pieces))]
-    out_spec = pl.BlockSpec((group, tokens, columns), lambda i, _: (i + number * steps, 0, 0))
-    operands = (marks, gain, *pieces, *[key_weight] * len(pieces), *[value_weight] * len(pieces), *held)
+    out_spec = pl.BlockSpec((group, tokens, columns), lambda i, marks: (jnp.maximum(marks[pieces + groups + first + i], first), 0, 0))
+    arrays = [piece for parts in rounds for piece in parts]
+    operands = (marks, gain, *arrays, *[key_weight] * pieces, *[value_weight] * pieces, *held)
     return pl.pallas_call(
         kernel,
         out_shape=(out, out),
         grid_spec=pltpu.PrefetchScalarGridSpec(
             num_scalar_prefetch=1,
-            grid=(steps,),
+            grid=(len(rounds) * each,),
             in_specs=[pl.BlockSpec((1, DE), lambda i, _: (0, 0))]
-            + [piece_spec] * len(pieces)
+            + [pl.BlockSpec(memory_space=pltpu.VMEM)] * len(arrays)
             + weight_specs * 2
             + [pl.BlockSpec(memory_space=pl.ANY)] * len(held),
             out_specs=(out_spec, out_spec),
+            scratch_shapes=[pltpu.VMEM((rows, DE), jnp.bfloat16)],
         ),
         input_output_aliases={len(operands) - len(held) + i: i for i in range(len(held))},
-        compiler_params=pltpu.CompilerParams(vmem_limit_bytes=VMEM_LIMIT),
+        compiler_params=pltpu.CompilerParams(vmem_limit_bytes=40 * 1024 * 1024),
         cost_estimate=LITTLE,
         name="project",
     )(*operands)
@@ -347,6 +358,10 @@
     return jnp.stack([block ^ i for i in range(4)]).astype(jnp.int32)
 
 
+def every_group(places, groups):
+    return jnp.concatenate([places, jnp.ones((groups,), jnp.int32), jnp.arange(groups, dtype=jnp.int32)])
+
+
 def exchanged_table(codes):
     own_part = [codes]
     for offset in range(1, CHIPS):
@@ -362,9 +377,10 @@
     me = lax.axis_index("parts") * CHIPS + seq
     kept = jnp.arange(KMAX, dtype=jnp.int32)[None, :] < nbr_count[:, None]
     codes = jnp.where(kept, nbr_owner * ENTRIES_EACH + nbr_slot, -1).reshape(-1)
-    first, second, codes = lax.optimization_barrier((store[:HALF], store[HALF:], codes))
+    first, second, codes, enc_gain = lax.optimization_barrier((store[:HALF], store[HALF:], codes, enc_gain))
     table = exchanged_table(codes)
     flights = [onward(first), onward(second)]
+    gain = jnp.concatenate(four_pieces(enc_gain[None]), axis=1)
     plan = make_plan(me.reshape(1).astype(jnp.int32), table.reshape(-1)).reshape(-1)
     missing = plan[3 * LANES]
 
@@ -377,42 +393,38 @@
     asked = jnp.stack([first, jnp.where(asked[:, 1] >= 0, asked[:, 1], first)], axis=1).reshape(-1)
 
     places = places_of_pieces()
-    wanted = plan[LANES : LANES + SWEEPS * CAP].reshape(SWEEPS, CAP)[:, ::GROUP] >= 0
-    marks = jnp.concatenate([jnp.broadcast_to(places, (SWEEPS, 4)), wanted.astype(jnp.int32)], axis=1).reshape(-1)
+    room = SWEEPS * CAP
+    wanted = plan[LANES : LANES + room].reshape(room // GROUP, GROUP)[:, 0] >= 0
+    group = jnp.arange(room // GROUP, dtype=jnp.int32)
+    latest = jnp.max(jnp.where((group[None, :] <= group[:, None]) & wanted[None, :], group[None, :], 0), axis=1)
+    marks = jnp.concatenate([places, wanted.astype(jnp.int32), latest])
     slots = plan[2 * LANES : 3 * LANES][asked]
 
-    room = SWEEPS * CAP
-    held, pieces, gain = (), [], None
-
-    def projected(number):
-        return project(marks, gain, pieces[number], key_weight, value_weight, GROUP, room, number, held)
-
+    pieces = []
     for number in range(SWEEPS):
         *ways, mine = pack(plan, number, [store] + flights[: number + 1])
         flights += [onward(way) for way in ways]
         pieces.append([mine, swapped(mine, "rep"), swapped(mine, "mp")])
-        if number == 0:
-            enc_gain, pieces[0][1] = lax.optimization_barrier((enc_gain, pieces[0][1]))
-            gain = jnp.concatenate(four_pieces(enc_gain[None]), axis=1)
-        if number > 1:
-            if number + 1 < SWEEPS:
-                pieces[number - 2], flights[number + 1] = lax.optimization_barrier((pieces[number - 2], flights[number + 1]))
-            held = projected(number - 2)
         if number > 0:
             pieces[number - 1].append(swapped(pieces[number - 1][2], "rep"))
         if number + 1 < SWEEPS:
-            flights[number + 1], pieces[: number], held, gain, slots, marks = lax.optimization_barrier(
-                (flights[number + 1], pieces[: number], held, gain, slots, marks)
+            across = [parts[2] for parts in pieces[:number]]
+            flights[number + 1], across, pieces[number][1], gain, slots, marks = lax.optimization_barrier(
+                (flights[number + 1], across, pieces[number][1], gain, slots, marks)
             )
-    held = projected(SWEEPS - 2)
+            for parts, arrived in zip(pieces, across):
+                parts[2] = arrived
+    pieces[:-1], _ = lax.optimization_barrier((pieces[:-1], mine))
+    held = project(marks, gain, pieces[:-1], key_weight, value_weight, GROUP, room)
     pieces[-1], held = lax.optimization_barrier((pieces[-1], held))
     pieces[-1].append(swapped(pieces[-1][2], "rep"))
-    keys, values = projected(SWEEPS - 1)
+    done = (SWEEPS - 1) * CAP // GROUP
+    keys, values = project(marks, gain, pieces[-1:], key_weight, value_weight, GROUP, room, done, held)
 
     def whole(state):
         mine = fetch_all(store, asked >> 4, asked & (ENTRIES_EACH - 1))
-        whole_marks = jnp.concatenate([places, jnp.ones((total // 4,), jnp.int32)])
-        keys, values = project(whole_marks, gain, four_pieces(mine), key_weight, value_weight, 4, room)
+        marks = every_group(places, room // 4)
+        keys, values = project(marks, gain, [four_pieces(mine)], key_weight, value_weight, 4, room)
         return jnp.zeros_like(state[0]), jnp.arange(total, dtype=jnp.int32), keys, values
 
     state = lax.while_loop(lambda state: state[0] > 0, whole, (missing, slots, keys, values))
@@ -424,8 +436,8 @@
     owners, slots, counts = previous_rows(nbr_owner, nbr_slot, nbr_count)
     total = owners.size
     pieces = [fetch_by_request(store, owners, slots)]
-    marks = jnp.concatenate([jnp.zeros((1,), jnp.int32), jnp.ones((total // 4,), jnp.int32)])
-    keys, values = project(marks, gain, pieces, key_weight, value_weight, 4, total)
+    marks = every_group(jnp.zeros((1,), jnp.int32), total // 4)
+    keys, values = project(marks, gain, [pieces], key_weight, value_weight, 4, total)
     return attend(jnp.arange(total, dtype=jnp.int32), counts, queries, keys, values)
 
 

time: 122 us -> 115 us (0.943); the launches traced: 119 us -> 115 us
  Pallas kernels: 53.5 us -> 45.2 us
  waiting for transfers between devices: 29.2 us -> 36.2 us
  starting transfers between devices: 23.4 us -> 20.3 us
    ppermute x7, waiting for transfers between devices: 10.1 us -> 25.8 us  [onward(): lax.ppermute(value, 'seq', [(chip, (chip + 1) % size) for chip in range(s...]
    pallas_call x7 -> x2, Pallas kernels: 26.9 us -> 18.7 us  [project(): pl.pallas_call(kernel, out_shape=(out, out), grid_spec=pltpu.PrefetchScal...]
    ppermute x25, waiting for transfers between devices: 16.2 us -> 9.48 us  [swapped(): return lax.ppermute(value, axis, [(0, 1), (1, 0)])]
    ppermute x3, waiting for transfers between devices: 2.85 us -> 0.92 us  [exchanged_table(): lax.ppermute(codes, 'seq', [(chip, chip ^ offset) for chip in range(CHIPS)])]
    ppermute x7, starting transfers between devices: 3.52 us -> 1.81 us  [onward(): lax.ppermute(value, 'seq', [(chip, (chip + 1) % size) for chip in range(s...]
    ppermute x25, starting transfers between devices: 14.2 us -> 12.7 us  [swapped(): return lax.ppermute(value, axis, [(0, 1), (1, 0)])]
  transfers between devices with their start and end apart: 35 -> 35, of which waited for: 13 -> 12; matrix products, arithmetic and copies ran while one was open for 5% -> 5% of each run, Pallas kernels for 32% -> 27%
where the time goes in v8:
time: 115 us
  Pallas kernels  45.2 us (39%)
  waiting for transfers between devices  36.2 us (31%)
  starting transfers between devices  20.3 us (18%)
  local copies, waits for them, and re-layouts  10 us (9%)
  other arithmetic  2.14 us (2%)
    ppermute x7, waiting for transfers between devices, onward(): lax.ppermute(value, 'seq', [(chip, (chip + 1) % size) for chip in range(s...  25.8 us
    pallas_call x2, Pallas kernels, project(): pl.pallas_call(kernel, out_shape=(out, out), grid_spec=pltpu.PrefetchScal...  18.7 us
    pallas_call x7, Pallas kernels, pack(): pl.pallas_call(kernel, out_shape=(jax.ShapeDtypeStruct((CAP,) + pool[0].s...  13.5 us
    ppermute x25, starting transfers between devices, swapped(): return lax.ppermute(value, axis, [(0, 1), (1, 0)])  12.7 us
    pallas_call x1, Pallas kernels, attend(): pl.pallas_call(attend_kernel, out_shape=jax.ShapeDtypeStruct(queries.shap...  10.5 us
    ppermute x25, waiting for transfers between devices, swapped(): return lax.ppermute(value, axis, [(0, 1), (1, 0)])  9.48 us
    ppermute x3, starting transfers between devices, exchanged_table(): lax.ppermute(codes, 'seq', [(chip, chip ^ offset) for chip in range(CHIPS)])  5.76 us
    unnamed x16, local copies, waits for them, and re-layouts  4.16 us
  transfers between devices with their start and end apart: 35, of which 12 were waited for; matrix products, arithmetic and copies ran while one was open for 5% of the time, Pallas kernels for 27%

profile of v8, /device:TPU:0, one launch (start us, length us, event | category | flops | bytes accessed | tf_op | source)
XLA Modules:
  0.0 114.8 jit_solution(4123918123750049155)
XLA Ops:
  2.2 5.1 %collective-permute-start.11 = (s32[24]{0:T(128)S(1)}, s32[24]{0:T(128)S(1)}, u32[]{:S(2)}, u32[]{:S(2)}) collective-permute-start(s32[24]{0:T(128)S(1)} %reshape.130), channel_id=1, source_target_pairs={{0,12},{4,8},{8,4},{12,0},{1,13},{5,9},{9,5},{13,1},{2,14},{6,10},... | collective-permute-start | bytes 296 | tf_op jit(solution)/shard_map/ppermute | solution.py:368
  7.9 1.6 %collective-permute-start.17 = (f32[1,256]{1,0:T(1,128)}, f32[1,256]{1,0:T(1,128)S(1)}, u32[]{:S(2)}, u32[]{:S(2)}) collective-permute-start(f32[1,256]{1,0:T(1,128)} %bitcast.40), channel_id=1, source_target_pairs={{0,2},{2,0},{1,3},{3,1},{4,6},{6,4},{5,7},{7,5},{8,10},{10,8},{9,1... | collective-permute-start | bytes 3080 | tf_op jit(solution)/shard_map/ppermute | solution.py:40
  11.7 1.6 %collective-permute-start.12 = (s32[4,24]{1,0:T(4,128)S(1)}, s32[4,24]{1,0:T(4,128)S(1)}, u32[]{:S(2)}, u32[]{:S(2)}) collective-permute-start(s32[4,24]{1,0:T(4,128)S(1)} %pad_add_fusion.2), channel_id=1, source_target_pairs={{0,16},{16,0},{1,17},{17,1},{2,18},{18,2},{3,19},{19,3},{4,20},{20... | collective-permute-start | bytes 1160 | tf_op jit(solution)/shard_map/ppermute | solution.py:40
  13.9 1.5 %collective-permute-done.12 = s32[4,24]{1,0:T(4,128)S(1)} collective-permute-done((s32[4,24]{1,0:T(4,128)S(1)}, s32[4,24]{1,0:T(4,128)S(1)}, u32[]{:S(2)}, u32[]{:S(2)}) %collective-permute-start.12) | collective-permute-done | bytes 416 | tf_op jit(solution)/shard_map/ppermute | solution.py:40
  16.6 2.5 %plan.1 = s32[8,128]{1,0:T(8,128)} custom-call(s32[1]{0:T(128)} %bitcast.2.place, s32[192]{0:T(256)} %reshape.131.table), custom_call_target="tpu_custom_call" | custom-call | tf_op jit(solution)/shard_map/plan/pallas_call | solution.py:272
  20.9 5.2 %collective-permute-done.13.refs_1_ = bf16[8,128,256]{2,1,0:T(8,128)(2,1)S(1)} collective-permute-done((bf16[8,128,256]{2,1,0:T(8,128)(2,1)S(1)}, bf16[8,128,256]{2,1,0:T(8,128)(2,1)S(1)}, u32[]{:S(2)}, u32[]{:S(2)}) %collective-permute-start.13) | collective-permute-done | bytes 524320 | tf_op jit(solution)/shard_map/ppermute | solution.py:336
  26.8 1.9 %pack.7 = (bf16[4,128,256]{2,1,0:T(8,128)(2,1)S(1)}, bf16[4,128,256]{2,1,0:T(8,128)(2,1)S(1)}) custom-call(s32[1024]{0:T(1024)S(1)} %bitcast.23, bf16[16,128,256]{2,1,0:T(8,128)(2,1)} %refs_0_.13, bf16[8,128,256]{2,1,0:T(8,128)(2,1)S(1)} %collective-permute-done.13.refs_1_), custom_call_target="tpu_custom_call" | custom-call | flops 1 | bytes 1 | tf_op jit(solution)/shard_map/pack/pallas_call | solution.py:300
  32.5 4.8 %collective-permute-done.14.refs_2_ = bf16[8,128,256]{2,1,0:T(8,128)(2,1)S(1)} collective-permute-done((bf16[8,128,256]{2,1,0:T(8,128)(2,1)S(1)}, bf16[8,128,256]{2,1,0:T(8,128)(2,1)S(1)}, u32[]{:S(2)}, u32[]{:S(2)}) %collective-permute-start.14) | collective-permute-done | bytes 524320 | tf_op jit(solution)/shard_map/ppermute | solution.py:336
  38.0 2.0 %pack.8 = (bf16[4,128,256]{2,1,0:T(8,128)(2,1)S(1)}, bf16[4,128,256]{2,1,0:T(8,128)(2,1)S(1)}) custom-call(s32[1024]{0:T(1024)S(1)} %bitcast.24, bf16[16,128,256]{2,1,0:T(8,128)(2,1)} %refs_0_.13, bf16[8,128,256]{2,1,0:T(8,128)(2,1)S(1)} %collective-permute-done.13.refs_1_, bf16[8,128,256]{2,1,0:T(8,128)(2,1)S(1)} %collective-permute-done.14.refs_2_), custom_call_target="tpu_custom_call" | custom-call | flops 1 | bytes 1 | tf_op jit(solution)/shard_map/pack/pallas_call | solution.py:300
  40.4 2.2 %collective-permute-done.19.refs_3_ = bf16[4,128,256]{2,1,0:T(8,128)(2,1)S(1)} collective-permute-done((bf16[4,128,256]{2,1,0:T(8,128)(2,1)S(1)}, bf16[4,128,256]{2,1,0:T(8,128)(2,1)S(1)}, u32[]{:S(2)}, u32[]{:S(2)}) %collective-permute-start.19) | collective-permute-done | bytes 262176 | tf_op jit(solution)/shard_map/ppermute | solution.py:336
  43.3 2.0 %pack.9 = (bf16[4,128,256]{2,1,0:T(8,128)(2,1)S(1)}, bf16[4,128,256]{2,1,0:T(8,128)(2,1)S(1)}) custom-call(s32[1024]{0:T(1024)S(1)} %bitcast.25, bf16[16,128,256]{2,1,0:T(8,128)(2,1)} %refs_0_.13, bf16[8,128,256]{2,1,0:T(8,128)(2,1)S(1)} %collective-permute-done.13.refs_1_, bf16[8,128,256]{2,1,0:T(8,128)(2,1)S(1)} %collective-permute-done.14.refs_2_, ...), custom_call_target="tpu_custom_call" | custom-call | flops 1 | bytes 1 | tf_op jit(solution)/shard_map/pack/pallas_call | solution.py:300
  46.1 4.5 %collective-permute-done.22.refs_4_ = bf16[4,128,256]{2,1,0:T(8,128)(2,1)S(1)} collective-permute-done((bf16[4,128,256]{2,1,0:T(8,128)(2,1)S(1)}, bf16[4,128,256]{2,1,0:T(8,128)(2,1)S(1)}, u32[]{:S(2)}, u32[]{:S(2)}) %collective-permute-start.22) | collective-permute-done | bytes 262176 | tf_op jit(solution)/shard_map/ppermute | solution.py:336
  51.3 2.0 %pack.10 = (bf16[4,128,256]{2,1,0:T(8,128)(2,1)S(1)}, bf16[4,128,256]{2,1,0:T(8,128)(2,1)S(1)}) custom-call(s32[1024]{0:T(1024)S(1)} %bitcast.26, bf16[16,128,256]{2,1,0:T(8,128)(2,1)} %refs_0_.13, bf16[8,128,256]{2,1,0:T(8,128)(2,1)S(1)} %collective-permute-done.13.refs_1_, bf16[8,128,256]{2,1,0:T(8,128)(2,1)S(1)} %collective-permute-done.14.refs_2_, ...), custom_call_target="tpu_custom_call" | custom-call | flops 1 | bytes 1 | tf_op jit(solution)/shard_map/pack/pallas_call | solution.py:300
  53.4 2.0 %collective-permute-start.30 = (bf16[4,128,256]{2,1,0:T(8,128)(2,1)S(1)}, bf16[4,128,256]{2,1,0:T(8,128)(2,1)S(1)}, u32[]{:S(2)}, u32[]{:S(2)}) collective-permute-start(bf16[4,128,256]{2,1,0:T(8,128)(2,1)S(1)} %get-tuple-element.220.refs_12_), channel_id=1, source_target_pairs={{0,2},{2,0},{1,3},{3,1},{4,6},{6,4},{5,7},{7,5},{8,10},{10,8},{9,1... | collective-permute-start | bytes 786440 | tf_op jit(solution)/shard_map/ppermute | solution.py:40
  56.3 1.8 %pack.11 = (bf16[4,128,256]{2,1,0:T(8,128)(2,1)S(1)}, bf16[4,128,256]{2,1,0:T(8,128)(2,1)S(1)}) custom-call(s32[1024]{0:T(1024)S(1)} %bitcast.27, bf16[16,128,256]{2,1,0:T(8,128)(2,1)} %refs_0_.13, bf16[8,128,256]{2,1,0:T(8,128)(2,1)S(1)} %collective-permute-done.13.refs_1_, bf16[8,128,256]{2,1,0:T(8,128)(2,1)S(1)} %collective-permute-done.14.refs_2_, ...), custom_call_target="tpu_custom_call" | custom-call | flops 1 | bytes 1 | tf_op jit(solution)/shard_map/pack/pallas_call | solution.py:300
  58.7 7.7 %collective-permute-done.29.refs_6_ = bf16[4,128,256]{2,1,0:T(8,128)(2,1)S(1)} collective-permute-done((bf16[4,128,256]{2,1,0:T(8,128)(2,1)S(1)}, bf16[4,128,256]{2,1,0:T(8,128)(2,1)S(1)}, u32[]{:S(2)}, u32[]{:S(2)}) %collective-permute-start.29) | collective-permute-done | bytes 262176 | tf_op jit(solution)/shard_map/ppermute | solution.py:336
  66.4 1.8 %pack.12.refs_20_ = bf16[4,128,256]{2,1,0:T(8,128)(2,1)S(1)} custom-call(s32[1024]{0:T(1024)S(1)} %bitcast.28, bf16[16,128,256]{2,1,0:T(8,128)(2,1)} %refs_0_.13, bf16[8,128,256]{2,1,0:T(8,128)(2,1)S(1)} %collective-permute-done.13.refs_1_, bf16[8,128,256]{2,1,0:T(8,128)(2,1)S(1)} %collective-permute-done.14.refs_2_, ...), custom_call_target="tpu_custom_call" | custom-call | flops 1 | bytes 1 | tf_op jit(solution)/shard_map/pack/pallas_call | solution.py:300
  68.3 2.0 %collective-permute-start.41 = (bf16[4,128,256]{2,1,0:T(8,128)(2,1)S(1)}, bf16[4,128,256]{2,1,0:T(8,128)(2,1)S(1)}, u32[]{:S(2)}, u32[]{:S(2)}) collective-permute-start(bf16[4,128,256]{2,1,0:T(8,128)(2,1)S(1)} %pack.12.refs_20_), channel_id=1, source_target_pairs={{0,2},{2,0},{1,3},{3,1},{4,6},{6,4},{5,7},{7,5},{8,10},{10,8},{9,1... | collective-permute-start | bytes 786440 | tf_op jit(solution)/shard_map/ppermute | solution.py:40
  71.2 4.4 %collective-permute-done.32.refs_18_ = bf16[4,128,256]{2,1,0:T(8,128)(2,1)S(1)} collective-permute-done((bf16[4,128,256]{2,1,0:T(8,128)(2,1)S(1)}, bf16[4,128,256]{2,1,0:T(8,128)(2,1)S(1)}, u32[]{:S(2)}, u32[]{:S(2)}) %collective-permute-start.32) | collective-permute-done | bytes 262176 | tf_op jit(solution)/shard_map/ppermute | solution.py:40
  75.6 3.1 %collective-permute-done.41.refs_22_ = bf16[4,128,256]{2,1,0:T(8,128)(2,1)S(1)} collective-permute-done((bf16[4,128,256]{2,1,0:T(8,128)(2,1)S(1)}, bf16[4,128,256]{2,1,0:T(8,128)(2,1)S(1)}, u32[]{:S(2)}, u32[]{:S(2)}) %collective-permute-start.41) | collective-permute-done | bytes 262176 | tf_op jit(solution)/shard_map/ppermute | solution.py:40
  79.3 1.8 %pack.13.refs_0_ = bf16[4,128,256]{2,1,0:T(8,128)(2,1)S(1)} custom-call(s32[1024]{0:T(1024)S(1)} %bitcast.29, bf16[16,128,256]{2,1,0:T(8,128)(2,1)} %refs_0_.13, bf16[8,128,256]{2,1,0:T(8,128)(2,1)S(1)} %collective-permute-done.13.refs_1_, bf16[8,128,256]{2,1,0:T(8,128)(2,1)S(1)} %collective-permute-done.14.refs_2_, ...), custom_call_target="tpu_custom_call" | custom-call | flops 1 | bytes 1 | tf_op jit(solution)/shard_map/pack/pallas_call | solution.py:300
  81.7 14.9 %project.4 = (bf16[28,128,1024]{2,1,0:T(8,128)(2,1)}, bf16[28,128,1024]{2,1,0:T(8,128)(2,1)}) custom-call(s32[32]{0:T(128)S(1)} %concatenate.23.marks_ref, f32[1,1024]{1,0:T(1,128)S(1)} %pad_maximum_fusion.gain_ref, bf16[4,128,256]{2,1,0:T(8,128)(2,1)S(1)} %get-tuple-element.208.refs_0_, bf16[4,128,256]{2,1,0:T(8,128)(2,1)S(1)} %collective-permute-done.15.refs_1_, ...), custom_call_target="tpu_custom_call" | custom-call | flops 1 | bytes 1 | tf_op jit(solution)/shard_map/project/pallas_call | solution.py:88
  98.3 3.8 %project.5 = (bf16[28,128,1024]{2,1,0:T(8,128)(2,1)}, bf16[28,128,1024]{2,1,0:T(8,128)(2,1)}) custom-call(s32[32]{0:T(128)S(1)} %concatenate.23.marks_ref, f32[1,1024]{1,0:T(1,128)S(1)} %pad_maximum_fusion.gain_ref, bf16[4,128,256]{2,1,0:T(8,128)(2,1)S(1)} %pack.13.refs_0_, ...), custom_call_target="tpu_custom_call", output_to_operand_aliasing={{0}: (14, {}), {1}: (15, {})} | custom-call | flops 1 | bytes 1 | tf_op jit(solution)/shard_map/project/pallas_call | solution.py:88
  104.3 10.5 %attend.1 = bf16[768,1024]{1,0:T(8,128)(2,1)} custom-call(s32[24]{0:T(128)} %get-tuple-element.241.slots, s32[12]{0:T(128)S(1)} %convert_reduce_fusion.counts, bf16[768,1024]{1,0:T(8,128)(2,1)S(1)} %copy-done, bf16[28,128,1024]{2,1,0:T(8,128)(2,1)} %get-tuple-element.242.refs_0_.refs_1_.refs_2_.refs_3_.refs_4_.refs_5_, ...), custom_call_target="tpu_custom_call" | custom-call | flops 1 | bytes 1 | tf_op jit(solution)/shard_map/attend/pallas_call | solution.py:167
  (102 shorter events, 23.6 us)
Async XLA Ops:
  2.2 7.4 %collective-permute-start.11 = (s32[24]{0:T(128)S(1)}, s32[24]{0:T(128)S(1)}, u32[]{:S(2)}, u32[]{:S(2)}) collective-permute-start(s32[24]{0:T(128)S(1)} %reshape.130), channel_id=1, source_target_pairs={{0,12},{4,8},{8,4},{12,0},{1,13},{5,9},{9,5},{13,1},{2,14},{6,10},... | collective-permute-start | bytes 296 | tf_op jit(solution)/shard_map/ppermute | solution.py:368
  7.9 21.0 %collective-permute-start.17 = (f32[1,256]{1,0:T(1,128)}, f32[1,256]{1,0:T(1,128)S(1)}, u32[]{:S(2)}, u32[]{:S(2)}) collective-permute-start(f32[1,256]{1,0:T(1,128)} %bitcast.40), channel_id=1, source_target_pairs={{0,2},{2,0},{1,3},{3,1},{4,6},{6,4},{5,7},{7,5},{8,10},{10,8},{9,1... | collective-permute-start | bytes 3080 | tf_op jit(solution)/shard_map/ppermute | solution.py:40
  9.6 21.2 %collective-permute-start.16 = (f32[1,256]{1,0:T(1,128)}, f32[1,256]{1,0:T(1,128)S(1)}, u32[]{:S(2)}, u32[]{:S(2)}) collective-permute-start(f32[1,256]{1,0:T(1,128)} %bitcast.41), channel_id=1, source_target_pairs={{0,1},{1,0},{2,3},{3,2},{4,5},{5,4},{6,7},{7,6},{8,9},{9,8},{10,11... | collective-permute-start | bytes 3080 | tf_op jit(solution)/shard_map/ppermute | solution.py:40
  9.6 16.5 %collective-permute-start.13 = (bf16[8,128,256]{2,1,0:T(8,128)(2,1)S(1)}, bf16[8,128,256]{2,1,0:T(8,128)(2,1)S(1)}, u32[]{:S(2)}, u32[]{:S(2)}) collective-permute-start(bf16[8,128,256]{2,1,0:T(8,128)(2,1)S(1)} %get-tuple-element.150), channel_id=1, source_target_pairs={{0,4},{4,8},{8,12},{12,0},{1,5},{5,9},{9,13},{13,1},{2,6},{6,10},{... | collective-permute-start | bytes 1572872 | tf_op jit(solution)/shard_map/ppermute | solution.py:336
  13.3 24.0 %collective-permute-start.14 = (bf16[8,128,256]{2,1,0:T(8,128)(2,1)S(1)}, bf16[8,128,256]{2,1,0:T(8,128)(2,1)S(1)}, u32[]{:S(2)}, u32[]{:S(2)}) collective-permute-start(bf16[8,128,256]{2,1,0:T(8,128)(2,1)S(1)} %get-tuple-element.151), channel_id=1, source_target_pairs={{0,4},{4,8},{8,12},{12,0},{1,5},{5,9},{9,13},{13,1},{2,6},{6,10},{... | collective-permute-start | bytes 1572872 | tf_op jit(solution)/shard_map/ppermute | solution.py:336
  28.7 8.6 %collective-permute-start.15 = (bf16[4,128,256]{2,1,0:T(8,128)(2,1)S(1)}, bf16[4,128,256]{2,1,0:T(8,128)(2,1)S(1)}, u32[]{:S(2)}, u32[]{:S(2)}) collective-permute-start(bf16[4,128,256]{2,1,0:T(8,128)(2,1)S(1)} %get-tuple-element.208.refs_0_), channel_id=1, source_target_pairs={{0,1},{1,0},{2,3},{3,2},{4,5},{5,4},{6,7},{7,6},{8,9},{9,8},{10,11... | collective-permute-start | bytes 786440 | tf_op jit(solution)/shard_map/ppermute | solution.py:40
  31.5 11.1 %collective-permute-start.20 = (bf16[4,128,256]{2,1,0:T(8,128)(2,1)S(1)}, bf16[4,128,256]{2,1,0:T(8,128)(2,1)S(1)}, u32[]{:S(2)}, u32[]{:S(2)}) collective-permute-start(bf16[4,128,256]{2,1,0:T(8,128)(2,1)S(1)} %get-tuple-element.208.refs_0_), channel_id=1, source_target_pairs={{0,2},{2,0},{1,3},{3,1},{4,6},{6,4},{5,7},{7,5},{8,10},{10,8},{9,1... | collective-permute-start | bytes 786440 | tf_op jit(solution)/shard_map/ppermute | solution.py:40
  32.5 10.1 %collective-permute-start.19 = (bf16[4,128,256]{2,1,0:T(8,128)(2,1)S(1)}, bf16[4,128,256]{2,1,0:T(8,128)(2,1)S(1)}, u32[]{:S(2)}, u32[]{:S(2)}) collective-permute-start(bf16[4,128,256]{2,1,0:T(8,128)(2,1)S(1)} %get-tuple-element.155), channel_id=1, source_target_pairs={{0,4},{4,8},{8,12},{12,0},{1,5},{5,9},{9,13},{13,1},{2,6},{6,10},{... | collective-permute-start | bytes 786440 | tf_op jit(solution)/shard_map/ppermute | solution.py:336
  40.1 10.5 %collective-permute-start.23 = (bf16[4,128,256]{2,1,0:T(8,128)(2,1)S(1)}, bf16[4,128,256]{2,1,0:T(8,128)(2,1)S(1)}, u32[]{:S(2)}, u32[]{:S(2)}) collective-permute-start(bf16[4,128,256]{2,1,0:T(8,128)(2,1)S(1)} %get-tuple-element.212.refs_4_), channel_id=1, source_target_pairs={{0,2},{2,0},{1,3},{3,1},{4,6},{6,4},{5,7},{7,5},{8,10},{10,8},{9,1... | collective-permute-start | bytes 786440 | tf_op jit(solution)/shard_map/ppermute | solution.py:40
  40.4 10.2 %collective-permute-start.22 = (bf16[4,128,256]{2,1,0:T(8,128)(2,1)S(1)}, bf16[4,128,256]{2,1,0:T(8,128)(2,1)S(1)}, u32[]{:S(2)}, u32[]{:S(2)}) collective-permute-start(bf16[4,128,256]{2,1,0:T(8,128)(2,1)S(1)} %get-tuple-element.161), channel_id=1, source_target_pairs={{0,4},{4,8},{8,12},{12,0},{1,5},{5,9},{9,13},{13,1},{2,6},{6,10},{... | collective-permute-start | bytes 786440 | tf_op jit(solution)/shard_map/ppermute | solution.py:336
  45.4 10.9 %collective-permute-start.26 = (bf16[4,128,256]{2,1,0:T(8,128)(2,1)S(1)}, bf16[4,128,256]{2,1,0:T(8,128)(2,1)S(1)}, u32[]{:S(2)}, u32[]{:S(2)}) collective-permute-start(bf16[4,128,256]{2,1,0:T(8,128)(2,1)S(1)} %get-tuple-element.216.refs_8_), channel_id=1, source_target_pairs={{0,2},{2,0},{1,3},{3,1},{4,6},{6,4},{5,7},{7,5},{8,10},{10,8},{9,1... | collective-permute-start | bytes 786440 | tf_op jit(solution)/shard_map/ppermute | solution.py:40
  46.1 10.2 %collective-permute-start.25 = (bf16[4,128,256]{2,1,0:T(8,128)(2,1)S(1)}, bf16[4,128,256]{2,1,0:T(8,128)(2,1)S(1)}, u32[]{:S(2)}, u32[]{:S(2)}) collective-permute-start(bf16[4,128,256]{2,1,0:T(8,128)(2,1)S(1)} %get-tuple-element.168), channel_id=1, source_target_pairs={{0,4},{4,8},{8,12},{12,0},{1,5},{5,9},{9,13},{13,1},{2,6},{6,10},{... | collective-permute-start | bytes 786440 | tf_op jit(solution)/shard_map/ppermute | solution.py:336
  53.4 13.0 %collective-permute-start.30 = (bf16[4,128,256]{2,1,0:T(8,128)(2,1)S(1)}, bf16[4,128,256]{2,1,0:T(8,128)(2,1)S(1)}, u32[]{:S(2)}, u32[]{:S(2)}) collective-permute-start(bf16[4,128,256]{2,1,0:T(8,128)(2,1)S(1)} %get-tuple-element.220.refs_12_), channel_id=1, source_target_pairs={{0,2},{2,0},{1,3},{3,1},{4,6},{6,4},{5,7},{7,5},{8,10},{10,8},{9,1... | collective-permute-start | bytes 786440 | tf_op jit(solution)/shard_map/ppermute | solution.py:40
  55.4 10.9 %collective-permute-start.29 = (bf16[4,128,256]{2,1,0:T(8,128)(2,1)S(1)}, bf16[4,128,256]{2,1,0:T(8,128)(2,1)S(1)}, u32[]{:S(2)}, u32[]{:S(2)}) collective-permute-start(bf16[4,128,256]{2,1,0:T(8,128)(2,1)S(1)} %get-tuple-element.177), channel_id=1, source_target_pairs={{0,4},{4,8},{8,12},{12,0},{1,5},{5,9},{9,13},{13,1},{2,6},{6,10},{... | collective-permute-start | bytes 786440 | tf_op jit(solution)/shard_map/ppermute | solution.py:336
  58.1 8.3 %collective-permute-start.31 = (bf16[4,128,256]{2,1,0:T(8,128)(2,1)S(1)}, bf16[4,128,256]{2,1,0:T(8,128)(2,1)S(1)}, u32[]{:S(2)}, u32[]{:S(2)}) collective-permute-start(bf16[4,128,256]{2,1,0:T(8,128)(2,1)S(1)} %get-tuple-element.224.refs_16_), channel_id=1, source_target_pairs={{0,1},{1,0},{2,3},{3,2},{4,5},{5,4},{6,7},{7,6},{8,9},{9,8},{10,11... | collective-permute-start | bytes 786440 | tf_op jit(solution)/shard_map/ppermute | solution.py:40
  58.2 12.1 %collective-permute-start.36 = (bf16[4,128,256]{2,1,0:T(8,128)(2,1)S(1)}, bf16[4,128,256]{2,1,0:T(8,128)(2,1)S(1)}, u32[]{:S(2)}, u32[]{:S(2)}) collective-permute-start(bf16[4,128,256]{2,1,0:T(8,128)(2,1)S(1)} %collective-permute-done.20.refs_2_), channel_id=1, source_target_pairs={{0,1},{1,0},{2,3},{3,2},{4,5},{5,4},{6,7},{7,6},{8,9},{9,8},{10,11... | collective-permute-start | bytes 786440 | tf_op jit(solution)/shard_map/ppermute | solution.py:40
  58.7 12.6 %collective-permute-start.28 = (bf16[4,128,256]{2,1,0:T(8,128)(2,1)S(1)}, bf16[4,128,256]{2,1,0:T(8,128)(2,1)S(1)}, u32[]{:S(2)}, u32[]{:S(2)}) collective-permute-start(bf16[4,128,256]{2,1,0:T(8,128)(2,1)S(1)} %get-tuple-element.176), channel_id=1, source_target_pairs={{0,4},{4,8},{8,12},{12,0},{1,5},{5,9},{9,13},{13,1},{2,6},{6,10},{... | collective-permute-start | bytes 786440 | tf_op jit(solution)/shard_map/ppermute | solution.py:336
  66.4 9.2 %collective-permute-start.32 = (bf16[4,128,256]{2,1,0:T(8,128)(2,1)S(1)}, bf16[4,128,256]{2,1,0:T(8,128)(2,1)S(1)}, u32[]{:S(2)}, u32[]{:S(2)}) collective-permute-start(bf16[4,128,256]{2,1,0:T(8,128)(2,1)S(1)} %get-tuple-element.224.refs_16_), channel_id=1, source_target_pairs={{0,2},{2,0},{1,3},{3,1},{4,6},{6,4},{5,7},{7,5},{8,10},{10,8},{9,1... | collective-permute-start | bytes 786440 | tf_op jit(solution)/shard_map/ppermute | solution.py:40
  68.3 10.5 %collective-permute-start.41 = (bf16[4,128,256]{2,1,0:T(8,128)(2,1)S(1)}, bf16[4,128,256]{2,1,0:T(8,128)(2,1)S(1)}, u32[]{:S(2)}, u32[]{:S(2)}) collective-permute-start(bf16[4,128,256]{2,1,0:T(8,128)(2,1)S(1)} %pack.12.refs_20_), channel_id=1, source_target_pairs={{0,2},{2,0},{1,3},{3,1},{4,6},{6,4},{5,7},{7,5},{8,10},{10,8},{9,1... | collective-permute-start | bytes 786440 | tf_op jit(solution)/shard_map/ppermute | solution.py:40
  70.2 8.5 %collective-permute-start.33 = (bf16[4,128,256]{2,1,0:T(8,128)(2,1)S(1)}, bf16[4,128,256]{2,1,0:T(8,128)(2,1)S(1)}, u32[]{:S(2)}, u32[]{:S(2)}) collective-permute-start(bf16[4,128,256]{2,1,0:T(8,128)(2,1)S(1)} %pack.12.refs_20_), channel_id=1, source_target_pairs={{0,1},{1,0},{2,3},{3,2},{4,5},{5,4},{6,7},{7,6},{8,9},{9,8},{10,11... | collective-permute-start | bytes 786440 | tf_op jit(solution)/shard_map/ppermute | solution.py:40
  70.3 10.9 %collective-permute-start.37 = (bf16[4,128,256]{2,1,0:T(8,128)(2,1)S(1)}, bf16[4,128,256]{2,1,0:T(8,128)(2,1)S(1)}, u32[]{:S(2)}, u32[]{:S(2)}) collective-permute-start(bf16[4,128,256]{2,1,0:T(8,128)(2,1)S(1)} %collective-permute-done.23.refs_6_), channel_id=1, source_target_pairs={{0,1},{1,0},{2,3},{3,2},{4,5},{5,4},{6,7},{7,6},{8,9},{9,8},{10,11... | collective-permute-start | bytes 786440 | tf_op jit(solution)/shard_map/ppermute | solution.py:40
  71.2 10.4 %collective-permute-start.38 = (bf16[4,128,256]{2,1,0:T(8,128)(2,1)S(1)}, bf16[4,128,256]{2,1,0:T(8,128)(2,1)S(1)}, u32[]{:S(2)}, u32[]{:S(2)}) collective-permute-start(bf16[4,128,256]{2,1,0:T(8,128)(2,1)S(1)} %collective-permute-done.26.refs_10_), channel_id=1, source_target_pairs={{0,1},{1,0},{2,3},{3,2},{4,5},{5,4},{6,7},{7,6},{8,9},{9,8},{10,11... | collective-permute-start | bytes 786440 | tf_op jit(solution)/shard_map/ppermute | solution.py:40
  81.1 15.5 %collective-permute-start.35 = (bf16[4,128,256]{2,1,0:T(8,128)(2,1)S(1)}, bf16[4,128,256]{2,1,0:T(8,128)(2,1)S(1)}, u32[]{:S(2)}, u32[]{:S(2)}) collective-permute-start(bf16[4,128,256]{2,1,0:T(8,128)(2,1)S(1)} %pack.13.refs_0_), channel_id=1, source_target_pairs={{0,2},{2,0},{1,3},{3,1},{4,6},{6,4},{5,7},{7,5},{8,10},{10,8},{9,1... | collective-permute-start | bytes 786440 | tf_op jit(solution)/shard_map/ppermute | solution.py:40
  81.6 15.0 %collective-permute-start.34 = (bf16[4,128,256]{2,1,0:T(8,128)(2,1)S(1)}, bf16[4,128,256]{2,1,0:T(8,128)(2,1)S(1)}, u32[]{:S(2)}, u32[]{:S(2)}) collective-permute-start(bf16[4,128,256]{2,1,0:T(8,128)(2,1)S(1)} %pack.13.refs_0_), channel_id=1, source_target_pairs={{0,1},{1,0},{2,3},{3,2},{4,5},{5,4},{6,7},{7,6},{8,9},{9,8},{10,11... | collective-permute-start | bytes 786440 | tf_op jit(solution)/shard_map/ppermute | solution.py:40
  (19 other events, 162.0 us)

commit v9 on v8

--- a/solution.py
+++ b/solution.py
@@ -49,9 +49,25 @@
     groups = total // group
 
     def kernel(marks_ref, gain_ref, *refs):
-        arrays, blocks = refs[: len(rounds) * pieces], refs[len(rounds) * pieces : (len(rounds) + 2) * pieces]
-        outs, normed = refs[-3:-1], refs[-1]
+        arrays, weights = refs[: len(rounds) * pieces], refs[len(rounds) * pieces : len(rounds) * pieces + 2]
+        *outs, normed, key_rows, value_rows, sems = refs[-6:]
         step = pl.program_id(0)
+        ordered = (key_rows, value_rows)
+        copies = [
+            pltpu.make_async_copy(
+                weight.at[pl.ds(pl.multiple_of(marks_ref[piece] * width, width), width)],
+                rows_ref.at[pl.ds(piece * width, width)],
+                sems.at[which * pieces + piece],
+            )
+            for which, (weight, rows_ref) in enumerate(zip(weights, ordered))
+            for piece in range(pieces)
+        ]
+
+        @pl.when(step == 0)
+        def _():
+            for copy in copies:
+                copy.start()
+
         wanted = marks_ref[pieces + first + step] > 0
         for number in range(len(rounds)):
             parts = arrays[number * pieces : (number + 1) * pieces]
@@ -66,25 +82,22 @@
                     place = slice(index * width, (index + 1) * width)
                     normed[:, place] = (part * scale * gain_ref[:, place]).astype(jnp.bfloat16)
 
+        @pl.when(step == 0)
+        def _():
+            for copy in copies:
+                copy.wait()
+
         @pl.when(wanted)
         def _():
-            for out, weight in zip(outs, (blocks[:pieces], blocks[pieces:])):
-                product = sum(
-                    jnp.dot(
-                        normed[:, index * width : (index + 1) * width], block[...], preferred_element_type=jnp.float32
-                    )
-                    for index, block in enumerate(weight)
-                )
+            states = normed[...]
+            for out, weight in zip(outs, ordered):
+                product = jnp.dot(states, weight[...], preferred_element_type=jnp.float32)
                 out[...] = product.astype(jnp.bfloat16).reshape(out.shape)
 
-    def weight_spec(piece):
-        return pl.BlockSpec((width, columns), lambda i, marks: (marks[piece], 0))
-
-    weight_specs = [weight_spec(piece) for piece in range(pieces)]
     out = jax.ShapeDtypeStruct((total, tokens, columns), jnp.bfloat16)
     out_spec = pl.BlockSpec((group, tokens, columns), lambda i, marks: (jnp.maximum(marks[pieces + groups + first + i], first), 0, 0))
     arrays = [piece for parts in rounds for piece in parts]
-    operands = (marks, gain, *arrays, *[key_weight] * pieces, *[value_weight] * pieces, *held)
+    operands = (marks, gain, *arrays, key_weight, value_weight, *held)
     return pl.pallas_call(
         kernel,
         out_shape=(out, out),
@@ -93,13 +106,14 @@
             grid=(len(rounds) * each,),
             in_specs=[pl.BlockSpec((1, DE), lambda i, _: (0, 0))]
             + [pl.BlockSpec(memory_space=pltpu.VMEM)] * len(arrays)
-            + weight_specs * 2
-            + [pl.BlockSpec(memory_space=pl.ANY)] * len(held),
+            + [pl.BlockSpec(memory_space=pl.ANY)] * (2 + len(held)),
             out_specs=(out_spec, out_spec),
-            scratch_shapes=[pltpu.VMEM((rows, DE), jnp.bfloat16)],
+            scratch_shapes=[pltpu.VMEM((rows, DE), jnp.bfloat16)]
+            + [pltpu.VMEM((DE, columns), jnp.bfloat16)] * 2
+            + [pltpu.SemaphoreType.DMA((2 * pieces,))],
         ),
         input_output_aliases={len(operands) - len(held) + i: i for i in range(len(held))},
-        compiler_params=pltpu.CompilerParams(vmem_limit_bytes=40 * 1024 * 1024),
+        compiler_params=pltpu.CompilerParams(vmem_limit_bytes=VMEM_LIMIT),
         cost_estimate=LITTLE,
         name="project",
     )(*operands)
@@ -400,26 +414,30 @@
     marks = jnp.concatenate([places, wanted.astype(jnp.int32), latest])
     slots = plan[2 * LANES : 3 * LANES][asked]
 
-    pieces = []
+    pieces, held = [], ()
     for number in range(SWEEPS):
         *ways, mine = pack(plan, number, [store] + flights[: number + 1])
         flights += [onward(way) for way in ways]
         pieces.append([mine, swapped(mine, "rep"), swapped(mine, "mp")])
         if number > 0:
             pieces[number - 1].append(swapped(pieces[number - 1][2], "rep"))
+        if number == SWEEPS - 3:
+            ripe, pieces[number - 1][2] = lax.optimization_barrier((pieces[:2], pieces[number - 1][2]))
+            held = project(marks, gain, ripe, key_weight, value_weight, GROUP, room)
         if number + 1 < SWEEPS:
-            across = [parts[2] for parts in pieces[:number]]
-            flights[number + 1], across, pieces[number][1], gain, slots, marks = lax.optimization_barrier(
-                (flights[number + 1], across, pieces[number][1], gain, slots, marks)
+            across = [parts[2] for parts in pieces[:number]] if number + 2 < SWEEPS else []
+            came = slice(number + 1, number + 2 if number + 3 < SWEEPS else None)
+            flights[came], across, pieces[number][1], gain, slots, marks, held = lax.optimization_barrier(
+                (flights[came], across, pieces[number][1], gain, slots, marks, held)
             )
             for parts, arrived in zip(pieces, across):
                 parts[2] = arrived
-    pieces[:-1], _ = lax.optimization_barrier((pieces[:-1], mine))
-    held = project(marks, gain, pieces[:-1], key_weight, value_weight, GROUP, room)
-    pieces[-1], held = lax.optimization_barrier((pieces[-1], held))
-    pieces[-1].append(swapped(pieces[-1][2], "rep"))
-    done = (SWEEPS - 1) * CAP // GROUP
-    keys, values = project(marks, gain, pieces[-1:], key_weight, value_weight, GROUP, room, done, held)
+    ripe, _ = lax.optimization_barrier((pieces[2:-2], mine))
+    held = project(marks, gain, ripe, key_weight, value_weight, GROUP, room, 2 * CAP // GROUP, held)
+    late, held = lax.optimization_barrier(([parts[:3] for parts in pieces[-2:]], held))
+    late = [[*parts, swapped(parts[2], "rep")] for parts in late]
+    done = (SWEEPS - 2) * CAP // GROUP
+    keys, values = project(marks, gain, late, key_weight, value_weight, GROUP, room, done, held)
 
     def whole(state):
         mine = fetch_all(store, asked >> 4, asked & (ENTRIES_EACH - 1))

time: 115 us -> 112 us (0.974)
  the two profiles are of different devices: /device:TPU:0 before, /device:TPU:5 now
where the time goes in v9:
time: 112 us
  Pallas kernels  46 us (41%)
  waiting for transfers between devices  26.7 us (24%)
  starting transfers between devices  21.2 us (19%)
  local copies, waits for them, and re-layouts  14.8 us (13%)
  other arithmetic  2.15 us (2%)
    ppermute x7, waiting for transfers between devices, onward(): lax.ppermute(value, 'seq', [(chip, (chip + 1) % size) for chip in range(s...  20.9 us
    pallas_call x3, Pallas kernels, project(): pl.pallas_call(kernel, out_shape=(out, out), grid_spec=pltpu.PrefetchScal...  19.9 us
    ppermute x25, starting transfers between devices, swapped(): return lax.ppermute(value, axis, [(0, 1), (1, 0)])  16.6 us
    pallas_call x7, Pallas kernels, pack(): pl.pallas_call(kernel, out_shape=(jax.ShapeDtypeStruct((CAP,) + pool[0].s...  13.6 us
    pallas_call x1, Pallas kernels, attend(): pl.pallas_call(attend_kernel, out_shape=jax.ShapeDtypeStruct(queries.shap...  9.93 us
    unnamed x20, local copies, waits for them, and re-layouts  8.95 us
    ppermute x25, waiting for transfers between devices, swapped(): return lax.ppermute(value, axis, [(0, 1), (1, 0)])  4.99 us
    ppermute x3, starting transfers between devices, exchanged_table(): lax.ppermute(codes, 'seq', [(chip, chip ^ offset) for chip in range(CHIPS)])  3.67 us
  transfers between devices with their start and end apart: 35, of which 12 were waited for; matrix products, arithmetic and copies ran while one was open for 5% of the time, Pallas kernels for 27%

profile of v9, /device:TPU:5, one launch (start us, length us, event | category | flops | bytes accessed | tf_op | source)
XLA Modules:
  0.0 111.9 jit_solution(3269081292778685396)
XLA Ops:
  3.5 2.3 %collective-permute-start.10 = (s32[24]{0:T(128)S(1)}, s32[24]{0:T(128)S(1)}, u32[]{:S(2)}, u32[]{:S(2)}) collective-permute-start(s32[24]{0:T(128)S(1)} %reshape.130), channel_id=1, source_target_pairs={{0,8},{4,12},{8,0},{12,4},{1,9},{5,13},{9,1},{13,5},{2,10},{6,14},... | collective-permute-start | bytes 296 | tf_op jit(solution)/shard_map/ppermute | solution.py:382
  7.0 1.7 %collective-permute-start.16 = (f32[1,256]{1,0:T(1,128)}, f32[1,256]{1,0:T(1,128)S(1)}, u32[]{:S(2)}, u32[]{:S(2)}) collective-permute-start(f32[1,256]{1,0:T(1,128)} %bitcast.41), channel_id=1, source_target_pairs={{0,1},{1,0},{2,3},{3,2},{4,5},{5,4},{6,7},{7,6},{8,9},{9,8},{10,11... | collective-permute-start | bytes 3080 | tf_op jit(solution)/shard_map/ppermute | solution.py:40
  10.8 1.7 %collective-permute-done.12 = s32[4,24]{1,0:T(4,128)S(1)} collective-permute-done((s32[4,24]{1,0:T(4,128)S(1)}, s32[4,24]{1,0:T(4,128)S(1)}, u32[]{:S(2)}, u32[]{:S(2)}) %collective-permute-start.12) | collective-permute-done | bytes 416 | tf_op jit(solution)/shard_map/ppermute | solution.py:40
  13.7 2.5 %plan.1 = s32[8,128]{1,0:T(8,128)} custom-call(s32[1]{0:T(128)} %bitcast.2.place, s32[192]{0:T(256)} %reshape.131.table), custom_call_target="tpu_custom_call" | custom-call | tf_op jit(solution)/shard_map/plan/pallas_call | solution.py:286
  18.0 6.3 %collective-permute-done.13.refs_1_ = bf16[8,128,256]{2,1,0:T(8,128)(2,1)S(1)} collective-permute-done((bf16[8,128,256]{2,1,0:T(8,128)(2,1)S(1)}, bf16[8,128,256]{2,1,0:T(8,128)(2,1)S(1)}, u32[]{:S(2)}, u32[]{:S(2)}) %collective-permute-start.13) | collective-permute-done | bytes 524320 | tf_op jit(solution)/shard_map/ppermute | solution.py:350
  25.0 1.9 %pack.7 = (bf16[4,128,256]{2,1,0:T(8,128)(2,1)S(1)}, bf16[4,128,256]{2,1,0:T(8,128)(2,1)S(1)}) custom-call(s32[1024]{0:T(1024)S(1)} %bitcast.23, bf16[16,128,256]{2,1,0:T(8,128)(2,1)} %refs_0_.13, bf16[8,128,256]{2,1,0:T(8,128)(2,1)S(1)} %collective-permute-done.13.refs_1_), custom_call_target="tpu_custom_call" | custom-call | flops 1 | bytes 1 | tf_op jit(solution)/shard_map/pack/pallas_call | solution.py:314
  30.4 5.1 %collective-permute-done.14.refs_2_ = bf16[8,128,256]{2,1,0:T(8,128)(2,1)S(1)} collective-permute-done((bf16[8,128,256]{2,1,0:T(8,128)(2,1)S(1)}, bf16[8,128,256]{2,1,0:T(8,128)(2,1)S(1)}, u32[]{:S(2)}, u32[]{:S(2)}) %collective-permute-start.14) | collective-permute-done | bytes 524320 | tf_op jit(solution)/shard_map/ppermute | solution.py:350
  36.2 2.0 %pack.8 = (bf16[4,128,256]{2,1,0:T(8,128)(2,1)S(1)}, bf16[4,128,256]{2,1,0:T(8,128)(2,1)S(1)}) custom-call(s32[1024]{0:T(1024)S(1)} %bitcast.24, bf16[16,128,256]{2,1,0:T(8,128)(2,1)} %refs_0_.13, bf16[8,128,256]{2,1,0:T(8,128)(2,1)S(1)} %collective-permute-done.13.refs_1_, bf16[8,128,256]{2,1,0:T(8,128)(2,1)S(1)} %collective-permute-done.14.refs_2_), custom_call_target="tpu_custom_call" | custom-call | flops 1 | bytes 1 | tf_op jit(solution)/shard_map/pack/pallas_call | solution.py:314
  39.3 1.7 %collective-permute-done.19.refs_3_ = bf16[4,128,256]{2,1,0:T(8,128)(2,1)S(1)} collective-permute-done((bf16[4,128,256]{2,1,0:T(8,128)(2,1)S(1)}, bf16[4,128,256]{2,1,0:T(8,128)(2,1)S(1)}, u32[]{:S(2)}, u32[]{:S(2)}) %collective-permute-start.19) | collective-permute-done | bytes 262176 | tf_op jit(solution)/shard_map/ppermute | solution.py:350
  41.7 2.0 %pack.9 = (bf16[4,128,256]{2,1,0:T(8,128)(2,1)S(1)}, bf16[4,128,256]{2,1,0:T(8,128)(2,1)S(1)}) custom-call(s32[1024]{0:T(1024)S(1)} %bitcast.25, bf16[16,128,256]{2,1,0:T(8,128)(2,1)} %refs_0_.13, bf16[8,128,256]{2,1,0:T(8,128)(2,1)S(1)} %collective-permute-done.13.refs_1_, bf16[8,128,256]{2,1,0:T(8,128)(2,1)S(1)} %collective-permute-done.14.refs_2_, ...), custom_call_target="tpu_custom_call" | custom-call | flops 1 | bytes 1 | tf_op jit(solution)/shard_map/pack/pallas_call | solution.py:314
  45.0 3.7 %collective-permute-done.22.refs_4_ = bf16[4,128,256]{2,1,0:T(8,128)(2,1)S(1)} collective-permute-done((bf16[4,128,256]{2,1,0:T(8,128)(2,1)S(1)}, bf16[4,128,256]{2,1,0:T(8,128)(2,1)S(1)}, u32[]{:S(2)}, u32[]{:S(2)}) %collective-permute-start.22) | collective-permute-done | bytes 262176 | tf_op jit(solution)/shard_map/ppermute | solution.py:350
  49.4 2.0 %pack.10 = (bf16[4,128,256]{2,1,0:T(8,128)(2,1)S(1)}, bf16[4,128,256]{2,1,0:T(8,128)(2,1)S(1)}) custom-call(s32[1024]{0:T(1024)S(1)} %bitcast.26, bf16[16,128,256]{2,1,0:T(8,128)(2,1)} %refs_0_.13, bf16[8,128,256]{2,1,0:T(8,128)(2,1)S(1)} %collective-permute-done.13.refs_1_, bf16[8,128,256]{2,1,0:T(8,128)(2,1)S(1)} %collective-permute-done.14.refs_2_, ...), custom_call_target="tpu_custom_call" | custom-call | flops 1 | bytes 1 | tf_op jit(solution)/shard_map/pack/pallas_call | solution.py:314
  56.0 1.9 %pack.11 = (bf16[4,128,256]{2,1,0:T(8,128)(2,1)S(1)}, bf16[4,128,256]{2,1,0:T(8,128)(2,1)S(1)}) custom-call(s32[1024]{0:T(1024)S(1)} %bitcast.27, bf16[16,128,256]{2,1,0:T(8,128)(2,1)} %refs_0_.13, bf16[8,128,256]{2,1,0:T(8,128)(2,1)S(1)} %collective-permute-done.13.refs_1_, bf16[8,128,256]{2,1,0:T(8,128)(2,1)S(1)} %collective-permute-done.14.refs_2_, ...), custom_call_target="tpu_custom_call" | custom-call | flops 1 | bytes 1 | tf_op jit(solution)/shard_map/pack/pallas_call | solution.py:314
  59.4 2.1 %collective-permute-done.32.refs_6_ = bf16[4,128,256]{2,1,0:T(8,128)(2,1)S(1)} collective-permute-done((bf16[4,128,256]{2,1,0:T(8,128)(2,1)S(1)}, bf16[4,128,256]{2,1,0:T(8,128)(2,1)S(1)}, u32[]{:S(2)}, u32[]{:S(2)}) %collective-permute-start.32) | collective-permute-done | bytes 262176 | tf_op jit(solution)/shard_map/ppermute | solution.py:40
  61.4 5.7 %project.5 = (bf16[28,128,1024]{2,1,0:T(8,128)(2,1)S(1)}, bf16[28,128,1024]{2,1,0:T(8,128)(2,1)S(1)}) custom-call(s32[32]{0:T(128)S(1)} %concatenate.23.marks_ref, f32[1,1024]{1,0:T(1,128)S(1)} %pad_maximum_fusion.gain_ref, bf16[4,128,256]{2,1,0:T(8,128)(2,1)S(1)} %get-tuple-element.188.refs_0_, bf16[4,128,256]{2,1,0:T(8,128)(2,1)S(1)} %collective-permute-done.15.refs_1_, ...), custom_call_target="tpu_custom_call" | custom-call | flops 1 | bytes 1 | tf_op jit(solution)/shard_map/project/pallas_call | solution.py:101
  67.2 2.9 %collective-permute-done.29.refs_7_ = bf16[4,128,256]{2,1,0:T(8,128)(2,1)S(1)} collective-permute-done((bf16[4,128,256]{2,1,0:T(8,128)(2,1)S(1)}, bf16[4,128,256]{2,1,0:T(8,128)(2,1)S(1)}, u32[]{:S(2)}, u32[]{:S(2)}) %collective-permute-start.29) | collective-permute-done | bytes 262176 | tf_op jit(solution)/shard_map/ppermute | solution.py:350
  70.1 1.9 %pack.12.refs_0_ = bf16[4,128,256]{2,1,0:T(8,128)(2,1)S(1)} custom-call(s32[1024]{0:T(1024)S(1)} %bitcast.28, bf16[16,128,256]{2,1,0:T(8,128)(2,1)} %refs_0_.13, bf16[8,128,256]{2,1,0:T(8,128)(2,1)S(1)} %collective-permute-done.13.refs_1_, bf16[8,128,256]{2,1,0:T(8,128)(2,1)S(1)} %collective-permute-done.14.refs_2_, ...), custom_call_target="tpu_custom_call" | custom-call | flops 1 | bytes 1 | tf_op jit(solution)/shard_map/pack/pallas_call | solution.py:314
  72.0 2.2 %collective-permute-start.34 = (bf16[4,128,256]{2,1,0:T(8,128)(2,1)S(1)}, bf16[4,128,256]{2,1,0:T(8,128)(2,1)S(1)}, u32[]{:S(2)}, u32[]{:S(2)}) collective-permute-start(bf16[4,128,256]{2,1,0:T(8,128)(2,1)S(1)} %pack.12.refs_0_), channel_id=1, source_target_pairs={{0,1},{1,0},{2,3},{3,2},{4,5},{5,4},{6,7},{7,6},{8,9},{9,8},{10,11... | collective-permute-start | bytes 786440 | tf_op jit(solution)/shard_map/ppermute | solution.py:40
  75.3 1.8 %pack.13.refs_4_ = bf16[4,128,256]{2,1,0:T(8,128)(2,1)S(1)} custom-call(s32[1024]{0:T(1024)S(1)} %bitcast.29, bf16[16,128,256]{2,1,0:T(8,128)(2,1)} %refs_0_.13, bf16[8,128,256]{2,1,0:T(8,128)(2,1)S(1)} %collective-permute-done.13.refs_1_, bf16[8,128,256]{2,1,0:T(8,128)(2,1)S(1)} %collective-permute-done.14.refs_2_, ...), custom_call_target="tpu_custom_call" | custom-call | flops 1 | bytes 1 | tf_op jit(solution)/shard_map/pack/pallas_call | solution.py:314
  78.8 8.9 %project.6 = (bf16[28,128,1024]{2,1,0:T(8,128)(2,1)S(1)}, bf16[28,128,1024]{2,1,0:T(8,128)(2,1)S(1)}) custom-call(s32[32]{0:T(128)S(1)} %concatenate.23.marks_ref, f32[1,1024]{1,0:T(1,128)S(1)} %pad_maximum_fusion.gain_ref, bf16[4,128,256]{2,1,0:T(8,128)(2,1)S(1)} %get-tuple-element.215.refs_0_, ...), custom_call_target="tpu_custom_call", output_to_operand_aliasing={{0}: (16, {}), {1}: (17, {})} | custom-call | flops 1 | bytes 1 | tf_op jit(solution)/shard_map/project/pallas_call | solution.py:101
  87.8 2.8 %copy-done.6 = bf16[28,128,1024]{2,1,0:T(8,128)(2,1)} copy-done((bf16[28,128,1024]{2,1,0:T(8,128)(2,1)}, bf16[28,128,1024]{2,1,0:T(8,128)(2,1)S(1)}, u32[]{:S(2)}) %copy-start.6) | copy-done | bytes 7340056
  90.9 2.0 %copy-done.7 = bf16[28,128,1024]{2,1,0:T(8,128)(2,1)} copy-done((bf16[28,128,1024]{2,1,0:T(8,128)(2,1)}, bf16[28,128,1024]{2,1,0:T(8,128)(2,1)S(1)}, u32[]{:S(2)}) %copy-start.7) | copy-done | bytes 7340056
  94.4 5.3 %project.7 = (bf16[28,128,1024]{2,1,0:T(8,128)(2,1)}, bf16[28,128,1024]{2,1,0:T(8,128)(2,1)}) custom-call(s32[32]{0:T(128)S(1)} %concatenate.23.marks_ref, f32[1,1024]{1,0:T(1,128)S(1)} %pad_maximum_fusion.gain_ref, bf16[4,128,256]{2,1,0:T(8,128)(2,1)S(1)} %pack.12.refs_0_, ...), custom_call_target="tpu_custom_call", output_to_operand_aliasing={{0}: (12, {}), {1}: (13, {})} | custom-call | flops 1 | bytes 1 | tf_op jit(solution)/shard_map/project/pallas_call | solution.py:101
  102.0 9.9 %attend.1 = bf16[768,1024]{1,0:T(8,128)(2,1)} custom-call(s32[24]{0:T(128)} %get-tuple-element.241.slots, s32[12]{0:T(128)S(1)} %convert_reduce_fusion.counts, bf16[768,1024]{1,0:T(8,128)(2,1)S(1)} %copy-done, bf16[28,128,1024]{2,1,0:T(8,128)(2,1)} %get-tuple-element.242.refs_0_.refs_1_.refs_2_.refs_3_.refs_4_.refs_5_, ...), custom_call_target="tpu_custom_call" | custom-call | flops 1 | bytes 1 | tf_op jit(solution)/shard_map/attend/pallas_call | solution.py:181
  (107 shorter events, 31.2 us)
Async XLA Ops:
  2.2 6.6 %collective-permute-start.9 = (s32[24]{0:T(128)S(1)}, s32[24]{0:T(128)S(1)}, u32[]{:S(2)}, u32[]{:S(2)}) collective-permute-start(s32[24]{0:T(128)S(1)} %reshape.130), channel_id=1, source_target_pairs={{0,4},{4,0},{8,12},{12,8},{1,5},{5,1},{9,13},{13,9},{2,6},{6,2},{1... | collective-permute-start | bytes 296 | tf_op jit(solution)/shard_map/ppermute | solution.py:382
  3.5 5.7 %collective-permute-start.10 = (s32[24]{0:T(128)S(1)}, s32[24]{0:T(128)S(1)}, u32[]{:S(2)}, u32[]{:S(2)}) collective-permute-start(s32[24]{0:T(128)S(1)} %reshape.130), channel_id=1, source_target_pairs={{0,8},{4,12},{8,0},{12,4},{1,9},{5,13},{9,1},{13,5},{2,10},{6,14},... | collective-permute-start | bytes 296 | tf_op jit(solution)/shard_map/ppermute | solution.py:382
  5.8 22.2 %collective-permute-start.17 = (f32[1,256]{1,0:T(1,128)}, f32[1,256]{1,0:T(1,128)S(1)}, u32[]{:S(2)}, u32[]{:S(2)}) collective-permute-start(f32[1,256]{1,0:T(1,128)} %bitcast.40), channel_id=1, source_target_pairs={{0,2},{2,0},{1,3},{3,1},{4,6},{6,4},{5,7},{7,5},{8,10},{10,8},{9,1... | collective-permute-start | bytes 3080 | tf_op jit(solution)/shard_map/ppermute | solution.py:40
  7.0 22.4 %collective-permute-start.16 = (f32[1,256]{1,0:T(1,128)}, f32[1,256]{1,0:T(1,128)S(1)}, u32[]{:S(2)}, u32[]{:S(2)}) collective-permute-start(f32[1,256]{1,0:T(1,128)} %bitcast.41), channel_id=1, source_target_pairs={{0,1},{1,0},{2,3},{3,2},{4,5},{5,4},{6,7},{7,6},{8,9},{9,8},{10,11... | collective-permute-start | bytes 3080 | tf_op jit(solution)/shard_map/ppermute | solution.py:40
  8.8 15.5 %collective-permute-start.13 = (bf16[8,128,256]{2,1,0:T(8,128)(2,1)S(1)}, bf16[8,128,256]{2,1,0:T(8,128)(2,1)S(1)}, u32[]{:S(2)}, u32[]{:S(2)}) collective-permute-start(bf16[8,128,256]{2,1,0:T(8,128)(2,1)S(1)} %get-tuple-element.150), channel_id=1, source_target_pairs={{0,4},{4,8},{8,12},{12,0},{1,5},{5,9},{9,13},{13,1},{2,6},{6,10},{... | collective-permute-start | bytes 1572872 | tf_op jit(solution)/shard_map/ppermute | solution.py:350
  10.3 25.2 %collective-permute-start.14 = (bf16[8,128,256]{2,1,0:T(8,128)(2,1)S(1)}, bf16[8,128,256]{2,1,0:T(8,128)(2,1)S(1)}, u32[]{:S(2)}, u32[]{:S(2)}) collective-permute-start(bf16[8,128,256]{2,1,0:T(8,128)(2,1)S(1)} %get-tuple-element.151), channel_id=1, source_target_pairs={{0,4},{4,8},{8,12},{12,0},{1,5},{5,9},{9,13},{13,1},{2,6},{6,10},{... | collective-permute-start | bytes 1572872 | tf_op jit(solution)/shard_map/ppermute | solution.py:350
  26.8 8.7 %collective-permute-start.15 = (bf16[4,128,256]{2,1,0:T(8,128)(2,1)S(1)}, bf16[4,128,256]{2,1,0:T(8,128)(2,1)S(1)}, u32[]{:S(2)}, u32[]{:S(2)}) collective-permute-start(bf16[4,128,256]{2,1,0:T(8,128)(2,1)S(1)} %get-tuple-element.188.refs_0_), channel_id=1, source_target_pairs={{0,1},{1,0},{2,3},{3,2},{4,5},{5,4},{6,7},{7,6},{8,9},{9,8},{10,11... | collective-permute-start | bytes 786440 | tf_op jit(solution)/shard_map/ppermute | solution.py:40
  30.2 9.1 %collective-permute-start.20 = (bf16[4,128,256]{2,1,0:T(8,128)(2,1)S(1)}, bf16[4,128,256]{2,1,0:T(8,128)(2,1)S(1)}, u32[]{:S(2)}, u32[]{:S(2)}) collective-permute-start(bf16[4,128,256]{2,1,0:T(8,128)(2,1)S(1)} %get-tuple-element.188.refs_0_), channel_id=1, source_target_pairs={{0,2},{2,0},{1,3},{3,1},{4,6},{6,4},{5,7},{7,5},{8,10},{10,8},{9,1... | collective-permute-start | bytes 786440 | tf_op jit(solution)/shard_map/ppermute | solution.py:40
  30.4 10.6 %collective-permute-start.19 = (bf16[4,128,256]{2,1,0:T(8,128)(2,1)S(1)}, bf16[4,128,256]{2,1,0:T(8,128)(2,1)S(1)}, u32[]{:S(2)}, u32[]{:S(2)}) collective-permute-start(bf16[4,128,256]{2,1,0:T(8,128)(2,1)S(1)} %get-tuple-element.155), channel_id=1, source_target_pairs={{0,4},{4,8},{8,12},{12,0},{1,5},{5,9},{9,13},{13,1},{2,6},{6,10},{... | collective-permute-start | bytes 786440 | tf_op jit(solution)/shard_map/ppermute | solution.py:350
  39.3 9.4 %collective-permute-start.23 = (bf16[4,128,256]{2,1,0:T(8,128)(2,1)S(1)}, bf16[4,128,256]{2,1,0:T(8,128)(2,1)S(1)}, u32[]{:S(2)}, u32[]{:S(2)}) collective-permute-start(bf16[4,128,256]{2,1,0:T(8,128)(2,1)S(1)} %get-tuple-element.192.refs_4_), channel_id=1, source_target_pairs={{0,2},{2,0},{1,3},{3,1},{4,6},{6,4},{5,7},{7,5},{8,10},{10,8},{9,1... | collective-permute-start | bytes 786440 | tf_op jit(solution)/shard_map/ppermute | solution.py:40
  39.3 9.4 %collective-permute-start.22 = (bf16[4,128,256]{2,1,0:T(8,128)(2,1)S(1)}, bf16[4,128,256]{2,1,0:T(8,128)(2,1)S(1)}, u32[]{:S(2)}, u32[]{:S(2)}) collective-permute-start(bf16[4,128,256]{2,1,0:T(8,128)(2,1)S(1)} %get-tuple-element.161), channel_id=1, source_target_pairs={{0,4},{4,8},{8,12},{12,0},{1,5},{5,9},{9,13},{13,1},{2,6},{6,10},{... | collective-permute-start | bytes 786440 | tf_op jit(solution)/shard_map/ppermute | solution.py:350
  43.8 4.9 %collective-permute-start.24 = (bf16[4,128,256]{2,1,0:T(8,128)(2,1)S(1)}, bf16[4,128,256]{2,1,0:T(8,128)(2,1)S(1)}, u32[]{:S(2)}, u32[]{:S(2)}) collective-permute-start(bf16[4,128,256]{2,1,0:T(8,128)(2,1)S(1)} %get-tuple-element.215.refs_0_), channel_id=1, source_target_pairs={{0,1},{1,0},{2,3},{3,2},{4,5},{5,4},{6,7},{7,6},{8,9},{9,8},{10,11... | collective-permute-start | bytes 786440 | tf_op jit(solution)/shard_map/ppermute | solution.py:40
  44.6 11.4 %collective-permute-start.27 = (bf16[4,128,256]{2,1,0:T(8,128)(2,1)S(1)}, bf16[4,128,256]{2,1,0:T(8,128)(2,1)S(1)}, u32[]{:S(2)}, u32[]{:S(2)}) collective-permute-start(bf16[4,128,256]{2,1,0:T(8,128)(2,1)S(1)} %get-tuple-element.215.refs_0_), channel_id=1, source_target_pairs={{0,2},{2,0},{1,3},{3,1},{4,6},{6,4},{5,7},{7,5},{8,10},{10,8},{9,1... | collective-permute-start | bytes 786440 | tf_op jit(solution)/shard_map/ppermute | solution.py:40
  45.0 9.3 %collective-permute-start.26 = (bf16[4,128,256]{2,1,0:T(8,128)(2,1)S(1)}, bf16[4,128,256]{2,1,0:T(8,128)(2,1)S(1)}, u32[]{:S(2)}, u32[]{:S(2)}) collective-permute-start(bf16[4,128,256]{2,1,0:T(8,128)(2,1)S(1)} %get-tuple-element.169), channel_id=1, source_target_pairs={{0,4},{4,8},{8,12},{12,0},{1,5},{5,9},{9,13},{13,1},{2,6},{6,10},{... | collective-permute-start | bytes 786440 | tf_op jit(solution)/shard_map/ppermute | solution.py:350
  52.6 5.5 %collective-permute-start.30 = (bf16[4,128,256]{2,1,0:T(8,128)(2,1)S(1)}, bf16[4,128,256]{2,1,0:T(8,128)(2,1)S(1)}, u32[]{:S(2)}, u32[]{:S(2)}) collective-permute-start(bf16[4,128,256]{2,1,0:T(8,128)(2,1)S(1)} %collective-permute-done.20.refs_2_), channel_id=1, source_target_pairs={{0,1},{1,0},{2,3},{3,2},{4,5},{5,4},{6,7},{7,6},{8,9},{9,8},{10,11... | collective-permute-start | bytes 786440 | tf_op jit(solution)/shard_map/ppermute | solution.py:40
  52.7 6.6 %collective-permute-start.31 = (bf16[4,128,256]{2,1,0:T(8,128)(2,1)S(1)}, bf16[4,128,256]{2,1,0:T(8,128)(2,1)S(1)}, u32[]{:S(2)}, u32[]{:S(2)}) collective-permute-start(bf16[4,128,256]{2,1,0:T(8,128)(2,1)S(1)} %collective-permute-done.23.refs_6_), channel_id=1, source_target_pairs={{0,1},{1,0},{2,3},{3,2},{4,5},{5,4},{6,7},{7,6},{8,9},{9,8},{10,11... | collective-permute-start | bytes 786440 | tf_op jit(solution)/shard_map/ppermute | solution.py:40
  54.3 7.1 %collective-permute-start.32 = (bf16[4,128,256]{2,1,0:T(8,128)(2,1)S(1)}, bf16[4,128,256]{2,1,0:T(8,128)(2,1)S(1)}, u32[]{:S(2)}, u32[]{:S(2)}) collective-permute-start(bf16[4,128,256]{2,1,0:T(8,128)(2,1)S(1)} %get-tuple-element.219.refs_4_), channel_id=1, source_target_pairs={{0,2},{2,0},{1,3},{3,1},{4,6},{6,4},{5,7},{7,5},{8,10},{10,8},{9,1... | collective-permute-start | bytes 786440 | tf_op jit(solution)/shard_map/ppermute | solution.py:40
  56.0 11.1 %collective-permute-start.25 = (bf16[4,128,256]{2,1,0:T(8,128)(2,1)S(1)}, bf16[4,128,256]{2,1,0:T(8,128)(2,1)S(1)}, u32[]{:S(2)}, u32[]{:S(2)}) collective-permute-start(bf16[4,128,256]{2,1,0:T(8,128)(2,1)S(1)} %get-tuple-element.168), channel_id=1, source_target_pairs={{0,4},{4,8},{8,12},{12,0},{1,5},{5,9},{9,13},{13,1},{2,6},{6,10},{... | collective-permute-start | bytes 786440 | tf_op jit(solution)/shard_map/ppermute | solution.py:350
  58.0 12.1 %collective-permute-start.29 = (bf16[4,128,256]{2,1,0:T(8,128)(2,1)S(1)}, bf16[4,128,256]{2,1,0:T(8,128)(2,1)S(1)}, u32[]{:S(2)}, u32[]{:S(2)}) collective-permute-start(bf16[4,128,256]{2,1,0:T(8,128)(2,1)S(1)} %get-tuple-element.177), channel_id=1, source_target_pairs={{0,4},{4,8},{8,12},{12,0},{1,5},{5,9},{9,13},{13,1},{2,6},{6,10},{... | collective-permute-start | bytes 786440 | tf_op jit(solution)/shard_map/ppermute | solution.py:350
  58.1 12.0 %collective-permute-start.33 = (bf16[4,128,256]{2,1,0:T(8,128)(2,1)S(1)}, bf16[4,128,256]{2,1,0:T(8,128)(2,1)S(1)}, u32[]{:S(2)}, u32[]{:S(2)}) collective-permute-start(bf16[4,128,256]{2,1,0:T(8,128)(2,1)S(1)} %get-tuple-element.223.refs_8_), channel_id=1, source_target_pairs={{0,1},{1,0},{2,3},{3,2},{4,5},{5,4},{6,7},{7,6},{8,9},{9,8},{10,11... | collective-permute-start | bytes 786440 | tf_op jit(solution)/shard_map/ppermute | solution.py:40
  59.3 15.3 %collective-permute-start.40 = (bf16[4,128,256]{2,1,0:T(8,128)(2,1)S(1)}, bf16[4,128,256]{2,1,0:T(8,128)(2,1)S(1)}, u32[]{:S(2)}, u32[]{:S(2)}) collective-permute-start(bf16[4,128,256]{2,1,0:T(8,128)(2,1)S(1)} %get-tuple-element.223.refs_8_), channel_id=1, source_target_pairs={{0,2},{2,0},{1,3},{3,1},{4,6},{6,4},{5,7},{7,5},{8,10},{10,8},{9,1... | collective-permute-start | bytes 786440 | tf_op jit(solution)/shard_map/ppermute | solution.py:40
  74.7 12.9 %collective-permute-start.35 = (bf16[4,128,256]{2,1,0:T(8,128)(2,1)S(1)}, bf16[4,128,256]{2,1,0:T(8,128)(2,1)S(1)}, u32[]{:S(2)}, u32[]{:S(2)}) collective-permute-start(bf16[4,128,256]{2,1,0:T(8,128)(2,1)S(1)} %pack.12.refs_0_), channel_id=1, source_target_pairs={{0,2},{2,0},{1,3},{3,1},{4,6},{6,4},{5,7},{7,5},{8,10},{10,8},{9,1... | collective-permute-start | bytes 786440 | tf_op jit(solution)/shard_map/ppermute | solution.py:40
  77.1 10.6 %collective-permute-start.36 = (bf16[4,128,256]{2,1,0:T(8,128)(2,1)S(1)}, bf16[4,128,256]{2,1,0:T(8,128)(2,1)S(1)}, u32[]{:S(2)}, u32[]{:S(2)}) collective-permute-start(bf16[4,128,256]{2,1,0:T(8,128)(2,1)S(1)} %pack.13.refs_4_), channel_id=1, source_target_pairs={{0,1},{1,0},{2,3},{3,2},{4,5},{5,4},{6,7},{7,6},{8,9},{9,8},{10,11... | collective-permute-start | bytes 786440 | tf_op jit(solution)/shard_map/ppermute | solution.py:40
  77.5 10.3 %collective-permute-start.37 = (bf16[4,128,256]{2,1,0:T(8,128)(2,1)S(1)}, bf16[4,128,256]{2,1,0:T(8,128)(2,1)S(1)}, u32[]{:S(2)}, u32[]{:S(2)}) collective-permute-start(bf16[4,128,256]{2,1,0:T(8,128)(2,1)S(1)} %pack.13.refs_4_), channel_id=1, source_target_pairs={{0,2},{2,0},{1,3},{3,1},{4,6},{6,4},{5,7},{7,5},{8,10},{10,8},{9,1... | collective-permute-start | bytes 786440 | tf_op jit(solution)/shard_map/ppermute | solution.py:40
  (21 other events, 132.8 us)

commit v10 on v9

--- a/solution.py
+++ b/solution.py
@@ -22,9 +22,10 @@
 ENTRIES_EACH = 16
 HALF = 8
 ROUNDS = 5
-SWEEPS = ROUNDS + 2
 CAP = 4
 GROUP = 2
+SWEEPS = ROUNDS + 1
+SWEPT = (CAP,) * ROUNDS + (2 * CAP,)
 LANES = 128
 
 LITTLE = pl.CostEstimate(flops=1, bytes_accessed=1, transcendentals=0)
@@ -152,12 +153,8 @@
         return (one * share).astype(jnp.bfloat16), (two * share).astype(jnp.bfloat16)
 
     def mix(g, start, weights):
-        mixed = sum(
-            lax.dot_general(
-                weights[k], values[g * KMAX + k][0, :, start : start + wide], SAME_ROWS, preferred_element_type=jnp.float32
-            )
-            for k in range(KMAX)
-        )
+        rows = jnp.concatenate([values[g * KMAX + k][0, :, start : start + wide] for k in range(KMAX)], 0)
+        mixed = lax.dot_general(jnp.concatenate(weights, 0), rows, SAME_ROWS, preferred_element_type=jnp.float32)
         mixed = jnp.where(count[g] > 0, mixed, 0.0).astype(jnp.bfloat16)
         rows = slice(g * STRETCH, (g + 1) * STRETCH)
         out_ref[rows, start : start + HEAD_DIM] = mixed[:STRETCH, :HEAD_DIM]
@@ -187,7 +184,7 @@
             in_specs=[query_spec] + entries * 2,
             out_specs=query_spec,
         ),
-        compiler_params=pltpu.CompilerParams(vmem_limit_bytes=VMEM_LIMIT),
+        compiler_params=pltpu.CompilerParams(vmem_limit_bytes=60 * 1024 * 1024),
         cost_estimate=LITTLE,
         name="attend",
     )(slots, counts, queries, *[keys] * len(entries), *[values] * len(entries))
@@ -243,20 +240,22 @@
     def ranked(mask):
         return jnp.dot(mask.astype(jnp.bfloat16), earlier, preferred_element_type=f32)
 
-    def listed(into, taken, rank, number):
-        for b in range(CAP):
+    def listed(into, taken, rank, number, cap):
+        for b in range(cap):
             pick = jnp.max(jnp.where((taken > 0) & (rank == b), loc, -1.0), axis=1, keepdims=True)
             into = jnp.where(entry == number * CAP + b, pick, into)
         return into
 
     for number in range(SWEEPS):
         loc = jnp.maximum(loc, flights[number])
+        if number == ROUNDS:
+            loc = jnp.maximum(loc, flights[number + 1])
         ready = jnp.where((needed > 0) & (loc >= 0) & (swept == 0), 1.0, 0.0)
         rank = ranked(ready)
-        taken = jnp.where((ready > 0) & (rank < CAP), 1.0, 0.0)
+        taken = jnp.where((ready > 0) & (rank < SWEPT[number]), 1.0, 0.0)
         swept = swept + taken
         slot_of = slot_of + taken * (rank + number * CAP)
-        picks = listed(picks, taken, rank, number)
+        picks = listed(picks, taken, rank, number, SWEPT[number])
         if number < ROUNDS:
             ready = jnp.where((far > 0) & (loc >= 0) & (sent == 0), 1.0, 0.0)
             rank = jnp.zeros((groups, LANES), f32)
@@ -267,7 +266,7 @@
                 above = above + jnp.sum(level, axis=1, keepdims=True)
             taken = jnp.where((ready > 0) & (rank < CAP), 1.0, 0.0)
             sent = sent + taken
-            lists = listed(lists, taken, rank, number)
+            lists = listed(lists, taken, rank, number, CAP)
             came = jnp.dot(step, (taken * (rank + 1)).astype(jnp.bfloat16), preferred_element_type=f32)
             flights.append(jnp.where(came > 0, came + float(2 * ENTRIES_EACH + number * CAP - 1), -1.0))
     lists_ref[...] = lists
@@ -294,7 +293,7 @@
 
 
 def pack(plan, number, pool):
-    lines = (0, 1) if number < ROUNDS else (1,)
+    lines, caps = ((0, 1), (CAP, CAP)) if number < ROUNDS else ((1,), SWEPT[-1:])
     starts = [0]
     for array in pool:
         starts.append(starts[-1] + array.shape[0])
@@ -302,7 +301,7 @@
     def kernel(plan_ref, *refs):
         sources, outs = refs[: len(pool)], refs[len(pool) :]
         for line, out in zip(lines, outs):
-            for b in range(CAP):
+            for b in range(out.shape[0]):
                 at = plan_ref[line * LANES + number * CAP + b]
                 for source, low, high in zip(sources, starts, starts[1:]):
 
@@ -313,7 +312,7 @@
     in_vmem = pl.BlockSpec(memory_space=pltpu.VMEM)
     return pl.pallas_call(
         kernel,
-        out_shape=(jax.ShapeDtypeStruct((CAP,) + pool[0].shape[1:], pool[0].dtype),) * len(lines),
+        out_shape=tuple(jax.ShapeDtypeStruct((cap,) + pool[0].shape[1:], pool[0].dtype) for cap in caps),
         grid_spec=pltpu.PrefetchScalarGridSpec(
             num_scalar_prefetch=1, in_specs=[in_vmem] * len(pool), out_specs=(in_vmem,) * len(lines)
         ),
@@ -407,7 +406,7 @@
     asked = jnp.stack([first, jnp.where(asked[:, 1] >= 0, asked[:, 1], first)], axis=1).reshape(-1)
 
     places = places_of_pieces()
-    room = SWEEPS * CAP
+    room = sum(SWEPT)
     wanted = plan[LANES : LANES + room].reshape(room // GROUP, GROUP)[:, 0] >= 0
     group = jnp.arange(room // GROUP, dtype=jnp.int32)
     latest = jnp.max(jnp.where((group[None, :] <= group[:, None]) & wanted[None, :], group[None, :], 0), axis=1)
@@ -416,28 +415,28 @@
 
     pieces, held = [], ()
     for number in range(SWEEPS):
-        *ways, mine = pack(plan, number, [store] + flights[: number + 1])
+        *ways, mine = pack(plan, number, [store] + flights[: number + 1 if number < ROUNDS else None])
         flights += [onward(way) for way in ways]
         pieces.append([mine, swapped(mine, "rep"), swapped(mine, "mp")])
         if number > 0:
             pieces[number - 1].append(swapped(pieces[number - 1][2], "rep"))
-        if number == SWEEPS - 3:
+        if number == SWEEPS - 2:
             ripe, pieces[number - 1][2] = lax.optimization_barrier((pieces[:2], pieces[number - 1][2]))
             held = project(marks, gain, ripe, key_weight, value_weight, GROUP, room)
         if number + 1 < SWEEPS:
             across = [parts[2] for parts in pieces[:number]] if number + 2 < SWEEPS else []
-            came = slice(number + 1, number + 2 if number + 3 < SWEEPS else None)
+            came = slice(number + 1, number + 2 if number + 2 < SWEEPS else None)
             flights[came], across, pieces[number][1], gain, slots, marks, held = lax.optimization_barrier(
                 (flights[came], across, pieces[number][1], gain, slots, marks, held)
             )
             for parts, arrived in zip(pieces, across):
                 parts[2] = arrived
-    ripe, _ = lax.optimization_barrier((pieces[2:-2], mine))
+    ripe, _ = lax.optimization_barrier((pieces[2:-1], mine))
     held = project(marks, gain, ripe, key_weight, value_weight, GROUP, room, 2 * CAP // GROUP, held)
-    late, held = lax.optimization_barrier(([parts[:3] for parts in pieces[-2:]], held))
-    late = [[*parts, swapped(parts[2], "rep")] for parts in late]
-    done = (SWEEPS - 2) * CAP // GROUP
-    keys, values = project(marks, gain, late, key_weight, value_weight, GROUP, room, done, held)
+    late, held = lax.optimization_barrier((pieces[-1], held))
+    late = [*late, swapped(late[2], "rep")]
+    done = (SWEEPS - 1) * CAP // GROUP
+    keys, values = project(marks, gain, [late], key_weight, value_weight, GROUP, room, done, held)
 
     def whole(state):
         mine = fetch_all(store, asked >> 4, asked & (ENTRIES_EACH - 1))

time: 112 us -> 112 us (level)
  the two profiles are of different devices: /device:TPU:5 before, /device:TPU:0 now
where the time goes in v10:
time: 112 us; the launch traced here: 111 us
  Pallas kernels  45.5 us (41%)
  waiting for transfers between devices  32.3 us (29%)
  starting transfers between devices  18 us (16%)
  local copies, waits for them, and re-layouts  11.9 us (11%)
  other arithmetic  2.72 us (2%)
    ppermute x7, waiting for transfers between devices, onward(): lax.ppermute(value, 'seq', [(chip, (chip + 1) % size) for chip in range(s...  21.9 us
    pallas_call x3, Pallas kernels, project(): pl.pallas_call(kernel, out_shape=(out, out), grid_spec=pltpu.PrefetchScal...  19.9 us
    pallas_call x6, Pallas kernels, pack(): pl.pallas_call(kernel, out_shape=tuple((jax.ShapeDtypeStruct((cap,) + poo...  12.2 us
    pallas_call x1, Pallas kernels, attend(): pl.pallas_call(attend_kernel, out_shape=jax.ShapeDtypeStruct(queries.shap...  10.9 us
    ppermute x22, starting transfers between devices, swapped(): return lax.ppermute(value, axis, [(0, 1), (1, 0)])  10.3 us
    ppermute x22, waiting for transfers between devices, swapped(): return lax.ppermute(value, axis, [(0, 1), (1, 0)])  9.48 us
    unnamed x16, local copies, waits for them, and re-layouts  6.06 us
    ppermute x3, starting transfers between devices, exchanged_table(): lax.ppermute(codes, 'seq', [(chip, chip ^ offset) for chip in range(CHIPS)])  5.76 us
  transfers between devices with their start and end apart: 32, of which 14 were waited for; matrix products, arithmetic and copies ran while one was open for 6% of the time, Pallas kernels for 25%

profile of v10, /device:TPU:0, one launch (start us, length us, event | category | flops | bytes accessed | tf_op | source)
XLA Modules:
  0.0 111.5 jit_solution(4205968651806449782)
XLA Ops:
  2.2 5.1 %collective-permute-start.11 = (s32[24]{0:T(128)S(1)}, s32[24]{0:T(128)S(1)}, u32[]{:S(2)}, u32[]{:S(2)}) collective-permute-start(s32[24]{0:T(128)S(1)} %reshape.130), channel_id=1, source_target_pairs={{0,12},{4,8},{8,4},{12,0},{1,13},{5,9},{9,5},{13,1},{2,14},{6,10},... | collective-permute-start | bytes 296 | tf_op jit(solution)/shard_map/ppermute | solution.py:381
  7.9 1.6 %collective-permute-start.17 = (f32[1,256]{1,0:T(1,128)}, f32[1,256]{1,0:T(1,128)S(1)}, u32[]{:S(2)}, u32[]{:S(2)}) collective-permute-start(f32[1,256]{1,0:T(1,128)} %bitcast.39), channel_id=1, source_target_pairs={{0,2},{2,0},{1,3},{3,1},{4,6},{6,4},{5,7},{7,5},{8,10},{10,8},{9,1... | collective-permute-start | bytes 3080 | tf_op jit(solution)/shard_map/ppermute | solution.py:41
  11.7 1.6 %collective-permute-start.12 = (s32[4,24]{1,0:T(4,128)S(1)}, s32[4,24]{1,0:T(4,128)S(1)}, u32[]{:S(2)}, u32[]{:S(2)}) collective-permute-start(s32[4,24]{1,0:T(4,128)S(1)} %pad_add_fusion.2), channel_id=1, source_target_pairs={{0,16},{16,0},{1,17},{17,1},{2,18},{18,2},{3,19},{19,3},{4,20},{20... | collective-permute-start | bytes 1160 | tf_op jit(solution)/shard_map/ppermute | solution.py:41
  16.5 2.5 %plan.1 = s32[8,128]{1,0:T(8,128)} custom-call(s32[1]{0:T(128)} %bitcast.2.place, s32[192]{0:T(256)} %reshape.131.table), custom_call_target="tpu_custom_call" | custom-call | tf_op jit(solution)/shard_map/plan/pallas_call | solution.py:285
  20.9 5.2 %collective-permute-done.13.refs_1_ = bf16[8,128,256]{2,1,0:T(8,128)(2,1)S(1)} collective-permute-done((bf16[8,128,256]{2,1,0:T(8,128)(2,1)S(1)}, bf16[8,128,256]{2,1,0:T(8,128)(2,1)S(1)}, u32[]{:S(2)}, u32[]{:S(2)}) %collective-permute-start.13) | collective-permute-done | bytes 524320 | tf_op jit(solution)/shard_map/ppermute | solution.py:349
  26.8 1.9 %pack.6 = (bf16[4,128,256]{2,1,0:T(8,128)(2,1)S(1)}, bf16[4,128,256]{2,1,0:T(8,128)(2,1)S(1)}) custom-call(s32[1024]{0:T(1024)S(1)} %bitcast.23, bf16[16,128,256]{2,1,0:T(8,128)(2,1)} %refs_0_.11, bf16[8,128,256]{2,1,0:T(8,128)(2,1)S(1)} %collective-permute-done.13.refs_1_), custom_call_target="tpu_custom_call" | custom-call | flops 1 | bytes 1 | tf_op jit(solution)/shard_map/pack/pallas_call | solution.py:313
  32.5 4.8 %collective-permute-done.14.refs_2_ = bf16[8,128,256]{2,1,0:T(8,128)(2,1)S(1)} collective-permute-done((bf16[8,128,256]{2,1,0:T(8,128)(2,1)S(1)}, bf16[8,128,256]{2,1,0:T(8,128)(2,1)S(1)}, u32[]{:S(2)}, u32[]{:S(2)}) %collective-permute-start.14) | collective-permute-done | bytes 524320 | tf_op jit(solution)/shard_map/ppermute | solution.py:349
  38.0 2.2 %pack.7 = (bf16[4,128,256]{2,1,0:T(8,128)(2,1)S(1)}, bf16[4,128,256]{2,1,0:T(8,128)(2,1)S(1)}) custom-call(s32[1024]{0:T(1024)S(1)} %bitcast.24, bf16[16,128,256]{2,1,0:T(8,128)(2,1)} %refs_0_.11, bf16[8,128,256]{2,1,0:T(8,128)(2,1)S(1)} %collective-permute-done.13.refs_1_, bf16[8,128,256]{2,1,0:T(8,128)(2,1)S(1)} %collective-permute-done.14.refs_2_), custom_call_target="tpu_custom_call" | custom-call | flops 1 | bytes 1 | tf_op jit(solution)/shard_map/pack/pallas_call | solution.py:313
  40.6 2.0 %collective-permute-done.19.refs_3_ = bf16[4,128,256]{2,1,0:T(8,128)(2,1)S(1)} collective-permute-done((bf16[4,128,256]{2,1,0:T(8,128)(2,1)S(1)}, bf16[4,128,256]{2,1,0:T(8,128)(2,1)S(1)}, u32[]{:S(2)}, u32[]{:S(2)}) %collective-permute-start.19) | collective-permute-done | bytes 262176 | tf_op jit(solution)/shard_map/ppermute | solution.py:349
  42.6 2.0 %pack.8 = (bf16[4,128,256]{2,1,0:T(8,128)(2,1)S(1)}, bf16[4,128,256]{2,1,0:T(8,128)(2,1)S(1)}) custom-call(s32[1024]{0:T(1024)S(1)} %bitcast.25, bf16[16,128,256]{2,1,0:T(8,128)(2,1)} %refs_0_.11, bf16[8,128,256]{2,1,0:T(8,128)(2,1)S(1)} %collective-permute-done.13.refs_1_, bf16[8,128,256]{2,1,0:T(8,128)(2,1)S(1)} %collective-permute-done.14.refs_2_, ...), custom_call_target="tpu_custom_call" | custom-call | flops 1 | bytes 1 | tf_op jit(solution)/shard_map/pack/pallas_call | solution.py:313
  45.4 6.1 %collective-permute-done.22.refs_4_ = bf16[4,128,256]{2,1,0:T(8,128)(2,1)S(1)} collective-permute-done((bf16[4,128,256]{2,1,0:T(8,128)(2,1)S(1)}, bf16[4,128,256]{2,1,0:T(8,128)(2,1)S(1)}, u32[]{:S(2)}, u32[]{:S(2)}) %collective-permute-start.22) | collective-permute-done | bytes 262176 | tf_op jit(solution)/shard_map/ppermute | solution.py:349
  52.2 2.0 %pack.9 = (bf16[4,128,256]{2,1,0:T(8,128)(2,1)S(1)}, bf16[4,128,256]{2,1,0:T(8,128)(2,1)S(1)}) custom-call(s32[1024]{0:T(1024)S(1)} %bitcast.26, bf16[16,128,256]{2,1,0:T(8,128)(2,1)} %refs_0_.11, bf16[8,128,256]{2,1,0:T(8,128)(2,1)S(1)} %collective-permute-done.13.refs_1_, bf16[8,128,256]{2,1,0:T(8,128)(2,1)S(1)} %collective-permute-done.14.refs_2_, ...), custom_call_target="tpu_custom_call" | custom-call | flops 1 | bytes 1 | tf_op jit(solution)/shard_map/pack/pallas_call | solution.py:313
  54.9 1.5 %collective-permute-done.26.refs_5_ = bf16[4,128,256]{2,1,0:T(8,128)(2,1)S(1)} collective-permute-done((bf16[4,128,256]{2,1,0:T(8,128)(2,1)S(1)}, bf16[4,128,256]{2,1,0:T(8,128)(2,1)S(1)}, u32[]{:S(2)}, u32[]{:S(2)}) %collective-permute-start.26) | collective-permute-done | bytes 262176 | tf_op jit(solution)/shard_map/ppermute | solution.py:349
  56.4 1.8 %collective-permute-start.33 = (bf16[4,128,256]{2,1,0:T(8,128)(2,1)S(1)}, bf16[4,128,256]{2,1,0:T(8,128)(2,1)S(1)}, u32[]{:S(2)}, u32[]{:S(2)}) collective-permute-start(bf16[4,128,256]{2,1,0:T(8,128)(2,1)S(1)} %get-tuple-element.198.refs_4_), channel_id=1, source_target_pairs={{0,2},{2,0},{1,3},{3,1},{4,6},{6,4},{5,7},{7,5},{8,10},{10,8},{9,1... | collective-permute-start | bytes 786440 | tf_op jit(solution)/shard_map/ppermute | solution.py:41
  58.2 1.9 %pack.10 = (bf16[4,128,256]{2,1,0:T(8,128)(2,1)S(1)}, bf16[4,128,256]{2,1,0:T(8,128)(2,1)S(1)}) custom-call(s32[1024]{0:T(1024)S(1)} %bitcast.27, bf16[16,128,256]{2,1,0:T(8,128)(2,1)} %refs_0_.11, bf16[8,128,256]{2,1,0:T(8,128)(2,1)S(1)} %collective-permute-done.13.refs_1_, bf16[8,128,256]{2,1,0:T(8,128)(2,1)S(1)} %collective-permute-done.14.refs_2_, ...), custom_call_target="tpu_custom_call" | custom-call | flops 1 | bytes 1 | tf_op jit(solution)/shard_map/pack/pallas_call | solution.py:313
  60.6 4.3 %collective-permute-done.33.refs_6_ = bf16[4,128,256]{2,1,0:T(8,128)(2,1)S(1)} collective-permute-done((bf16[4,128,256]{2,1,0:T(8,128)(2,1)S(1)}, bf16[4,128,256]{2,1,0:T(8,128)(2,1)S(1)}, u32[]{:S(2)}, u32[]{:S(2)}) %collective-permute-start.33) | collective-permute-done | bytes 262176 | tf_op jit(solution)/shard_map/ppermute | solution.py:41
  64.9 5.7 %project.5 = (bf16[28,128,1024]{2,1,0:T(8,128)(2,1)S(1)}, bf16[28,128,1024]{2,1,0:T(8,128)(2,1)S(1)}) custom-call(s32[32]{0:T(128)S(1)} %concatenate.23.marks_ref, f32[1,1024]{1,0:T(1,128)S(1)} %pad_maximum_fusion.gain_ref, bf16[4,128,256]{2,1,0:T(8,128)(2,1)S(1)} %get-tuple-element.174.refs_0_, bf16[4,128,256]{2,1,0:T(8,128)(2,1)S(1)} %collective-permute-done.15.refs_1_, ...), custom_call_target="tpu_custom_call" | custom-call | flops 1 | bytes 1 | tf_op jit(solution)/shard_map/project/pallas_call | solution.py:102
  70.7 2.2 %collective-permute-done.29.refs_7_ = bf16[4,128,256]{2,1,0:T(8,128)(2,1)S(1)} collective-permute-done((bf16[4,128,256]{2,1,0:T(8,128)(2,1)S(1)}, bf16[4,128,256]{2,1,0:T(8,128)(2,1)S(1)}, u32[]{:S(2)}, u32[]{:S(2)}) %collective-permute-start.29) | collective-permute-done | bytes 262176 | tf_op jit(solution)/shard_map/ppermute | solution.py:349
  72.8 2.1 %pack.11.refs_0_ = bf16[8,128,256]{2,1,0:T(8,128)(2,1)S(1)} custom-call(s32[1024]{0:T(1024)S(1)} %bitcast.28, bf16[16,128,256]{2,1,0:T(8,128)(2,1)} %refs_0_.11, bf16[8,128,256]{2,1,0:T(8,128)(2,1)S(1)} %collective-permute-done.13.refs_1_, bf16[8,128,256]{2,1,0:T(8,128)(2,1)S(1)} %collective-permute-done.14.refs_2_, ...), custom_call_target="tpu_custom_call" | custom-call | flops 1 | bytes 1 | tf_op jit(solution)/shard_map/pack/pallas_call | solution.py:313
  78.4 7.4 %project.6 = (bf16[28,128,1024]{2,1,0:T(8,128)(2,1)S(1)}, bf16[28,128,1024]{2,1,0:T(8,128)(2,1)S(1)}) custom-call(s32[32]{0:T(128)S(1)} %concatenate.23.marks_ref, f32[1,1024]{1,0:T(1,128)S(1)} %pad_maximum_fusion.gain_ref, bf16[4,128,256]{2,1,0:T(8,128)(2,1)S(1)} %get-tuple-element.194.refs_0_, ...), custom_call_target="tpu_custom_call", output_to_operand_aliasing={{0}: (16, {}), {1}: (17, {})} | custom-call | flops 1 | bytes 1 | tf_op jit(solution)/shard_map/project/pallas_call | solution.py:102
  87.0 1.7 %copy-done.4 = bf16[28,128,1024]{2,1,0:T(8,128)(2,1)} copy-done((bf16[28,128,1024]{2,1,0:T(8,128)(2,1)}, bf16[28,128,1024]{2,1,0:T(8,128)(2,1)S(1)}, u32[]{:S(2)}) %copy-start.4) | copy-done | bytes 7340056
  88.7 2.3 %copy-done.5 = bf16[28,128,1024]{2,1,0:T(8,128)(2,1)} copy-done((bf16[28,128,1024]{2,1,0:T(8,128)(2,1)}, bf16[28,128,1024]{2,1,0:T(8,128)(2,1)S(1)}, u32[]{:S(2)}) %copy-start.5) | copy-done | bytes 7340056
  92.9 6.8 %project.7 = (bf16[28,128,1024]{2,1,0:T(8,128)(2,1)}, bf16[28,128,1024]{2,1,0:T(8,128)(2,1)}) custom-call(s32[32]{0:T(128)S(1)} %concatenate.23.marks_ref, f32[1,1024]{1,0:T(1,128)S(1)} %pad_maximum_fusion.gain_ref, bf16[8,128,256]{2,1,0:T(8,128)(2,1)S(1)} %pack.11.refs_0_, ...), custom_call_target="tpu_custom_call", output_to_operand_aliasing={{0}: (8, {}), {1}: (9, {})} | custom-call | flops 1 | bytes 1 | tf_op jit(solution)/shard_map/project/pallas_call | solution.py:102
  100.6 10.9 %attend.1 = bf16[768,1024]{1,0:T(8,128)(2,1)} custom-call(s32[24]{0:T(128)} %get-tuple-element.217.slots, s32[12]{0:T(128)} %convert_reduce_fusion.counts, bf16[768,1024]{1,0:T(8,128)(2,1)} %query_ref.1, bf16[28,128,1024]{2,1,0:T(8,128)(2,1)} %get-tuple-element.218.refs_0_.refs_1_.refs_2_.refs_3_.refs_4_.refs_5_, ...), custom_call_target="tpu_custom_call" | custom-call | flops 1 | bytes 1 | tf_op jit(solution)/shard_map/attend/pallas_call | solution.py:178
  (96 shorter events, 25.5 us)
Async XLA Ops:
  2.2 7.4 %collective-permute-start.11 = (s32[24]{0:T(128)S(1)}, s32[24]{0:T(128)S(1)}, u32[]{:S(2)}, u32[]{:S(2)}) collective-permute-start(s32[24]{0:T(128)S(1)} %reshape.130), channel_id=1, source_target_pairs={{0,12},{4,8},{8,4},{12,0},{1,13},{5,9},{9,5},{13,1},{2,14},{6,10},... | collective-permute-start | bytes 296 | tf_op jit(solution)/shard_map/ppermute | solution.py:381
  7.3 4.4 %collective-permute-start.10 = (s32[24]{0:T(128)S(1)}, s32[24]{0:T(128)S(1)}, u32[]{:S(2)}, u32[]{:S(2)}) collective-permute-start(s32[24]{0:T(128)S(1)} %reshape.130), channel_id=1, source_target_pairs={{0,8},{4,12},{8,0},{12,4},{1,9},{5,13},{9,1},{13,5},{2,10},{6,14},... | collective-permute-start | bytes 296 | tf_op jit(solution)/shard_map/ppermute | solution.py:381
  7.3 4.4 %collective-permute-start.9 = (s32[24]{0:T(128)S(1)}, s32[24]{0:T(128)S(1)}, u32[]{:S(2)}, u32[]{:S(2)}) collective-permute-start(s32[24]{0:T(128)S(1)} %reshape.130), channel_id=1, source_target_pairs={{0,4},{4,0},{8,12},{12,8},{1,5},{5,1},{9,13},{13,9},{2,6},{6,2},{1... | collective-permute-start | bytes 296 | tf_op jit(solution)/shard_map/ppermute | solution.py:381
  7.9 21.0 %collective-permute-start.17 = (f32[1,256]{1,0:T(1,128)}, f32[1,256]{1,0:T(1,128)S(1)}, u32[]{:S(2)}, u32[]{:S(2)}) collective-permute-start(f32[1,256]{1,0:T(1,128)} %bitcast.39), channel_id=1, source_target_pairs={{0,2},{2,0},{1,3},{3,1},{4,6},{6,4},{5,7},{7,5},{8,10},{10,8},{9,1... | collective-permute-start | bytes 3080 | tf_op jit(solution)/shard_map/ppermute | solution.py:41
  9.6 21.2 %collective-permute-start.16 = (f32[1,256]{1,0:T(1,128)}, f32[1,256]{1,0:T(1,128)S(1)}, u32[]{:S(2)}, u32[]{:S(2)}) collective-permute-start(f32[1,256]{1,0:T(1,128)} %bitcast.40), channel_id=1, source_target_pairs={{0,1},{1,0},{2,3},{3,2},{4,5},{5,4},{6,7},{7,6},{8,9},{9,8},{10,11... | collective-permute-start | bytes 3080 | tf_op jit(solution)/shard_map/ppermute | solution.py:41
  9.6 16.5 %collective-permute-start.13 = (bf16[8,128,256]{2,1,0:T(8,128)(2,1)S(1)}, bf16[8,128,256]{2,1,0:T(8,128)(2,1)S(1)}, u32[]{:S(2)}, u32[]{:S(2)}) collective-permute-start(bf16[8,128,256]{2,1,0:T(8,128)(2,1)S(1)} %get-tuple-element.138), channel_id=1, source_target_pairs={{0,4},{4,8},{8,12},{12,0},{1,5},{5,9},{9,13},{13,1},{2,6},{6,10},{... | collective-permute-start | bytes 1572872 | tf_op jit(solution)/shard_map/ppermute | solution.py:349
  13.3 24.0 %collective-permute-start.14 = (bf16[8,128,256]{2,1,0:T(8,128)(2,1)S(1)}, bf16[8,128,256]{2,1,0:T(8,128)(2,1)S(1)}, u32[]{:S(2)}, u32[]{:S(2)}) collective-permute-start(bf16[8,128,256]{2,1,0:T(8,128)(2,1)S(1)} %get-tuple-element.139), channel_id=1, source_target_pairs={{0,4},{4,8},{8,12},{12,0},{1,5},{5,9},{9,13},{13,1},{2,6},{6,10},{... | collective-permute-start | bytes 1572872 | tf_op jit(solution)/shard_map/ppermute | solution.py:349
  28.7 8.6 %collective-permute-start.15 = (bf16[4,128,256]{2,1,0:T(8,128)(2,1)S(1)}, bf16[4,128,256]{2,1,0:T(8,128)(2,1)S(1)}, u32[]{:S(2)}, u32[]{:S(2)}) collective-permute-start(bf16[4,128,256]{2,1,0:T(8,128)(2,1)S(1)} %get-tuple-element.174.refs_0_), channel_id=1, source_target_pairs={{0,1},{1,0},{2,3},{3,2},{4,5},{5,4},{6,7},{7,6},{8,9},{9,8},{10,11... | collective-permute-start | bytes 786440 | tf_op jit(solution)/shard_map/ppermute | solution.py:41
  31.5 11.1 %collective-permute-start.20 = (bf16[4,128,256]{2,1,0:T(8,128)(2,1)S(1)}, bf16[4,128,256]{2,1,0:T(8,128)(2,1)S(1)}, u32[]{:S(2)}, u32[]{:S(2)}) collective-permute-start(bf16[4,128,256]{2,1,0:T(8,128)(2,1)S(1)} %get-tuple-element.174.refs_0_), channel_id=1, source_target_pairs={{0,2},{2,0},{1,3},{3,1},{4,6},{6,4},{5,7},{7,5},{8,10},{10,8},{9,1... | collective-permute-start | bytes 786440 | tf_op jit(solution)/shard_map/ppermute | solution.py:41
  32.5 10.1 %collective-permute-start.19 = (bf16[4,128,256]{2,1,0:T(8,128)(2,1)S(1)}, bf16[4,128,256]{2,1,0:T(8,128)(2,1)S(1)}, u32[]{:S(2)}, u32[]{:S(2)}) collective-permute-start(bf16[4,128,256]{2,1,0:T(8,128)(2,1)S(1)} %get-tuple-element.143), channel_id=1, source_target_pairs={{0,4},{4,8},{8,12},{12,0},{1,5},{5,9},{9,13},{13,1},{2,6},{6,10},{... | collective-permute-start | bytes 786440 | tf_op jit(solution)/shard_map/ppermute | solution.py:349
  40.3 11.2 %collective-permute-start.23 = (bf16[4,128,256]{2,1,0:T(8,128)(2,1)S(1)}, bf16[4,128,256]{2,1,0:T(8,128)(2,1)S(1)}, u32[]{:S(2)}, u32[]{:S(2)}) collective-permute-start(bf16[4,128,256]{2,1,0:T(8,128)(2,1)S(1)} %get-tuple-element.178.refs_4_), channel_id=1, source_target_pairs={{0,2},{2,0},{1,3},{3,1},{4,6},{6,4},{5,7},{7,5},{8,10},{10,8},{9,1... | collective-permute-start | bytes 786440 | tf_op jit(solution)/shard_map/ppermute | solution.py:41
  40.6 10.9 %collective-permute-start.22 = (bf16[4,128,256]{2,1,0:T(8,128)(2,1)S(1)}, bf16[4,128,256]{2,1,0:T(8,128)(2,1)S(1)}, u32[]{:S(2)}, u32[]{:S(2)}) collective-permute-start(bf16[4,128,256]{2,1,0:T(8,128)(2,1)S(1)} %get-tuple-element.149), channel_id=1, source_target_pairs={{0,4},{4,8},{8,12},{12,0},{1,5},{5,9},{9,13},{13,1},{2,6},{6,10},{... | collective-permute-start | bytes 786440 | tf_op jit(solution)/shard_map/ppermute | solution.py:349
  44.6 6.9 %collective-permute-start.24 = (bf16[4,128,256]{2,1,0:T(8,128)(2,1)S(1)}, bf16[4,128,256]{2,1,0:T(8,128)(2,1)S(1)}, u32[]{:S(2)}, u32[]{:S(2)}) collective-permute-start(bf16[4,128,256]{2,1,0:T(8,128)(2,1)S(1)} %get-tuple-element.194.refs_0_), channel_id=1, source_target_pairs={{0,1},{1,0},{2,3},{3,2},{4,5},{5,4},{6,7},{7,6},{8,9},{9,8},{10,11... | collective-permute-start | bytes 786440 | tf_op jit(solution)/shard_map/ppermute | solution.py:41
  44.7 13.5 %collective-permute-start.27 = (bf16[4,128,256]{2,1,0:T(8,128)(2,1)S(1)}, bf16[4,128,256]{2,1,0:T(8,128)(2,1)S(1)}, u32[]{:S(2)}, u32[]{:S(2)}) collective-permute-start(bf16[4,128,256]{2,1,0:T(8,128)(2,1)S(1)} %get-tuple-element.194.refs_0_), channel_id=1, source_target_pairs={{0,2},{2,0},{1,3},{3,1},{4,6},{6,4},{5,7},{7,5},{8,10},{10,8},{9,1... | collective-permute-start | bytes 786440 | tf_op jit(solution)/shard_map/ppermute | solution.py:41
  45.4 11.0 %collective-permute-start.26 = (bf16[4,128,256]{2,1,0:T(8,128)(2,1)S(1)}, bf16[4,128,256]{2,1,0:T(8,128)(2,1)S(1)}, u32[]{:S(2)}, u32[]{:S(2)}) collective-permute-start(bf16[4,128,256]{2,1,0:T(8,128)(2,1)S(1)} %get-tuple-element.157), channel_id=1, source_target_pairs={{0,4},{4,8},{8,12},{12,0},{1,5},{5,9},{9,13},{13,1},{2,6},{6,10},{... | collective-permute-start | bytes 786440 | tf_op jit(solution)/shard_map/ppermute | solution.py:349
  54.3 5.9 %collective-permute-start.31 = (bf16[4,128,256]{2,1,0:T(8,128)(2,1)S(1)}, bf16[4,128,256]{2,1,0:T(8,128)(2,1)S(1)}, u32[]{:S(2)}, u32[]{:S(2)}) collective-permute-start(bf16[4,128,256]{2,1,0:T(8,128)(2,1)S(1)} %collective-permute-done.20.refs_2_), channel_id=1, source_target_pairs={{0,1},{1,0},{2,3},{3,2},{4,5},{5,4},{6,7},{7,6},{8,9},{9,8},{10,11... | collective-permute-start | bytes 786440 | tf_op jit(solution)/shard_map/ppermute | solution.py:41
  54.8 5.5 %collective-permute-start.32 = (bf16[4,128,256]{2,1,0:T(8,128)(2,1)S(1)}, bf16[4,128,256]{2,1,0:T(8,128)(2,1)S(1)}, u32[]{:S(2)}, u32[]{:S(2)}) collective-permute-start(bf16[4,128,256]{2,1,0:T(8,128)(2,1)S(1)} %collective-permute-done.23.refs_6_), channel_id=1, source_target_pairs={{0,1},{1,0},{2,3},{3,2},{4,5},{5,4},{6,7},{7,6},{8,9},{9,8},{10,11... | collective-permute-start | bytes 786440 | tf_op jit(solution)/shard_map/ppermute | solution.py:41
  56.4 8.5 %collective-permute-start.33 = (bf16[4,128,256]{2,1,0:T(8,128)(2,1)S(1)}, bf16[4,128,256]{2,1,0:T(8,128)(2,1)S(1)}, u32[]{:S(2)}, u32[]{:S(2)}) collective-permute-start(bf16[4,128,256]{2,1,0:T(8,128)(2,1)S(1)} %get-tuple-element.198.refs_4_), channel_id=1, source_target_pairs={{0,2},{2,0},{1,3},{3,1},{4,6},{6,4},{5,7},{7,5},{8,10},{10,8},{9,1... | collective-permute-start | bytes 786440 | tf_op jit(solution)/shard_map/ppermute | solution.py:41
  58.2 12.5 %collective-permute-start.25 = (bf16[4,128,256]{2,1,0:T(8,128)(2,1)S(1)}, bf16[4,128,256]{2,1,0:T(8,128)(2,1)S(1)}, u32[]{:S(2)}, u32[]{:S(2)}) collective-permute-start(bf16[4,128,256]{2,1,0:T(8,128)(2,1)S(1)} %get-tuple-element.156), channel_id=1, source_target_pairs={{0,4},{4,8},{8,12},{12,0},{1,5},{5,9},{9,13},{13,1},{2,6},{6,10},{... | collective-permute-start | bytes 786440 | tf_op jit(solution)/shard_map/ppermute | solution.py:349
  60.1 12.7 %collective-permute-start.29 = (bf16[4,128,256]{2,1,0:T(8,128)(2,1)S(1)}, bf16[4,128,256]{2,1,0:T(8,128)(2,1)S(1)}, u32[]{:S(2)}, u32[]{:S(2)}) collective-permute-start(bf16[4,128,256]{2,1,0:T(8,128)(2,1)S(1)} %get-tuple-element.165), channel_id=1, source_target_pairs={{0,4},{4,8},{8,12},{12,0},{1,5},{5,9},{9,13},{13,1},{2,6},{6,10},{... | collective-permute-start | bytes 786440 | tf_op jit(solution)/shard_map/ppermute | solution.py:349
  60.2 12.7 %collective-permute-start.30 = (bf16[4,128,256]{2,1,0:T(8,128)(2,1)S(1)}, bf16[4,128,256]{2,1,0:T(8,128)(2,1)S(1)}, u32[]{:S(2)}, u32[]{:S(2)}) collective-permute-start(bf16[4,128,256]{2,1,0:T(8,128)(2,1)S(1)} %get-tuple-element.202.refs_8_), channel_id=1, source_target_pairs={{0,1},{1,0},{2,3},{3,2},{4,5},{5,4},{6,7},{7,6},{8,9},{9,8},{10,11... | collective-permute-start | bytes 786440 | tf_op jit(solution)/shard_map/ppermute | solution.py:41
  60.3 15.6 %collective-permute-start.38 = (bf16[4,128,256]{2,1,0:T(8,128)(2,1)S(1)}, bf16[4,128,256]{2,1,0:T(8,128)(2,1)S(1)}, u32[]{:S(2)}, u32[]{:S(2)}) collective-permute-start(bf16[4,128,256]{2,1,0:T(8,128)(2,1)S(1)} %get-tuple-element.202.refs_8_), channel_id=1, source_target_pairs={{0,2},{2,0},{1,3},{3,1},{4,6},{6,4},{5,7},{7,5},{8,10},{10,8},{9,1... | collective-permute-start | bytes 786440 | tf_op jit(solution)/shard_map/ppermute | solution.py:41
  75.0 12.0 %collective-permute-start.35 = (bf16[8,128,256]{2,1,0:T(8,128)(2,1)S(1)}, bf16[8,128,256]{2,1,0:T(8,128)(2,1)S(1)}, u32[]{:S(2)}, u32[]{:S(2)}) collective-permute-start(bf16[8,128,256]{2,1,0:T(8,128)(2,1)S(1)} %pack.11.refs_0_), channel_id=1, source_target_pairs={{0,2},{2,0},{1,3},{3,1},{4,6},{6,4},{5,7},{7,5},{8,10},{10,8},{9,1... | collective-permute-start | bytes 1572872 | tf_op jit(solution)/shard_map/ppermute | solution.py:41
  75.4 11.6 %collective-permute-start.34 = (bf16[8,128,256]{2,1,0:T(8,128)(2,1)S(1)}, bf16[8,128,256]{2,1,0:T(8,128)(2,1)S(1)}, u32[]{:S(2)}, u32[]{:S(2)}) collective-permute-start(bf16[8,128,256]{2,1,0:T(8,128)(2,1)S(1)} %pack.11.refs_0_), channel_id=1, source_target_pairs={{0,1},{1,0},{2,3},{3,2},{4,5},{5,4},{6,7},{7,6},{8,9},{9,8},{10,11... | collective-permute-start | bytes 1572872 | tf_op jit(solution)/shard_map/ppermute | solution.py:41
  (16 other events, 123.9 us)

commit v11 on v10

--- a/solution.py
+++ b/solution.py
@@ -184,7 +184,7 @@
             in_specs=[query_spec] + entries * 2,
             out_specs=query_spec,
         ),
-        compiler_params=pltpu.CompilerParams(vmem_limit_bytes=60 * 1024 * 1024),
+        compiler_params=pltpu.CompilerParams(vmem_limit_bytes=VMEM_LIMIT),
         cost_estimate=LITTLE,
         name="attend",
     )(slots, counts, queries, *[keys] * len(entries), *[values] * len(entries))
@@ -438,14 +438,16 @@
     done = (SWEEPS - 1) * CAP // GROUP
     keys, values = project(marks, gain, [late], key_weight, value_weight, GROUP, room, done, held)
 
+    result = attend(slots, counts, queries, keys, values)
+
     def whole(state):
         mine = fetch_all(store, asked >> 4, asked & (ENTRIES_EACH - 1))
-        marks = every_group(places, room // 4)
-        keys, values = project(marks, gain, [four_pieces(mine)], key_weight, value_weight, 4, room)
-        return jnp.zeros_like(state[0]), jnp.arange(total, dtype=jnp.int32), keys, values
-
-    state = lax.while_loop(lambda state: state[0] > 0, whole, (missing, slots, keys, values))
-    return attend(state[1], counts, queries, *state[2:])
+        marks = every_group(places, total // 4)
+        keys, values = project(marks, gain, [four_pieces(mine)], key_weight, value_weight, 4, total)
+        order = jnp.arange(total, dtype=jnp.int32)
+        return jnp.zeros_like(state[0]), attend(order, counts, queries, keys, values)
+
+    return lax.while_loop(lambda state: state[0] > 0, whole, (missing, result))[1]
 
 
 def requested(queries, key_weight, value_weight, enc_gain, store, nbr_owner, nbr_slot, nbr_count):

time: 112 us -> 123 us (1.098)
  local copies, waits for them, and re-layouts: 11.9 us -> 32.4 us
  Pallas kernels: 45.5 us -> 32.8 us
  waiting for transfers between devices: 32.3 us -> 35.5 us
    unnamed x16 -> x32, local copies, waits for them, and re-layouts: 6.06 us -> 26.2 us
    pallas_call x1, Pallas kernels: 10.9 us -> 5.27 us  [attend(): pl.pallas_call(attend_kernel, out_shape=jax.ShapeDtypeStruct(queries.shap...]
    pallas_call x6, Pallas kernels: 12.2 us -> 7.73 us  [pack(): pl.pallas_call(kernel, out_shape=tuple((jax.ShapeDtypeStruct((cap,) + poo...]
    pallas_call x3, Pallas kernels: 19.9 us -> 17.3 us  [project(): pl.pallas_call(kernel, out_shape=(out, out), grid_spec=pltpu.PrefetchScal...]
    ppermute x7, waiting for transfers between devices: 21.9 us -> 24.1 us  [onward(): lax.ppermute(value, 'seq', [(chip, (chip + 1) % size) for chip in range(s...]
  transfers between devices with their start and end apart: 32 -> 32, of which waited for: 14 -> 13; matrix products, arithmetic and copies ran while one was open for 6% -> 4% of each run, Pallas kernels for 25% -> 19%
where the time goes in v11:
time: 123 us; the launch traced here: 122 us
  waiting for transfers between devices  35.5 us (29%)
  Pallas kernels  32.8 us (27%)
  local copies, waits for them, and re-layouts  32.4 us (26%)
  starting transfers between devices  18 us (15%)
  other arithmetic  2.23 us (2%)
    unnamed x32, local copies, waits for them, and re-layouts  26.2 us
    ppermute x7, waiting for transfers between devices, onward(): lax.ppermute(value, 'seq', [(chip, (chip + 1) % size) for chip in range(s...  24.1 us
    pallas_call x3, Pallas kernels, project(): pl.pallas_call(kernel, out_shape=(out, out), grid_spec=pltpu.PrefetchScal...  17.3 us
    ppermute x22, waiting for transfers between devices, swapped(): return lax.ppermute(value, axis, [(0, 1), (1, 0)])  10.5 us
    ppermute x22, starting transfers between devices, swapped(): return lax.ppermute(value, axis, [(0, 1), (1, 0)])  10.4 us
    pallas_call x6, Pallas kernels, pack(): pl.pallas_call(kernel, out_shape=tuple((jax.ShapeDtypeStruct((cap,) + poo...  7.73 us
    ppermute x3, starting transfers between devices, exchanged_table(): lax.ppermute(codes, 'seq', [(chip, chip ^ offset) for chip in range(CHIPS)])  5.62 us
    pallas_call x1, Pallas kernels, attend(): pl.pallas_call(attend_kernel, out_shape=jax.ShapeDtypeStruct(queries.shap...  5.27 us
  transfers between devices with their start and end apart: 32, of which 13 were waited for; matrix products, arithmetic and copies ran while one was open for 4% of the time, Pallas kernels for 19%

profile of v11, /device:TPU:0, one launch (start us, length us, event | category | flops | bytes accessed | tf_op | source)
XLA Modules:
  0.0 122.1 jit_solution(13297490382336454355)
XLA Ops:
  1.0 2.1 %fusion.7 = (bf16[8,128,256]{2,1,0:T(8,128)(2,1)}, bf16[8,128,256]{2,1,0:T(8,128)(2,1)S(1)}) fusion(bf16[16,128,256]{2,1,0:T(8,128)(2,1)} %refs_0_.11), kind=kLoop, calls=%fused_computation.38 | loop fusion | bytes 2097152 | tf_op jit(solution)/shard_map/slice | solution.py:393
  3.1 5.0 %collective-permute-start.11 = (s32[24]{0:T(128)S(1)}, s32[24]{0:T(128)S(1)}, u32[]{:S(2)}, u32[]{:S(2)}) collective-permute-start(s32[24]{0:T(128)S(1)} %reshape.130), channel_id=1, source_target_pairs={{0,12},{4,8},{8,4},{12,0},{1,13},{5,9},{9,5},{13,1},{2,14},{6,10},... | collective-permute-start | bytes 296 | tf_op jit(solution)/shard_map/ppermute | solution.py:381
  8.7 1.7 %collective-permute-start.17 = (f32[1,256]{1,0:T(1,128)}, f32[1,256]{1,0:T(1,128)S(1)}, u32[]{:S(2)}, u32[]{:S(2)}) collective-permute-start(f32[1,256]{1,0:T(1,128)} %bitcast.39), channel_id=1, source_target_pairs={{0,2},{2,0},{1,3},{3,1},{4,6},{6,4},{5,7},{7,5},{8,10},{10,8},{9,1... | collective-permute-start | bytes 3080 | tf_op jit(solution)/shard_map/ppermute | solution.py:41
  17.4 2.5 %plan.1 = s32[8,128]{1,0:T(8,128)} custom-call(s32[1]{0:T(128)} %bitcast.2.place, s32[192]{0:T(256)} %reshape.131.table), custom_call_target="tpu_custom_call" | custom-call | tf_op jit(solution)/shard_map/plan/pallas_call | solution.py:285
  21.7 5.2 %collective-permute-done.13.refs_1_ = bf16[8,128,256]{2,1,0:T(8,128)(2,1)S(1)} collective-permute-done((bf16[8,128,256]{2,1,0:T(8,128)(2,1)S(1)}, bf16[8,128,256]{2,1,0:T(8,128)(2,1)S(1)}, u32[]{:S(2)}, u32[]{:S(2)}) %collective-permute-start.13) | collective-permute-done | bytes 524320 | tf_op jit(solution)/shard_map/ppermute | solution.py:349
  27.6 1.9 %pack.6 = (bf16[4,128,256]{2,1,0:T(8,128)(2,1)S(1)}, bf16[4,128,256]{2,1,0:T(8,128)(2,1)S(1)}) custom-call(s32[1024]{0:T(1024)S(1)} %bitcast.23, bf16[16,128,256]{2,1,0:T(8,128)(2,1)} %refs_0_.11, bf16[8,128,256]{2,1,0:T(8,128)(2,1)S(1)} %collective-permute-done.13.refs_1_), custom_call_target="tpu_custom_call" | custom-call | flops 1 | bytes 1 | tf_op jit(solution)/shard_map/pack/pallas_call | solution.py:313
  32.8 5.4 %collective-permute-done.14.refs_2_ = bf16[8,128,256]{2,1,0:T(8,128)(2,1)S(1)} collective-permute-done((bf16[8,128,256]{2,1,0:T(8,128)(2,1)}, bf16[8,128,256]{2,1,0:T(8,128)(2,1)S(1)}, u32[]{:S(2)}, u32[]{:S(2)}) %collective-permute-start.14) | collective-permute-done | bytes 524320 | tf_op jit(solution)/shard_map/ppermute | solution.py:349
  38.8 2.2 %pack.7 = (bf16[4,128,256]{2,1,0:T(8,128)(2,1)S(1)}, bf16[4,128,256]{2,1,0:T(8,128)(2,1)S(1)}) custom-call(s32[1024]{0:T(1024)S(1)} %bitcast.24, bf16[16,128,256]{2,1,0:T(8,128)(2,1)} %refs_0_.11, bf16[8,128,256]{2,1,0:T(8,128)(2,1)S(1)} %collective-permute-done.13.refs_1_, bf16[8,128,256]{2,1,0:T(8,128)(2,1)S(1)} %collective-permute-done.14.refs_2_), custom_call_target="tpu_custom_call" | custom-call | flops 1 | bytes 1 | tf_op jit(solution)/shard_map/pack/pallas_call | solution.py:313
  41.5 1.9 %collective-permute-done.19.refs_3_ = bf16[4,128,256]{2,1,0:T(8,128)(2,1)S(1)} collective-permute-done((bf16[4,128,256]{2,1,0:T(8,128)(2,1)S(1)}, bf16[4,128,256]{2,1,0:T(8,128)(2,1)S(1)}, u32[]{:S(2)}, u32[]{:S(2)}) %collective-permute-start.19) | collective-permute-done | bytes 262176 | tf_op jit(solution)/shard_map/ppermute | solution.py:349
  45.1 7.4 %collective-permute-done.22.refs_4_ = bf16[4,128,256]{2,1,0:T(8,128)(2,1)S(1)} collective-permute-done((bf16[4,128,256]{2,1,0:T(8,128)(2,1)S(1)}, bf16[4,128,256]{2,1,0:T(8,128)(2,1)S(1)}, u32[]{:S(2)}, u32[]{:S(2)}) %collective-permute-start.22) | collective-permute-done | bytes 262176 | tf_op jit(solution)/shard_map/ppermute | solution.py:349
  54.7 2.6 %collective-permute-done.26.refs_5_ = bf16[4,128,256]{2,1,0:T(8,128)(2,1)S(1)} collective-permute-done((bf16[4,128,256]{2,1,0:T(8,128)(2,1)S(1)}, bf16[4,128,256]{2,1,0:T(8,128)(2,1)S(1)}, u32[]{:S(2)}, u32[]{:S(2)}) %collective-permute-start.26) | collective-permute-done | bytes 262176 | tf_op jit(solution)/shard_map/ppermute | solution.py:349
  60.5 5.9 %collective-permute-done.33.refs_6_ = bf16[4,128,256]{2,1,0:T(8,128)(2,1)S(1)} collective-permute-done((bf16[4,128,256]{2,1,0:T(8,128)(2,1)S(1)}, bf16[4,128,256]{2,1,0:T(8,128)(2,1)S(1)}, u32[]{:S(2)}, u32[]{:S(2)}) %collective-permute-start.33) | collective-permute-done | bytes 262176 | tf_op jit(solution)/shard_map/ppermute | solution.py:41
  66.4 5.7 %project.5 = (bf16[28,128,1024]{2,1,0:T(8,128)(2,1)S(1)}, bf16[28,128,1024]{2,1,0:T(8,128)(2,1)S(1)}) custom-call(s32[32]{0:T(128)S(1)} %concatenate.23.marks_ref, f32[1,1024]{1,0:T(1,128)S(1)} %pad_maximum_fusion.gain_ref, bf16[4,128,256]{2,1,0:T(8,128)(2,1)S(1)} %get-tuple-element.174.refs_0_, bf16[4,128,256]{2,1,0:T(8,128)(2,1)S(1)} %collective-permute-done.15.refs_1_, ...), custom_call_target="tpu_custom_call" | custom-call | flops 1 | bytes 1 | tf_op jit(solution)/shard_map/project/pallas_call | solution.py:102
  78.2 7.4 %project.6 = (bf16[28,128,1024]{2,1,0:T(8,128)(2,1)S(1)}, bf16[28,128,1024]{2,1,0:T(8,128)(2,1)S(1)}) custom-call(s32[32]{0:T(128)S(1)} %concatenate.23.marks_ref, f32[1,1024]{1,0:T(1,128)S(1)} %pad_maximum_fusion.gain_ref, bf16[4,128,256]{2,1,0:T(8,128)(2,1)S(1)} %get-tuple-element.194.refs_0_, ...), custom_call_target="tpu_custom_call", output_to_operand_aliasing={{0}: (16, {}), {1}: (17, {})} | custom-call | flops 1 | bytes 1 | tf_op jit(solution)/shard_map/project/pallas_call | solution.py:102
  85.5 2.9 %copy-done = bf16[28,128,1024]{2,1,0:T(8,128)(2,1)} copy-done((bf16[28,128,1024]{2,1,0:T(8,128)(2,1)}, bf16[28,128,1024]{2,1,0:T(8,128)(2,1)S(1)}, u32[]{:S(2)}) %copy-start) | copy-done | bytes 7340056
  88.5 3.0 %copy-done.4 = bf16[28,128,1024]{2,1,0:T(8,128)(2,1)} copy-done((bf16[28,128,1024]{2,1,0:T(8,128)(2,1)}, bf16[28,128,1024]{2,1,0:T(8,128)(2,1)S(1)}, u32[]{:S(2)}) %copy-start.4) | copy-done | bytes 7340056
  93.4 3.1 %copy-done.1 = bf16[28,128,1024]{2,1,0:T(8,128)(2,1)S(1)} copy-done((bf16[28,128,1024]{2,1,0:T(8,128)(2,1)S(1)}, bf16[28,128,1024]{2,1,0:T(8,128)(2,1)}, u32[]{:S(2)}) %copy-start.1) | copy-done | bytes 7340056
  96.5 3.1 %copy-done.5 = bf16[28,128,1024]{2,1,0:T(8,128)(2,1)S(1)} copy-done((bf16[28,128,1024]{2,1,0:T(8,128)(2,1)S(1)}, bf16[28,128,1024]{2,1,0:T(8,128)(2,1)}, u32[]{:S(2)}) %copy-start.5) | copy-done | bytes 7340056
  99.5 4.2 %project.7 = (bf16[28,128,1024]{2,1,0:T(8,128)(2,1)S(1)}, bf16[28,128,1024]{2,1,0:T(8,128)(2,1)S(1)}) custom-call(s32[32]{0:T(128)S(1)} %concatenate.23.marks_ref, f32[1,1024]{1,0:T(1,128)S(1)} %pad_maximum_fusion.gain_ref, bf16[8,128,256]{2,1,0:T(8,128)(2,1)S(1)} %pack.11.refs_0_, ...), custom_call_target="tpu_custom_call", output_to_operand_aliasing={{0}: (8, {}), {1}: (9, {})} | custom-call | flops 1 | bytes 1 | tf_op jit(solution)/shard_map/project/pallas_call | solution.py:102
  103.8 2.9 %copy-done.2 = bf16[28,128,1024]{2,1,0:T(8,128)(2,1)} copy-done((bf16[28,128,1024]{2,1,0:T(8,128)(2,1)}, bf16[28,128,1024]{2,1,0:T(8,128)(2,1)S(1)}, u32[]{:S(2)}) %copy-start.2) | copy-done | bytes 7340056
  106.7 3.0 %copy-done.6 = bf16[28,128,1024]{2,1,0:T(8,128)(2,1)} copy-done((bf16[28,128,1024]{2,1,0:T(8,128)(2,1)}, bf16[28,128,1024]{2,1,0:T(8,128)(2,1)S(1)}, u32[]{:S(2)}) %copy-start.6) | copy-done | bytes 7340056
  109.7 3.1 %copy-done.3 = bf16[28,128,1024]{2,1,0:T(8,128)(2,1)S(1)} copy-done((bf16[28,128,1024]{2,1,0:T(8,128)(2,1)S(1)}, bf16[28,128,1024]{2,1,0:T(8,128)(2,1)}, u32[]{:S(2)}) %copy-start.3) | copy-done | bytes 7340056
  112.8 3.1 %copy-done.7 = bf16[28,128,1024]{2,1,0:T(8,128)(2,1)S(1)} copy-done((bf16[28,128,1024]{2,1,0:T(8,128)(2,1)S(1)}, bf16[28,128,1024]{2,1,0:T(8,128)(2,1)}, u32[]{:S(2)}) %copy-start.7) | copy-done | bytes 7340056
  115.8 5.3 %attend.3 = bf16[768,1024]{1,0:T(8,128)(2,1)} custom-call(s32[24]{0:T(128)S(1)} %gather_fusion.1, s32[12]{0:T(128)S(1)} %convert_reduce_fusion.counts, bf16[768,1024]{1,0:T(8,128)(2,1)S(1)} %copy-done.16, bf16[28,128,1024]{2,1,0:T(8,128)(2,1)S(1)} %copy-done.3, bf16[28,128,1024]{2,1,0:T(8,128)(2,1)S(1)} %copy-done.3, bf16[28,128,1024]{2,1,0:T(8,128)(2,1)S(1)} %copy-done.3, ...), custom_call_target="tpu_custom_call" | custom-call | flops 1 | bytes 1 | tf_op jit(solution)/shard_map/attend/pallas_call | solution.py:178
  (112 shorter events, 31.0 us)
Async XLA Ops:
  3.1 7.3 %collective-permute-start.11 = (s32[24]{0:T(128)S(1)}, s32[24]{0:T(128)S(1)}, u32[]{:S(2)}, u32[]{:S(2)}) collective-permute-start(s32[24]{0:T(128)S(1)} %reshape.130), channel_id=1, source_target_pairs={{0,12},{4,8},{8,4},{12,0},{1,13},{5,9},{9,5},{13,1},{2,14},{6,10},... | collective-permute-start | bytes 296 | tf_op jit(solution)/shard_map/ppermute | solution.py:381
  8.1 4.4 %collective-permute-start.10 = (s32[24]{0:T(128)S(1)}, s32[24]{0:T(128)S(1)}, u32[]{:S(2)}, u32[]{:S(2)}) collective-permute-start(s32[24]{0:T(128)S(1)} %reshape.130), channel_id=1, source_target_pairs={{0,8},{4,12},{8,0},{12,4},{1,9},{5,13},{9,1},{13,5},{2,10},{6,14},... | collective-permute-start | bytes 296 | tf_op jit(solution)/shard_map/ppermute | solution.py:381
  8.7 21.0 %collective-permute-start.17 = (f32[1,256]{1,0:T(1,128)}, f32[1,256]{1,0:T(1,128)S(1)}, u32[]{:S(2)}, u32[]{:S(2)}) collective-permute-start(f32[1,256]{1,0:T(1,128)} %bitcast.39), channel_id=1, source_target_pairs={{0,2},{2,0},{1,3},{3,1},{4,6},{6,4},{5,7},{7,5},{8,10},{10,8},{9,1... | collective-permute-start | bytes 3080 | tf_op jit(solution)/shard_map/ppermute | solution.py:41
  10.4 20.6 %collective-permute-start.16 = (f32[1,256]{1,0:T(1,128)}, f32[1,256]{1,0:T(1,128)S(1)}, u32[]{:S(2)}, u32[]{:S(2)}) collective-permute-start(f32[1,256]{1,0:T(1,128)} %bitcast.40), channel_id=1, source_target_pairs={{0,1},{1,0},{2,3},{3,2},{4,5},{5,4},{6,7},{7,6},{8,9},{9,8},{10,11... | collective-permute-start | bytes 3080 | tf_op jit(solution)/shard_map/ppermute | solution.py:41
  10.4 16.5 %collective-permute-start.13 = (bf16[8,128,256]{2,1,0:T(8,128)(2,1)S(1)}, bf16[8,128,256]{2,1,0:T(8,128)(2,1)S(1)}, u32[]{:S(2)}, u32[]{:S(2)}) collective-permute-start(bf16[8,128,256]{2,1,0:T(8,128)(2,1)S(1)} %get-tuple-element.138), channel_id=1, source_target_pairs={{0,4},{4,8},{8,12},{12,0},{1,5},{5,9},{9,13},{13,1},{2,6},{6,10},{... | collective-permute-start | bytes 1572872 | tf_op jit(solution)/shard_map/ppermute | solution.py:349
  14.1 24.0 %collective-permute-start.14 = (bf16[8,128,256]{2,1,0:T(8,128)(2,1)}, bf16[8,128,256]{2,1,0:T(8,128)(2,1)S(1)}, u32[]{:S(2)}, u32[]{:S(2)}) collective-permute-start(bf16[8,128,256]{2,1,0:T(8,128)(2,1)} %get-tuple-element.139), channel_id=1, source_target_pairs={{0,4},{4,8},{8,12},{12,0},{1,5},{5,9},{9,13},{13,1},{2,6},{6,10},{... | collective-permute-start | bytes 1572872 | tf_op jit(solution)/shard_map/ppermute | solution.py:349
  29.5 8.7 %collective-permute-start.15 = (bf16[4,128,256]{2,1,0:T(8,128)(2,1)S(1)}, bf16[4,128,256]{2,1,0:T(8,128)(2,1)S(1)}, u32[]{:S(2)}, u32[]{:S(2)}) collective-permute-start(bf16[4,128,256]{2,1,0:T(8,128)(2,1)S(1)} %get-tuple-element.174.refs_0_), channel_id=1, source_target_pairs={{0,1},{1,0},{2,3},{3,2},{4,5},{5,4},{6,7},{7,6},{8,9},{9,8},{10,11... | collective-permute-start | bytes 786440 | tf_op jit(solution)/shard_map/ppermute | solution.py:41
  31.8 11.7 %collective-permute-start.20 = (bf16[4,128,256]{2,1,0:T(8,128)(2,1)S(1)}, bf16[4,128,256]{2,1,0:T(8,128)(2,1)S(1)}, u32[]{:S(2)}, u32[]{:S(2)}) collective-permute-start(bf16[4,128,256]{2,1,0:T(8,128)(2,1)S(1)} %get-tuple-element.174.refs_0_), channel_id=1, source_target_pairs={{0,2},{2,0},{1,3},{3,1},{4,6},{6,4},{5,7},{7,5},{8,10},{10,8},{9,1... | collective-permute-start | bytes 786440 | tf_op jit(solution)/shard_map/ppermute | solution.py:41
  32.8 10.7 %collective-permute-start.19 = (bf16[4,128,256]{2,1,0:T(8,128)(2,1)S(1)}, bf16[4,128,256]{2,1,0:T(8,128)(2,1)S(1)}, u32[]{:S(2)}, u32[]{:S(2)}) collective-permute-start(bf16[4,128,256]{2,1,0:T(8,128)(2,1)S(1)} %get-tuple-element.143), channel_id=1, source_target_pairs={{0,4},{4,8},{8,12},{12,0},{1,5},{5,9},{9,13},{13,1},{2,6},{6,10},{... | collective-permute-start | bytes 786440 | tf_op jit(solution)/shard_map/ppermute | solution.py:349
  41.2 11.3 %collective-permute-start.23 = (bf16[4,128,256]{2,1,0:T(8,128)(2,1)S(1)}, bf16[4,128,256]{2,1,0:T(8,128)(2,1)S(1)}, u32[]{:S(2)}, u32[]{:S(2)}) collective-permute-start(bf16[4,128,256]{2,1,0:T(8,128)(2,1)S(1)} %get-tuple-element.178.refs_4_), channel_id=1, source_target_pairs={{0,2},{2,0},{1,3},{3,1},{4,6},{6,4},{5,7},{7,5},{8,10},{10,8},{9,1... | collective-permute-start | bytes 786440 | tf_op jit(solution)/shard_map/ppermute | solution.py:41
  41.5 10.9 %collective-permute-start.22 = (bf16[4,128,256]{2,1,0:T(8,128)(2,1)S(1)}, bf16[4,128,256]{2,1,0:T(8,128)(2,1)S(1)}, u32[]{:S(2)}, u32[]{:S(2)}) collective-permute-start(bf16[4,128,256]{2,1,0:T(8,128)(2,1)S(1)} %get-tuple-element.149), channel_id=1, source_target_pairs={{0,4},{4,8},{8,12},{12,0},{1,5},{5,9},{9,13},{13,1},{2,6},{6,10},{... | collective-permute-start | bytes 786440 | tf_op jit(solution)/shard_map/ppermute | solution.py:349
  44.3 8.2 %collective-permute-start.24 = (bf16[4,128,256]{2,1,0:T(8,128)(2,1)S(1)}, bf16[4,128,256]{2,1,0:T(8,128)(2,1)S(1)}, u32[]{:S(2)}, u32[]{:S(2)}) collective-permute-start(bf16[4,128,256]{2,1,0:T(8,128)(2,1)S(1)} %get-tuple-element.194.refs_0_), channel_id=1, source_target_pairs={{0,1},{1,0},{2,3},{3,2},{4,5},{5,4},{6,7},{7,6},{8,9},{9,8},{10,11... | collective-permute-start | bytes 786440 | tf_op jit(solution)/shard_map/ppermute | solution.py:41
  44.4 14.7 %collective-permute-start.27 = (bf16[4,128,256]{2,1,0:T(8,128)(2,1)S(1)}, bf16[4,128,256]{2,1,0:T(8,128)(2,1)S(1)}, u32[]{:S(2)}, u32[]{:S(2)}) collective-permute-start(bf16[4,128,256]{2,1,0:T(8,128)(2,1)S(1)} %get-tuple-element.194.refs_0_), channel_id=1, source_target_pairs={{0,2},{2,0},{1,3},{3,1},{4,6},{6,4},{5,7},{7,5},{8,10},{10,8},{9,1... | collective-permute-start | bytes 786440 | tf_op jit(solution)/shard_map/ppermute | solution.py:41
  45.0 12.4 %collective-permute-start.26 = (bf16[4,128,256]{2,1,0:T(8,128)(2,1)S(1)}, bf16[4,128,256]{2,1,0:T(8,128)(2,1)S(1)}, u32[]{:S(2)}, u32[]{:S(2)}) collective-permute-start(bf16[4,128,256]{2,1,0:T(8,128)(2,1)S(1)} %get-tuple-element.157), channel_id=1, source_target_pairs={{0,4},{4,8},{8,12},{12,0},{1,5},{5,9},{9,13},{13,1},{2,6},{6,10},{... | collective-permute-start | bytes 786440 | tf_op jit(solution)/shard_map/ppermute | solution.py:349
  54.0 5.0 %collective-permute-start.28 = (bf16[4,128,256]{2,1,0:T(8,128)(2,1)S(1)}, bf16[4,128,256]{2,1,0:T(8,128)(2,1)S(1)}, u32[]{:S(2)}, u32[]{:S(2)}) collective-permute-start(bf16[4,128,256]{2,1,0:T(8,128)(2,1)S(1)} %get-tuple-element.198.refs_4_), channel_id=1, source_target_pairs={{0,1},{1,0},{2,3},{3,2},{4,5},{5,4},{6,7},{7,6},{8,9},{9,8},{10,11... | collective-permute-start | bytes 786440 | tf_op jit(solution)/shard_map/ppermute | solution.py:41
  54.1 5.9 %collective-permute-start.31 = (bf16[4,128,256]{2,1,0:T(8,128)(2,1)S(1)}, bf16[4,128,256]{2,1,0:T(8,128)(2,1)S(1)}, u32[]{:S(2)}, u32[]{:S(2)}) collective-permute-start(bf16[4,128,256]{2,1,0:T(8,128)(2,1)S(1)} %collective-permute-done.20.refs_2_), channel_id=1, source_target_pairs={{0,1},{1,0},{2,3},{3,2},{4,5},{5,4},{6,7},{7,6},{8,9},{9,8},{10,11... | collective-permute-start | bytes 786440 | tf_op jit(solution)/shard_map/ppermute | solution.py:41
  54.6 5.5 %collective-permute-start.32 = (bf16[4,128,256]{2,1,0:T(8,128)(2,1)S(1)}, bf16[4,128,256]{2,1,0:T(8,128)(2,1)S(1)}, u32[]{:S(2)}, u32[]{:S(2)}) collective-permute-start(bf16[4,128,256]{2,1,0:T(8,128)(2,1)S(1)} %collective-permute-done.23.refs_6_), channel_id=1, source_target_pairs={{0,1},{1,0},{2,3},{3,2},{4,5},{5,4},{6,7},{7,6},{8,9},{9,8},{10,11... | collective-permute-start | bytes 786440 | tf_op jit(solution)/shard_map/ppermute | solution.py:41
  57.3 9.1 %collective-permute-start.33 = (bf16[4,128,256]{2,1,0:T(8,128)(2,1)S(1)}, bf16[4,128,256]{2,1,0:T(8,128)(2,1)S(1)}, u32[]{:S(2)}, u32[]{:S(2)}) collective-permute-start(bf16[4,128,256]{2,1,0:T(8,128)(2,1)S(1)} %get-tuple-element.198.refs_4_), channel_id=1, source_target_pairs={{0,2},{2,0},{1,3},{3,1},{4,6},{6,4},{5,7},{7,5},{8,10},{10,8},{9,1... | collective-permute-start | bytes 786440 | tf_op jit(solution)/shard_map/ppermute | solution.py:41
  59.0 13.1 %collective-permute-start.25 = (bf16[4,128,256]{2,1,0:T(8,128)(2,1)S(1)}, bf16[4,128,256]{2,1,0:T(8,128)(2,1)S(1)}, u32[]{:S(2)}, u32[]{:S(2)}) collective-permute-start(bf16[4,128,256]{2,1,0:T(8,128)(2,1)S(1)} %get-tuple-element.156), channel_id=1, source_target_pairs={{0,4},{4,8},{8,12},{12,0},{1,5},{5,9},{9,13},{13,1},{2,6},{6,10},{... | collective-permute-start | bytes 786440 | tf_op jit(solution)/shard_map/ppermute | solution.py:349
  60.0 13.7 %collective-permute-start.29 = (bf16[4,128,256]{2,1,0:T(8,128)(2,1)S(1)}, bf16[4,128,256]{2,1,0:T(8,128)(2,1)S(1)}, u32[]{:S(2)}, u32[]{:S(2)}) collective-permute-start(bf16[4,128,256]{2,1,0:T(8,128)(2,1)S(1)} %get-tuple-element.165), channel_id=1, source_target_pairs={{0,4},{4,8},{8,12},{12,0},{1,5},{5,9},{9,13},{13,1},{2,6},{6,10},{... | collective-permute-start | bytes 786440 | tf_op jit(solution)/shard_map/ppermute | solution.py:349
  60.1 13.7 %collective-permute-start.30 = (bf16[4,128,256]{2,1,0:T(8,128)(2,1)S(1)}, bf16[4,128,256]{2,1,0:T(8,128)(2,1)S(1)}, u32[]{:S(2)}, u32[]{:S(2)}) collective-permute-start(bf16[4,128,256]{2,1,0:T(8,128)(2,1)S(1)} %get-tuple-element.202.refs_8_), channel_id=1, source_target_pairs={{0,1},{1,0},{2,3},{3,2},{4,5},{5,4},{6,7},{7,6},{8,9},{9,8},{10,11... | collective-permute-start | bytes 786440 | tf_op jit(solution)/shard_map/ppermute | solution.py:41
  60.1 15.5 %collective-permute-start.38 = (bf16[4,128,256]{2,1,0:T(8,128)(2,1)S(1)}, bf16[4,128,256]{2,1,0:T(8,128)(2,1)S(1)}, u32[]{:S(2)}, u32[]{:S(2)}) collective-permute-start(bf16[4,128,256]{2,1,0:T(8,128)(2,1)S(1)} %get-tuple-element.202.refs_8_), channel_id=1, source_target_pairs={{0,2},{2,0},{1,3},{3,1},{4,6},{6,4},{5,7},{7,5},{8,10},{10,8},{9,1... | collective-permute-start | bytes 786440 | tf_op jit(solution)/shard_map/ppermute | solution.py:41
  74.7 16.7 %collective-permute-start.35 = (bf16[8,128,256]{2,1,0:T(8,128)(2,1)S(1)}, bf16[8,128,256]{2,1,0:T(8,128)(2,1)S(1)}, u32[]{:S(2)}, u32[]{:S(2)}) collective-permute-start(bf16[8,128,256]{2,1,0:T(8,128)(2,1)S(1)} %pack.11.refs_0_), channel_id=1, source_target_pairs={{0,2},{2,0},{1,3},{3,1},{4,6},{6,4},{5,7},{7,5},{8,10},{10,8},{9,1... | collective-permute-start | bytes 1572872 | tf_op jit(solution)/shard_map/ppermute | solution.py:41
  75.1 16.4 %collective-permute-start.34 = (bf16[8,128,256]{2,1,0:T(8,128)(2,1)S(1)}, bf16[8,128,256]{2,1,0:T(8,128)(2,1)S(1)}, u32[]{:S(2)}, u32[]{:S(2)}) collective-permute-start(bf16[8,128,256]{2,1,0:T(8,128)(2,1)S(1)} %pack.11.refs_0_), channel_id=1, source_target_pairs={{0,1},{1,0},{2,3},{3,2},{4,5},{5,4},{6,7},{7,6},{8,9},{9,8},{10,11... | collective-permute-start | bytes 1572872 | tf_op jit(solution)/shard_map/ppermute | solution.py:41
  (24 other events, 194.9 us)

commit v12 on v11

--- a/solution.py
+++ b/solution.py
@@ -16,7 +16,7 @@
 
 SEQ_SPEC = ("parts", "seq")
 FEATURES = ("mp", "rep")
-VMEM_LIMIT = 28 * 1024 * 1024
+MIB = 1024 * 1024
 
 CHIPS = 4
 ENTRIES_EACH = 16
@@ -114,7 +114,7 @@
             + [pltpu.SemaphoreType.DMA((2 * pieces,))],
         ),
         input_output_aliases={len(operands) - len(held) + i: i for i in range(len(held))},
-        compiler_params=pltpu.CompilerParams(vmem_limit_bytes=VMEM_LIMIT),
+        compiler_params=pltpu.CompilerParams(vmem_limit_bytes=20 * MIB),
         cost_estimate=LITTLE,
         name="project",
     )(*operands)
@@ -184,7 +184,7 @@
             in_specs=[query_spec] + entries * 2,
             out_specs=query_spec,
         ),
-        compiler_params=pltpu.CompilerParams(vmem_limit_bytes=VMEM_LIMIT),
+        compiler_params=pltpu.CompilerParams(vmem_limit_bytes=16 * MIB),
         cost_estimate=LITTLE,
         name="attend",
     )(slots, counts, queries, *[keys] * len(entries), *[values] * len(entries))
@@ -316,7 +316,7 @@
         grid_spec=pltpu.PrefetchScalarGridSpec(
             num_scalar_prefetch=1, in_specs=[in_vmem] * len(pool), out_specs=(in_vmem,) * len(lines)
         ),
-        compiler_params=pltpu.CompilerParams(vmem_limit_bytes=VMEM_LIMIT),
+        compiler_params=pltpu.CompilerParams(vmem_limit_bytes=12 * MIB),
         cost_estimate=LITTLE,
         name="pack",
     )(plan, *pool)

time: 123 us -> 125 us (1.016)
  Pallas kernels: 32.8 us -> 34.4 us
    pallas_call x3, Pallas kernels: 17.3 us -> 18.8 us  [project(): pl.pallas_call(kernel, out_shape=(out, out), grid_spec=pltpu.PrefetchScal...]
    unnamed x32 -> x30, local copies, waits for them, and re-layouts: 26.2 us -> 25.5 us
where the time goes in v12:
time: 125 us; the launch traced here: 124 us
  waiting for transfers between devices  36.1 us (29%)
  Pallas kernels  34.4 us (28%)
  local copies, waits for them, and re-layouts  31.6 us (25%)
  starting transfers between devices  18.1 us (14%)
  other arithmetic  2.23 us (2%)
    unnamed x30, local copies, waits for them, and re-layouts  25.5 us
    ppermute x7, waiting for transfers between devices, onward(): lax.ppermute(value, 'seq', [(chip, (chip + 1) % size) for chip in range(s...  24.7 us
    pallas_call x3, Pallas kernels, project(): pl.pallas_call(kernel, out_shape=(out, out), grid_spec=pltpu.PrefetchScal...  18.8 us
    ppermute x22, waiting for transfers between devices, swapped(): return lax.ppermute(value, axis, [(0, 1), (1, 0)])  10.4 us
    ppermute x22, starting transfers between devices, swapped(): return lax.ppermute(value, axis, [(0, 1), (1, 0)])  10.3 us
    pallas_call x6, Pallas kernels, pack(): pl.pallas_call(kernel, out_shape=tuple((jax.ShapeDtypeStruct((cap,) + poo...  7.77 us
    ppermute x3, starting transfers between devices, exchanged_table(): lax.ppermute(codes, 'seq', [(chip, chip ^ offset) for chip in range(CHIPS)])  5.62 us
    pallas_call x1, Pallas kernels, attend(): pl.pallas_call(attend_kernel, out_shape=jax.ShapeDtypeStruct(queries.shap...  5.27 us
  transfers between devices with their start and end apart: 32, of which 13 were waited for; matrix products, arithmetic and copies ran while one was open for 4% of the time, Pallas kernels for 19%

profile of v12, /device:TPU:0, one launch (start us, length us, event | category | flops | bytes accessed | tf_op | source)
XLA Modules:
  0.0 123.6 jit_solution(16609910759543717711)
XLA Ops:
  1.0 2.1 %fusion.7 = (bf16[8,128,256]{2,1,0:T(8,128)(2,1)}, bf16[8,128,256]{2,1,0:T(8,128)(2,1)S(1)}) fusion(bf16[16,128,256]{2,1,0:T(8,128)(2,1)} %refs_0_.11), kind=kLoop, calls=%fused_computation.38 | loop fusion | bytes 2097152 | tf_op jit(solution)/shard_map/slice | solution.py:393
  3.1 5.0 %collective-permute-start.11 = (s32[24]{0:T(128)S(1)}, s32[24]{0:T(128)S(1)}, u32[]{:S(2)}, u32[]{:S(2)}) collective-permute-start(s32[24]{0:T(128)S(1)} %reshape.130), channel_id=1, source_target_pairs={{0,12},{4,8},{8,4},{12,0},{1,13},{5,9},{9,5},{13,1},{2,14},{6,10},... | collective-permute-start | bytes 296 | tf_op jit(solution)/shard_map/ppermute | solution.py:381
  17.4 2.5 %plan.1 = s32[8,128]{1,0:T(8,128)} custom-call(s32[1]{0:T(128)} %bitcast.2.place, s32[192]{0:T(256)} %reshape.131.table), custom_call_target="tpu_custom_call" | custom-call | tf_op jit(solution)/shard_map/plan/pallas_call | solution.py:285
  21.6 5.3 %collective-permute-done.13.refs_1_ = bf16[8,128,256]{2,1,0:T(8,128)(2,1)S(1)} collective-permute-done((bf16[8,128,256]{2,1,0:T(8,128)(2,1)S(1)}, bf16[8,128,256]{2,1,0:T(8,128)(2,1)S(1)}, u32[]{:S(2)}, u32[]{:S(2)}) %collective-permute-start.13) | collective-permute-done | bytes 524320 | tf_op jit(solution)/shard_map/ppermute | solution.py:349
  27.6 1.9 %pack.6 = (bf16[4,128,256]{2,1,0:T(8,128)(2,1)S(1)}, bf16[4,128,256]{2,1,0:T(8,128)(2,1)S(1)}) custom-call(s32[1024]{0:T(1024)S(1)} %bitcast.23, bf16[16,128,256]{2,1,0:T(8,128)(2,1)} %refs_0_.11, bf16[8,128,256]{2,1,0:T(8,128)(2,1)S(1)} %collective-permute-done.13.refs_1_), custom_call_target="tpu_custom_call" | custom-call | flops 1 | bytes 1 | tf_op jit(solution)/shard_map/pack/pallas_call | solution.py:313
  32.8 5.3 %collective-permute-done.14.refs_2_ = bf16[8,128,256]{2,1,0:T(8,128)(2,1)S(1)} collective-permute-done((bf16[8,128,256]{2,1,0:T(8,128)(2,1)}, bf16[8,128,256]{2,1,0:T(8,128)(2,1)S(1)}, u32[]{:S(2)}, u32[]{:S(2)}) %collective-permute-start.14) | collective-permute-done | bytes 524320 | tf_op jit(solution)/shard_map/ppermute | solution.py:349
  38.8 2.2 %pack.7 = (bf16[4,128,256]{2,1,0:T(8,128)(2,1)S(1)}, bf16[4,128,256]{2,1,0:T(8,128)(2,1)S(1)}) custom-call(s32[1024]{0:T(1024)S(1)} %bitcast.24, bf16[16,128,256]{2,1,0:T(8,128)(2,1)} %refs_0_.11, bf16[8,128,256]{2,1,0:T(8,128)(2,1)S(1)} %collective-permute-done.13.refs_1_, bf16[8,128,256]{2,1,0:T(8,128)(2,1)S(1)} %collective-permute-done.14.refs_2_), custom_call_target="tpu_custom_call" | custom-call | flops 1 | bytes 1 | tf_op jit(solution)/shard_map/pack/pallas_call | solution.py:313
  41.5 1.9 %collective-permute-done.19.refs_3_ = bf16[4,128,256]{2,1,0:T(8,128)(2,1)S(1)} collective-permute-done((bf16[4,128,256]{2,1,0:T(8,128)(2,1)S(1)}, bf16[4,128,256]{2,1,0:T(8,128)(2,1)S(1)}, u32[]{:S(2)}, u32[]{:S(2)}) %collective-permute-start.19) | collective-permute-done | bytes 262176 | tf_op jit(solution)/shard_map/ppermute | solution.py:349
  45.2 7.3 %collective-permute-done.22.refs_4_ = bf16[4,128,256]{2,1,0:T(8,128)(2,1)S(1)} collective-permute-done((bf16[4,128,256]{2,1,0:T(8,128)(2,1)S(1)}, bf16[4,128,256]{2,1,0:T(8,128)(2,1)S(1)}, u32[]{:S(2)}, u32[]{:S(2)}) %collective-permute-start.22) | collective-permute-done | bytes 262176 | tf_op jit(solution)/shard_map/ppermute | solution.py:349
  54.0 3.3 %collective-permute-done.26.refs_5_ = bf16[4,128,256]{2,1,0:T(8,128)(2,1)S(1)} collective-permute-done((bf16[4,128,256]{2,1,0:T(8,128)(2,1)S(1)}, bf16[4,128,256]{2,1,0:T(8,128)(2,1)S(1)}, u32[]{:S(2)}, u32[]{:S(2)}) %collective-permute-start.26) | collective-permute-done | bytes 262176 | tf_op jit(solution)/shard_map/ppermute | solution.py:349
  57.3 1.8 %collective-permute-start.33 = (bf16[4,128,256]{2,1,0:T(8,128)(2,1)S(1)}, bf16[4,128,256]{2,1,0:T(8,128)(2,1)S(1)}, u32[]{:S(2)}, u32[]{:S(2)}) collective-permute-start(bf16[4,128,256]{2,1,0:T(8,128)(2,1)S(1)} %get-tuple-element.198.refs_4_), channel_id=1, source_target_pairs={{0,2},{2,0},{1,3},{3,1},{4,6},{6,4},{5,7},{7,5},{8,10},{10,8},{9,1... | collective-permute-start | bytes 786440 | tf_op jit(solution)/shard_map/ppermute | solution.py:41
  60.5 5.9 %collective-permute-done.33.refs_6_ = bf16[4,128,256]{2,1,0:T(8,128)(2,1)S(1)} collective-permute-done((bf16[4,128,256]{2,1,0:T(8,128)(2,1)S(1)}, bf16[4,128,256]{2,1,0:T(8,128)(2,1)S(1)}, u32[]{:S(2)}, u32[]{:S(2)}) %collective-permute-start.33) | collective-permute-done | bytes 262176 | tf_op jit(solution)/shard_map/ppermute | solution.py:41
  66.4 5.7 %project.5 = (bf16[28,128,1024]{2,1,0:T(8,128)(2,1)S(1)}, bf16[28,128,1024]{2,1,0:T(8,128)(2,1)S(1)}) custom-call(s32[32]{0:T(128)S(1)} %concatenate.23.marks_ref, f32[1,1024]{1,0:T(1,128)S(1)} %pad_maximum_fusion.gain_ref, bf16[4,128,256]{2,1,0:T(8,128)(2,1)S(1)} %get-tuple-element.174.refs_0_, bf16[4,128,256]{2,1,0:T(8,128)(2,1)S(1)} %collective-permute-done.15.refs_1_, ...), custom_call_target="tpu_custom_call" | custom-call | flops 1 | bytes 1 | tf_op jit(solution)/shard_map/project/pallas_call | solution.py:102
  78.2 7.4 %project.6 = (bf16[28,128,1024]{2,1,0:T(8,128)(2,1)S(1)}, bf16[28,128,1024]{2,1,0:T(8,128)(2,1)S(1)}) custom-call(s32[32]{0:T(128)S(1)} %concatenate.23.marks_ref, f32[1,1024]{1,0:T(1,128)S(1)} %pad_maximum_fusion.gain_ref, bf16[4,128,256]{2,1,0:T(8,128)(2,1)S(1)} %get-tuple-element.194.refs_0_, ...), custom_call_target="tpu_custom_call", output_to_operand_aliasing={{0}: (16, {}), {1}: (17, {})} | custom-call | flops 1 | bytes 1 | tf_op jit(solution)/shard_map/project/pallas_call | solution.py:102
  85.6 2.9 %copy-done = bf16[28,128,1024]{2,1,0:T(8,128)(2,1)} copy-done((bf16[28,128,1024]{2,1,0:T(8,128)(2,1)}, bf16[28,128,1024]{2,1,0:T(8,128)(2,1)S(1)}, u32[]{:S(2)}) %copy-start) | copy-done | bytes 7340056
  88.5 3.0 %copy-done.4 = bf16[28,128,1024]{2,1,0:T(8,128)(2,1)} copy-done((bf16[28,128,1024]{2,1,0:T(8,128)(2,1)}, bf16[28,128,1024]{2,1,0:T(8,128)(2,1)S(1)}, u32[]{:S(2)}) %copy-start.4) | copy-done | bytes 7340056
  93.4 3.1 %copy-done.1 = bf16[28,128,1024]{2,1,0:T(8,128)(2,1)S(1)} copy-done((bf16[28,128,1024]{2,1,0:T(8,128)(2,1)S(1)}, bf16[28,128,1024]{2,1,0:T(8,128)(2,1)}, u32[]{:S(2)}) %copy-start.1) | copy-done | bytes 7340056
  96.5 3.1 %copy-done.5 = bf16[28,128,1024]{2,1,0:T(8,128)(2,1)S(1)} copy-done((bf16[28,128,1024]{2,1,0:T(8,128)(2,1)S(1)}, bf16[28,128,1024]{2,1,0:T(8,128)(2,1)}, u32[]{:S(2)}) %copy-start.5) | copy-done | bytes 7340056
  99.5 5.7 %project.7 = (bf16[28,128,1024]{2,1,0:T(8,128)(2,1)S(1)}, bf16[28,128,1024]{2,1,0:T(8,128)(2,1)S(1)}) custom-call(s32[32]{0:T(128)S(1)} %concatenate.23.marks_ref, f32[1,1024]{1,0:T(1,128)S(1)} %pad_maximum_fusion.gain_ref, bf16[8,128,256]{2,1,0:T(8,128)(2,1)S(1)} %pack.11.refs_0_, ...), custom_call_target="tpu_custom_call", output_to_operand_aliasing={{0}: (8, {}), {1}: (9, {})} | custom-call | flops 1 | bytes 1 | tf_op jit(solution)/shard_map/project/pallas_call | solution.py:102
  105.3 2.9 %copy-done.2 = bf16[28,128,1024]{2,1,0:T(8,128)(2,1)} copy-done((bf16[28,128,1024]{2,1,0:T(8,128)(2,1)}, bf16[28,128,1024]{2,1,0:T(8,128)(2,1)S(1)}, u32[]{:S(2)}) %copy-start.2) | copy-done | bytes 7340056
  108.2 3.0 %copy-done.6 = bf16[28,128,1024]{2,1,0:T(8,128)(2,1)} copy-done((bf16[28,128,1024]{2,1,0:T(8,128)(2,1)}, bf16[28,128,1024]{2,1,0:T(8,128)(2,1)S(1)}, u32[]{:S(2)}) %copy-start.6) | copy-done | bytes 7340056
  111.2 3.1 %copy-done.3 = bf16[28,128,1024]{2,1,0:T(8,128)(2,1)S(1)} copy-done((bf16[28,128,1024]{2,1,0:T(8,128)(2,1)S(1)}, bf16[28,128,1024]{2,1,0:T(8,128)(2,1)}, u32[]{:S(2)}) %copy-start.3) | copy-done | bytes 7340056
  114.3 3.1 %copy-done.7 = bf16[28,128,1024]{2,1,0:T(8,128)(2,1)S(1)} copy-done((bf16[28,128,1024]{2,1,0:T(8,128)(2,1)S(1)}, bf16[28,128,1024]{2,1,0:T(8,128)(2,1)}, u32[]{:S(2)}) %copy-start.7) | copy-done | bytes 7340056
  117.3 5.3 %attend.3 = bf16[768,1024]{1,0:T(8,128)(2,1)} custom-call(s32[24]{0:T(128)S(1)} %gather_fusion.1, s32[12]{0:T(128)S(1)} %convert_reduce_fusion.counts, bf16[768,1024]{1,0:T(8,128)(2,1)S(1)} %copy-done.15, bf16[28,128,1024]{2,1,0:T(8,128)(2,1)S(1)} %copy-done.3, bf16[28,128,1024]{2,1,0:T(8,128)(2,1)S(1)} %copy-done.3, bf16[28,128,1024]{2,1,0:T(8,128)(2,1)S(1)} %copy-done.3, ...), custom_call_target="tpu_custom_call" | custom-call | flops 1 | bytes 1 | tf_op jit(solution)/shard_map/attend/pallas_call | solution.py:178
  (110 shorter events, 30.4 us)
Async XLA Ops:
  3.1 7.3 %collective-permute-start.11 = (s32[24]{0:T(128)S(1)}, s32[24]{0:T(128)S(1)}, u32[]{:S(2)}, u32[]{:S(2)}) collective-permute-start(s32[24]{0:T(128)S(1)} %reshape.130), channel_id=1, source_target_pairs={{0,12},{4,8},{8,4},{12,0},{1,13},{5,9},{9,5},{13,1},{2,14},{6,10},... | collective-permute-start | bytes 296 | tf_op jit(solution)/shard_map/ppermute | solution.py:381
  8.1 4.4 %collective-permute-start.10 = (s32[24]{0:T(128)S(1)}, s32[24]{0:T(128)S(1)}, u32[]{:S(2)}, u32[]{:S(2)}) collective-permute-start(s32[24]{0:T(128)S(1)} %reshape.130), channel_id=1, source_target_pairs={{0,8},{4,12},{8,0},{12,4},{1,9},{5,13},{9,1},{13,5},{2,10},{6,14},... | collective-permute-start | bytes 296 | tf_op jit(solution)/shard_map/ppermute | solution.py:381
  8.7 21.0 %collective-permute-start.17 = (f32[1,256]{1,0:T(1,128)}, f32[1,256]{1,0:T(1,128)S(1)}, u32[]{:S(2)}, u32[]{:S(2)}) collective-permute-start(f32[1,256]{1,0:T(1,128)} %bitcast.39), channel_id=1, source_target_pairs={{0,2},{2,0},{1,3},{3,1},{4,6},{6,4},{5,7},{7,5},{8,10},{10,8},{9,1... | collective-permute-start | bytes 3080 | tf_op jit(solution)/shard_map/ppermute | solution.py:41
  10.4 20.7 %collective-permute-start.16 = (f32[1,256]{1,0:T(1,128)}, f32[1,256]{1,0:T(1,128)S(1)}, u32[]{:S(2)}, u32[]{:S(2)}) collective-permute-start(f32[1,256]{1,0:T(1,128)} %bitcast.40), channel_id=1, source_target_pairs={{0,1},{1,0},{2,3},{3,2},{4,5},{5,4},{6,7},{7,6},{8,9},{9,8},{10,11... | collective-permute-start | bytes 3080 | tf_op jit(solution)/shard_map/ppermute | solution.py:41
  10.4 16.5 %collective-permute-start.13 = (bf16[8,128,256]{2,1,0:T(8,128)(2,1)S(1)}, bf16[8,128,256]{2,1,0:T(8,128)(2,1)S(1)}, u32[]{:S(2)}, u32[]{:S(2)}) collective-permute-start(bf16[8,128,256]{2,1,0:T(8,128)(2,1)S(1)} %get-tuple-element.138), channel_id=1, source_target_pairs={{0,4},{4,8},{8,12},{12,0},{1,5},{5,9},{9,13},{13,1},{2,6},{6,10},{... | collective-permute-start | bytes 1572872 | tf_op jit(solution)/shard_map/ppermute | solution.py:349
  14.1 24.0 %collective-permute-start.14 = (bf16[8,128,256]{2,1,0:T(8,128)(2,1)}, bf16[8,128,256]{2,1,0:T(8,128)(2,1)S(1)}, u32[]{:S(2)}, u32[]{:S(2)}) collective-permute-start(bf16[8,128,256]{2,1,0:T(8,128)(2,1)} %get-tuple-element.139), channel_id=1, source_target_pairs={{0,4},{4,8},{8,12},{12,0},{1,5},{5,9},{9,13},{13,1},{2,6},{6,10},{... | collective-permute-start | bytes 1572872 | tf_op jit(solution)/shard_map/ppermute | solution.py:349
  29.5 8.6 %collective-permute-start.15 = (bf16[4,128,256]{2,1,0:T(8,128)(2,1)S(1)}, bf16[4,128,256]{2,1,0:T(8,128)(2,1)S(1)}, u32[]{:S(2)}, u32[]{:S(2)}) collective-permute-start(bf16[4,128,256]{2,1,0:T(8,128)(2,1)S(1)} %get-tuple-element.174.refs_0_), channel_id=1, source_target_pairs={{0,1},{1,0},{2,3},{3,2},{4,5},{5,4},{6,7},{7,6},{8,9},{9,8},{10,11... | collective-permute-start | bytes 786440 | tf_op jit(solution)/shard_map/ppermute | solution.py:41
  31.8 11.6 %collective-permute-start.20 = (bf16[4,128,256]{2,1,0:T(8,128)(2,1)S(1)}, bf16[4,128,256]{2,1,0:T(8,128)(2,1)S(1)}, u32[]{:S(2)}, u32[]{:S(2)}) collective-permute-start(bf16[4,128,256]{2,1,0:T(8,128)(2,1)S(1)} %get-tuple-element.174.refs_0_), channel_id=1, source_target_pairs={{0,2},{2,0},{1,3},{3,1},{4,6},{6,4},{5,7},{7,5},{8,10},{10,8},{9,1... | collective-permute-start | bytes 786440 | tf_op jit(solution)/shard_map/ppermute | solution.py:41
  32.8 10.6 %collective-permute-start.19 = (bf16[4,128,256]{2,1,0:T(8,128)(2,1)S(1)}, bf16[4,128,256]{2,1,0:T(8,128)(2,1)S(1)}, u32[]{:S(2)}, u32[]{:S(2)}) collective-permute-start(bf16[4,128,256]{2,1,0:T(8,128)(2,1)S(1)} %get-tuple-element.143), channel_id=1, source_target_pairs={{0,4},{4,8},{8,12},{12,0},{1,5},{5,9},{9,13},{13,1},{2,6},{6,10},{... | collective-permute-start | bytes 786440 | tf_op jit(solution)/shard_map/ppermute | solution.py:349
  41.2 11.3 %collective-permute-start.23 = (bf16[4,128,256]{2,1,0:T(8,128)(2,1)S(1)}, bf16[4,128,256]{2,1,0:T(8,128)(2,1)S(1)}, u32[]{:S(2)}, u32[]{:S(2)}) collective-permute-start(bf16[4,128,256]{2,1,0:T(8,128)(2,1)S(1)} %get-tuple-element.178.refs_4_), channel_id=1, source_target_pairs={{0,2},{2,0},{1,3},{3,1},{4,6},{6,4},{5,7},{7,5},{8,10},{10,8},{9,1... | collective-permute-start | bytes 786440 | tf_op jit(solution)/shard_map/ppermute | solution.py:41
  41.5 10.9 %collective-permute-start.22 = (bf16[4,128,256]{2,1,0:T(8,128)(2,1)S(1)}, bf16[4,128,256]{2,1,0:T(8,128)(2,1)S(1)}, u32[]{:S(2)}, u32[]{:S(2)}) collective-permute-start(bf16[4,128,256]{2,1,0:T(8,128)(2,1)S(1)} %get-tuple-element.149), channel_id=1, source_target_pairs={{0,4},{4,8},{8,12},{12,0},{1,5},{5,9},{9,13},{13,1},{2,6},{6,10},{... | collective-permute-start | bytes 786440 | tf_op jit(solution)/shard_map/ppermute | solution.py:349
  44.3 8.2 %collective-permute-start.24 = (bf16[4,128,256]{2,1,0:T(8,128)(2,1)S(1)}, bf16[4,128,256]{2,1,0:T(8,128)(2,1)S(1)}, u32[]{:S(2)}, u32[]{:S(2)}) collective-permute-start(bf16[4,128,256]{2,1,0:T(8,128)(2,1)S(1)} %get-tuple-element.194.refs_0_), channel_id=1, source_target_pairs={{0,1},{1,0},{2,3},{3,2},{4,5},{5,4},{6,7},{7,6},{8,9},{9,8},{10,11... | collective-permute-start | bytes 786440 | tf_op jit(solution)/shard_map/ppermute | solution.py:41
  44.4 14.7 %collective-permute-start.27 = (bf16[4,128,256]{2,1,0:T(8,128)(2,1)S(1)}, bf16[4,128,256]{2,1,0:T(8,128)(2,1)S(1)}, u32[]{:S(2)}, u32[]{:S(2)}) collective-permute-start(bf16[4,128,256]{2,1,0:T(8,128)(2,1)S(1)} %get-tuple-element.194.refs_0_), channel_id=1, source_target_pairs={{0,2},{2,0},{1,3},{3,1},{4,6},{6,4},{5,7},{7,5},{8,10},{10,8},{9,1... | collective-permute-start | bytes 786440 | tf_op jit(solution)/shard_map/ppermute | solution.py:41
  45.0 12.3 %collective-permute-start.26 = (bf16[4,128,256]{2,1,0:T(8,128)(2,1)S(1)}, bf16[4,128,256]{2,1,0:T(8,128)(2,1)S(1)}, u32[]{:S(2)}, u32[]{:S(2)}) collective-permute-start(bf16[4,128,256]{2,1,0:T(8,128)(2,1)S(1)} %get-tuple-element.157), channel_id=1, source_target_pairs={{0,4},{4,8},{8,12},{12,0},{1,5},{5,9},{9,13},{13,1},{2,6},{6,10},{... | collective-permute-start | bytes 786440 | tf_op jit(solution)/shard_map/ppermute | solution.py:349
  53.3 5.7 %collective-permute-start.28 = (bf16[4,128,256]{2,1,0:T(8,128)(2,1)S(1)}, bf16[4,128,256]{2,1,0:T(8,128)(2,1)S(1)}, u32[]{:S(2)}, u32[]{:S(2)}) collective-permute-start(bf16[4,128,256]{2,1,0:T(8,128)(2,1)S(1)} %get-tuple-element.198.refs_4_), channel_id=1, source_target_pairs={{0,1},{1,0},{2,3},{3,2},{4,5},{5,4},{6,7},{7,6},{8,9},{9,8},{10,11... | collective-permute-start | bytes 786440 | tf_op jit(solution)/shard_map/ppermute | solution.py:41
  53.4 6.7 %collective-permute-start.31 = (bf16[4,128,256]{2,1,0:T(8,128)(2,1)S(1)}, bf16[4,128,256]{2,1,0:T(8,128)(2,1)S(1)}, u32[]{:S(2)}, u32[]{:S(2)}) collective-permute-start(bf16[4,128,256]{2,1,0:T(8,128)(2,1)S(1)} %collective-permute-done.20.refs_2_), channel_id=1, source_target_pairs={{0,1},{1,0},{2,3},{3,2},{4,5},{5,4},{6,7},{7,6},{8,9},{9,8},{10,11... | collective-permute-start | bytes 786440 | tf_op jit(solution)/shard_map/ppermute | solution.py:41
  53.9 6.3 %collective-permute-start.32 = (bf16[4,128,256]{2,1,0:T(8,128)(2,1)S(1)}, bf16[4,128,256]{2,1,0:T(8,128)(2,1)S(1)}, u32[]{:S(2)}, u32[]{:S(2)}) collective-permute-start(bf16[4,128,256]{2,1,0:T(8,128)(2,1)S(1)} %collective-permute-done.23.refs_6_), channel_id=1, source_target_pairs={{0,1},{1,0},{2,3},{3,2},{4,5},{5,4},{6,7},{7,6},{8,9},{9,8},{10,11... | collective-permute-start | bytes 786440 | tf_op jit(solution)/shard_map/ppermute | solution.py:41
  57.3 9.1 %collective-permute-start.33 = (bf16[4,128,256]{2,1,0:T(8,128)(2,1)S(1)}, bf16[4,128,256]{2,1,0:T(8,128)(2,1)S(1)}, u32[]{:S(2)}, u32[]{:S(2)}) collective-permute-start(bf16[4,128,256]{2,1,0:T(8,128)(2,1)S(1)} %get-tuple-element.198.refs_4_), channel_id=1, source_target_pairs={{0,2},{2,0},{1,3},{3,1},{4,6},{6,4},{5,7},{7,5},{8,10},{10,8},{9,1... | collective-permute-start | bytes 786440 | tf_op jit(solution)/shard_map/ppermute | solution.py:41
  59.1 13.1 %collective-permute-start.25 = (bf16[4,128,256]{2,1,0:T(8,128)(2,1)S(1)}, bf16[4,128,256]{2,1,0:T(8,128)(2,1)S(1)}, u32[]{:S(2)}, u32[]{:S(2)}) collective-permute-start(bf16[4,128,256]{2,1,0:T(8,128)(2,1)S(1)} %get-tuple-element.156), channel_id=1, source_target_pairs={{0,4},{4,8},{8,12},{12,0},{1,5},{5,9},{9,13},{13,1},{2,6},{6,10},{... | collective-permute-start | bytes 786440 | tf_op jit(solution)/shard_map/ppermute | solution.py:349
  60.0 13.8 %collective-permute-start.29 = (bf16[4,128,256]{2,1,0:T(8,128)(2,1)S(1)}, bf16[4,128,256]{2,1,0:T(8,128)(2,1)S(1)}, u32[]{:S(2)}, u32[]{:S(2)}) collective-permute-start(bf16[4,128,256]{2,1,0:T(8,128)(2,1)S(1)} %get-tuple-element.165), channel_id=1, source_target_pairs={{0,4},{4,8},{8,12},{12,0},{1,5},{5,9},{9,13},{13,1},{2,6},{6,10},{... | collective-permute-start | bytes 786440 | tf_op jit(solution)/shard_map/ppermute | solution.py:349
  60.1 13.7 %collective-permute-start.30 = (bf16[4,128,256]{2,1,0:T(8,128)(2,1)S(1)}, bf16[4,128,256]{2,1,0:T(8,128)(2,1)S(1)}, u32[]{:S(2)}, u32[]{:S(2)}) collective-permute-start(bf16[4,128,256]{2,1,0:T(8,128)(2,1)S(1)} %get-tuple-element.202.refs_8_), channel_id=1, source_target_pairs={{0,1},{1,0},{2,3},{3,2},{4,5},{5,4},{6,7},{7,6},{8,9},{9,8},{10,11... | collective-permute-start | bytes 786440 | tf_op jit(solution)/shard_map/ppermute | solution.py:41
  60.2 15.5 %collective-permute-start.38 = (bf16[4,128,256]{2,1,0:T(8,128)(2,1)S(1)}, bf16[4,128,256]{2,1,0:T(8,128)(2,1)S(1)}, u32[]{:S(2)}, u32[]{:S(2)}) collective-permute-start(bf16[4,128,256]{2,1,0:T(8,128)(2,1)S(1)} %get-tuple-element.202.refs_8_), channel_id=1, source_target_pairs={{0,2},{2,0},{1,3},{3,1},{4,6},{6,4},{5,7},{7,5},{8,10},{10,8},{9,1... | collective-permute-start | bytes 786440 | tf_op jit(solution)/shard_map/ppermute | solution.py:41
  74.8 16.7 %collective-permute-start.35 = (bf16[8,128,256]{2,1,0:T(8,128)(2,1)S(1)}, bf16[8,128,256]{2,1,0:T(8,128)(2,1)S(1)}, u32[]{:S(2)}, u32[]{:S(2)}) collective-permute-start(bf16[8,128,256]{2,1,0:T(8,128)(2,1)S(1)} %pack.11.refs_0_), channel_id=1, source_target_pairs={{0,2},{2,0},{1,3},{3,1},{4,6},{6,4},{5,7},{7,5},{8,10},{10,8},{9,1... | collective-permute-start | bytes 1572872 | tf_op jit(solution)/shard_map/ppermute | solution.py:41
  75.1 16.3 %collective-permute-start.34 = (bf16[8,128,256]{2,1,0:T(8,128)(2,1)S(1)}, bf16[8,128,256]{2,1,0:T(8,128)(2,1)S(1)}, u32[]{:S(2)}, u32[]{:S(2)}) collective-permute-start(bf16[8,128,256]{2,1,0:T(8,128)(2,1)S(1)} %pack.11.refs_0_), channel_id=1, source_target_pairs={{0,1},{1,0},{2,3},{3,2},{4,5},{5,4},{6,7},{7,6},{8,9},{9,8},{10,11... | collective-permute-start | bytes 1572872 | tf_op jit(solution)/shard_map/ppermute | solution.py:41
  (23 other events, 189.1 us)
